TPU v7x, 512 devices: a whole 4x4x16 slice. The times are simulated.
512 devices in a mesh: ctx: 64 (over z, y_hi, core), tp: 8 (over x, y_lo).
Axes of the slice: x: 4, y: 4 (y_hi: 2, y_lo: 2; y = y_hi * 2 + y_lo), z: 16, core: 2. Of those that a mesh axis runs over, the one named last changes fastest.
Arguments:
- out_grad: bfloat16 [16384, 4096], P('ctx', 'tp'), may hold values from -6 to 6
- out_weight: bfloat16 [8192, 4096], P('tp', 'ctx'), may hold values from -0.0625 to 0.0625
- signal: bfloat16 [16384, 8192], P('ctx', 'tp'), may hold values from -6 to 6
- gate_input: bfloat16 [16384, 8192], P('ctx', 'tp'), may hold values from -6 to 6
- filter_taps: float32 [128, 8192], P(None, ('tp', 'ctx')), may hold values from -0.5 to 0.5
Outputs:
- signal_grad: bfloat16 [16384, 8192], P('ctx', 'tp')
- gate_grad: bfloat16 [16384, 8192], P('ctx', 'tp')
- filter_grad: float32 [128, 8192], P(None, ('tp', 'ctx'))
All inputs are finite; a program needn't handle non-finite values.
Results may differ from a plain program's by a relative error of at most 0.0057.
Values may be sent and summed in bfloat16 or wider, within the bound.
No kernel may reach another device: no remote copies, remote signals or barrier semaphores. Data moves between devices by JAX's collectives and lax.ppermute only.
A program may use at most 128 MiB of HBM per device.

v0:
```python
import jax
import jax.numpy as jnp
from jax import lax
from jax.sharding import PartitionSpec as P

K = 128
SPAN = 8192


def banded(band_row):
    count, span = band_row.shape
    width = (span - 1) // 2
    repeated = jnp.broadcast_to(band_row[:, None, :], (count, width, span)).reshape(
        count, width * span
    )
    return repeated[:, : width * 2 * width].reshape(count, width, 2 * width)


def split_pair(matrix):
    upper = lax.optimization_barrier(matrix.astype(jnp.bfloat16))
    lower = (matrix - upper.astype(jnp.float32)).astype(jnp.bfloat16)
    return (upper, lower)


def band_apply(window, matrix):
    upper, lower = split_pair(matrix)
    first = jnp.einsum("cbj,cij->cbi", window, upper, preferred_element_type=jnp.float32)
    second = jnp.einsum("cbj,cij->cbi", window, lower, preferred_element_type=jnp.float32)
    return first + second


def blocks_before(blocks, rim_rows, period):
    shifted = jnp.concatenate([rim_rows[:, None, :], blocks[:, :-1, :]], axis=1)
    positions = lax.iota(jnp.int32, blocks.shape[1])
    retain = positions % period != 0
    return jnp.where(retain[None, :, None], shifted, jnp.zeros_like(shifted))


def blocks_after(blocks, rim_rows, period):
    shifted = jnp.concatenate([blocks[:, 1:, :], rim_rows[:, None, :]], axis=1)
    positions = lax.iota(jnp.int32, blocks.shape[1])
    retain = (positions + 1) % period != 0
    return jnp.where(retain[None, :, None], shifted, jnp.zeros_like(shifted))


def first_section(sig_blocks, sig_before, mix_blocks, gate_blocks, taps):
    count, width = taps.shape
    window = jnp.concatenate([sig_before, sig_blocks], axis=2)
    reverse_row = jnp.concatenate(
        [jnp.zeros((count, 1), jnp.float32), taps[:, ::-1], jnp.zeros((count, width), jnp.float32)],
        axis=1,
    )
    conv_out = band_apply(window, banded(reverse_row))
    mix_wide = mix_blocks.astype(jnp.float32)
    gate_part = (mix_wide * conv_out).astype(jnp.bfloat16)
    conv_grad = (mix_wide * gate_blocks.astype(jnp.float32)).astype(jnp.bfloat16)
    return (gate_part, conv_grad)


def second_section(grad_blocks, grad_after, sig_blocks, sig_before, taps):
    count, width = taps.shape
    grad_window = jnp.concatenate([grad_blocks, grad_after], axis=2)
    forward_row = jnp.concatenate([taps, jnp.zeros((count, width + 1), jnp.float32)], axis=1)
    sig_part = band_apply(grad_window, banded(forward_row)).astype(jnp.bfloat16)
    window = jnp.concatenate([sig_before, sig_blocks], axis=2)
    product = jnp.einsum("cbi,cbj->cij", grad_blocks, window, preferred_element_type=jnp.float32)
    spread = jnp.concatenate(
        [product.reshape(count, width * 2 * width), jnp.zeros((count, width), jnp.float32)], axis=1
    )
    spread = spread.reshape(count, width, 2 * width + 1)
    tap_grads = jnp.sum(spread[:, :, 1 : width + 1], axis=1)[:, ::-1]
    return (sig_part, tap_grads)


def by_groups(section, arrays, channels):
    group_size = min(channels, 64)
    group_count = channels // group_size
    shaped = tuple(
        (values.reshape((group_count, group_size) + values.shape[1:]) for values in arrays)
    )
    results = lax.map(lambda parts: section(*parts), shaped)
    return tuple((values.reshape((channels,) + values.shape[2:]) for values in results))


def weight_product(full_grad, out_weight):
    summed = lax.dot_general(
        lax.all_gather(out_weight, "ctx", axis=1, tiled=True),
        full_grad,
        (((1,), (1,)), ((), ())),
        preferred_element_type=jnp.float32,
    )
    return summed.astype(jnp.bfloat16)


def on_device(out_grad, out_weight, signal, gate_input, filter_taps):
    tok_count = signal.shape[0]
    period = min(SPAN, tok_count * lax.axis_size("ctx")) // K
    full_grad = lax.all_gather(out_grad, "tp", axis=1, tiled=True)
    signal_cols = signal.T
    gate_cols = gate_input.T
    mixed = weight_product(full_grad, out_weight)
    mix_here, gate_here, signal_here = (
        lax.all_to_all(mixed, "ctx", split_axis=0, concat_axis=1, tiled=True),
        lax.all_to_all(gate_cols, "ctx", split_axis=0, concat_axis=1, tiled=True),
        lax.all_to_all(signal_cols, "ctx", split_axis=0, concat_axis=1, tiled=True),
    )
    owned = mix_here.shape[0]
    total_tokens = mix_here.shape[1]
    block_count = total_tokens // K
    taps = filter_taps.T
    empty_rim = jnp.zeros((owned, K), jnp.bfloat16)
    sig_blocks = signal_here.reshape(owned, block_count, K)
    sig_before = blocks_before(sig_blocks, empty_rim, period)
    gate_blocks, grad_blocks = by_groups(
        first_section,
        (
            sig_blocks,
            sig_before,
            mix_here.reshape(owned, block_count, K),
            gate_here.reshape(owned, block_count, K),
            taps,
        ),
        owned,
    )
    grad_after = blocks_after(grad_blocks, empty_rim, period)
    sig_blocks_grad, tap_grads = by_groups(
        second_section, (grad_blocks, grad_after, sig_blocks, sig_before, taps), owned
    )
    sig_back, gate_back = (
        lax.all_to_all(
            sig_blocks_grad.reshape(owned, total_tokens),
            "ctx",
            split_axis=1,
            concat_axis=0,
            tiled=True,
        ),
        lax.all_to_all(
            gate_blocks.reshape(owned, total_tokens), "ctx", split_axis=1, concat_axis=0, tiled=True
        ),
    )
    filter_grad = tap_grads.T
    return (sig_back.T, gate_back.T, filter_grad)


def solution(mesh):
    in_specs = (
        P("ctx", "tp"),
        P("tp", "ctx"),
        P("ctx", "tp"),
        P("ctx", "tp"),
        P(None, ("tp", "ctx")),
    )
    out_specs = (P("ctx", "tp"), P("ctx", "tp"), P(None, ("tp", "ctx")))
    return jax.shard_map(
        on_device, mesh=mesh, in_specs=in_specs, out_specs=out_specs, check_vma=False
    )
```

profile of v0, /device:TPU:1, one launch (start us, length us, event | category | flops | bytes accessed | tf_op | source)
XLA Modules:
  0.0 424.4 jit_solution(666133843000146612)
XLA Ops:
  8.6 2.0 copy.15
  10.7 19.8 %all-to-all-start.1 = ((bf16[64,16,256]{2,1,0:T(8,128)(2,1)}), bf16[64,16,256]{2,1,0:T(8,128)(2,1)S(1)}, u32[]{:S(2)}, u32[]{:S(2)}) async-start(bf16[64,16,256]{2,1,0:T(8,128)(2,1)} %bitcast.3), calls=%async_computation.1 | async-start | bytes 1048576 | tf_op jit(solution)/shard_map/all_to_all | solution.py:104
  30.5 48.6 %all-gather.5.cloned.1.call-done = bf16[256,4096]{1,0:T(8,128)(2,1)} async-done(((bf16[256,512]{1,0:T(8,128)(2,1)}), bf16[256,4096]{1,0:T(8,128)(2,1)}) %all-gather.5.cloned.1.call-update) | async-done | bytes 2097168 | tf_op jit(solution)/shard_map/all_gather | solution.py:98
  79.1 169.6 %all-gather.3.cloned.1.call-done = bf16[1024,4096]{0,1:T(8,128)(2,1)} async-done(((bf16[1024,64]{0,1:T(8,128)(2,1)}), bf16[1024,4096]{0,1:T(8,128)(2,1)}) %all-gather.3.cloned.1.call-update) | async-done | bytes 8388624 | tf_op jit(solution)/shard_map/all_gather | solution.py:87
  248.7 7.2 %convolution_convert_fusion = bf16[1024,256]{1,0:T(8,128)(2,1)} fusion(bf16[1024,4096]{0,1:T(8,128)(2,1)} %all-gather.3.cloned.1.call-done, bf16[256,4096]{1,0:T(8,128)(2,1)} %all-gather.5.cloned.1.call-done), kind=kOutput, calls=%fused_computation.10 | convolution fusion | flops 2147745792 | bytes 11010048 | tf_op jit(solution)/shard_map/dot_general | solution.py:86
  255.9 8.6 %all-to-all-start = ((bf16[64,16,256]{2,1,0:T(8,128)(2,1)}), bf16[64,16,256]{2,1,0:T(8,128)(2,1)}, u32[]{:S(2)}, u32[]{:S(2)}) async-start(bf16[64,16,256]{2,1,0:T(8,128)(2,1)} %bitcast), calls=%async_computation | async-start | bytes 1048576 | tf_op jit(solution)/shard_map/all_to_all | solution.py:103
  265.7 2.5 reshape.110
  268.2 1.6 slice-done
  270.5 27.9 %all-to-all-done = bf16[64,16,256]{2,1,0:T(8,128)(2,1)} async-done(((bf16[64,16,256]{2,1,0:T(8,128)(2,1)}), bf16[64,16,256]{2,1,0:T(8,128)(2,1)}, u32[]{:S(2)}, u32[]{:S(2)}) %all-to-all-start) | async-done | bytes 524320 | tf_op jit(solution)/shard_map/all_to_all | solution.py:103
  298.4 5.1 %all-to-all-start.3 = ((bf16[64,16,256]{2,1,0:T(8,128)(2,1)}), bf16[64,16,256]{2,1,0:T(8,128)(2,1)}, u32[]{:S(2)}, u32[]{:S(2)}) async-start(bf16[64,16,256]{2,1,0:T(8,128)(2,1)} %bitcast.53), calls=%async_computation.3 | async-start | bytes 1048576 | tf_op jit(solution)/shard_map/all_to_all | solution.py:105
  307.8 1.6 copy.14
  309.4 1.3 reshape.117
  310.7 1.7 multiply_convert_fusion
  315.6 21.9 %all-to-all-done.3 = bf16[64,16,256]{2,1,0:T(8,128)(2,1)} async-done(((bf16[64,16,256]{2,1,0:T(8,128)(2,1)}), bf16[64,16,256]{2,1,0:T(8,128)(2,1)}, u32[]{:S(2)}, u32[]{:S(2)}) %all-to-all-start.3) | async-done | bytes 524320 | tf_op jit(solution)/shard_map/all_to_all | solution.py:105
  337.5 5.0 %all-to-all-start.2 = ((bf16[16,64,256]{2,0,1:T(8,128)(2,1)}), bf16[16,64,256]{2,0,1:T(8,128)(2,1)S(1)}, u32[]{:S(2)}, u32[]{:S(2)}) async-start(bf16[16,64,256]{2,0,1:T(8,128)(2,1)} %copy.17), calls=%async_computation.2 | async-start | bytes 1048576 | tf_op jit(solution)/shard_map/all_to_all | solution.py:130
  342.7 1.8 broadcast_in_dim.49
  344.5 2.9 reshape.113
  348.3 1.4 fusion
  354.4 22.0 %all-to-all-done.2 = bf16[16,64,256]{2,0,1:T(8,128)(2,1)S(1)} async-done(((bf16[16,64,256]{2,0,1:T(8,128)(2,1)}), bf16[16,64,256]{2,0,1:T(8,128)(2,1)S(1)}, u32[]{:S(2)}, u32[]{:S(2)}) %all-to-all-start.2) | async-done | bytes 524320 | tf_op jit(solution)/shard_map/all_to_all | solution.py:130
  376.4 5.1 %all-to-all-start.4 = ((bf16[16,64,256]{2,0,1:T(8,128)(2,1)}), bf16[16,64,256]{2,0,1:T(8,128)(2,1)}, u32[]{:S(2)}, u32[]{:S(2)}) async-start(bf16[16,64,256]{2,0,1:T(8,128)(2,1)} %copy.20), calls=%async_computation.4 | async-start | bytes 1048576 | tf_op jit(solution)/shard_map/all_to_all | solution.py:137
  383.5 3.6 reshape.116
  387.1 1.9 slice_reduce_fusion
  390.7 24.8 %all-to-all-done.4 = bf16[16,64,256]{2,0,1:T(8,128)(2,1)} async-done(((bf16[16,64,256]{2,0,1:T(8,128)(2,1)}), bf16[16,64,256]{2,0,1:T(8,128)(2,1)}, u32[]{:S(2)}, u32[]{:S(2)}) %all-to-all-start.4) | async-done | bytes 524320 | tf_op jit(solution)/shard_map/all_to_all | solution.py:137
  415.5 2.0 copy.23
  (60 shorter events, 20.0 us)
Async XLA Ops:
  7.2 72.0 %all-gather.5.cloned.1.call-start = ((), (), s32[]{:S(2)}) async-start(), calls=%async_computation.6 | async-start | bytes 2359296 | tf_op jit(solution)/shard_map/all_gather | solution.py:98
  7.9 240.8 %all-gather.3.cloned.1.call-start = ((), (), s32[]{:S(2)}) async-start(), calls=%async_computation.5 | async-start | bytes 8519680 | tf_op jit(solution)/shard_map/all_gather | solution.py:87
  10.7 245.2 %all-to-all-start.1 = ((bf16[64,16,256]{2,1,0:T(8,128)(2,1)}), bf16[64,16,256]{2,1,0:T(8,128)(2,1)S(1)}, u32[]{:S(2)}, u32[]{:S(2)}) async-start(bf16[64,16,256]{2,1,0:T(8,128)(2,1)} %bitcast.3), calls=%async_computation.1 | async-start | bytes 1048576 | tf_op jit(solution)/shard_map/all_to_all | solution.py:104
  30.5 234.0 %copy-start.6 = (bf16[256,1024]{1,0:T(8,128)(2,1)S(1)}, bf16[256,1024]{1,0:T(8,128)(2,1)}, u32[]{:S(2)}) copy-start(bf16[256,1024]{1,0:T(8,128)(2,1)} %param.7) | copy-start | bytes 1572868
  255.9 9.6 %copy-start.7 = (f32[128,16]{0,1:T(8,128)S(1)}, f32[128,16]{0,1:T(8,128)}, u32[]{:S(2)}) copy-start(f32[128,16]{0,1:T(8,128)} %param.9) | copy-start | bytes 24580
  255.9 9.6 %copy-start.4 = (bf16[64,16,256]{2,1,0:T(8,128)(2,1)}, bf16[64,16,256]{2,1,0:T(8,128)(2,1)S(1)}, u32[]{:S(2)}) copy-start(bf16[64,16,256]{2,1,0:T(8,128)(2,1)S(1)} %all-to-all-done.1) | copy-start | bytes 1572868
  255.9 42.5 %all-to-all-start = ((bf16[64,16,256]{2,1,0:T(8,128)(2,1)}), bf16[64,16,256]{2,1,0:T(8,128)(2,1)}, u32[]{:S(2)}, u32[]{:S(2)}) async-start(bf16[64,16,256]{2,1,0:T(8,128)(2,1)} %bitcast), calls=%async_computation | async-start | bytes 1048576 | tf_op jit(solution)/shard_map/all_to_all | solution.py:103
  268.2 1.6 slice-start
  298.4 39.1 %all-to-all-start.3 = ((bf16[64,16,256]{2,1,0:T(8,128)(2,1)}), bf16[64,16,256]{2,1,0:T(8,128)(2,1)}, u32[]{:S(2)}, u32[]{:S(2)}) async-start(bf16[64,16,256]{2,1,0:T(8,128)(2,1)} %bitcast.53), calls=%async_computation.3 | async-start | bytes 1048576 | tf_op jit(solution)/shard_map/all_to_all | solution.py:105
  303.6 1.3 copy-start.5
  310.7 2.1 copy-start
  312.6 1.2 copy-start.2
  337.5 39.0 %all-to-all-start.2 = ((bf16[16,64,256]{2,0,1:T(8,128)(2,1)}), bf16[16,64,256]{2,0,1:T(8,128)(2,1)S(1)}, u32[]{:S(2)}, u32[]{:S(2)}) async-start(bf16[16,64,256]{2,0,1:T(8,128)(2,1)} %copy.17), calls=%async_computation.2 | async-start | bytes 1048576 | tf_op jit(solution)/shard_map/all_to_all | solution.py:130
  351.1 1.2 copy-start.1
  351.1 1.5 copy-start.3
  376.4 39.1 %all-to-all-start.4 = ((bf16[16,64,256]{2,0,1:T(8,128)(2,1)}), bf16[16,64,256]{2,0,1:T(8,128)(2,1)}, u32[]{:S(2)}, u32[]{:S(2)}) async-start(bf16[16,64,256]{2,0,1:T(8,128)(2,1)} %copy.20), calls=%async_computation.4 | async-start | bytes 1048576 | tf_op jit(solution)/shard_map/all_to_all | solution.py:137
Sparse Core Ops, SparseCore 0:
  10.1 68.9 all-gather.4
  82.4 166.2 all-gather.2
where the time goes:
time: 425 us; the launch traced here: 424 us
  waiting for transfers between devices  316 us (74%)
  starting transfers between devices  43.7 us (10%)
  local copies, waits for them, and re-layouts  32.3 us (8%)
  between operations  14.3 us (3%)
  matrix products  9.46 us (2%)
  other arithmetic  8.4 us (2%)
    all_gather x1, waiting for transfers between devices, weight_product(): lax.all_gather(out_weight, 'ctx', axis=1, tiled=True)  170 us
    all_gather x1, waiting for transfers between devices, on_device(): full_grad = lax.all_gather(out_grad, 'tp', axis=1, tiled=True)  48.6 us
    all_to_all x1, waiting for transfers between devices, on_device(): lax.all_to_all(mixed, 'ctx', split_axis=0, concat_axis=1, tiled=True)  27.9 us
    all_to_all x1, waiting for transfers between devices, on_device(): lax.all_to_all(gate_blocks.reshape(owned, total_tokens), 'ctx', split_axi...  24.8 us
    all_to_all x1, waiting for transfers between devices, on_device(): lax.all_to_all(sig_blocks_grad.reshape(owned, total_tokens), 'ctx', split...  22 us
    all_to_all x1, waiting for transfers between devices, on_device(): lax.all_to_all(signal_cols, 'ctx', split_axis=0, concat_axis=1, tiled=True)  21.9 us
    all_to_all x1, starting transfers between devices, on_device(): lax.all_to_all(gate_cols, 'ctx', split_axis=0, concat_axis=1, tiled=True)  19.8 us
    unnamed x23, local copies, waits for them, and re-layouts  9.92 us
  transfers between devices with their start and end apart: 7, of which 6 were waited for; matrix products, arithmetic and copies ran while one was open for 11% of the time, Pallas kernels for 0%

commit v1 on v0

v1 whole, which is shorter than its diff:
```python
import jax
import jax.numpy as jnp
import numpy as np
from jax import lax
from jax.sharding import Mesh, PartitionSpec as P

K = 128
TOK = 256
SPAN = 8192
N = K + TOK
HALF = N // 2

BF = jnp.bfloat16
F32 = jnp.float32


def transforms():
    freq = 2.0 * np.pi * (np.arange(HALF) + 0.5) / N
    angle = freq[:, None] * np.arange(N + K)[None, :]
    forward = np.concatenate([np.cos(angle), -np.sin(angle)], axis=0)
    angle = angle[:, :N].T
    inverse = np.concatenate([np.cos(angle), -np.sin(angle)], axis=1) * (2.0 / N)
    return forward.astype(np.float32), inverse.astype(np.float32)


def two(values):
    values = np.asarray(values, np.float32)
    upper = values.astype(jnp.bfloat16)
    lower = (values - upper.astype(np.float32)).astype(jnp.bfloat16)
    return upper, lower


def split(values):
    upper = lax.optimization_barrier(values.astype(BF))
    return upper, (values - upper.astype(F32)).astype(BF)


def dot(a, b, dims=((1,), (0,))):
    return lax.dot_general(a, b, (dims, ((), ())), preferred_element_type=F32)


def exact_side(matrix, values, dims=((1,), (0,))):
    upper, lower = matrix
    return dot(upper, values, dims) + dot(lower, values, dims)


def both_sides(matrix, values, dims=((1,), (0,))):
    upper, lower = matrix
    high, low = split(values)
    return dot(upper, high, dims) + dot(lower, high, dims) + dot(upper, low, dims)


def times(a, b):
    ar, ai, br, bi = a[:HALF], a[HALF:], b[:HALF], b[HALF:]
    return jnp.concatenate([ar * br - ai * bi, ar * bi + ai * br], axis=0)


def times_conj(a, b):
    ar, ai, br, bi = a[:HALF], a[HALF:], b[:HALF], b[HALF:]
    return jnp.concatenate([ar * br + ai * bi, ai * br - ar * bi], axis=0)


def on_device(out_grad, out_weight, signal, gate_input, filter_taps):
    ctx = ("z", "h", "c")
    n_ctx = 64
    period = SPAN // TOK
    forward, inverse = transforms()
    fwd = two(forward)
    inv = two(inverse)

    turned = out_weight.T.reshape(64, 2, 512).transpose(1, 0, 2)
    tap_rows = filter_taps.T
    tap_high, tap_low = split(tap_rows)
    tap_pack = jnp.concatenate([tap_high, tap_low, jnp.zeros((16, 256), BF)], axis=1)
    message = jnp.concatenate([turned, jnp.broadcast_to(tap_pack[None], (2, 16, 512))], axis=1)
    got = lax.all_to_all(message, "h", split_axis=0, concat_axis=0)
    block = jnp.concatenate(
        [
            got[:, :64].reshape(128, 512),
            jnp.concatenate([got[0, 64:, :256], got[1, 64:, :256]], axis=1),
        ],
        axis=0,
    )
    gathered = lax.all_gather(block, "z", axis=0, tiled=False)

    ahead = [(i, i + 1) for i in range(n_ctx - 1) if (i + 1) % period]
    back = [(j, i) for i, j in ahead]
    sig_halo = lax.ppermute(signal[TOK - K :], ctx, ahead)

    cols = out_grad.reshape(TOK, 4, 2, 64).transpose(2, 0, 1, 3).reshape(2, TOK, 256)
    cols = lax.all_to_all(cols, "c", split_axis=0, concat_axis=0).reshape(2 * TOK, 256)
    cols = lax.all_to_all(
        jnp.broadcast_to(cols[None], (4, 2 * TOK, 256)), ("h", "l"), split_axis=0, concat_axis=0
    )
    cols = lax.all_to_all(
        jnp.broadcast_to(cols[None], (4, 4, 2 * TOK, 256)), "x", split_axis=0, concat_axis=0
    )
    cols = cols.reshape(4, 2, 2, 512, 256)

    window = jnp.concatenate([sig_halo, signal], axis=0)
    sig_freq = exact_side((fwd[0][:, :N], fwd[1][:, :N]), window)

    weights = gathered[:, :128].reshape(4, 2, 256, 512)
    partial = jnp.einsum("xhltf,xlfn->htn", cols, weights, preferred_element_type=F32)
    partial = lax.all_to_all(partial.reshape(2, 2, TOK, 512), "c", split_axis=1, concat_axis=1)
    half = (partial[:, 0] + partial[:, 1]).astype(BF)
    half = lax.all_to_all(half, "h", split_axis=0, concat_axis=0)
    mixed = jnp.concatenate([half[0], half[1]], axis=1)

    tap_part = gathered[:, 128:].reshape(16, 16, 2, 2, K)
    tap_all = lax.all_gather(tap_part, "c", axis=0)
    tap_all = tap_all.transpose(4, 1, 3, 0, 2, 5)
    tap_all = tap_all.reshape(2, 1024, K)
    head = (fwd[0][:, :K], fwd[1][:, :K])
    across = ((1,), (1,))
    tap_freq = (
        dot(head[0], tap_all[0], across)
        + dot(head[1], tap_all[0], across)
        + dot(head[0], tap_all[1], across)
    )
    own = (inv[0][K:], inv[1][K:])
    conv_out = both_sides(own, times(sig_freq, tap_freq))

    wide = mixed.astype(F32)
    gate_grad = (wide * conv_out).astype(BF)
    conv_grad = (wide * gate_input.astype(F32)).astype(BF)
    grad_halo = lax.ppermute(conv_grad[:K], ctx, back)

    own_freq = exact_side((fwd[0][:, K:N], fwd[1][:, K:N]), conv_grad)
    cross = times_conj(own_freq, sig_freq)
    lag = (inv[0][:K], inv[1][:K])
    high, low = split(cross)
    turn = ((0,), (1,))
    tap_grad = dot(high, lag[0], turn) + dot(high, lag[1], turn) + dot(low, lag[0], turn)
    tap_grad = tap_grad.astype(BF).reshape(16, 4, 16, K).transpose(1, 0, 2, 3)
    tap_grad = lax.all_to_all(tap_grad, ("h", "c"), split_axis=0, concat_axis=0)
    tap_grad = jnp.sum(tap_grad.astype(F32), axis=0).astype(BF)
    tap_grad = lax.all_to_all(tap_grad, "z", split_axis=0, concat_axis=0)
    filter_grad = jnp.sum(tap_grad.astype(F32), axis=0).T

    full_freq = own_freq + exact_side((fwd[0][:, N:], fwd[1][:, N:]), grad_halo)
    signal_grad = both_sides(own, times_conj(full_freq, tap_freq)).astype(BF)
    return signal_grad, gate_grad, filter_grad


def solution(mesh):
    fine = Mesh(mesh.devices.reshape(16, 2, 2, 4, 2), ("z", "h", "c", "x", "l"))
    ctx, tp = ("z", "h", "c"), ("x", "l")
    in_specs = (P(ctx, tp), P(tp, ctx), P(ctx, tp), P(ctx, tp), P(None, tp + ctx))
    out_specs = (P(ctx, tp), P(ctx, tp), P(None, tp + ctx))
    return jax.shard_map(
        on_device, mesh=fine, in_specs=in_specs, out_specs=out_specs, check_vma=False
    )
```

time: 425 us -> 192 us (0.45)
  waiting for transfers between devices: 316 us -> 41.1 us
  blocking collectives: 0 us -> 52 us
  starting transfers between devices: 43.7 us -> 29.6 us
  local copies, waits for them, and re-layouts: 32.3 us -> 18.4 us
  matrix products: 9.46 us -> 23.1 us
    all_gather x2 -> x1, waiting for transfers between devices: 218 us -> 26.5 us  [on_device(): gathered = lax.all_gather(block, 'z', axis=0, tiled=False)]
    all_to_all x5 -> x4, waiting for transfers between devices: 96.6 us -> 13.1 us  [the longest x1 7.22 us: on_device(): half = lax.all_to_all(half, 'h', split_axis=0, concat_axis=0)]
    all_to_all x0 -> x4, blocking collectives: none -> 41.7 us  [the longest x1 17.3 us: on_device(): lax.all_to_all(jnp.broadcast_to(cols[None], (4, 2 * TOK, 256)), ('h', 'l'...]
    all_to_all x5 -> x4, starting transfers between devices: 43.6 us -> 23.8 us  [the longest x1 8.64 us: on_device(): tap_grad = lax.all_to_all(tap_grad, 'z', split_axis=0, concat_axis=0)]
    dot_general x6 -> x21, matrix products: 9.46 us -> 23.1 us  [the longest x20 17.3 us: dot(): return lax.dot_general(a, b, (dims, ((), ())), preferred_element_type=F32)]
    all_gather x0 -> x1, blocking collectives: none -> 10.3 us  [on_device(): tap_all = lax.all_gather(tap_part, 'c', axis=0)]
    ppermute x0 -> x2, starting transfers between devices: none -> 5.77 us  [the longest x1 3.67 us: on_device(): sig_halo = lax.ppermute(signal[TOK - K:], ctx, ahead)]
    reshape x4 -> x3, local copies, waits for them, and re-layouts: 9.2 us -> 3.63 us  [the longest x1 1.93 us: on_device(): partial.reshape(2, 2, TOK, 512)]
  transfers between devices with their start and end apart: 7 -> 7, of which waited for: 6 -> 4; matrix products, arithmetic and copies ran while one was open for 11% -> 14% of each run, Pallas kernels for 0% -> 0%
where the time goes in v1:
time: 192 us; the launch traced here: 188 us
  blocking collectives  52 us (27%)
  waiting for transfers between devices  41.1 us (21%)
  starting transfers between devices  29.6 us (15%)
  matrix products  23.1 us (12%)
  local copies, waits for them, and re-layouts  18.4 us (10%)
  between operations  14.6 us (8%)
  other arithmetic  9.62 us (5%)
    all_gather x1, waiting for transfers between devices, on_device(): gathered = lax.all_gather(block, 'z', axis=0, tiled=False)  26.5 us
    all_to_all x1, blocking collectives, on_device(): lax.all_to_all(jnp.broadcast_to(cols[None], (4, 2 * TOK, 256)), ('h', 'l'...  17.3 us
    dot_general x20, matrix products, dot(): return lax.dot_general(a, b, (dims, ((), ())), preferred_element_type=F32)  17.3 us
    all_gather x1, blocking collectives, on_device(): tap_all = lax.all_gather(tap_part, 'c', axis=0)  10.3 us
    all_to_all x1, blocking collectives, on_device(): got = lax.all_to_all(message, 'h', split_axis=0, concat_axis=0)  9.81 us
    all_to_all x1, blocking collectives, on_device(): lax.all_to_all(cols, 'c', split_axis=0, concat_axis=0).reshape(2 * TOK, 256)  9.16 us
    all_to_all x1, starting transfers between devices, on_device(): tap_grad = lax.all_to_all(tap_grad, 'z', split_axis=0, concat_axis=0)  8.64 us
    unnamed x54, local copies, waits for them, and re-layouts  7.25 us
  transfers between devices with their start and end apart: 7, of which 4 were waited for; matrix products, arithmetic and copies ran while one was open for 14% of the time, Pallas kernels for 0%

profile of v1, /device:TPU:1, one launch (start us, length us, event | category | flops | bytes accessed | tf_op | source)
XLA Modules:
  0.0 188.4 jit_solution(9428566159897788419)
XLA Ops:
  10.0 9.8 %all_to_all.40 = bf16[2,80,512]{2,1,0:T(8,128)(2,1)S(1)} all-to-all(bf16[2,80,512]{2,1,0:T(8,128)(2,1)S(1)} %copy.61), channel_id=1, replica_groups=mesh['z'=16,'h'=2,'c'=2,'x'=4,'l'=2] {'h'}, dimensions={0} | all-to-all | bytes 327680 | tf_op jit(solution)/shard_map/all_to_all | solution.py:76
  20.7 9.2 %all_to_all.41 = bf16[2,256,256]{1,2,0:T(8,128)(2,1)S(1)} all-to-all(bf16[2,256,256]{1,2,0:T(8,128)(2,1)S(1)} %bitcast.109), channel_id=1, replica_groups=mesh['z'=16,'h'=2,'c'=2,'x'=4,'l'=2] {'c'}, dimensions={0} | all-to-all | bytes 524288 | tf_op jit(solution)/shard_map/all_to_all | solution.py:91
  30.0 17.3 %all_to_all.42 = bf16[4,512,256]{2,1,0:T(8,128)(2,1)S(1)} all-to-all(bf16[4,512,256]{2,1,0:T(8,128)(2,1)S(1)} %broadcast_in_dim.25), channel_id=1, replica_groups=mesh['z'=16,'h'=2,'c'=2,'x'=4,'l'=2] {'h','l'}, dimensions={0} | all-to-all | bytes 2097152 | tf_op jit(solution)/shard_map/all_to_all | solution.py:92
  47.3 2.5 %broadcast_in_dim.26 = bf16[4,4,512,256]{3,2,1,0:T(8,128)(2,1)} broadcast(bf16[4,512,256]{2,1,0:T(8,128)(2,1)S(1)} %all_to_all.42), dimensions={1,2,3} | broadcast | bytes 5242880 | tf_op jit(solution)/shard_map/broadcast_in_dim | solution.py:96
  49.8 5.0 %all-to-all-start.3 = ((bf16[4,4,512,256]{3,2,1,0:T(8,128)(2,1)}), bf16[4,4,512,256]{3,2,1,0:T(8,128)(2,1)}, u32[]{:S(2)}, u32[]{:S(2)}) async-start(bf16[4,4,512,256]{3,2,1,0:T(8,128)(2,1)} %broadcast_in_dim.26), calls=%async_computation.3 | async-start | bytes 8388608 | tf_op jit(solution)/shard_map/all_to_all | solution.py:95
  54.9 3.7 %collective-permute-start.1 = (bf16[128,1024]{1,0:T(8,128)(2,1)S(1)}, bf16[128,1024]{1,0:T(8,128)(2,1)S(1)}, u32[]{:S(2)}, u32[]{:S(2)}) collective-permute-start(bf16[128,1024]{1,0:T(8,128)(2,1)S(1)} %slice.86), channel_id=1, source_target_pairs={{0,8},{8,16},{16,24},{24,32},{32,40},{40,48},{48,56},{56,64},{64,7... | collective-permute-start | bytes 786440 | tf_op jit(solution)/shard_map/ppermute | solution.py:88
  63.8 26.5 %all-gather.3.cloned.1.call-done = bf16[2304,512]{1,0:T(8,128)(2,1)} async-done(((bf16[144,512]{1,0:T(8,128)(2,1)}), bf16[2304,512]{1,0:T(8,128)(2,1)}) %all-gather.3.cloned.1.call-update) | async-done | bytes 2359312 | tf_op jit(solution)/shard_map/all_gather | solution.py:84
  90.3 1.8 slice.98
  93.2 10.3 %all_gather.11 = bf16[2,16,16,2,2,128]{5,2,0,3,1,4:T(8,128)(2,1)S(1)} all-gather(bf16[1,16,16,2,2,128]{5,2,0,3,1,4:T(8,128)(2,1)S(1)} %copy.67), channel_id=1, replica_groups=mesh['z'=16,'h'=2,'c'=2,'x'=4,'l'=2] {'c'}, dimensions={0}, use_global_device_ids=true | all-gather | bytes 786432 | tf_op jit(solution)/shard_map/all_gather | solution.py:111
  103.5 1.5 fusion.20
  105.0 1.6 fusion.21
  106.7 5.8 %fusion.17 = f32[512,2,512,1,1]{0,2,3,1,4:T(8,128)} fusion(bf16[4,2,256,512,1]{3,2,1,4,0:T(8,128)(2,1)S(1)} %bitcast.102, bf16[4,2,2,512,256]{4,3,2,1,0:T(8,128)(2,1)} %bitcast.14), kind=kOutput, calls=%fused_computation.53 | convolution fusion | flops 2147483648 | bytes 8388608 | tf_op jit(solution)/shard_map/xhltf,xlfn->htn/dot_general | solution.py:104
  112.5 1.9 %copy.65 = f32[2,2,256,512]{2,3,0,1:T(8,128)S(1)} copy(f32[2,2,256,512]{3,2,1,0:T(8,128)} %bitcast.103) | data formatting | bytes 4194304 | tf_op jit(solution)/shard_map/reshape | solution.py:105
  114.4 5.4 %all_to_all.43 = f32[2,2,256,512]{2,3,0,1:T(8,128)S(1)} all-to-all(f32[2,2,256,512]{2,3,0,1:T(8,128)S(1)} %copy.65), channel_id=1, replica_groups=mesh['z'=16,'h'=2,'c'=2,'x'=4,'l'=2] {'c'}, dimensions={1} | all-to-all | bytes 4194304 | tf_op jit(solution)/shard_map/all_to_all | solution.py:105
  120.7 4.7 %all-to-all-start.5 = ((bf16[2,256,512]{1,2,0:T(8,128)(2,1)}), bf16[2,256,512]{1,2,0:T(8,128)(2,1)}, u32[]{:S(2)}, u32[]{:S(2)}) async-start(bf16[2,256,512]{1,2,0:T(8,128)(2,1)} %fusion.11), calls=%async_computation.5 | async-start | bytes 1048576 | tf_op jit(solution)/shard_map/all_to_all | solution.py:107
  125.4 1.8 add_bitcast_fusion
  127.2 7.2 %all-to-all-done.5 = bf16[2,256,512]{1,2,0:T(8,128)(2,1)} async-done(((bf16[2,256,512]{1,2,0:T(8,128)(2,1)}), bf16[2,256,512]{1,2,0:T(8,128)(2,1)}, u32[]{:S(2)}, u32[]{:S(2)}) %all-to-all-start.5) | async-done | bytes 524320 | tf_op jit(solution)/shard_map/all_to_all | solution.py:107
  144.0 5.5 %all-to-all-start.6 = ((bf16[4,16,16,128]{3,2,1,0:T(8,128)(2,1)}), bf16[4,16,16,128]{3,2,1,0:T(8,128)(2,1)}, u32[]{:S(2)}, u32[]{:S(2)}) async-start(bf16[4,16,16,128]{3,2,1,0:T(8,128)(2,1)} %bitcast.108), calls=%async_computation.6 | async-start | bytes 524288 | tf_op jit(solution)/shard_map/all_to_all | solution.py:136
  149.5 2.1 %collective-permute-start = (bf16[128,1024]{0,1:T(8,128)(2,1)}, bf16[128,1024]{0,1:T(8,128)(2,1)}, u32[]{:S(2)}, u32[]{:S(2)}) collective-permute-start(bf16[128,1024]{0,1:T(8,128)(2,1)} %slice.103), channel_id=1, source_target_pairs={{8,0},{16,8},{24,16},{32,24},{40,32},{48,40},{56,48},{64,56},{72,6... | collective-permute-start | bytes 786440 | tf_op jit(solution)/shard_map/ppermute | solution.py:127
  151.6 1.6 fusion.26
  156.1 2.0 %copy.70 = bf16[256,1024]{1,0:T(8,128)(2,1)} copy(bf16[256,1024]{0,1:T(8,128)(2,1)} %fusion.2) | data formatting | bytes 1048576
  158.2 1.6 reduce_sum.21
  159.8 8.6 %all-to-all-start.7 = ((bf16[16,16,128]{2,1,0:T(8,128)(2,1)}), bf16[16,16,128]{2,1,0:T(8,128)(2,1)}, u32[]{:S(2)}, u32[]{:S(2)}) async-start(bf16[16,16,128]{2,1,0:T(8,128)(2,1)} %reduce_sum.21), calls=%async_computation.7 | async-start | bytes 131072 | tf_op jit(solution)/shard_map/all_to_all | solution.py:138
  174.2 5.8 %all-to-all-done.7 = bf16[16,16,128]{2,1,0:T(8,128)(2,1)} async-done(((bf16[16,16,128]{2,1,0:T(8,128)(2,1)}), bf16[16,16,128]{2,1,0:T(8,128)(2,1)}, u32[]{:S(2)}, u32[]{:S(2)}) %all-to-all-start.7) | async-done | bytes 65568 | tf_op jit(solution)/shard_map/all_to_all | solution.py:138
  (105 shorter events, 30.4 us)
Async XLA Ops:
  7.2 13.3 %copy-start.22 = (bf16[256,512]{1,0:T(8,128)(2,1)S(1)}, bf16[256,512]{1,0:T(8,128)(2,1)}, u32[]{:S(2)}) copy-start(bf16[256,512]{1,0:T(8,128)(2,1)} %param.17) | copy-start | bytes 786436
  7.2 83.1 %all-gather.3.cloned.1.call-start = ((), (), s32[]{:S(2)}) async-start(), calls=%async_computation.8 | async-start | bytes 2506752 | tf_op jit(solution)/shard_map/all_gather | solution.py:84
  49.8 5.0 %copy-start.7 = (bf16[256,1024]{1,0:T(8,128)(2,1)S(1)}, bf16[256,1024]{1,0:T(8,128)(2,1)}, u32[]{:S(2)}) copy-start(bf16[256,1024]{1,0:T(8,128)(2,1)} %param.19) | copy-start | bytes 1572868
  49.8 8.7 %copy-start.19 = (bf16[256,1024]{1,0:T(8,128)(2,1)S(1)}, bf16[256,1024]{1,0:T(8,128)(2,1)}, u32[]{:S(2)}) copy-start(bf16[256,1024]{1,0:T(8,128)(2,1)} %param.20) | copy-start | bytes 1572868
  49.8 56.8 %all-to-all-start.3 = ((bf16[4,4,512,256]{3,2,1,0:T(8,128)(2,1)}), bf16[4,4,512,256]{3,2,1,0:T(8,128)(2,1)}, u32[]{:S(2)}, u32[]{:S(2)}) async-start(bf16[4,4,512,256]{3,2,1,0:T(8,128)(2,1)} %broadcast_in_dim.26), calls=%async_computation.3 | async-start | bytes 8388608 | tf_op jit(solution)/shard_map/all_to_all | solution.py:95
  54.8 4.7 %copy-start.15 = (bf16[384,256]{1,0:T(8,128)(2,1)S(1)}, bf16[384,256]{1,0:T(8,128)(2,1)}, u32[]{:S(2)}) copy-start(bf16[384,256]{1,0:T(8,128)(2,1)} %constant.35.clone) | copy-start | bytes 589828
  54.9 5.1 %copy-start.17 = (bf16[384,256]{1,0:T(8,128)(2,1)S(1)}, bf16[384,256]{1,0:T(8,128)(2,1)}, u32[]{:S(2)}) copy-start(bf16[384,256]{1,0:T(8,128)(2,1)} %constant.36.clone) | copy-start | bytes 589828
  54.9 7.0 %collective-permute-start.1 = (bf16[128,1024]{1,0:T(8,128)(2,1)S(1)}, bf16[128,1024]{1,0:T(8,128)(2,1)S(1)}, u32[]{:S(2)}, u32[]{:S(2)}) collective-permute-start(bf16[128,1024]{1,0:T(8,128)(2,1)S(1)} %slice.86), channel_id=1, source_target_pairs={{0,8},{8,16},{16,24},{24,32},{32,40},{40,48},{48,56},{56,64},{64,7... | collective-permute-start | bytes 786440 | tf_op jit(solution)/shard_map/ppermute | solution.py:88
  60.0 1.9 %copy-start.13 = (bf16[384,128]{1,0:T(8,128)(2,1)S(1)}, bf16[384,128]{1,0:T(8,128)(2,1)}, u32[]{:S(2)}) copy-start(bf16[384,128]{1,0:T(8,128)(2,1)} %constant.31.clone) | copy-start | bytes 294916
  60.0 2.2 %copy-start.21 = (bf16[384,128]{1,0:T(8,128)(2,1)S(1)}, bf16[384,128]{1,0:T(8,128)(2,1)}, u32[]{:S(2)}) copy-start(bf16[384,128]{1,0:T(8,128)(2,1)} %constant.32.clone) | copy-start | bytes 294916
  119.8 5.6 %copy-start.5 = (f32[1024,384]{0,1:T(8,128)S(1)}, f32[1024,384]{0,1:T(8,128)}, u32[]{:S(2)}) copy-start(f32[1024,384]{0,1:T(8,128)} %fusion.20) | copy-start | bytes 4718596
  120.7 13.7 %all-to-all-start.5 = ((bf16[2,256,512]{1,2,0:T(8,128)(2,1)}), bf16[2,256,512]{1,2,0:T(8,128)(2,1)}, u32[]{:S(2)}, u32[]{:S(2)}) async-start(bf16[2,256,512]{1,2,0:T(8,128)(2,1)} %fusion.11), calls=%async_computation.5 | async-start | bytes 1048576 | tf_op jit(solution)/shard_map/all_to_all | solution.py:107
  127.2 10.3 %copy-start.16 = (bf16[384,256]{1,0:T(8,128)(2,1)S(1)}, bf16[384,256]{1,0:T(8,128)(2,1)}, u32[]{:S(2)}) copy-start(bf16[384,256]{1,0:T(8,128)(2,1)} %constant.35.clone) | copy-start | bytes 589828
  138.6 1.4 copy-start.6
  140.6 1.4 copy-start.3
  140.6 1.8 copy-start.24
  142.8 8.8 %copy-start.8 = (bf16[256,384]{1,0:T(8,128)(2,1)S(1)}, bf16[256,384]{1,0:T(8,128)(2,1)}, u32[]{:S(2)}) copy-start(bf16[256,384]{1,0:T(8,128)(2,1)} %constant.33.clone) | copy-start | bytes 589828
  143.3 10.0 %copy-start.14 = (bf16[256,384]{1,0:T(8,128)(2,1)S(1)}, bf16[256,384]{1,0:T(8,128)(2,1)}, u32[]{:S(2)}) copy-start(bf16[256,384]{1,0:T(8,128)(2,1)} %constant.34.clone) | copy-start | bytes 589828
  144.0 14.1 %all-to-all-start.6 = ((bf16[4,16,16,128]{3,2,1,0:T(8,128)(2,1)}), bf16[4,16,16,128]{3,2,1,0:T(8,128)(2,1)}, u32[]{:S(2)}, u32[]{:S(2)}) async-start(bf16[4,16,16,128]{3,2,1,0:T(8,128)(2,1)} %bitcast.108), calls=%async_computation.6 | async-start | bytes 524288 | tf_op jit(solution)/shard_map/all_to_all | solution.py:136
  149.5 3.8 %copy-start = (bf16[384,1024]{1,0:T(8,128)(2,1)S(1)}, bf16[384,1024]{1,0:T(8,128)(2,1)}, u32[]{:S(2)}) copy-start(bf16[384,1024]{1,0:T(8,128)(2,1)} %get-tuple-element.36) | copy-start | bytes 2359300
  149.5 18.9 %collective-permute-start = (bf16[128,1024]{0,1:T(8,128)(2,1)}, bf16[128,1024]{0,1:T(8,128)(2,1)}, u32[]{:S(2)}, u32[]{:S(2)}) collective-permute-start(bf16[128,1024]{0,1:T(8,128)(2,1)} %slice.103), channel_id=1, source_target_pairs={{8,0},{16,8},{24,16},{32,24},{40,32},{48,40},{56,48},{64,56},{72,6... | collective-permute-start | bytes 786440 | tf_op jit(solution)/shard_map/ppermute | solution.py:127
  153.3 1.4 copy-start.10
  153.3 1.5 copy-start.12
  159.8 20.3 %all-to-all-start.7 = ((bf16[16,16,128]{2,1,0:T(8,128)(2,1)}), bf16[16,16,128]{2,1,0:T(8,128)(2,1)}, u32[]{:S(2)}, u32[]{:S(2)}) async-start(bf16[16,16,128]{2,1,0:T(8,128)(2,1)} %reduce_sum.21), calls=%async_computation.7 | async-start | bytes 131072 | tf_op jit(solution)/shard_map/all_to_all | solution.py:138
  (8 other events, 9.1 us)
Sparse Core Ops, SparseCore 0:
  20.6 69.6 all-gather.2

commit v2 on v1

v2 whole, which is shorter than its diff:
```python
import jax
import jax.numpy as jnp
import numpy as np
from jax import lax
from jax.experimental import pallas as pl
from jax.experimental.pallas import tpu as pltpu
from jax.sharding import Mesh, PartitionSpec as P

K = 128
TOK = 256
CH = 1024
SPAN = 8192
N = K + TOK
HALF = N // 2
TILE = 256

BF = jnp.bfloat16
F32 = jnp.float32
ROWS = ((1,), (0,))
LANES = ((1,), (1,))


def transforms():
    freq = 2.0 * np.pi * (np.arange(HALF) + 0.5) / N
    angle = freq[:, None] * np.arange(N + K)[None, :]
    forward = np.concatenate([np.cos(angle), -np.sin(angle)], axis=0)
    angle = angle[:, :N].T
    inverse = np.concatenate([np.cos(angle), -np.sin(angle)], axis=1) * (2.0 / N)
    return two(forward), two(inverse)


def two(values):
    values = np.asarray(values, np.float32)
    upper = values.astype(jnp.bfloat16)
    lower = (values - upper.astype(np.float32)).astype(jnp.bfloat16)
    return np.stack([upper, lower])


def dot(a, b, dims=ROWS):
    return lax.dot_general(a, b, (dims, ((), ())), preferred_element_type=F32)


def exact_side(matrix, values):
    return dot(matrix[0], values) + dot(matrix[1], values)


def both_sides(matrix, values):
    high = values.astype(BF)
    low = (values - high.astype(F32)).astype(BF)
    return dot(matrix[0], high) + dot(matrix[1], high) + dot(matrix[0], low)


def times(a, b):
    ar, ai, br, bi = a[:HALF], a[HALF:], b[:HALF], b[HALF:]
    return jnp.concatenate([ar * br - ai * bi, ar * bi + ai * br], axis=0)


def times_conj(a, b):
    ar, ai, br, bi = a[:HALF], a[HALF:], b[:HALF], b[HALF:]
    return jnp.concatenate([ar * br + ai * bi, ai * br - ar * bi], axis=0)


def params():
    return pltpu.CompilerParams(
        dimension_semantics=("arbitrary",), vmem_limit_bytes=40 * 1024 * 1024
    )


def product_kernel(cols_ref, weight_ref, out_ref):
    weight = weight_ref[:, :K, :].reshape(2 * K, 512)

    @pl.when(pl.program_id(0) == 0)
    def _():
        out_ref[...] = jnp.zeros_like(out_ref)

    for h in range(2):
        for c in range(2):
            out_ref[c, h] += dot(cols_ref[0, h, 0, c * TOK : (c + 1) * TOK, :], weight)


def product(cols, weights):
    return pl.pallas_call(
        product_kernel,
        grid=(8,),
        in_specs=[
            pl.BlockSpec((1, 2, 1, 512, 256), lambda i: (i // 2, 0, i % 2, 0, 0)),
            pl.BlockSpec((2, 144, 512), lambda i: (i, 0, 0)),
        ],
        out_specs=pl.BlockSpec((2, 2, TOK, 512), lambda i: (0, 0, 0, 0)),
        out_shape=jax.ShapeDtypeStruct((2, 2, TOK, 512), F32),
        compiler_params=params(),
        cost_estimate=pl.CostEstimate(
            flops=2 * 1024 * 2048 * 512, bytes_accessed=9 << 20, transcendentals=0
        ),
    )(cols, weights)


def grad_kernel(mix_ref, gate_ref, freq_ref, own_ref, lag_ref, head_ref, spec_ref, tap_ref):
    mixed = mix_ref[0].astype(F32)
    conv_grad = (mixed * gate_ref[...].astype(F32)).astype(BF)
    head_ref[...] = conv_grad[:K]
    spec = exact_side(own_ref, conv_grad)
    spec_ref[...] = spec
    taps = both_sides(lag_ref, times_conj(spec, freq_ref[...]))
    taps = taps.T.reshape(8, 2, 16, K)
    tap_ref[0] = taps[:, 0]
    tap_ref[1] = taps[:, 1]


def whole(shape):
    return pl.BlockSpec(shape, lambda j: (0,) * len(shape))


def tile(rows):
    return pl.BlockSpec((rows, TILE), lambda j: (0, j))


MIX_TILE = pl.BlockSpec((1, TOK, TILE), lambda j: (j // 2, 0, j % 2))


def grad_part(mix, gate, sig_freq, own, lag):
    return pl.pallas_call(
        grad_kernel,
        grid=(CH // TILE,),
        in_specs=[MIX_TILE, tile(TOK), tile(N), whole((2, N, TOK)), whole((2, K, N))],
        out_specs=[
            tile(K),
            tile(N),
            pl.BlockSpec((2, 8, 16, K), lambda j: (0, j, 0, 0)),
        ],
        out_shape=[
            jax.ShapeDtypeStruct((K, CH), BF),
            jax.ShapeDtypeStruct((N, CH), F32),
            jax.ShapeDtypeStruct((2, 32, 16, K), F32),
        ],
        compiler_params=params(),
        cost_estimate=pl.CostEstimate(
            flops=2 * CH * N * (2 * TOK + 3 * K), bytes_accessed=6 << 20, transcendentals=0
        ),
    )(mix, gate, sig_freq, own, lag)


def out_kernel(
    mix_ref, freq_ref, spec_ref, halo_ref, tap_ref, head_ref, tail_ref, inv_ref, gate_ref, sig_ref
):
    upper, lower = tap_ref[0], tap_ref[1]
    tap_freq = (
        dot(head_ref[0], upper, LANES)
        + dot(head_ref[1], upper, LANES)
        + dot(head_ref[0], lower, LANES)
    )
    conv_out = both_sides(inv_ref, times(freq_ref[...], tap_freq))
    gate_ref[...] = (mix_ref[0].astype(F32) * conv_out).astype(BF)
    full = spec_ref[...] + exact_side(tail_ref, halo_ref[...])
    sig_ref[...] = both_sides(inv_ref, times_conj(full, tap_freq)).astype(BF)


def out_part(mix, sig_freq, spec, halo, taps, head, tail, inv):
    return pl.pallas_call(
        out_kernel,
        grid=(CH // TILE,),
        in_specs=[
            MIX_TILE,
            tile(N),
            tile(N),
            tile(K),
            pl.BlockSpec((2, TILE, K), lambda j: (0, j, 0)),
            whole((2, N, K)),
            whole((2, N, K)),
            whole((2, TOK, N)),
        ],
        out_specs=[tile(TOK), tile(TOK)],
        out_shape=[jax.ShapeDtypeStruct((TOK, CH), BF)] * 2,
        compiler_params=params(),
        cost_estimate=pl.CostEstimate(
            flops=2 * CH * N * (5 * K + 6 * TOK), bytes_accessed=6 << 20, transcendentals=0
        ),
    )(mix, sig_freq, spec, halo, taps, head, tail, inv)


def on_device(out_grad, out_weight, signal, gate_input, filter_taps):
    ctx = ("z", "h", "c")
    n_ctx = 64
    period = SPAN // TOK
    fwd, inv = transforms()

    turned = out_weight.T.reshape(64, 2, 512).transpose(1, 0, 2)
    tap_rows = filter_taps.T
    tap_high = lax.optimization_barrier(tap_rows.astype(BF))
    tap_low = (tap_rows - tap_high.astype(F32)).astype(BF)
    tap_pack = jnp.concatenate([tap_high, tap_low, jnp.zeros((16, 256), BF)], axis=1)
    message = jnp.concatenate([turned, jnp.broadcast_to(tap_pack[None], (2, 16, 512))], axis=1)
    got = lax.all_to_all(message, "h", split_axis=0, concat_axis=0)
    block = jnp.concatenate(
        [
            got[:, :64].reshape(128, 512),
            jnp.concatenate([got[0, 64:, :256], got[1, 64:, :256]], axis=1),
        ],
        axis=0,
    )
    gathered = lax.all_gather(block, "z", axis=0, tiled=False)

    ahead = [(i, i + 1) for i in range(n_ctx - 1) if (i + 1) % period]
    back = [(j, i) for i, j in ahead]
    sig_halo = lax.ppermute(signal[TOK - K :], ctx, ahead)

    cols = out_grad.reshape(TOK, 4, 2, 64).transpose(2, 0, 1, 3).reshape(2, TOK, 256)
    cols = lax.all_to_all(cols, "c", split_axis=0, concat_axis=0).reshape(2 * TOK, 256)
    cols = lax.all_to_all(
        jnp.broadcast_to(cols[None], (4, 2 * TOK, 256)), ("h", "l"), split_axis=0, concat_axis=0
    )
    cols = lax.all_to_all(
        jnp.broadcast_to(cols[None], (4, 4, 2 * TOK, 256)), "x", split_axis=0, concat_axis=0
    )
    cols = cols.reshape(4, 2, 2, 512, 256)

    window = jnp.concatenate([sig_halo, signal], axis=0)
    sig_freq = exact_side(fwd[:, :, :N], window)

    partial = product(cols, gathered)
    partial = lax.all_to_all(partial, "c", split_axis=0, concat_axis=0)
    half = (partial[0] + partial[1]).astype(BF)
    half = lax.all_to_all(half, "h", split_axis=0, concat_axis=0)

    grad_head, spec, tap_grad = grad_part(
        half, gate_input, sig_freq, fwd[:, :, K:N], inv[:, :K]
    )
    grad_halo = lax.ppermute(grad_head, ctx, back)
    tap_grad = lax.all_to_all(tap_grad, "c", split_axis=0, concat_axis=0)
    tap_grad = (tap_grad[0] + tap_grad[1]).astype(BF)
    tap_grad = lax.all_to_all(tap_grad, ("z", "h"), split_axis=0, concat_axis=0)
    filter_grad = jnp.sum(tap_grad.astype(F32), axis=0).T

    tap_part, _ = lax.optimization_barrier((gathered[:, 128:], half))
    tap_all = lax.all_gather(tap_part.reshape(16, 16, 2, 2, K), "c", axis=0)
    tap_all = tap_all.transpose(4, 1, 3, 0, 2, 5).reshape(2, CH, K)
    gate_grad, signal_grad = out_part(
        half, sig_freq, spec, grad_halo, tap_all, fwd[:, :, :K], fwd[:, :, N:], inv[:, K:]
    )
    return signal_grad, gate_grad, filter_grad


def solution(mesh):
    fine = Mesh(mesh.devices.reshape(16, 2, 2, 4, 2), ("z", "h", "c", "x", "l"))
    ctx, tp = ("z", "h", "c"), ("x", "l")
    in_specs = (P(ctx, tp), P(tp, ctx), P(ctx, tp), P(ctx, tp), P(None, tp + ctx))
    out_specs = (P(ctx, tp), P(ctx, tp), P(None, tp + ctx))
    return jax.shard_map(
        on_device, mesh=fine, in_specs=in_specs, out_specs=out_specs, check_vma=False
    )
```

time: 192 us -> 181 us (0.943); the launches traced: 188 us -> 180 us
  Pallas kernels: 0 us -> 17.5 us
  matrix products: 23.1 us -> 7.41 us
  local copies, waits for them, and re-layouts: 18.4 us -> 12.4 us
  waiting for transfers between devices: 41.1 us -> 46.8 us
  other arithmetic: 9.62 us -> 4.38 us
  starting transfers between devices: 29.6 us -> 26.5 us
    all_to_all x1, waiting for transfers between devices: 0.01 us -> 39.1 us  [on_device(): lax.all_to_all(jnp.broadcast_to(cols[None], (4, 4, 2 * TOK, 256)), 'x', s...]
    all_gather x1, waiting for transfers between devices: 26.5 us -> 0.01 us  [on_device(): gathered = lax.all_gather(block, 'z', axis=0, tiled=False)]
    pallas_call x0 -> x3, Pallas kernels: none -> 17.5 us  [the longest x1 7.06 us: out_part(): pl.pallas_call(out_kernel, grid=(CH // TILE,), in_specs=[MIX_TILE, tile(N...]
    dot_general x20 -> x4, matrix products: 17.3 us -> 7.41 us  [dot(): return lax.dot_general(a, b, (dims, ((), ())), preferred_element_type=F32)]
    all_gather x1, blocking collectives: 10.3 us -> 2.18 us  [on_device(): tap_all = lax.all_gather(tap_part.reshape(16, 16, 2, 2, K), 'c', axis=0)]
    all_to_all x1 -> x2, blocking collectives: 5.42 us -> 12.1 us  [the longest x1 7.16 us: on_device(): partial = lax.all_to_all(partial, 'c', split_axis=0, concat_axis=0)]
    all_to_all x2 -> x1, waiting for transfers between devices: 5.85 us -> 0.01 us  [on_device(): tap_grad = lax.all_to_all(tap_grad, ('z', 'h'), split_axis=0, concat_axis=0)]
    dot_general x1 -> x0, matrix products: 5.81 us -> none  [on_device(): jnp.einsum('xhltf,xlfn->htn', cols, weights, preferred_element_type=F32)]
  transfers between devices with their start and end apart: 7 -> 6, of which waited for: 4 -> 4; matrix products, arithmetic and copies ran while one was open for 14% -> 8% of each run, Pallas kernels for 0% -> 4%
where the time goes in v2:
time: 181 us; the launch traced here: 180 us
  blocking collectives  50.6 us (28%)
  waiting for transfers between devices  46.8 us (26%)
  starting transfers between devices  26.5 us (15%)
  Pallas kernels  17.5 us (10%)
  between operations  14.3 us (8%)
  local copies, waits for them, and re-layouts  12.4 us (7%)
  matrix products  7.41 us (4%)
  other arithmetic  4.38 us (2%)
    all_to_all x1, waiting for transfers between devices, on_device(): lax.all_to_all(jnp.broadcast_to(cols[None], (4, 4, 2 * TOK, 256)), 'x', s...  39.1 us
    all_to_all x1, blocking collectives, on_device(): lax.all_to_all(jnp.broadcast_to(cols[None], (4, 2 * TOK, 256)), ('h', 'l'...  17.3 us
    all_to_all x1, starting transfers between devices, on_device(): tap_grad = lax.all_to_all(tap_grad, ('z', 'h'), split_axis=0, concat_axis=0)  11.7 us
    all_to_all x1, blocking collectives, on_device(): got = lax.all_to_all(message, 'h', split_axis=0, concat_axis=0)  9.81 us
    all_to_all x1, blocking collectives, on_device(): lax.all_to_all(cols, 'c', split_axis=0, concat_axis=0).reshape(2 * TOK, 256)  9.16 us
    dot_general x4, matrix products, dot(): return lax.dot_general(a, b, (dims, ((), ())), preferred_element_type=F32)  7.41 us
    all_to_all x1, blocking collectives, on_device(): partial = lax.all_to_all(partial, 'c', split_axis=0, concat_axis=0)  7.16 us
    pallas_call x1, Pallas kernels, out_part(): pl.pallas_call(out_kernel, grid=(CH // TILE,), in_specs=[MIX_TILE, tile(N...  7.06 us
  transfers between devices with their start and end apart: 6, of which 4 were waited for; matrix products, arithmetic and copies ran while one was open for 8% of the time, Pallas kernels for 4%

profile of v2, /device:TPU:1, one launch (start us, length us, event | category | flops | bytes accessed | tf_op | source)
XLA Modules:
  0.0 179.8 jit_solution(16854042559172038360)
XLA Ops:
  9.6 9.8 %all_to_all.40 = bf16[2,80,512]{2,1,0:T(8,128)(2,1)S(1)} all-to-all(bf16[2,80,512]{2,1,0:T(8,128)(2,1)S(1)} %pad_maximum_fusion), channel_id=1, replica_groups=mesh['z'=16,'h'=2,'c'=2,'x'=4,'l'=2] {'h'}, dimensions={0} | all-to-all | bytes 327680 | tf_op jit(solution)/shard_map/all_to_all | solution.py:193
  20.3 9.2 %all_to_all.41 = bf16[2,256,256]{1,2,0:T(8,128)(2,1)S(1)} all-to-all(bf16[2,256,256]{1,2,0:T(8,128)(2,1)S(1)} %bitcast.45), channel_id=1, replica_groups=mesh['z'=16,'h'=2,'c'=2,'x'=4,'l'=2] {'c'}, dimensions={0} | all-to-all | bytes 524288 | tf_op jit(solution)/shard_map/all_to_all | solution.py:208
  29.7 17.3 %all_to_all.42 = bf16[4,512,256]{2,1,0:T(8,128)(2,1)S(1)} all-to-all(bf16[4,512,256]{2,1,0:T(8,128)(2,1)S(1)} %broadcast_in_dim.11), channel_id=1, replica_groups=mesh['z'=16,'h'=2,'c'=2,'x'=4,'l'=2] {'h','l'}, dimensions={0} | all-to-all | bytes 2097152 | tf_op jit(solution)/shard_map/all_to_all | solution.py:209
  47.0 2.4 %broadcast_in_dim.24 = bf16[4,4,512,256]{3,2,1,0:T(8,128)(2,1)} broadcast(bf16[4,512,256]{2,1,0:T(8,128)(2,1)S(1)} %all_to_all.42), dimensions={1,2,3} | broadcast | bytes 5242880 | tf_op jit(solution)/shard_map/broadcast_in_dim | solution.py:213
  49.4 5.0 %all-to-all-start.2 = ((bf16[4,4,512,256]{3,2,1,0:T(8,128)(2,1)}), bf16[4,4,512,256]{3,2,1,0:T(8,128)(2,1)}, u32[]{:S(2)}, u32[]{:S(2)}) async-start(bf16[4,4,512,256]{3,2,1,0:T(8,128)(2,1)} %broadcast_in_dim.24), calls=%async_computation.2 | async-start | bytes 8388608 | tf_op jit(solution)/shard_map/all_to_all | solution.py:212
  54.5 3.7 %collective-permute-start = (bf16[128,1024]{1,0:T(8,128)(2,1)S(1)}, bf16[128,1024]{1,0:T(8,128)(2,1)S(1)}, u32[]{:S(2)}, u32[]{:S(2)}) collective-permute-start(bf16[128,1024]{1,0:T(8,128)(2,1)S(1)} %slice.32), channel_id=1, source_target_pairs={{0,8},{8,16},{16,24},{24,32},{32,40},{40,48},{48,56},{56,64},{64,7... | collective-permute-start | bytes 786440 | tf_op jit(solution)/shard_map/ppermute | solution.py:205
  58.2 1.5 fusion.7
  59.7 1.5 fusion.6
  61.5 1.5 fusion.5
  63.0 39.1 %all-to-all-done.2 = bf16[4,4,512,256]{3,2,1,0:T(8,128)(2,1)} async-done(((bf16[4,4,512,256]{3,2,1,0:T(8,128)(2,1)}), bf16[4,4,512,256]{3,2,1,0:T(8,128)(2,1)}, u32[]{:S(2)}, u32[]{:S(2)}) %all-to-all-start.2) | async-done | bytes 4194336 | tf_op jit(solution)/shard_map/all_to_all | solution.py:212
  102.1 1.7 copy-done
  103.8 6.8 %shard_map.139 = f32[2,2,256,512]{3,2,1,0:T(8,128)S(1)} custom-call(bf16[4,2,2,512,256]{4,3,2,1,0:T(8,128)(2,1)} %bitcast.4.cols_ref, bf16[16,144,512]{2,1,0:T(8,128)(2,1)S(1)} %bitcast.42), custom_call_target="tpu_custom_call" | custom-call | flops 2147483648 | bytes 9437184 | tf_op jit(solution)/shard_map/pallas_call | solution.py:82
  110.6 7.2 %all_to_all.43 = f32[2,2,256,512]{3,2,1,0:T(8,128)S(1)} all-to-all(f32[2,2,256,512]{3,2,1,0:T(8,128)S(1)} %shard_map.139), channel_id=1, replica_groups=mesh['z'=16,'h'=2,'c'=2,'x'=4,'l'=2] {'c'}, dimensions={0} | all-to-all | bytes 4194304 | tf_op jit(solution)/shard_map/all_to_all | solution.py:221
  118.7 3.5 %all-to-all-start.5 = ((bf16[2,256,512]{2,1,0:T(8,128)(2,1)}), bf16[2,256,512]{2,1,0:T(8,128)(2,1)S(1)}, u32[]{:S(2)}, u32[]{:S(2)}) async-start(bf16[2,256,512]{2,1,0:T(8,128)(2,1)} %fusion.1), calls=%async_computation.5 | async-start | bytes 1048576 | tf_op jit(solution)/shard_map/all_to_all | solution.py:223
  122.3 2.8 %add_add_fusion.freq_ref = f32[384,1024]{1,0:T(8,128)S(1)} fusion(f32[384,1024]{1,0:T(8,128)} %fusion.7, f32[384,1024]{1,0:T(8,128)} %fusion.5, f32[384,1024]{1,0:T(8,128)} %fusion.6, bf16[384,128]{1,0:T(8,128)(2,1)} %constant.28, bf16[128,1024]{1,0:T(8,128)(2,1)S(1)} %collective-permute-done), kind=kOutput, calls=%fused_computation | convolution fusion | flops 101842944 | bytes 6651904 | tf_op jit(solution)/shard_map/dot_general | solution.py:40
  125.1 6.3 %all-to-all-done.5.mix_ref = bf16[2,256,512]{2,1,0:T(8,128)(2,1)S(1)} async-done(((bf16[2,256,512]{2,1,0:T(8,128)(2,1)}), bf16[2,256,512]{2,1,0:T(8,128)(2,1)S(1)}, u32[]{:S(2)}, u32[]{:S(2)}) %all-to-all-start.5) | async-done | bytes 524320 | tf_op jit(solution)/shard_map/all_to_all | solution.py:223
  131.4 3.6 %shard_map.140 = (bf16[128,1024]{1,0:T(8,128)(2,1)S(1)}, f32[384,1024]{1,0:T(8,128)S(1)}, f32[2,32,16,128]{3,2,1,0:T(8,128)S(1)}) custom-call(bf16[2,256,512]{2,1,0:T(8,128)(2,1)S(1)} %all-to-all-done.5.mix_ref, bf16[256,1024]{1,0:T(8,128)(2,1)S(1)} %copy-done.1, f32[384,1024]{1,0:T(8,128)S(1)} %add_add_fusion.freq_ref, bf16[2,384,256]{2,1,0:T(8,128)(2,1)S(1)} %copy-done.2, ...), custom_call_target="tpu_custom_call" | custom-call | flops 704643072 | bytes 6291456 | tf_op jit(solution)/shard_map/pallas_call | solution.py:122
  136.2 5.0 %all_to_all.44 = f32[2,32,16,128]{3,2,1,0:T(8,128)S(1)} all-to-all(f32[2,32,16,128]{3,2,1,0:T(8,128)S(1)} %get-tuple-element.14), channel_id=1, replica_groups=mesh['z'=16,'h'=2,'c'=2,'x'=4,'l'=2] {'c'}, dimensions={0} | all-to-all | bytes 1048576 | tf_op jit(solution)/shard_map/all_to_all | solution.py:229
  141.9 11.7 %all-to-all-start.7 = ((bf16[32,16,128]{2,1,0:T(8,128)(2,1)}), bf16[32,16,128]{2,1,0:T(8,128)(2,1)S(1)}, u32[]{:S(2)}, u32[]{:S(2)}) async-start(bf16[32,16,128]{2,1,0:T(8,128)(2,1)} %fusion.3), calls=%async_computation.7 | async-start | bytes 262144 | tf_op jit(solution)/shard_map/all_to_all | solution.py:231
  153.6 2.6 %collective-permute-start.1 = (bf16[128,1024]{1,0:T(8,128)(2,1)S(1)}, bf16[128,1024]{1,0:T(8,128)(2,1)S(1)}, u32[]{:S(2)}, u32[]{:S(2)}) collective-permute-start(bf16[128,1024]{1,0:T(8,128)(2,1)S(1)} %get-tuple-element.10), channel_id=1, source_target_pairs={{8,0},{16,8},{24,16},{32,24},{40,32},{48,40},{56,48},{64,56},{72,6... | collective-permute-start | bytes 786440 | tf_op jit(solution)/shard_map/ppermute | solution.py:228
  156.2 1.7 slice.45
  157.9 1.7 all_gather_reshape.3
  160.6 2.2 %all_gather.11 = bf16[2,16,16,2,2,128]{5,2,0,3,1,4:T(8,128)(2,1)S(1)} all-gather(bf16[1,16,16,2,2,128]{5,2,0,3,1,4:T(8,128)(2,1)S(1)} %copy.25), channel_id=1, replica_groups=mesh['z'=16,'h'=2,'c'=2,'x'=4,'l'=2] {'c'}, dimensions={0}, use_global_device_ids=true | all-gather | bytes 786432 | tf_op jit(solution)/shard_map/all_gather | solution.py:235
  165.2 7.1 %shard_map.141 = (bf16[256,1024]{1,0:T(8,128)(2,1)}, bf16[256,1024]{1,0:T(8,128)(2,1)}) custom-call(bf16[2,256,512]{2,1,0:T(8,128)(2,1)S(1)} %all-to-all-done.5.mix_ref, f32[384,1024]{1,0:T(8,128)S(1)} %add_add_fusion.freq_ref, f32[384,1024]{1,0:T(8,128)S(1)} %copy-done.5, bf16[128,1024]{1,0:T(8,128)(2,1)S(1)} %collective-permute-done.1.halo_ref, ...), custom_call_target="tpu_custom_call" | custom-call | flops 1711276032 | bytes 6291456 | tf_op jit(solution)/shard_map/pallas_call | solution.py:159
  (53 shorter events, 10.6 us)
Async XLA Ops:
  7.2 13.0 %copy-start.10 = (bf16[256,512]{1,0:T(8,128)(2,1)S(1)}, bf16[256,512]{1,0:T(8,128)(2,1)}, u32[]{:S(2)}) copy-start(bf16[256,512]{1,0:T(8,128)(2,1)} %param.12) | copy-start | bytes 786436
  7.2 95.0 %all-gather.3.cloned.1.call-start = ((), (), s32[]{:S(2)}) async-start(), calls=%async_computation.8 | async-start | bytes 2506752 | tf_op jit(solution)/shard_map/all_gather | solution.py:201
  49.4 5.0 %copy-start.9 = (bf16[256,1024]{1,0:T(8,128)(2,1)S(1)}, bf16[256,1024]{1,0:T(8,128)(2,1)}, u32[]{:S(2)}) copy-start(bf16[256,1024]{1,0:T(8,128)(2,1)} %param.14) | copy-start | bytes 1572868
  49.4 8.7 %copy-start.12 = (bf16[384,256]{1,0:T(8,128)(2,1)S(1)}, bf16[384,256]{1,0:T(8,128)(2,1)}, u32[]{:S(2)}) copy-start(bf16[384,256]{1,0:T(8,128)(2,1)} %constant.29) | copy-start | bytes 589828
  49.4 52.7 %all-to-all-start.2 = ((bf16[4,4,512,256]{3,2,1,0:T(8,128)(2,1)}), bf16[4,4,512,256]{3,2,1,0:T(8,128)(2,1)}, u32[]{:S(2)}, u32[]{:S(2)}) async-start(bf16[4,4,512,256]{3,2,1,0:T(8,128)(2,1)} %broadcast_in_dim.24), calls=%async_computation.2 | async-start | bytes 8388608 | tf_op jit(solution)/shard_map/all_to_all | solution.py:212
  54.4 5.3 %copy-start.11 = (bf16[384,256]{1,0:T(8,128)(2,1)S(1)}, bf16[384,256]{1,0:T(8,128)(2,1)}, u32[]{:S(2)}) copy-start(bf16[384,256]{1,0:T(8,128)(2,1)} %constant.27) | copy-start | bytes 589828
  54.5 7.0 %collective-permute-start = (bf16[128,1024]{1,0:T(8,128)(2,1)S(1)}, bf16[128,1024]{1,0:T(8,128)(2,1)S(1)}, u32[]{:S(2)}, u32[]{:S(2)}) collective-permute-start(bf16[128,1024]{1,0:T(8,128)(2,1)S(1)} %slice.32), channel_id=1, source_target_pairs={{0,8},{8,16},{16,24},{24,32},{32,40},{40,48},{48,56},{56,64},{64,7... | collective-permute-start | bytes 786440 | tf_op jit(solution)/shard_map/ppermute | solution.py:205
  59.7 1.7 copy-start.13
  102.1 1.7 copy-start
  118.7 12.7 %all-to-all-start.5 = ((bf16[2,256,512]{2,1,0:T(8,128)(2,1)}), bf16[2,256,512]{2,1,0:T(8,128)(2,1)S(1)}, u32[]{:S(2)}, u32[]{:S(2)}) async-start(bf16[2,256,512]{2,1,0:T(8,128)(2,1)} %fusion.1), calls=%async_computation.5 | async-start | bytes 1048576 | tf_op jit(solution)/shard_map/all_to_all | solution.py:223
  122.2 9.2 %copy-start.1 = (bf16[256,1024]{1,0:T(8,128)(2,1)S(1)}, bf16[256,1024]{1,0:T(8,128)(2,1)}, u32[]{:S(2)}) copy-start(bf16[256,1024]{1,0:T(8,128)(2,1)} %gate_ref.1) | copy-start | bytes 1572868
  122.2 9.2 %copy-start.2 = (bf16[2,384,256]{2,1,0:T(8,128)(2,1)S(1)}, bf16[2,384,256]{2,1,0:T(8,128)(2,1)}, u32[]{:S(2)}) copy-start(bf16[2,384,256]{2,1,0:T(8,128)(2,1)} %constant.20.clone.own_ref) | copy-start | bytes 1179652
  122.2 9.2 %copy-start.3 = (bf16[2,128,384]{2,1,0:T(8,128)(2,1)S(1)}, bf16[2,128,384]{2,1,0:T(8,128)(2,1)}, u32[]{:S(2)}) copy-start(bf16[2,128,384]{2,1,0:T(8,128)(2,1)} %constant.21.clone.lag_ref) | copy-start | bytes 589828
  135.1 1.2 copy-start.4
  141.2 22.6 %copy-start.6 = (bf16[2,256,384]{2,1,0:T(8,128)(2,1)S(1)}, bf16[2,256,384]{2,1,0:T(8,128)(2,1)}, u32[]{:S(2)}) copy-start(bf16[2,256,384]{2,1,0:T(8,128)(2,1)} %constant.24.clone.inv_ref) | copy-start | bytes 1179652
  141.2 22.6 %copy-start.7 = (bf16[2,384,128]{2,1,0:T(8,128)(2,1)S(1)}, bf16[2,384,128]{2,1,0:T(8,128)(2,1)}, u32[]{:S(2)}) copy-start(bf16[2,384,128]{2,1,0:T(8,128)(2,1)} %constant.22.clone.head_ref) | copy-start | bytes 589828
  141.2 22.6 %copy-start.8 = (bf16[2,384,128]{2,1,0:T(8,128)(2,1)S(1)}, bf16[2,384,128]{2,1,0:T(8,128)(2,1)}, u32[]{:S(2)}) copy-start(bf16[2,384,128]{2,1,0:T(8,128)(2,1)} %constant.23.clone.tail_ref) | copy-start | bytes 589828
  141.9 30.4 %all-to-all-start.7 = ((bf16[32,16,128]{2,1,0:T(8,128)(2,1)}), bf16[32,16,128]{2,1,0:T(8,128)(2,1)S(1)}, u32[]{:S(2)}, u32[]{:S(2)}) async-start(bf16[32,16,128]{2,1,0:T(8,128)(2,1)} %fusion.3), calls=%async_computation.7 | async-start | bytes 262144 | tf_op jit(solution)/shard_map/all_to_all | solution.py:231
  153.6 10.2 %collective-permute-start.1 = (bf16[128,1024]{1,0:T(8,128)(2,1)S(1)}, bf16[128,1024]{1,0:T(8,128)(2,1)S(1)}, u32[]{:S(2)}, u32[]{:S(2)}) collective-permute-start(bf16[128,1024]{1,0:T(8,128)(2,1)S(1)} %get-tuple-element.10), channel_id=1, source_target_pairs={{8,0},{16,8},{24,16},{32,24},{40,32},{48,40},{56,48},{64,56},{72,6... | collective-permute-start | bytes 786440 | tf_op jit(solution)/shard_map/ppermute | solution.py:228
  163.8 1.4 copy-start.5
Sparse Core Ops, SparseCore 0:
  20.3 69.5 all-gather.2

commit v3 on v2

v3 whole, which is shorter than its diff:
```python
import jax
import jax.numpy as jnp
import numpy as np
from jax import lax
from jax.experimental import pallas as pl
from jax.experimental.pallas import tpu as pltpu
from jax.sharding import Mesh, PartitionSpec as P

K = 128
TOK = 256
CH = 1024
SPAN = 8192
N = K + TOK
HALF = N // 2
TILE = 256

BF = jnp.bfloat16
F32 = jnp.float32
ROWS = ((1,), (0,))
LANES = ((1,), (1,))


def transforms():
    freq = 2.0 * np.pi * (np.arange(HALF) + 0.5) / N
    angle = freq[:, None] * np.arange(N + K)[None, :]
    forward = np.concatenate([np.cos(angle), -np.sin(angle)], axis=0)
    angle = angle[:, :N].T
    inverse = np.concatenate([np.cos(angle), -np.sin(angle)], axis=1) * (2.0 / N)
    return two(forward), two(inverse)


def two(values):
    values = np.asarray(values, np.float32)
    upper = values.astype(jnp.bfloat16)
    lower = (values - upper.astype(np.float32)).astype(jnp.bfloat16)
    return np.stack([upper, lower])


def dot(a, b, dims=ROWS):
    return lax.dot_general(a, b, (dims, ((), ())), preferred_element_type=F32)


def exact_side(matrix, values):
    return dot(matrix[0], values) + dot(matrix[1], values)


def both_sides(matrix, values):
    high = values.astype(BF)
    low = (values - high.astype(F32)).astype(BF)
    return dot(matrix[0], high) + dot(matrix[1], high) + dot(matrix[0], low)


def times(a, b):
    ar, ai, br, bi = a[:HALF], a[HALF:], b[:HALF], b[HALF:]
    return jnp.concatenate([ar * br - ai * bi, ar * bi + ai * br], axis=0)


def times_conj(a, b):
    ar, ai, br, bi = a[:HALF], a[HALF:], b[:HALF], b[HALF:]
    return jnp.concatenate([ar * br + ai * bi, ai * br - ar * bi], axis=0)


def params():
    return pltpu.CompilerParams(
        dimension_semantics=("arbitrary",), vmem_limit_bytes=40 * 1024 * 1024
    )


def product_kernel(core_ref, own_ref, other_ref, weight_ref, out_ref):
    weight = weight_ref[...].reshape(8 * K, 512)

    def run(source):
        rows = jnp.concatenate([source[i, 0] for i in range(8)], axis=1)
        out_ref[0, 0] = dot(rows, weight).astype(BF)

    @pl.when(pl.program_id(0) == 0)
    def _():
        run(own_ref)

    @pl.when(pl.program_id(0) == 1)
    def _():
        run(other_ref)


def product(core, own, other, weights):
    def place(i, j, core_ref):
        return (j, jnp.where(i == 0, core_ref[0], 1 - core_ref[0]), 0, 0)

    return pl.pallas_call(
        product_kernel,
        grid_spec=pltpu.PrefetchScalarGridSpec(
            num_scalar_prefetch=1,
            grid=(2, 4),
            in_specs=[
                pl.BlockSpec((8, 1, TOK, K), lambda i, j, s: (0, jnp.where(i == 0, j, 3), 0, 0)),
                pl.BlockSpec((8, 1, TOK, K), lambda i, j, s: (0, jnp.where(i == 1, j, 0), 0, 0)),
                pl.BlockSpec((8, K, 512), lambda i, j, s: (0, 0, 0)),
            ],
            out_specs=pl.BlockSpec((1, 1, TOK, 512), place),
        ),
        out_shape=jax.ShapeDtypeStruct((4, 2, TOK, 512), BF),
        compiler_params=pltpu.CompilerParams(
            dimension_semantics=("arbitrary", "arbitrary"), vmem_limit_bytes=40 * 1024 * 1024
        ),
        cost_estimate=pl.CostEstimate(
            flops=2 * 2048 * 1024 * 512, bytes_accessed=7 << 20, transcendentals=0
        ),
    )(core, own, other, weights)


def whole(shape):
    return pl.BlockSpec(shape, lambda j: (0,) * len(shape))


def tile(rows):
    return pl.BlockSpec((rows, TILE), lambda j: (0, j))


def front_kernel(window_ref, tap_ref, forward_ref, inv_ref, freq_ref, tap_freq_ref, conv_ref):
    upper, lower = tap_ref[0], tap_ref[1]
    high, low = forward_ref[0, :, :K], forward_ref[1, :, :K]
    tap_freq = dot(high, upper, LANES) + dot(low, upper, LANES) + dot(high, lower, LANES)
    tap_freq_ref[...] = tap_freq
    freq = exact_side(forward_ref, window_ref[...])
    freq_ref[...] = freq
    conv_ref[...] = both_sides(inv_ref, times(freq, tap_freq))


def front_part(window, taps, forward, inv):
    return pl.pallas_call(
        front_kernel,
        grid=(CH // TILE,),
        in_specs=[
            tile(N),
            pl.BlockSpec((2, TILE, K), lambda j: (0, j, 0)),
            whole((2, N, N)),
            whole((2, TOK, N)),
        ],
        out_specs=[tile(N), tile(N), tile(TOK)],
        out_shape=[
            jax.ShapeDtypeStruct((N, CH), F32),
            jax.ShapeDtypeStruct((N, CH), F32),
            jax.ShapeDtypeStruct((TOK, CH), F32),
        ],
        compiler_params=params(),
        cost_estimate=pl.CostEstimate(
            flops=2 * CH * N * (3 * K + 2 * N + 3 * TOK), bytes_accessed=8 << 20, transcendentals=0
        ),
    )(window, taps, forward, inv)


def grad_kernel(
    mix_ref,
    gate_ref,
    conv_ref,
    freq_ref,
    own_ref,
    lag_ref,
    gate_grad_ref,
    head_ref,
    spec_ref,
    tap_ref,
):
    parts = mix_ref[:, 0].astype(F32)
    mixed = (parts[0] + parts[1] + (parts[2] + parts[3])).astype(BF).astype(F32)
    gate_grad_ref[...] = (mixed * conv_ref[...]).astype(BF)
    conv_grad = (mixed * gate_ref[...].astype(F32)).astype(BF)
    head_ref[...] = conv_grad[:K]
    spec = exact_side(own_ref, conv_grad)
    spec_ref[...] = spec
    taps = both_sides(lag_ref, times_conj(spec, freq_ref[...]))
    taps = taps.T.reshape(8, 2, 16, K)
    tap_ref[0] = taps[:, 0]
    tap_ref[1] = taps[:, 1]


def grad_part(mix, gate, conv, sig_freq, own, lag):
    return pl.pallas_call(
        grad_kernel,
        grid=(CH // TILE,),
        in_specs=[
            pl.BlockSpec((4, 1, TOK, TILE), lambda j: (0, j // 2, 0, j % 2)),
            tile(TOK),
            tile(TOK),
            tile(N),
            whole((2, N, TOK)),
            whole((2, K, N)),
        ],
        out_specs=[
            tile(TOK),
            tile(K),
            tile(N),
            pl.BlockSpec((2, 8, 16, K), lambda j: (0, j, 0, 0)),
        ],
        out_shape=[
            jax.ShapeDtypeStruct((TOK, CH), BF),
            jax.ShapeDtypeStruct((K, CH), BF),
            jax.ShapeDtypeStruct((N, CH), F32),
            jax.ShapeDtypeStruct((2, 32, 16, K), F32),
        ],
        compiler_params=params(),
        cost_estimate=pl.CostEstimate(
            flops=2 * CH * N * (2 * TOK + 3 * K), bytes_accessed=9 << 20, transcendentals=0
        ),
    )(mix, gate, conv, sig_freq, own, lag)


def out_kernel(spec_ref, halo_ref, tap_ref, tail_ref, inv_ref, sig_ref):
    full = spec_ref[...] + exact_side(tail_ref, halo_ref[...])
    sig_ref[...] = both_sides(inv_ref, times_conj(full, tap_ref[...])).astype(BF)


def out_part(spec, halo, tap_freq, tail, inv):
    return pl.pallas_call(
        out_kernel,
        grid=(CH // TILE,),
        in_specs=[tile(N), tile(K), tile(N), whole((2, N, K)), whole((2, TOK, N))],
        out_specs=tile(TOK),
        out_shape=jax.ShapeDtypeStruct((TOK, CH), BF),
        compiler_params=params(),
        cost_estimate=pl.CostEstimate(
            flops=2 * CH * N * (2 * K + 3 * TOK), bytes_accessed=5 << 20, transcendentals=0
        ),
    )(spec, halo, tap_freq, tail, inv)


def on_device(out_grad, out_weight, signal, gate_input, filter_taps):
    ctx = ("m", "p", "h", "c")
    n_ctx = 64
    period = SPAN // TOK
    fwd, inv = transforms()
    core = lax.axis_index("c")

    turned = out_weight.T.reshape(64, 2, 512).transpose(1, 0, 2)
    turned = lax.all_to_all(turned, "c", split_axis=0, concat_axis=0).reshape(K, 512)

    tap_rows = filter_taps.T
    tap_high = lax.optimization_barrier(tap_rows.astype(BF))
    tap_low = (tap_rows - tap_high.astype(F32)).astype(BF)
    tap_pack = jnp.concatenate([tap_high, tap_low], axis=0)
    cols = out_grad.reshape(TOK, 4, K).transpose(1, 0, 2)
    cols = jnp.concatenate([cols, jnp.broadcast_to(tap_pack[None], (4, 32, K))], axis=1)
    turned, cols = lax.optimization_barrier((turned, cols))
    weights = lax.all_gather(turned, "m", axis=0, tiled=False)
    cols = lax.all_to_all(cols, ("p", "h"), split_axis=0, concat_axis=0)
    tap_part = cols[:, TOK:]
    cols = lax.all_gather(cols[:, :TOK], "l", axis=0, tiled=False)
    cols = lax.all_to_all(
        jnp.broadcast_to(cols[None], (4, 2, 4, TOK, K)), "x", split_axis=0, concat_axis=0
    ).reshape(8, 4, TOK, K)
    cols_other = lax.ppermute(cols, "c", [(0, 1), (1, 0)])

    ahead = [(i, i + 1) for i in range(n_ctx - 1) if (i + 1) % period]
    back = [(j, i) for i, j in ahead]
    sig_halo = lax.ppermute(signal[TOK - K :], ctx, ahead)
    window = jnp.concatenate([sig_halo, signal], axis=0)
    taps = lax.all_gather(tap_part, "m", axis=0, tiled=False)
    taps = lax.all_gather(taps, "c", axis=0, tiled=False)
    taps = taps.reshape(2, 8, 4, 2, 16, K).transpose(3, 1, 2, 0, 4, 5).reshape(2, CH, K)
    sig_freq, tap_freq, conv = front_part(window, taps, fwd[:, :, :N], inv[:, K:])

    partial = product(core.reshape(1), cols, cols_other, weights)
    mix = lax.all_to_all(
        partial.reshape(8, TOK, 512), ("p", "h", "c"), split_axis=0, concat_axis=0
    ).reshape(4, 2, TOK, 512)

    gate_grad, grad_head, spec, tap_grad = grad_part(
        mix, gate_input, conv, sig_freq, fwd[:, :, K:N], inv[:, :K]
    )
    grad_halo = lax.ppermute(grad_head, ctx, back)
    tap_grad = lax.all_to_all(tap_grad, "c", split_axis=0, concat_axis=0)
    tap_grad = (tap_grad[0] + tap_grad[1]).astype(BF)
    tap_grad = lax.all_to_all(tap_grad, ("m", "p", "h"), split_axis=0, concat_axis=0)
    filter_grad = jnp.sum(tap_grad.astype(F32), axis=0).T

    signal_grad = out_part(spec, grad_halo, tap_freq, fwd[:, :, N:], inv[:, K:])
    return signal_grad, gate_grad, filter_grad


def solution(mesh):
    fine = Mesh(mesh.devices.reshape(8, 2, 2, 2, 4, 2), ("m", "p", "h", "c", "x", "l"))
    ctx, tp = ("m", "p", "h", "c"), ("x", "l")
    in_specs = (P(ctx, tp), P(tp, ctx), P(ctx, tp), P(ctx, tp), P(None, tp + ctx))
    out_specs = (P(ctx, tp), P(ctx, tp), P(None, tp + ctx))
    return jax.shard_map(
        on_device, mesh=fine, in_specs=in_specs, out_specs=out_specs, check_vma=False
    )
```

time: 181 us -> 252 us (1.39)
  waiting for transfers between devices: 46.8 us -> 75.1 us
  blocking collectives: 50.6 us -> 74.6 us
  starting transfers between devices: 26.5 us -> 47.5 us
  matrix products: 7.41 us -> 0 us
  local copies, waits for them, and re-layouts: 12.4 us -> 15.5 us
  Pallas kernels: 17.5 us -> 20.3 us
    all_gather x1, waiting for transfers between devices: 0.01 us -> 46.5 us  [on_device(): weights = lax.all_gather(turned, 'm', axis=0, tiled=False)]
    all_to_all x3, waiting for transfers between devices: 45.5 us -> 0.01 us  [the longest x1 0.01 us: on_device(): lax.all_to_all(partial.reshape(8, TOK, 512), ('p', 'h', 'c'), split_axis=...]
    all_gather x1 -> x3, blocking collectives: 2.18 us -> 33.1 us  [the longest x1 22.9 us: on_device(): taps = lax.all_gather(tap_part, 'm', axis=0, tiled=False)]
    ppermute x1, waiting for transfers between devices: 0.22 us -> 20.8 us  [on_device(): sig_halo = lax.ppermute(signal[TOK - K:], ctx, ahead)]
    all_to_all x3, starting transfers between devices: 20.2 us -> 35.1 us  [the longest x1 16.4 us: on_device(): lax.all_to_all(tap_grad, ('m', 'p', 'h'), split_axis=0, concat_axis=0)]
    unnamed x29 -> x35, local copies, waits for them, and re-layouts: 4.42 us -> 12.9 us
    dot_general x4 -> x0, matrix products: 7.41 us -> none  [dot(): return lax.dot_general(a, b, (dims, ((), ())), preferred_element_type=F32)]
    ppermute x1, waiting for transfers between devices: 1.06 us -> 7.8 us  [on_device(): grad_halo = lax.ppermute(grad_head, ctx, back)]
  transfers between devices with their start and end apart: 6 -> 7, of which waited for: 4 -> 3; matrix products, arithmetic and copies ran while one was open for 8% -> 1% of each run, Pallas kernels for 4% -> 4%
where the time goes in v3:
time: 252 us; the launch traced here: 250 us
  waiting for transfers between devices  75.1 us (30%)
  blocking collectives  74.6 us (30%)
  starting transfers between devices  47.5 us (19%)
  Pallas kernels  20.3 us (8%)
  local copies, waits for them, and re-layouts  15.5 us (6%)
  between operations  14.2 us (6%)
  other arithmetic  2.82 us (1%)
    all_gather x1, waiting for transfers between devices, on_device(): weights = lax.all_gather(turned, 'm', axis=0, tiled=False)  46.5 us
    all_to_all x1, blocking collectives, on_device(): lax.all_to_all(jnp.broadcast_to(cols[None], (4, 2, 4, TOK, K)), 'x', spli...  27 us
    all_gather x1, blocking collectives, on_device(): taps = lax.all_gather(tap_part, 'm', axis=0, tiled=False)  22.9 us
    ppermute x1, waiting for transfers between devices, on_device(): sig_halo = lax.ppermute(signal[TOK - K:], ctx, ahead)  20.8 us
    all_to_all x1, starting transfers between devices, on_device(): lax.all_to_all(tap_grad, ('m', 'p', 'h'), split_axis=0, concat_axis=0)  16.4 us
    unnamed x35, local copies, waits for them, and re-layouts  12.9 us
    all_to_all x1, starting transfers between devices, on_device(): lax.all_to_all(turned, 'c', split_axis=0, concat_axis=0).reshape(K, 512)  10.2 us
    all_to_all x1, blocking collectives, on_device(): cols = lax.all_to_all(cols, ('p', 'h'), split_axis=0, concat_axis=0)  10.2 us
  transfers between devices with their start and end apart: 7, of which 3 were waited for; matrix products, arithmetic and copies ran while one was open for 1% of the time, Pallas kernels for 4%

profile of v3, /device:TPU:1, one launch (start us, length us, event | category | flops | bytes accessed | tf_op | source)
XLA Modules:
  0.0 250.0 jit_solution(6607806617214114077)
XLA Ops:
  8.8 10.2 %all-to-all-start = ((bf16[2,64,512]{2,1,0:T(8,128)(2,1)}), bf16[2,64,512]{2,1,0:T(8,128)(2,1)S(1)}, u32[]{:S(2)}, u32[]{:S(2)}) async-start(bf16[2,64,512]{2,1,0:T(8,128)(2,1)} %copy.26), calls=%async_computation | async-start | bytes 262144 | tf_op jit(solution)/shard_map/all_to_all | solution.py:235
  22.0 10.2 %all_to_all.30 = bf16[4,288,128]{2,1,0:T(8,128)(2,1)S(1)} all-to-all(bf16[4,288,128]{2,1,0:T(8,128)(2,1)S(1)} %copy.29), channel_id=1, replica_groups=mesh['m'=8,'p'=2,'h'=2,'c'=2,'x'=4,'l'=2] {'p','h'}, dimensions={0} | all-to-all | bytes 589824 | tf_op jit(solution)/shard_map/all_to_all | solution.py:245
  32.2 7.5 %all-gather = bf16[8,256,128]{2,1,0:T(8,128)(2,1)S(1)} all-gather(bf16[4,256,128]{2,1,0:T(8,128)(2,1)S(1)} %slice.20), channel_id=2, replica_groups=mesh['m'=8,'p'=2,'h'=2,'c'=2,'x'=4,'l'=2] {'l'}, dimensions={0}, use_global_device_ids=true | all-gather | bytes 786432 | tf_op jit(solution)/shard_map/all_gather | solution.py:247
  40.3 27.0 %all_to_all.31 = bf16[4,2,4,256,128]{4,3,2,1,0:T(8,128)(2,1)S(1)} all-to-all(bf16[4,2,4,256,128]{4,3,2,1,0:T(8,128)(2,1)S(1)} %broadcast_in_dim.5), channel_id=1, replica_groups=mesh['m'=8,'p'=2,'h'=2,'c'=2,'x'=4,'l'=2] {'x'}, dimensions={0} | all-to-all | bytes 4194304 | tf_op jit(solution)/shard_map/all_to_all | solution.py:248
  67.2 4.7 %collective-permute-start = (bf16[8,4,256,128]{3,2,1,0:T(8,128)(2,1)S(1)}, bf16[8,4,256,128]{3,2,1,0:T(8,128)(2,1)}, u32[]{:S(2)}, u32[]{:S(2)}) collective-permute-start(bf16[8,4,256,128]{3,2,1,0:T(8,128)(2,1)S(1)} %bitcast.27), channel_id=1, source_target_pairs={{0,8},{8,0},{1,9},{9,1},{2,10},{10,2},{3,11},{11,3},{4,12},{12,4},... | collective-permute-start | bytes 6291464 | tf_op jit(solution)/shard_map/ppermute | solution.py:251
  71.9 46.5 %all-gather.6.cloned.1.call-done = bf16[1024,512]{1,0:T(8,128)(2,1)} async-done(((bf16[128,512]{1,0:T(8,128)(2,1)}), bf16[1024,512]{1,0:T(8,128)(2,1)}) %all-gather.6.cloned.1.call-update) | async-done | bytes 1048592 | tf_op jit(solution)/shard_map/all_gather | solution.py:244
  118.5 1.2 copy-done.12
  119.7 6.4 %shard_map.130 = bf16[4,2,256,512]{3,2,1,0:T(8,128)(2,1)S(1)} custom-call(s32[1]{0:T(128)} %bitcast.core_ref, bf16[8,4,256,128]{3,2,1,0:T(8,128)(2,1)S(1)} %bitcast.28, bf16[8,4,256,128]{3,2,1,0:T(8,128)(2,1)} %collective-permute-done.other_ref, bf16[8,128,512]{2,1,0:T(8,128)(2,1)S(1)} %bitcast.30), custom_call_target="tpu_custom_call" | custom-call | flops 2147483648 | bytes 7340032 | tf_op jit(solution)/shard_map/pallas_call | solution.py:89
  126.2 1.3 copy-done
  127.5 8.4 %all-to-all-start.3 = ((bf16[8,256,512]{2,1,0:T(8,128)(2,1)}), bf16[8,256,512]{2,1,0:T(8,128)(2,1)S(1)}, u32[]{:S(2)}, u32[]{:S(2)}) async-start(bf16[8,256,512]{2,1,0:T(8,128)(2,1)} %bitcast.26), calls=%async_computation.3 | async-start | bytes 4194304 | tf_op jit(solution)/shard_map/all_to_all | solution.py:263
  136.0 5.2 %collective-permute-start.1 = (bf16[128,1024]{1,0:T(8,128)(2,1)S(1)}, bf16[128,1024]{1,0:T(8,128)(2,1)S(1)}, u32[]{:S(2)}, u32[]{:S(2)}) collective-permute-start(bf16[128,1024]{1,0:T(8,128)(2,1)S(1)} %slice.16), channel_id=1, source_target_pairs={{0,8},{8,16},{16,24},{24,32},{32,40},{40,48},{48,56},{56,64},{64,7... | collective-permute-start | bytes 786440 | tf_op jit(solution)/shard_map/ppermute | solution.py:255
  141.2 20.8 %collective-permute-done.1 = bf16[128,1024]{1,0:T(8,128)(2,1)S(1)} collective-permute-done((bf16[128,1024]{1,0:T(8,128)(2,1)S(1)}, bf16[128,1024]{1,0:T(8,128)(2,1)S(1)}, u32[]{:S(2)}, u32[]{:S(2)}) %collective-permute-start.1) | collective-permute-done | bytes 262176 | tf_op jit(solution)/shard_map/ppermute | solution.py:255
  162.0 22.9 %all-gather.2 = bf16[32,32,128]{2,1,0:T(8,128)(2,1)S(1)} all-gather(bf16[4,32,128]{2,1,0:T(8,128)(2,1)S(1)} %slice.21), channel_id=4, replica_groups=mesh['m'=8,'p'=2,'h'=2,'c'=2,'x'=4,'l'=2] {'m'}, dimensions={0}, use_global_device_ids=true | all-gather | bytes 294912 | tf_op jit(solution)/shard_map/all_gather | solution.py:257
  185.0 2.6 %all-gather.3 = bf16[16,4,32,128]{3,2,1,0:T(8,128)(2,1)S(1)} all-gather(bf16[8,4,32,128]{3,2,1,0:T(8,128)(2,1)S(1)} %bitcast.34), channel_id=5, replica_groups=mesh['m'=8,'p'=2,'h'=2,'c'=2,'x'=4,'l'=2] {'c'}, dimensions={0}, use_global_device_ids=true | all-gather | bytes 786432 | tf_op jit(solution)/shard_map/all_gather | solution.py:258
  187.6 5.5 %shard_map.131 = (f32[384,1024]{1,0:T(8,128)S(1)}, f32[384,1024]{1,0:T(8,128)S(1)}, f32[256,1024]{1,0:T(8,128)S(1)}) custom-call(bf16[384,1024]{1,0:T(8,128)(2,1)S(1)} %pad_maximum_fusion.window_ref, bf16[2,1024,128]{2,1,0:T(8,128)(2,1)S(1)} %bitcast.29, bf16[2,384,384]{2,1,0:T(8,128)(2,1)S(1)} %copy-done.14, bf16[2,256,384]{2,1,0:T(8,128)(2,1)S(1)} %copy-done.8), custom_call_target="tpu_custom_call" | custom-call | flops 1509949440 | bytes 8388608 | tf_op jit(solution)/shard_map/pallas_call | solution.py:130
  195.5 1.4 copy-done.6
  199.8 4.3 %shard_map.132 = (bf16[256,1024]{1,0:T(8,128)(2,1)}, bf16[128,1024]{1,0:T(8,128)(2,1)S(1)}, f32[384,1024]{1,0:T(8,128)S(1)}, f32[2,32,16,128]{3,2,1,0:T(8,128)S(1)}) custom-call(bf16[4,2,256,512]{3,2,1,0:T(8,128)(2,1)S(1)} %bitcast.25, bf16[256,1024]{1,0:T(8,128)(2,1)S(1)} %copy-done.7, f32[256,1024]{1,0:T(8,128)S(1)} %get-tuple-element.14.conv_ref, ...), custom_call_target="tpu_custom_call" | custom-call | flops 704643072 | bytes 9437184 | tf_op jit(solution)/shard_map/pallas_call | solution.py:178
  204.1 1.2 copy-done.3
  205.3 4.3 %all_to_all.32 = f32[2,32,16,128]{3,2,1,0:T(8,128)S(1)} all-to-all(f32[2,32,16,128]{3,2,1,0:T(8,128)S(1)} %get-tuple-element.20), channel_id=1, replica_groups=mesh['m'=8,'p'=2,'h'=2,'c'=2,'x'=4,'l'=2] {'c'}, dimensions={0} | all-to-all | bytes 1048576 | tf_op jit(solution)/shard_map/all_to_all | solution.py:271
  210.3 16.4 %all-to-all-start.5 = ((bf16[32,16,128]{2,1,0:T(8,128)(2,1)}), bf16[32,16,128]{2,1,0:T(8,128)(2,1)S(1)}, u32[]{:S(2)}, u32[]{:S(2)}) async-start(bf16[32,16,128]{2,1,0:T(8,128)(2,1)} %fusion.1), calls=%async_computation.5 | async-start | bytes 262144 | tf_op jit(solution)/shard_map/all_to_all | solution.py:273
  226.7 2.6 %collective-permute-start.2 = (bf16[128,1024]{1,0:T(8,128)(2,1)}, bf16[128,1024]{1,0:T(8,128)(2,1)S(1)}, u32[]{:S(2)}, u32[]{:S(2)}) collective-permute-start(bf16[128,1024]{1,0:T(8,128)(2,1)} %copy-done.13), channel_id=1, source_target_pairs={{8,0},{16,8},{24,16},{32,24},{40,32},{48,40},{56,48},{64,56},{72,6... | collective-permute-start | bytes 786440 | tf_op jit(solution)/shard_map/ppermute | solution.py:270
  229.2 7.8 %collective-permute-done.2.halo_ref = bf16[128,1024]{1,0:T(8,128)(2,1)S(1)} collective-permute-done((bf16[128,1024]{1,0:T(8,128)(2,1)}, bf16[128,1024]{1,0:T(8,128)(2,1)S(1)}, u32[]{:S(2)}, u32[]{:S(2)}) %collective-permute-start.2) | collective-permute-done | bytes 262176 | tf_op jit(solution)/shard_map/ppermute | solution.py:270
  237.0 1.4 copy-done.4
  238.4 4.1 %shard_map.133 = bf16[256,1024]{1,0:T(8,128)(2,1)} custom-call(f32[384,1024]{1,0:T(8,128)S(1)} %copy-done.4, bf16[128,1024]{1,0:T(8,128)(2,1)S(1)} %collective-permute-done.2.halo_ref, f32[384,1024]{1,0:T(8,128)S(1)} %copy-done.2, bf16[2,384,128]{2,1,0:T(8,128)(2,1)S(1)} %copy-done.10, bf16[2,256,384]{2,1,0:T(8,128)(2,1)S(1)} %copy-done.8), custom_call_target="tpu_custom_call" | custom-call | flops 805306368 | bytes 5242880 | tf_op jit(solution)/shard_map/pallas_call | solution.py:214
  (53 shorter events, 11.8 us)
Async XLA Ops:
  8.8 13.0 %all-to-all-start = ((bf16[2,64,512]{2,1,0:T(8,128)(2,1)}), bf16[2,64,512]{2,1,0:T(8,128)(2,1)S(1)}, u32[]{:S(2)}, u32[]{:S(2)}) async-start(bf16[2,64,512]{2,1,0:T(8,128)(2,1)} %copy.26), calls=%async_computation | async-start | bytes 262144 | tf_op jit(solution)/shard_map/all_to_all | solution.py:235
  19.1 99.4 %all-gather.6.cloned.1.call-start = ((), (), s32[]{:S(2)}) async-start(), calls=%async_computation.6 | async-start | bytes 1179648 | tf_op jit(solution)/shard_map/all_gather | solution.py:244
  21.8 18.5 %copy-start.16 = (bf16[2,64,512]{2,1,0:T(8,128)(2,1)}, bf16[2,64,512]{2,1,0:T(8,128)(2,1)S(1)}, u32[]{:S(2)}) copy-start(bf16[2,64,512]{2,1,0:T(8,128)(2,1)S(1)} %all-to-all-done) | copy-start | bytes 393220
  67.2 51.2 %collective-permute-start = (bf16[8,4,256,128]{3,2,1,0:T(8,128)(2,1)S(1)}, bf16[8,4,256,128]{3,2,1,0:T(8,128)(2,1)}, u32[]{:S(2)}, u32[]{:S(2)}) collective-permute-start(bf16[8,4,256,128]{3,2,1,0:T(8,128)(2,1)S(1)} %bitcast.27), channel_id=1, source_target_pairs={{0,8},{8,0},{1,9},{9,1},{2,10},{10,2},{3,11},{11,3},{4,12},{12,4},... | collective-permute-start | bytes 6291464 | tf_op jit(solution)/shard_map/ppermute | solution.py:251
  118.5 1.2 copy-start.12
  126.1 1.3 copy-start
  127.5 8.5 %copy-start.15 = (bf16[256,1024]{1,0:T(8,128)(2,1)S(1)}, bf16[256,1024]{1,0:T(8,128)(2,1)}, u32[]{:S(2)}) copy-start(bf16[256,1024]{1,0:T(8,128)(2,1)} %param.13) | copy-start | bytes 1572868
  127.5 68.0 %all-to-all-start.3 = ((bf16[8,256,512]{2,1,0:T(8,128)(2,1)}), bf16[8,256,512]{2,1,0:T(8,128)(2,1)S(1)}, u32[]{:S(2)}, u32[]{:S(2)}) async-start(bf16[8,256,512]{2,1,0:T(8,128)(2,1)} %bitcast.26), calls=%async_computation.3 | async-start | bytes 4194304 | tf_op jit(solution)/shard_map/all_to_all | solution.py:263
  136.0 51.7 %copy-start.8 = (bf16[2,256,384]{2,1,0:T(8,128)(2,1)S(1)}, bf16[2,256,384]{2,1,0:T(8,128)(2,1)}, u32[]{:S(2)}) copy-start(bf16[2,256,384]{2,1,0:T(8,128)(2,1)} %constant.19.clone.inv_ref) | copy-start | bytes 1179652
  136.0 51.7 %copy-start.14 = (bf16[2,384,384]{2,1,0:T(8,128)(2,1)S(1)}, bf16[2,384,384]{2,1,0:T(8,128)(2,1)}, u32[]{:S(2)}) copy-start(bf16[2,384,384]{2,1,0:T(8,128)(2,1)} %constant.18.clone.forward_ref) | copy-start | bytes 1769476
  136.0 25.9 %collective-permute-start.1 = (bf16[128,1024]{1,0:T(8,128)(2,1)S(1)}, bf16[128,1024]{1,0:T(8,128)(2,1)S(1)}, u32[]{:S(2)}, u32[]{:S(2)}) collective-permute-start(bf16[128,1024]{1,0:T(8,128)(2,1)S(1)} %slice.16), channel_id=1, source_target_pairs={{0,8},{8,16},{16,24},{24,32},{32,40},{40,48},{48,56},{56,64},{64,7... | collective-permute-start | bytes 786440 | tf_op jit(solution)/shard_map/ppermute | solution.py:255
  193.1 1.1 copy-start.1
  194.3 1.2 copy-start.5
  195.5 1.4 copy-start.6
  196.9 1.0 copy-start.7
  197.9 1.0 copy-start.9
  198.9 0.9 copy-start.11
  204.1 1.2 copy-start.3
  205.3 4.3 %copy-start.13 = (bf16[128,1024]{1,0:T(8,128)(2,1)}, bf16[128,1024]{1,0:T(8,128)(2,1)S(1)}, u32[]{:S(2)}) copy-start(bf16[128,1024]{1,0:T(8,128)(2,1)S(1)} %get-tuple-element.17) | copy-start | bytes 786436
  205.3 31.7 %copy-start.2 = (f32[384,1024]{1,0:T(8,128)S(1)}, f32[384,1024]{1,0:T(8,128)}, u32[]{:S(2)}) copy-start(f32[384,1024]{1,0:T(8,128)} %copy-done.1) | copy-start | bytes 4718596
  205.3 31.8 %copy-start.10 = (bf16[2,384,128]{2,1,0:T(8,128)(2,1)S(1)}, bf16[2,384,128]{2,1,0:T(8,128)(2,1)}, u32[]{:S(2)}) copy-start(bf16[2,384,128]{2,1,0:T(8,128)(2,1)} %constant.22.clone.tail_ref) | copy-start | bytes 589828
  210.3 32.3 %all-to-all-start.5 = ((bf16[32,16,128]{2,1,0:T(8,128)(2,1)}), bf16[32,16,128]{2,1,0:T(8,128)(2,1)S(1)}, u32[]{:S(2)}, u32[]{:S(2)}) async-start(bf16[32,16,128]{2,1,0:T(8,128)(2,1)} %fusion.1), calls=%async_computation.5 | async-start | bytes 262144 | tf_op jit(solution)/shard_map/all_to_all | solution.py:273
  226.7 10.4 %collective-permute-start.2 = (bf16[128,1024]{1,0:T(8,128)(2,1)}, bf16[128,1024]{1,0:T(8,128)(2,1)S(1)}, u32[]{:S(2)}, u32[]{:S(2)}) collective-permute-start(bf16[128,1024]{1,0:T(8,128)(2,1)} %copy-done.13), channel_id=1, source_target_pairs={{8,0},{16,8},{24,16},{32,24},{40,32},{48,40},{56,48},{64,56},{72,6... | collective-permute-start | bytes 786440 | tf_op jit(solution)/shard_map/ppermute | solution.py:270
  237.0 1.4 copy-start.4
Sparse Core Ops, SparseCore 0:
  72.1 46.3 all-gather.5

commit v4 on v2

v4 whole, which is shorter than its diff:
```python
import jax
import jax.numpy as jnp
import numpy as np
from jax import lax
from jax.experimental import pallas as pl
from jax.experimental.pallas import tpu as pltpu
from jax.sharding import Mesh, PartitionSpec as P

K = 128
TOK = 256
CH = 1024
SPAN = 8192
N = K + TOK
HALF = N // 2
TILE = 256
VMEM = 56 * 1024 * 1024

BF = jnp.bfloat16
F32 = jnp.float32
ROWS = ((1,), (0,))
LANES = ((1,), (1,))


def transforms():
    freq = 2.0 * np.pi * (np.arange(HALF) + 0.5) / N
    angle = freq[:, None] * np.arange(N + K)[None, :]
    forward = np.concatenate([np.cos(angle), -np.sin(angle)], axis=0)
    angle = angle[:, :N].T
    inverse = np.concatenate([np.cos(angle), -np.sin(angle)], axis=1) * (2.0 / N)
    return two(forward), two(inverse)


def two(values):
    values = np.asarray(values, np.float32)
    upper = values.astype(jnp.bfloat16)
    lower = (values - upper.astype(np.float32)).astype(jnp.bfloat16)
    return np.stack([upper, lower])


def dot(a, b, dims=ROWS):
    return lax.dot_general(a, b, (dims, ((), ())), preferred_element_type=F32)


def exact_side(matrix, values):
    return dot(matrix[0], values) + dot(matrix[1], values)


def both_sides(matrix, values):
    high = values.astype(BF)
    low = (values - high.astype(F32)).astype(BF)
    return dot(matrix[0], high) + dot(matrix[1], high) + dot(matrix[0], low)


def times(a, b):
    ar, ai, br, bi = a[:HALF], a[HALF:], b[:HALF], b[HALF:]
    return jnp.concatenate([ar * br - ai * bi, ar * bi + ai * br], axis=0)


def times_conj(a, b):
    ar, ai, br, bi = a[:HALF], a[HALF:], b[:HALF], b[HALF:]
    return jnp.concatenate([ar * br + ai * bi, ai * br - ar * bi], axis=0)


def params():
    return pltpu.CompilerParams(
        dimension_semantics=("arbitrary",), vmem_limit_bytes=VMEM
    )


def product_kernel(cols_ref, weight_ref, out_ref):
    weight = weight_ref[:, :K].reshape(8 * K, 512)
    rows = jnp.concatenate([cols_ref[0, i, 0] for i in range(8)], axis=1)
    out_ref[0] = dot(rows, weight).astype(BF)


def product(cols, weights):
    return pl.pallas_call(
        product_kernel,
        grid=(8,),
        in_specs=[
            pl.BlockSpec((1, 8, 1, TOK, K), lambda i: (i % 2, 0, i // 2, 0, 0)),
            pl.BlockSpec((8, K + 16, 512), lambda i: (0, 0, 0)),
        ],
        out_specs=pl.BlockSpec((1, TOK, 512), lambda i: (i, 0, 0)),
        out_shape=jax.ShapeDtypeStruct((8, TOK, 512), BF),
        compiler_params=params(),
        cost_estimate=pl.CostEstimate(
            flops=2 * 2048 * 1024 * 512, bytes_accessed=7 << 20, transcendentals=0
        ),
    )(cols, weights)


def whole(shape):
    return pl.BlockSpec(shape, lambda j: (0,) * len(shape))


def tile(rows):
    return pl.BlockSpec((rows, TILE), lambda j: (0, j))


def front_kernel(window_ref, forward_ref, freq_ref):
    freq_ref[...] = exact_side(forward_ref, window_ref[...])


def front_part(window, forward):
    return pl.pallas_call(
        front_kernel,
        grid=(CH // TILE,),
        in_specs=[tile(N), whole((2, N, N))],
        out_specs=tile(N),
        out_shape=jax.ShapeDtypeStruct((N, CH), F32),
        compiler_params=params(),
        cost_estimate=pl.CostEstimate(
            flops=2 * CH * N * 2 * N, bytes_accessed=3 << 20, transcendentals=0
        ),
    )(window, forward)


def grad_kernel(
    mix_ref, gate_ref, freq_ref, own_ref, lag_ref, mixed_ref, head_ref, spec_ref, tap_ref
):
    parts = mix_ref[:, 0].astype(F32)
    mixed = (parts[0] + parts[1] + (parts[2] + parts[3])).astype(BF)
    mixed_ref[...] = mixed
    conv_grad = (mixed.astype(F32) * gate_ref[...].astype(F32)).astype(BF)
    head_ref[...] = conv_grad[:K]
    spec = exact_side(own_ref, conv_grad)
    spec_ref[...] = spec
    taps = both_sides(lag_ref, times_conj(spec, freq_ref[...]))
    taps = taps.T.reshape(8, 2, 16, K)
    tap_ref[0] = taps[:, 0]
    tap_ref[1] = taps[:, 1]


def grad_part(mix, gate, sig_freq, own, lag):
    return pl.pallas_call(
        grad_kernel,
        grid=(CH // TILE,),
        in_specs=[
            pl.BlockSpec((4, 1, TOK, TILE), lambda j: (0, j // 2, 0, j % 2)),
            tile(TOK),
            tile(N),
            whole((2, N, TOK)),
            whole((2, K, N)),
        ],
        out_specs=[
            tile(TOK),
            tile(K),
            tile(N),
            pl.BlockSpec((2, 8, 16, K), lambda j: (0, j, 0, 0)),
        ],
        out_shape=[
            jax.ShapeDtypeStruct((TOK, CH), BF),
            jax.ShapeDtypeStruct((K, CH), BF),
            jax.ShapeDtypeStruct((N, CH), F32),
            jax.ShapeDtypeStruct((2, 32, 16, K), F32),
        ],
        compiler_params=params(),
        cost_estimate=pl.CostEstimate(
            flops=2 * CH * N * (2 * TOK + 3 * K), bytes_accessed=8 << 20, transcendentals=0
        ),
    )(mix, gate, sig_freq, own, lag)


def out_kernel(
    mixed_ref, freq_ref, spec_ref, halo_ref, tap_ref, head_ref, tail_ref, inv_ref, gate_ref, sig_ref
):
    upper, lower = tap_ref[0], tap_ref[1]
    high, low = head_ref[0], head_ref[1]
    tap_freq = dot(high, upper, LANES) + dot(low, upper, LANES) + dot(high, lower, LANES)
    conv_out = both_sides(inv_ref, times(freq_ref[...], tap_freq))
    gate_ref[...] = (mixed_ref[...].astype(F32) * conv_out).astype(BF)
    full = spec_ref[...] + exact_side(tail_ref, halo_ref[...])
    sig_ref[...] = both_sides(inv_ref, times_conj(full, tap_freq)).astype(BF)


def out_part(mixed, sig_freq, spec, halo, taps, head, tail, inv):
    return pl.pallas_call(
        out_kernel,
        grid=(CH // TILE,),
        in_specs=[
            tile(TOK),
            tile(N),
            tile(N),
            tile(K),
            pl.BlockSpec((2, TILE, K), lambda j: (0, j, 0)),
            whole((2, N, K)),
            whole((2, N, K)),
            whole((2, TOK, N)),
        ],
        out_specs=[tile(TOK), tile(TOK)],
        out_shape=[jax.ShapeDtypeStruct((TOK, CH), BF)] * 2,
        compiler_params=params(),
        cost_estimate=pl.CostEstimate(
            flops=2 * CH * N * (5 * K + 6 * TOK), bytes_accessed=6 << 20, transcendentals=0
        ),
    )(mixed, sig_freq, spec, halo, taps, head, tail, inv)


def with_partner(values, axis):
    other = lax.ppermute(values, axis, [(0, 1), (1, 0)])
    first = lax.axis_index(axis) == 0
    return jnp.stack([jnp.where(first, values, other), jnp.where(first, other, values)])


def on_device(out_grad, out_weight, signal, gate_input, filter_taps):
    ctx = ("m", "p", "h", "c")
    n_ctx = 64
    period = SPAN // TOK
    fwd, inv = transforms()

    turned = out_weight.T.reshape(64, 2, 512).transpose(1, 0, 2)
    turned = lax.all_to_all(turned, "c", split_axis=0, concat_axis=0).reshape(K, 512)
    tap_rows = filter_taps.T
    tap_high = lax.optimization_barrier(tap_rows.astype(BF))
    tap_low = (tap_rows - tap_high.astype(F32)).astype(BF)
    tap_pack = jnp.concatenate([tap_high, tap_low, jnp.zeros((16, 256), BF)], axis=1)
    block = jnp.concatenate([turned, tap_pack], axis=0)

    cols = out_grad.reshape(TOK, 4, K).transpose(1, 0, 2)
    block, cols = lax.optimization_barrier((block, cols))
    weights = lax.all_gather(block, "m", axis=0, tiled=False)
    cols = lax.all_to_all(cols, ("p", "h"), split_axis=0, concat_axis=0)

    ahead = [(i, i + 1) for i in range(n_ctx - 1) if (i + 1) % period]
    back = [(j, i) for i, j in ahead]
    sig_halo = lax.ppermute(signal[TOK - K :], ctx, ahead)
    window = jnp.concatenate([sig_halo, signal], axis=0)
    sig_freq = front_part(window, fwd[:, :, :N])

    cols, sig_freq = lax.optimization_barrier((cols, sig_freq))
    cols = lax.all_to_all(
        jnp.broadcast_to(cols[None], (8, 4, TOK, K)), ("x", "l"), split_axis=0, concat_axis=0
    )
    cols = lax.all_to_all(
        jnp.broadcast_to(cols[None], (2, 8, 4, TOK, K)), "c", split_axis=0, concat_axis=0
    )

    partial = product(cols, weights)
    weights, partial = lax.optimization_barrier((weights, partial))
    mix = lax.all_to_all(
        partial, ("p", "h", "c"), split_axis=0, concat_axis=0
    ).reshape(4, 2, TOK, 512)

    mixed, grad_head, spec, tap_grad = grad_part(
        mix, gate_input, sig_freq, fwd[:, :, K:N], inv[:, :K]
    )
    grad_halo = lax.ppermute(grad_head, ctx, back)
    tap_grad = lax.all_to_all(tap_grad, "c", split_axis=0, concat_axis=0)
    tap_grad = (tap_grad[0] + tap_grad[1]).astype(BF)
    tap_grad = lax.all_to_all(tap_grad, ("m", "p", "h"), split_axis=0, concat_axis=0)
    filter_grad = jnp.sum(tap_grad.astype(F32), axis=0).T

    taps = weights[:, K:, : 2 * K].reshape(8, 16, 2, K).transpose(2, 0, 1, 3)
    taps = with_partner(with_partner(with_partner(taps, "p"), "h"), "c")
    taps = taps.transpose(3, 4, 2, 1, 0, 5, 6).reshape(2, CH, K)
    gate_grad, signal_grad = out_part(
        mixed, sig_freq, spec, grad_halo, taps, fwd[:, :, :K], fwd[:, :, N:], inv[:, K:]
    )
    return signal_grad, gate_grad, filter_grad


def solution(mesh):
    fine = Mesh(mesh.devices.reshape(8, 2, 2, 2, 4, 2), ("m", "p", "h", "c", "x", "l"))
    ctx, tp = ("m", "p", "h", "c"), ("x", "l")
    in_specs = (P(ctx, tp), P(tp, ctx), P(ctx, tp), P(ctx, tp), P(None, tp + ctx))
    out_specs = (P(ctx, tp), P(ctx, tp), P(None, tp + ctx))
    return jax.shard_map(
        on_device, mesh=fine, in_specs=in_specs, out_specs=out_specs, check_vma=False
    )
```

time: 181 us -> 189 us (1.044)
  starting transfers between devices: 26.5 us -> 57.9 us
  blocking collectives: 50.6 us -> 29.9 us
  Pallas kernels: 17.5 us -> 26.6 us
  matrix products: 7.41 us -> 0 us
  waiting for transfers between devices: 46.8 us -> 42.1 us
  local copies, waits for them, and re-layouts: 12.4 us -> 10 us
    all_to_all x3 -> x5, waiting for transfers between devices: 45.5 us -> 5.37 us  [the longest x1 5.36 us: on_device(): lax.all_to_all(tap_grad, ('m', 'p', 'h'), split_axis=0, concat_axis=0)]
    ppermute x0 -> x3, waiting for transfers between devices: none -> 25 us  [with_partner(): other = lax.ppermute(values, axis, [(0, 1), (1, 0)])]
    all_to_all x3 -> x5, starting transfers between devices: 20.2 us -> 39.4 us  [the longest x1 13.6 us: on_device(): lax.all_to_all(tap_grad, ('m', 'p', 'h'), split_axis=0, concat_axis=0)]
    all_to_all x4 -> x1, blocking collectives: 43.4 us -> 25.1 us  [on_device(): lax.all_to_all(jnp.broadcast_to(cols[None], (8, 4, TOK, K)), ('x', 'l'),...]
    ppermute x0 -> x3, starting transfers between devices: none -> 11.6 us  [with_partner(): other = lax.ppermute(values, axis, [(0, 1), (1, 0)])]
    pallas_call x3 -> x4, Pallas kernels: 17.5 us -> 26.6 us  [the longest x1 8.21 us: out_part(): pl.pallas_call(out_kernel, grid=(CH // TILE,), in_specs=[tile(TOK), tile(...]
    all_gather x1, waiting for transfers between devices: 0.01 us -> 8.47 us  [on_device(): weights = lax.all_gather(block, 'm', axis=0, tiled=False)]
    dot_general x4 -> x0, matrix products: 7.41 us -> none  [dot(): return lax.dot_general(a, b, (dims, ((), ())), preferred_element_type=F32)]
  transfers between devices with their start and end apart: 6 -> 11, of which waited for: 4 -> 5; matrix products, arithmetic and copies ran while one was open for 8% -> 5% of each run, Pallas kernels for 4% -> 10%
where the time goes in v4:
time: 189 us; the launch traced here: 187 us
  starting transfers between devices  57.9 us (31%)
  waiting for transfers between devices  42.1 us (22%)
  blocking collectives  29.9 us (16%)
  Pallas kernels  26.6 us (14%)
  between operations  14.2 us (8%)
  local copies, waits for them, and re-layouts  10 us (5%)
  other arithmetic  6.15 us (3%)
    all_to_all x1, blocking collectives, on_device(): lax.all_to_all(jnp.broadcast_to(cols[None], (8, 4, TOK, K)), ('x', 'l'),...  25.1 us
    ppermute x3, waiting for transfers between devices, with_partner(): other = lax.ppermute(values, axis, [(0, 1), (1, 0)])  25 us
    all_to_all x1, starting transfers between devices, on_device(): lax.all_to_all(tap_grad, ('m', 'p', 'h'), split_axis=0, concat_axis=0)  13.6 us
    ppermute x3, starting transfers between devices, with_partner(): other = lax.ppermute(values, axis, [(0, 1), (1, 0)])  11.6 us
    all_to_all x1, starting transfers between devices, on_device(): lax.all_to_all(turned, 'c', split_axis=0, concat_axis=0).reshape(K, 512)  10.2 us
    all_gather x1, waiting for transfers between devices, on_device(): weights = lax.all_gather(block, 'm', axis=0, tiled=False)  8.47 us
    pallas_call x1, Pallas kernels, out_part(): pl.pallas_call(out_kernel, grid=(CH // TILE,), in_specs=[tile(TOK), tile(...  8.21 us
    pallas_call x1, Pallas kernels, product(): pl.pallas_call(product_kernel, grid=(8,), in_specs=[pl.BlockSpec((1, 8, 1...  8.05 us
  transfers between devices with their start and end apart: 11, of which 5 were waited for; matrix products, arithmetic and copies ran while one was open for 5% of the time, Pallas kernels for 10%

profile of v4, /device:TPU:1, one launch (start us, length us, event | category | flops | bytes accessed | tf_op | source)
XLA Modules:
  0.0 187.0 jit_solution(11303930209460962054)
XLA Ops:
  8.9 10.2 %all-to-all-start = ((bf16[2,64,512]{2,1,0:T(8,128)(2,1)}), bf16[2,64,512]{2,1,0:T(8,128)(2,1)S(1)}, u32[]{:S(2)}, u32[]{:S(2)}) async-start(bf16[2,64,512]{2,1,0:T(8,128)(2,1)} %copy.24), calls=%async_computation | async-start | bytes 262144 | tf_op jit(solution)/shard_map/all_to_all | solution.py:213
  20.5 1.1 copy.25
  23.2 3.4 %all-to-all-start.1 = ((bf16[4,256,128]{2,1,0:T(8,128)(2,1)}), bf16[4,256,128]{2,1,0:T(8,128)(2,1)S(1)}, u32[]{:S(2)}, u32[]{:S(2)}) async-start(bf16[4,256,128]{2,1,0:T(8,128)(2,1)} %copy.26), calls=%async_computation.1 | async-start | bytes 524288 | tf_op jit(solution)/shard_map/all_to_all | solution.py:223
  26.7 5.0 %collective-permute-start = (bf16[128,1024]{1,0:T(8,128)(2,1)S(1)}, bf16[128,1024]{1,0:T(8,128)(2,1)S(1)}, u32[]{:S(2)}, u32[]{:S(2)}) collective-permute-start(bf16[128,1024]{1,0:T(8,128)(2,1)S(1)} %slice.12), channel_id=1, source_target_pairs={{0,8},{8,16},{16,24},{24,32},{32,40},{40,48},{48,56},{56,64},{64,7... | collective-permute-start | bytes 786440 | tf_op jit(solution)/shard_map/ppermute | solution.py:227
  31.7 3.3 %collective-permute-done = bf16[128,1024]{1,0:T(8,128)(2,1)S(1)} collective-permute-done((bf16[128,1024]{1,0:T(8,128)(2,1)S(1)}, bf16[128,1024]{1,0:T(8,128)(2,1)S(1)}, u32[]{:S(2)}, u32[]{:S(2)}) %collective-permute-start) | collective-permute-done | bytes 262176 | tf_op jit(solution)/shard_map/ppermute | solution.py:227
  35.9 4.4 %shard_map.130.freq_ref = f32[384,1024]{1,0:T(8,128)} custom-call(bf16[384,1024]{1,0:T(8,128)(2,1)} %pad_maximum_fusion.window_ref, bf16[2,384,384]{2,1,0:T(8,128)(2,1)} %constant.32.clone.forward_ref), custom_call_target="tpu_custom_call" | custom-call | flops 603979776 | bytes 3145728 | tf_op jit(solution)/shard_map/pallas_call | solution.py:106
  40.8 25.1 %all_to_all.35 = bf16[8,4,256,128]{3,2,1,0:T(8,128)(2,1)S(1)} all-to-all(bf16[8,4,256,128]{3,2,1,0:T(8,128)(2,1)S(1)} %broadcast_in_dim.7), channel_id=1, replica_groups=mesh['m'=8,'p'=2,'h'=2,'c'=2,'x'=4,'l'=2] {'x','l'}, dimensions={0} | all-to-all | bytes 4194304 | tf_op jit(solution)/shard_map/all_to_all | solution.py:232
  65.8 3.0 %broadcast_in_dim.8 = bf16[2,8,4,256,128]{4,3,2,1,0:T(8,128)(2,1)} broadcast(bf16[8,4,256,128]{3,2,1,0:T(8,128)(2,1)S(1)} %all_to_all.35), dimensions={1,2,3,4} | broadcast | bytes 6291456 | tf_op jit(solution)/shard_map/broadcast_in_dim | solution.py:236
  68.8 5.6 %all-to-all-start.3 = ((bf16[2,8,4,256,128]{4,3,2,1,0:T(8,128)(2,1)}), bf16[2,8,4,256,128]{4,3,2,1,0:T(8,128)(2,1)}, u32[]{:S(2)}, u32[]{:S(2)}) async-start(bf16[2,8,4,256,128]{4,3,2,1,0:T(8,128)(2,1)} %broadcast_in_dim.8), calls=%async_computation.3 | async-start | bytes 8388608 | tf_op jit(solution)/shard_map/all_to_all | solution.py:235
  74.4 8.5 %all-gather.3.cloned.1.call-done = bf16[1152,512]{1,0:T(8,128)(2,1)} async-done(((bf16[144,512]{1,0:T(8,128)(2,1)}), bf16[1152,512]{1,0:T(8,128)(2,1)}) %all-gather.3.cloned.1.call-update) | async-done | bytes 1179664 | tf_op jit(solution)/shard_map/all_gather | solution.py:222
  82.9 8.0 %shard_map.131 = bf16[8,256,512]{2,1,0:T(8,128)(2,1)} custom-call(bf16[2,8,4,256,128]{4,3,2,1,0:T(8,128)(2,1)} %all-to-all-done.3.cols_ref, bf16[8,144,512]{2,1,0:T(8,128)(2,1)} %bitcast.59), custom_call_target="tpu_custom_call" | custom-call | flops 2147483648 | bytes 7340032 | tf_op jit(solution)/shard_map/pallas_call | solution.py:77
  90.9 6.6 %all-to-all-start.4 = ((bf16[8,256,512]{2,1,0:T(8,128)(2,1)}), bf16[8,256,512]{2,1,0:T(8,128)(2,1)S(1)}, u32[]{:S(2)}, u32[]{:S(2)}) async-start(bf16[8,256,512]{2,1,0:T(8,128)(2,1)} %shard_map.131), calls=%async_computation.4 | async-start | bytes 4194304 | tf_op jit(solution)/shard_map/all_to_all | solution.py:241
  98.4 3.3 %collective-permute-start.2 = (bf16[2,8,16,128]{3,2,1,0:T(8,128)(2,1)S(1)}, bf16[2,8,16,128]{3,2,1,0:T(8,128)(2,1)S(1)}, u32[]{:S(2)}, u32[]{:S(2)}) collective-permute-start(bf16[2,8,16,128]{3,2,1,0:T(8,128)(2,1)S(1)} %bitcast_bitcast_fusion), channel_id=1, source_target_pairs={{0,32},{32,0},{1,33},{33,1},{2,34},{34,2},{3,35},{35,3},{4,36},{36... | collective-permute-start | bytes 196616 | tf_op jit(solution)/shard_map/ppermute | solution.py:201
  101.7 22.1 %collective-permute-done.2 = bf16[2,8,16,128]{3,2,1,0:T(8,128)(2,1)S(1)} collective-permute-done((bf16[2,8,16,128]{3,2,1,0:T(8,128)(2,1)S(1)}, bf16[2,8,16,128]{3,2,1,0:T(8,128)(2,1)S(1)}, u32[]{:S(2)}, u32[]{:S(2)}) %collective-permute-start.2) | collective-permute-done | bytes 65568 | tf_op jit(solution)/shard_map/ppermute | solution.py:201
  124.7 4.6 %collective-permute-start.3 = (bf16[2,2,8,16,128]{4,3,0,2,1:T(8,128)(2,1)S(1)}, bf16[2,2,8,16,128]{4,3,0,2,1:T(8,128)(2,1)S(1)}, u32[]{:S(2)}, u32[]{:S(2)}) collective-permute-start(bf16[2,2,8,16,128]{4,3,0,2,1:T(8,128)(2,1)S(1)} %pad_maximum_fusion.3), channel_id=1, source_target_pairs={{0,16},{16,0},{1,17},{17,1},{2,18},{18,2},{3,19},{19,3},{4,20},{20... | collective-permute-start | bytes 393224 | tf_op jit(solution)/shard_map/ppermute | solution.py:201
  129.3 2.9 %collective-permute-done.3 = bf16[2,2,8,16,128]{4,3,0,2,1:T(8,128)(2,1)S(1)} collective-permute-done((bf16[2,2,8,16,128]{4,3,0,2,1:T(8,128)(2,1)S(1)}, bf16[2,2,8,16,128]{4,3,0,2,1:T(8,128)(2,1)S(1)}, u32[]{:S(2)}, u32[]{:S(2)}) %collective-permute-start.3) | collective-permute-done | bytes 131104 | tf_op jit(solution)/shard_map/ppermute | solution.py:201
  132.3 3.7 %collective-permute-start.4 = (bf16[2,2,2,8,16,128]{5,4,0,1,3,2:T(8,128)(2,1)S(1)}, bf16[2,2,2,8,16,128]{5,4,0,1,3,2:T(8,128)(2,1)S(1)}, u32[]{:S(2)}, u32[]{:S(2)}) collective-permute-start(bf16[2,2,2,8,16,128]{5,4,0,1,3,2:T(8,128)(2,1)S(1)} %pad_maximum_fusion.2), channel_id=1, source_target_pairs={{0,8},{8,0},{1,9},{9,1},{2,10},{10,2},{3,11},{11,3},{4,12},{12,4},... | collective-permute-start | bytes 786440 | tf_op jit(solution)/shard_map/ppermute | solution.py:201
  136.0 1.3 copy-done
  137.3 5.9 %shard_map.132 = (bf16[256,1024]{1,0:T(8,128)(2,1)}, bf16[128,1024]{1,0:T(8,128)(2,1)}, f32[384,1024]{1,0:T(8,128)}, f32[2,32,16,128]{3,2,1,0:T(8,128)}) custom-call(bf16[4,2,256,512]{3,2,1,0:T(8,128)(2,1)} %bitcast.53, bf16[256,1024]{1,0:T(8,128)(2,1)} %gate_ref.1, f32[384,1024]{1,0:T(8,128)} %shard_map.130.freq_ref, ...), custom_call_target="tpu_custom_call" | custom-call | flops 704643072 | bytes 8388608 | tf_op jit(solution)/shard_map/pallas_call | solution.py:136
  143.2 1.9 %collective-permute-start.1 = (bf16[128,1024]{1,0:T(8,128)(2,1)}, bf16[128,1024]{1,0:T(8,128)(2,1)S(1)}, u32[]{:S(2)}, u32[]{:S(2)}) collective-permute-start(bf16[128,1024]{1,0:T(8,128)(2,1)} %get-tuple-element.22), channel_id=1, source_target_pairs={{8,0},{16,8},{24,16},{32,24},{40,32},{48,40},{56,48},{64,56},{72,6... | collective-permute-start | bytes 786440 | tf_op jit(solution)/shard_map/ppermute | solution.py:248
  145.1 4.9 %all_to_all.36 = f32[2,32,16,128]{3,2,1,0:T(8,128)S(1)} all-to-all(f32[2,32,16,128]{3,2,1,0:T(8,128)} %get-tuple-element.26), channel_id=1, replica_groups=mesh['m'=8,'p'=2,'h'=2,'c'=2,'x'=4,'l'=2] {'c'}, dimensions={0} | all-to-all | bytes 1048576 | tf_op jit(solution)/shard_map/all_to_all | solution.py:249
  150.7 13.6 %all-to-all-start.6 = ((bf16[32,16,128]{2,1,0:T(8,128)(2,1)}), bf16[32,16,128]{2,1,0:T(8,128)(2,1)S(1)}, u32[]{:S(2)}, u32[]{:S(2)}) async-start(bf16[32,16,128]{2,1,0:T(8,128)(2,1)} %fusion.1), calls=%async_computation.6 | async-start | bytes 262144 | tf_op jit(solution)/shard_map/all_to_all | solution.py:251
  165.9 8.2 %shard_map.133 = (bf16[256,1024]{1,0:T(8,128)(2,1)}, bf16[256,1024]{1,0:T(8,128)(2,1)}) custom-call(bf16[256,1024]{1,0:T(8,128)(2,1)} %get-tuple-element.20.mixed_ref, f32[384,1024]{1,0:T(8,128)} %shard_map.130.freq_ref, f32[384,1024]{1,0:T(8,128)} %get-tuple-element.21.spec_ref, bf16[128,1024]{1,0:T(8,128)(2,1)} %copy-done.2, ...), custom_call_target="tpu_custom_call" | custom-call | flops 1711276032 | bytes 6291456 | tf_op jit(solution)/shard_map/pallas_call | solution.py:178
  174.1 5.4 %all-to-all-done.6 = bf16[32,16,128]{2,1,0:T(8,128)(2,1)S(1)} async-done(((bf16[32,16,128]{2,1,0:T(8,128)(2,1)}), bf16[32,16,128]{2,1,0:T(8,128)(2,1)S(1)}, u32[]{:S(2)}, u32[]{:S(2)}) %all-to-all-start.6) | async-done | bytes 131104 | tf_op jit(solution)/shard_map/all_to_all | solution.py:251
  (32 shorter events, 10.8 us)
Async XLA Ops:
  7.2 19.5 %copy-start.1 = (bf16[256,1024]{1,0:T(8,128)(2,1)S(1)}, bf16[256,1024]{1,0:T(8,128)(2,1)}, u32[]{:S(2)}) copy-start(bf16[256,1024]{1,0:T(8,128)(2,1)} %param.13) | copy-start | bytes 1572868
  8.9 12.7 %all-to-all-start = ((bf16[2,64,512]{2,1,0:T(8,128)(2,1)}), bf16[2,64,512]{2,1,0:T(8,128)(2,1)S(1)}, u32[]{:S(2)}, u32[]{:S(2)}) async-start(bf16[2,64,512]{2,1,0:T(8,128)(2,1)} %copy.24), calls=%async_computation | async-start | bytes 262144 | tf_op jit(solution)/shard_map/all_to_all | solution.py:213
  23.2 17.1 %all-to-all-start.1 = ((bf16[4,256,128]{2,1,0:T(8,128)(2,1)}), bf16[4,256,128]{2,1,0:T(8,128)(2,1)S(1)}, u32[]{:S(2)}, u32[]{:S(2)}) async-start(bf16[4,256,128]{2,1,0:T(8,128)(2,1)} %copy.26), calls=%async_computation.1 | async-start | bytes 524288 | tf_op jit(solution)/shard_map/all_to_all | solution.py:223
  26.6 56.3 %all-gather.3.cloned.1.call-start = ((), (), s32[]{:S(2)}) async-start(), calls=%async_computation.7 | async-start | bytes 1327104 | tf_op jit(solution)/shard_map/all_gather | solution.py:222
  26.7 8.3 %collective-permute-start = (bf16[128,1024]{1,0:T(8,128)(2,1)S(1)}, bf16[128,1024]{1,0:T(8,128)(2,1)S(1)}, u32[]{:S(2)}, u32[]{:S(2)}) collective-permute-start(bf16[128,1024]{1,0:T(8,128)(2,1)S(1)} %slice.12), channel_id=1, source_target_pairs={{0,8},{8,16},{16,24},{24,32},{32,40},{40,48},{48,56},{56,64},{64,7... | collective-permute-start | bytes 786440 | tf_op jit(solution)/shard_map/ppermute | solution.py:227
  68.8 14.0 %all-to-all-start.3 = ((bf16[2,8,4,256,128]{4,3,2,1,0:T(8,128)(2,1)}), bf16[2,8,4,256,128]{4,3,2,1,0:T(8,128)(2,1)}, u32[]{:S(2)}, u32[]{:S(2)}) async-start(bf16[2,8,4,256,128]{4,3,2,1,0:T(8,128)(2,1)} %broadcast_in_dim.8), calls=%async_computation.3 | async-start | bytes 8388608 | tf_op jit(solution)/shard_map/all_to_all | solution.py:235
  90.9 45.0 %all-to-all-start.4 = ((bf16[8,256,512]{2,1,0:T(8,128)(2,1)}), bf16[8,256,512]{2,1,0:T(8,128)(2,1)S(1)}, u32[]{:S(2)}, u32[]{:S(2)}) async-start(bf16[8,256,512]{2,1,0:T(8,128)(2,1)} %shard_map.131), calls=%async_computation.4 | async-start | bytes 4194304 | tf_op jit(solution)/shard_map/all_to_all | solution.py:241
  98.4 25.4 %collective-permute-start.2 = (bf16[2,8,16,128]{3,2,1,0:T(8,128)(2,1)S(1)}, bf16[2,8,16,128]{3,2,1,0:T(8,128)(2,1)S(1)}, u32[]{:S(2)}, u32[]{:S(2)}) collective-permute-start(bf16[2,8,16,128]{3,2,1,0:T(8,128)(2,1)S(1)} %bitcast_bitcast_fusion), channel_id=1, source_target_pairs={{0,32},{32,0},{1,33},{33,1},{2,34},{34,2},{3,35},{35,3},{4,36},{36... | collective-permute-start | bytes 196616 | tf_op jit(solution)/shard_map/ppermute | solution.py:201
  124.7 7.5 %collective-permute-start.3 = (bf16[2,2,8,16,128]{4,3,0,2,1:T(8,128)(2,1)S(1)}, bf16[2,2,8,16,128]{4,3,0,2,1:T(8,128)(2,1)S(1)}, u32[]{:S(2)}, u32[]{:S(2)}) collective-permute-start(bf16[2,2,8,16,128]{4,3,0,2,1:T(8,128)(2,1)S(1)} %pad_maximum_fusion.3), channel_id=1, source_target_pairs={{0,16},{16,0},{1,17},{17,1},{2,18},{18,2},{3,19},{19,3},{4,20},{20... | collective-permute-start | bytes 393224 | tf_op jit(solution)/shard_map/ppermute | solution.py:201
  132.3 32.1 %collective-permute-start.4 = (bf16[2,2,2,8,16,128]{5,4,0,1,3,2:T(8,128)(2,1)S(1)}, bf16[2,2,2,8,16,128]{5,4,0,1,3,2:T(8,128)(2,1)S(1)}, u32[]{:S(2)}, u32[]{:S(2)}) collective-permute-start(bf16[2,2,2,8,16,128]{5,4,0,1,3,2:T(8,128)(2,1)S(1)} %pad_maximum_fusion.2), channel_id=1, source_target_pairs={{0,8},{8,0},{1,9},{9,1},{2,10},{10,2},{3,11},{11,3},{4,12},{12,4},... | collective-permute-start | bytes 786440 | tf_op jit(solution)/shard_map/ppermute | solution.py:201
  136.0 1.3 copy-start
  143.2 22.0 %collective-permute-start.1 = (bf16[128,1024]{1,0:T(8,128)(2,1)}, bf16[128,1024]{1,0:T(8,128)(2,1)S(1)}, u32[]{:S(2)}, u32[]{:S(2)}) collective-permute-start(bf16[128,1024]{1,0:T(8,128)(2,1)} %get-tuple-element.22), channel_id=1, source_target_pairs={{8,0},{16,8},{24,16},{32,24},{40,32},{48,40},{56,48},{64,56},{72,6... | collective-permute-start | bytes 786440 | tf_op jit(solution)/shard_map/ppermute | solution.py:248
  150.7 28.8 %all-to-all-start.6 = ((bf16[32,16,128]{2,1,0:T(8,128)(2,1)}), bf16[32,16,128]{2,1,0:T(8,128)(2,1)S(1)}, u32[]{:S(2)}, u32[]{:S(2)}) async-start(bf16[32,16,128]{2,1,0:T(8,128)(2,1)} %fusion.1), calls=%async_computation.6 | async-start | bytes 262144 | tf_op jit(solution)/shard_map/all_to_all | solution.py:251
  165.2 0.7 copy-start.2
Sparse Core Ops, SparseCore 0:
  31.8 51.0 all-gather.2

commit v5 on v4

--- a/solution.py
+++ b/solution.py
@@ -68,24 +68,24 @@
 
 
 def product_kernel(cols_ref, weight_ref, out_ref):
-    weight = weight_ref[:, :K].reshape(8 * K, 512)
-    rows = jnp.concatenate([cols_ref[0, i, 0] for i in range(8)], axis=1)
+    weight = weight_ref[:, :K].reshape(16 * K, 512)
+    rows = jnp.concatenate([cols_ref[0, i, 0, j] for i in range(8) for j in range(2)], axis=1)
     out_ref[0] = dot(rows, weight).astype(BF)
 
 
 def product(cols, weights):
     return pl.pallas_call(
         product_kernel,
-        grid=(8,),
+        grid=(4,),
         in_specs=[
-            pl.BlockSpec((1, 8, 1, TOK, K), lambda i: (i % 2, 0, i // 2, 0, 0)),
-            pl.BlockSpec((8, K + 16, 512), lambda i: (0, 0, 0)),
+            pl.BlockSpec((1, 8, 1, 2, TOK, K), lambda i: (i % 2, 0, i // 2, 0, 0, 0)),
+            pl.BlockSpec((16, K + 16, 512), lambda i: (0, 0, 0)),
         ],
         out_specs=pl.BlockSpec((1, TOK, 512), lambda i: (i, 0, 0)),
-        out_shape=jax.ShapeDtypeStruct((8, TOK, 512), BF),
-        compiler_params=params(),
-        cost_estimate=pl.CostEstimate(
-            flops=2 * 2048 * 1024 * 512, bytes_accessed=7 << 20, transcendentals=0
+        out_shape=jax.ShapeDtypeStruct((4, TOK, 512), BF),
+        compiler_params=params(),
+        cost_estimate=pl.CostEstimate(
+            flops=2 * 1024 * 2048 * 512, bytes_accessed=8 << 20, transcendentals=0
         ),
     )(cols, weights)
 
@@ -119,8 +119,7 @@
 def grad_kernel(
     mix_ref, gate_ref, freq_ref, own_ref, lag_ref, mixed_ref, head_ref, spec_ref, tap_ref
 ):
-    parts = mix_ref[:, 0].astype(F32)
-    mixed = (parts[0] + parts[1] + (parts[2] + parts[3])).astype(BF)
+    mixed = (mix_ref[0, 0].astype(F32) + mix_ref[1, 0].astype(F32)).astype(BF)
     mixed_ref[...] = mixed
     conv_grad = (mixed.astype(F32) * gate_ref[...].astype(F32)).astype(BF)
     head_ref[...] = conv_grad[:K]
@@ -137,7 +136,7 @@
         grad_kernel,
         grid=(CH // TILE,),
         in_specs=[
-            pl.BlockSpec((4, 1, TOK, TILE), lambda j: (0, j // 2, 0, j % 2)),
+            pl.BlockSpec((2, 1, TOK, TILE), lambda j: (0, j // 2, 0, j % 2)),
             tile(TOK),
             tile(N),
             whole((2, N, TOK)),
@@ -197,30 +196,31 @@
     )(mixed, sig_freq, spec, halo, taps, head, tail, inv)
 
 
-def with_partner(values, axis):
-    other = lax.ppermute(values, axis, [(0, 1), (1, 0)])
-    first = lax.axis_index(axis) == 0
-    return jnp.stack([jnp.where(first, values, other), jnp.where(first, other, values)])
-
-
 def on_device(out_grad, out_weight, signal, gate_input, filter_taps):
-    ctx = ("m", "p", "h", "c")
+    ctx = ("z", "h", "c")
     n_ctx = 64
     period = SPAN // TOK
     fwd, inv = transforms()
 
     turned = out_weight.T.reshape(64, 2, 512).transpose(1, 0, 2)
-    turned = lax.all_to_all(turned, "c", split_axis=0, concat_axis=0).reshape(K, 512)
     tap_rows = filter_taps.T
     tap_high = lax.optimization_barrier(tap_rows.astype(BF))
     tap_low = (tap_rows - tap_high.astype(F32)).astype(BF)
     tap_pack = jnp.concatenate([tap_high, tap_low, jnp.zeros((16, 256), BF)], axis=1)
-    block = jnp.concatenate([turned, tap_pack], axis=0)
-
-    cols = out_grad.reshape(TOK, 4, K).transpose(1, 0, 2)
+    message = jnp.concatenate([turned, jnp.broadcast_to(tap_pack[None], (2, 16, 512))], axis=1)
+    got = lax.all_to_all(message, "c", split_axis=0, concat_axis=0)
+    block = jnp.concatenate(
+        [
+            got[:, :64].reshape(K, 512),
+            jnp.concatenate([got[0, 64:, :256], got[1, 64:, :256]], axis=1),
+        ],
+        axis=0,
+    )
+
+    cols = out_grad.reshape(TOK, 2, 2, K).transpose(2, 1, 0, 3)
     block, cols = lax.optimization_barrier((block, cols))
-    weights = lax.all_gather(block, "m", axis=0, tiled=False)
-    cols = lax.all_to_all(cols, ("p", "h"), split_axis=0, concat_axis=0)
+    weights = lax.all_gather(block, "z", axis=0, tiled=False)
+    cols = lax.all_to_all(cols, "h", split_axis=0, concat_axis=0)
 
     ahead = [(i, i + 1) for i in range(n_ctx - 1) if (i + 1) % period]
     back = [(j, i) for i, j in ahead]
@@ -230,30 +230,32 @@
 
     cols, sig_freq = lax.optimization_barrier((cols, sig_freq))
     cols = lax.all_to_all(
-        jnp.broadcast_to(cols[None], (8, 4, TOK, K)), ("x", "l"), split_axis=0, concat_axis=0
+        jnp.broadcast_to(cols[None], (8, 2, 2, TOK, K)), ("x", "l"), split_axis=0, concat_axis=0
     )
     cols = lax.all_to_all(
-        jnp.broadcast_to(cols[None], (2, 8, 4, TOK, K)), "c", split_axis=0, concat_axis=0
+        jnp.broadcast_to(cols[None], (2, 8, 2, 2, TOK, K)), "c", split_axis=0, concat_axis=0
     )
 
     partial = product(cols, weights)
-    weights, partial = lax.optimization_barrier((weights, partial))
-    mix = lax.all_to_all(
-        partial, ("p", "h", "c"), split_axis=0, concat_axis=0
-    ).reshape(4, 2, TOK, 512)
-
+    mix = lax.all_to_all(partial, ("h", "c"), split_axis=0, concat_axis=0)
     mixed, grad_head, spec, tap_grad = grad_part(
-        mix, gate_input, sig_freq, fwd[:, :, K:N], inv[:, :K]
+        mix.reshape(2, 2, TOK, 512), gate_input, sig_freq, fwd[:, :, K:N], inv[:, :K]
     )
     grad_halo = lax.ppermute(grad_head, ctx, back)
+
+    weights, spec = lax.optimization_barrier((weights, spec))
+    taps = weights[:, K:].reshape(16, 16, 2, 2, K).transpose(3, 0, 2, 1, 4)
+    other = lax.ppermute(taps, "h", [(0, 1), (1, 0)])
+    first = lax.axis_index("h") == 0
+    taps = jnp.stack(
+        [jnp.where(first, taps, other), jnp.where(first, other, taps)], axis=2
+    ).reshape(2, CH, K)
+
     tap_grad = lax.all_to_all(tap_grad, "c", split_axis=0, concat_axis=0)
     tap_grad = (tap_grad[0] + tap_grad[1]).astype(BF)
-    tap_grad = lax.all_to_all(tap_grad, ("m", "p", "h"), split_axis=0, concat_axis=0)
+    tap_grad = lax.all_to_all(tap_grad, ("z", "h"), split_axis=0, concat_axis=0)
     filter_grad = jnp.sum(tap_grad.astype(F32), axis=0).T
 
-    taps = weights[:, K:, : 2 * K].reshape(8, 16, 2, K).transpose(2, 0, 1, 3)
-    taps = with_partner(with_partner(with_partner(taps, "p"), "h"), "c")
-    taps = taps.transpose(3, 4, 2, 1, 0, 5, 6).reshape(2, CH, K)
     gate_grad, signal_grad = out_part(
         mixed, sig_freq, spec, grad_halo, taps, fwd[:, :, :K], fwd[:, :, N:], inv[:, K:]
     )
@@ -261,8 +263,8 @@
 
 
 def solution(mesh):
-    fine = Mesh(mesh.devices.reshape(8, 2, 2, 2, 4, 2), ("m", "p", "h", "c", "x", "l"))
-    ctx, tp = ("m", "p", "h", "c"), ("x", "l")
+    fine = Mesh(mesh.devices.reshape(16, 2, 2, 4, 2), ("z", "h", "c", "x", "l"))
+    ctx, tp = ("z", "h", "c"), ("x", "l")
     in_specs = (P(ctx, tp), P(tp, ctx), P(ctx, tp), P(ctx, tp), P(None, tp + ctx))
     out_specs = (P(ctx, tp), P(ctx, tp), P(None, tp + ctx))
     return jax.shard_map(

time: 189 us -> 176 us (0.931)
  blocking collectives: 29.9 us -> 71.2 us
  starting transfers between devices: 57.9 us -> 31.2 us
  waiting for transfers between devices: 42.1 us -> 20 us
  local copies, waits for them, and re-layouts: 10 us -> 6.61 us
  Pallas kernels: 26.6 us -> 24.6 us
    all_to_all x1 -> x3, blocking collectives: 25.1 us -> 66.3 us  [the longest x1 28.5 us: on_device(): mix = lax.all_to_all(partial, ('h', 'c'), split_axis=0, concat_axis=0)]
    ppermute x3 -> x1, waiting for transfers between devices: 25 us -> 0.01 us  [on_device(): other = lax.ppermute(taps, 'h', [(0, 1), (1, 0)])]
    all_to_all x5 -> x3, starting transfers between devices: 39.4 us -> 24.1 us  [the longest x1 10.3 us: on_device(): tap_grad = lax.all_to_all(tap_grad, ('z', 'h'), split_axis=0, concat_axis=0)]
    ppermute x3 -> x1, starting transfers between devices: 11.6 us -> 2.41 us  [on_device(): other = lax.ppermute(taps, 'h', [(0, 1), (1, 0)])]
    all_gather x1, waiting for transfers between devices: 8.47 us -> 13.8 us  [on_device(): weights = lax.all_gather(block, 'z', axis=0, tiled=False)]
    ppermute x1, waiting for transfers between devices: 3.27 us -> 0.01 us  [on_device(): sig_halo = lax.ppermute(signal[TOK - K:], ctx, ahead)]
    ppermute x1, starting transfers between devices: 4.97 us -> 1.92 us  [on_device(): sig_halo = lax.ppermute(signal[TOK - K:], ctx, ahead)]
    pallas_call x2, Pallas kernels: 14 us -> 12 us  [the longest x1 6.29 us: product(): pl.pallas_call(product_kernel, grid=(4,), in_specs=[pl.BlockSpec((1, 8, 1...]
  transfers between devices with their start and end apart: 11 -> 7, of which waited for: 5 -> 3; matrix products, arithmetic and copies ran while one was open for 5% -> 4% of each run, Pallas kernels for 10% -> 7%
where the time goes in v5:
time: 176 us; the launch traced here: 174 us
  blocking collectives  71.2 us (40%)
  starting transfers between devices  31.2 us (18%)
  Pallas kernels  24.6 us (14%)
  waiting for transfers between devices  20 us (11%)
  between operations  14.2 us (8%)
  local copies, waits for them, and re-layouts  6.61 us (4%)
  other arithmetic  5.99 us (3%)
    all_to_all x1, blocking collectives, on_device(): mix = lax.all_to_all(partial, ('h', 'c'), split_axis=0, concat_axis=0)  28.5 us
    all_to_all x1, blocking collectives, on_device(): lax.all_to_all(jnp.broadcast_to(cols[None], (8, 2, 2, TOK, K)), ('x', 'l'...  27.5 us
    all_gather x1, waiting for transfers between devices, on_device(): weights = lax.all_gather(block, 'z', axis=0, tiled=False)  13.8 us
    all_to_all x1, starting transfers between devices, on_device(): tap_grad = lax.all_to_all(tap_grad, ('z', 'h'), split_axis=0, concat_axis=0)  10.3 us
    all_to_all x1, starting transfers between devices, on_device(): got = lax.all_to_all(message, 'c', split_axis=0, concat_axis=0)  10.3 us
    all_to_all x1, blocking collectives, on_device(): lax.all_to_all(jnp.broadcast_to(cols[None], (2, 8, 2, 2, TOK, K)), 'c', s...  10.3 us
    pallas_call x1, Pallas kernels, out_part(): pl.pallas_call(out_kernel, grid=(CH // TILE,), in_specs=[tile(TOK), tile(...  8.22 us
    pallas_call x1, Pallas kernels, product(): pl.pallas_call(product_kernel, grid=(4,), in_specs=[pl.BlockSpec((1, 8, 1...  6.29 us
  transfers between devices with their start and end apart: 7, of which 3 were waited for; matrix products, arithmetic and copies ran while one was open for 4% of the time, Pallas kernels for 7%

profile of v5, /device:TPU:1, one launch (start us, length us, event | category | flops | bytes accessed | tf_op | source)
XLA Modules:
  0.0 173.8 jit_solution(9458189895137094349)
XLA Ops:
  8.6 0.9 copy.36
  10.3 10.3 %all-to-all-start = ((bf16[2,80,512]{2,1,0:T(8,128)(2,1)}), bf16[2,80,512]{2,1,0:T(8,128)(2,1)S(1)}, u32[]{:S(2)}, u32[]{:S(2)}) async-start(bf16[2,80,512]{2,1,0:T(8,128)(2,1)} %pad_maximum_fusion.2), calls=%async_computation | async-start | bytes 327680 | tf_op jit(solution)/shard_map/all_to_all | solution.py:211
  20.6 1.1 copy.23
  22.5 1.9 %collective-permute-start = (bf16[128,1024]{1,0:T(8,128)(2,1)S(1)}, bf16[128,1024]{1,0:T(8,128)(2,1)S(1)}, u32[]{:S(2)}, u32[]{:S(2)}) collective-permute-start(bf16[128,1024]{1,0:T(8,128)(2,1)S(1)} %slice.24), channel_id=1, source_target_pairs={{0,8},{8,16},{16,24},{24,32},{32,40},{40,48},{48,56},{56,64},{64,7... | collective-permute-start | bytes 786440 | tf_op jit(solution)/shard_map/ppermute | solution.py:227
  24.4 0.9 copy.24
  25.3 3.4 %all-to-all-start.1 = ((bf16[2,2,256,128]{3,1,2,0:T(2,128)(2,1)}), bf16[2,2,256,128]{3,1,2,0:T(2,128)(2,1)S(1)}, u32[]{:S(2)}, u32[]{:S(2)}) async-start(bf16[2,2,256,128]{3,1,2,0:T(2,128)(2,1)} %copy.24), calls=%async_computation.1 | async-start | bytes 524288 | tf_op jit(solution)/shard_map/all_to_all | solution.py:223
  28.7 1.0 pad_maximum_fusion.window_ref
  29.7 4.4 %shard_map.130.freq_ref = f32[384,1024]{1,0:T(8,128)} custom-call(bf16[384,1024]{1,0:T(8,128)(2,1)} %pad_maximum_fusion.window_ref, bf16[2,384,384]{2,1,0:T(8,128)(2,1)} %constant.24.clone.forward_ref), custom_call_target="tpu_custom_call" | custom-call | flops 603979776 | bytes 3145728 | tf_op jit(solution)/shard_map/pallas_call | solution.py:106
  34.1 0.8 all-to-all-done.1
  35.5 27.5 %all_to_all.35 = bf16[8,2,2,256,128]{4,3,2,1,0:T(8,128)(2,1)S(1)} all-to-all(bf16[8,2,2,256,128]{4,3,2,1,0:T(8,128)(2,1)S(1)} %broadcast_in_dim.10), channel_id=1, replica_groups=mesh['z'=16,'h'=2,'c'=2,'x'=4,'l'=2] {'x','l'}, dimensions={0} | all-to-all | bytes 4194304 | tf_op jit(solution)/shard_map/all_to_all | solution.py:232
  63.0 1.4 broadcast_in_dim.11
  64.4 10.3 %all_to_all.36.cols_ref = bf16[2,8,2,2,256,128]{5,4,3,2,1,0:T(8,128)(2,1)} all-to-all(bf16[2,8,2,2,256,128]{5,4,3,2,1,0:T(8,128)(2,1)S(1)} %broadcast_in_dim.11), channel_id=1, replica_groups=mesh['z'=16,'h'=2,'c'=2,'x'=4,'l'=2] {'c'}, dimensions={0} | all-to-all | bytes 8388608 | tf_op jit(solution)/shard_map/all_to_all | solution.py:235
  74.7 13.8 %all-gather.3.cloned.1.call-done = bf16[2304,512]{1,0:T(8,128)(2,1)} async-done(((bf16[144,512]{1,0:T(8,128)(2,1)}), bf16[2304,512]{1,0:T(8,128)(2,1)}) %all-gather.3.cloned.1.call-update) | async-done | bytes 2359312 | tf_op jit(solution)/shard_map/all_gather | solution.py:222
  88.4 6.3 %shard_map.131 = bf16[4,256,512]{2,1,0:T(8,128)(2,1)} custom-call(bf16[2,8,2,2,256,128]{5,4,3,2,1,0:T(8,128)(2,1)} %all_to_all.36.cols_ref, bf16[16,144,512]{2,1,0:T(8,128)(2,1)} %bitcast.47), custom_call_target="tpu_custom_call" | custom-call | flops 2147483648 | bytes 8388608 | tf_op jit(solution)/shard_map/pallas_call | solution.py:77
  94.7 28.5 %all_to_all.37 = bf16[4,256,512]{2,1,0:T(8,128)(2,1)} all-to-all(bf16[4,256,512]{2,1,0:T(8,128)(2,1)} %shard_map.131), channel_id=1, replica_groups=mesh['z'=16,'h'=2,'c'=2,'x'=4,'l'=2] {'h','c'}, dimensions={0} | all-to-all | bytes 2097152 | tf_op jit(solution)/shard_map/all_to_all | solution.py:240
  123.2 5.7 %shard_map.132 = (bf16[256,1024]{1,0:T(8,128)(2,1)}, bf16[128,1024]{1,0:T(8,128)(2,1)}, f32[384,1024]{1,0:T(8,128)}, f32[2,32,16,128]{3,2,1,0:T(8,128)}) custom-call(bf16[2,2,256,512]{3,2,1,0:T(8,128)(2,1)} %bitcast.40, bf16[256,1024]{1,0:T(8,128)(2,1)} %gate_ref.1, f32[384,1024]{1,0:T(8,128)} %shard_map.130.freq_ref, ...), custom_call_target="tpu_custom_call" | custom-call | flops 704643072 | bytes 8388608 | tf_op jit(solution)/shard_map/pallas_call | solution.py:135
  128.9 1.0 slice.25
  130.0 2.4 %collective-permute-start.2 = (bf16[2,16,2,16,128]{4,3,2,1,0:T(8,128)(2,1)S(1)}, bf16[2,16,2,16,128]{4,3,2,1,0:T(8,128)(2,1)S(1)}, u32[]{:S(2)}, u32[]{:S(2)}) collective-permute-start(bf16[2,16,2,16,128]{4,3,2,1,0:T(8,128)(2,1)S(1)} %bitcast.45), channel_id=1, source_target_pairs={{0,16},{16,0},{1,17},{17,1},{2,18},{18,2},{3,19},{19,3},{4,20},{20... | collective-permute-start | bytes 786440 | tf_op jit(solution)/shard_map/ppermute | solution.py:248
  132.5 2.8 %collective-permute-start.1 = (bf16[128,1024]{1,0:T(8,128)(2,1)}, bf16[128,1024]{1,0:T(8,128)(2,1)S(1)}, u32[]{:S(2)}, u32[]{:S(2)}) collective-permute-start(bf16[128,1024]{1,0:T(8,128)(2,1)} %get-tuple-element.22), channel_id=1, source_target_pairs={{8,0},{16,8},{24,16},{32,24},{40,32},{48,40},{56,48},{64,56},{72,6... | collective-permute-start | bytes 786440 | tf_op jit(solution)/shard_map/ppermute | solution.py:244
  135.3 4.9 %all_to_all.38 = f32[2,32,16,128]{3,2,1,0:T(8,128)S(1)} all-to-all(f32[2,32,16,128]{3,2,1,0:T(8,128)} %get-tuple-element.26), channel_id=1, replica_groups=mesh['z'=16,'h'=2,'c'=2,'x'=4,'l'=2] {'c'}, dimensions={0} | all-to-all | bytes 1048576 | tf_op jit(solution)/shard_map/all_to_all | solution.py:254
  140.8 10.3 %all-to-all-start.6 = ((bf16[32,16,128]{2,1,0:T(8,128)(2,1)}), bf16[32,16,128]{2,1,0:T(8,128)(2,1)S(1)}, u32[]{:S(2)}, u32[]{:S(2)}) async-start(bf16[32,16,128]{2,1,0:T(8,128)(2,1)} %fusion.1), calls=%async_computation.6 | async-start | bytes 262144 | tf_op jit(solution)/shard_map/all_to_all | solution.py:256
  151.2 0.9 pad_maximum_fusion.1
  152.8 8.2 %shard_map.133 = (bf16[256,1024]{1,0:T(8,128)(2,1)}, bf16[256,1024]{1,0:T(8,128)(2,1)}) custom-call(bf16[256,1024]{1,0:T(8,128)(2,1)} %get-tuple-element.19.mixed_ref, f32[384,1024]{1,0:T(8,128)} %shard_map.130.freq_ref, f32[384,1024]{1,0:T(8,128)} %get-tuple-element.21.spec_ref, bf16[128,1024]{1,0:T(8,128)(2,1)} %copy-done.1, ...), custom_call_target="tpu_custom_call" | custom-call | flops 1711276032 | bytes 6291456 | tf_op jit(solution)/shard_map/pallas_call | solution.py:177
  161.0 5.3 %all-to-all-done.6 = bf16[32,16,128]{2,1,0:T(8,128)(2,1)S(1)} async-done(((bf16[32,16,128]{2,1,0:T(8,128)(2,1)}), bf16[32,16,128]{2,1,0:T(8,128)(2,1)S(1)}, u32[]{:S(2)}, u32[]{:S(2)}) %all-to-all-start.6) | async-done | bytes 131104 | tf_op jit(solution)/shard_map/all_to_all | solution.py:256
  (28 shorter events, 5.6 us)
Async XLA Ops:
  7.2 15.3 %copy-start = (bf16[256,1024]{1,0:T(8,128)(2,1)S(1)}, bf16[256,1024]{1,0:T(8,128)(2,1)}, u32[]{:S(2)}) copy-start(bf16[256,1024]{1,0:T(8,128)(2,1)} %param.13) | copy-start | bytes 1572868
  10.3 11.4 %all-to-all-start = ((bf16[2,80,512]{2,1,0:T(8,128)(2,1)}), bf16[2,80,512]{2,1,0:T(8,128)(2,1)S(1)}, u32[]{:S(2)}, u32[]{:S(2)}) async-start(bf16[2,80,512]{2,1,0:T(8,128)(2,1)} %pad_maximum_fusion.2), calls=%async_computation | async-start | bytes 327680 | tf_op jit(solution)/shard_map/all_to_all | solution.py:211
  20.6 67.9 %all-gather.3.cloned.1.call-start = ((), (), s32[]{:S(2)}) async-start(), calls=%async_computation.7 | async-start | bytes 2506752 | tf_op jit(solution)/shard_map/all_gather | solution.py:222
  22.5 6.3 %collective-permute-start = (bf16[128,1024]{1,0:T(8,128)(2,1)S(1)}, bf16[128,1024]{1,0:T(8,128)(2,1)S(1)}, u32[]{:S(2)}, u32[]{:S(2)}) collective-permute-start(bf16[128,1024]{1,0:T(8,128)(2,1)S(1)} %slice.24), channel_id=1, source_target_pairs={{0,8},{8,16},{16,24},{24,32},{32,40},{40,48},{48,56},{56,64},{64,7... | collective-permute-start | bytes 786440 | tf_op jit(solution)/shard_map/ppermute | solution.py:227
  25.3 9.7 %all-to-all-start.1 = ((bf16[2,2,256,128]{3,1,2,0:T(2,128)(2,1)}), bf16[2,2,256,128]{3,1,2,0:T(2,128)(2,1)S(1)}, u32[]{:S(2)}, u32[]{:S(2)}) async-start(bf16[2,2,256,128]{3,1,2,0:T(2,128)(2,1)} %copy.24), calls=%async_computation.1 | async-start | bytes 524288 | tf_op jit(solution)/shard_map/all_to_all | solution.py:223
  130.0 21.1 %collective-permute-start.2 = (bf16[2,16,2,16,128]{4,3,2,1,0:T(8,128)(2,1)S(1)}, bf16[2,16,2,16,128]{4,3,2,1,0:T(8,128)(2,1)S(1)}, u32[]{:S(2)}, u32[]{:S(2)}) collective-permute-start(bf16[2,16,2,16,128]{4,3,2,1,0:T(8,128)(2,1)S(1)} %bitcast.45), channel_id=1, source_target_pairs={{0,16},{16,0},{1,17},{17,1},{2,18},{18,2},{3,19},{19,3},{4,20},{20... | collective-permute-start | bytes 786440 | tf_op jit(solution)/shard_map/ppermute | solution.py:248
  132.5 19.6 %collective-permute-start.1 = (bf16[128,1024]{1,0:T(8,128)(2,1)}, bf16[128,1024]{1,0:T(8,128)(2,1)S(1)}, u32[]{:S(2)}, u32[]{:S(2)}) collective-permute-start(bf16[128,1024]{1,0:T(8,128)(2,1)} %get-tuple-element.22), channel_id=1, source_target_pairs={{8,0},{16,8},{24,16},{32,24},{40,32},{48,40},{56,48},{64,56},{72,6... | collective-permute-start | bytes 786440 | tf_op jit(solution)/shard_map/ppermute | solution.py:244
  140.8 25.5 %all-to-all-start.6 = ((bf16[32,16,128]{2,1,0:T(8,128)(2,1)}), bf16[32,16,128]{2,1,0:T(8,128)(2,1)S(1)}, u32[]{:S(2)}, u32[]{:S(2)}) async-start(bf16[32,16,128]{2,1,0:T(8,128)(2,1)} %fusion.1), calls=%async_computation.6 | async-start | bytes 262144 | tf_op jit(solution)/shard_map/all_to_all | solution.py:256
  152.1 0.7 copy-start.1
Sparse Core Ops, SparseCore 0:
  24.1 64.3 all-gather.2

commit v6 on v5

v6 whole, which is shorter than its diff:
```python
import jax
import jax.numpy as jnp
import numpy as np
from jax import lax
from jax.experimental import pallas as pl
from jax.experimental.pallas import tpu as pltpu
from jax.sharding import Mesh, PartitionSpec as P

K = 128
TOK = 256
CH = 1024
SPAN = 8192
N = K + TOK
HALF = N // 2
TILE = 256
VMEM = 56 * 1024 * 1024

BF = jnp.bfloat16
F32 = jnp.float32
ROWS = ((1,), (0,))
LANES = ((1,), (1,))


def transforms():
    freq = 2.0 * np.pi * (np.arange(HALF) + 0.5) / N
    angle = freq[:, None] * np.arange(N + K)[None, :]
    forward = np.concatenate([np.cos(angle), -np.sin(angle)], axis=0)
    angle = angle[:, :N].T
    inverse = np.concatenate([np.cos(angle), -np.sin(angle)], axis=1) * (2.0 / N)
    return two(forward), two(inverse)


def two(values):
    values = np.asarray(values, np.float32)
    upper = values.astype(jnp.bfloat16)
    lower = (values - upper.astype(np.float32)).astype(jnp.bfloat16)
    return np.stack([upper, lower])


def dot(a, b, dims=ROWS):
    return lax.dot_general(a, b, (dims, ((), ())), preferred_element_type=F32)


def exact_side(matrix, values):
    return dot(matrix[0], values) + dot(matrix[1], values)


def both_sides(matrix, values):
    high = values.astype(BF)
    low = (values - high.astype(F32)).astype(BF)
    return dot(matrix[0], high) + dot(matrix[1], high) + dot(matrix[0], low)


def times(a, b):
    ar, ai, br, bi = a[:HALF], a[HALF:], b[:HALF], b[HALF:]
    return jnp.concatenate([ar * br - ai * bi, ar * bi + ai * br], axis=0)


def times_conj(a, b):
    ar, ai, br, bi = a[:HALF], a[HALF:], b[:HALF], b[HALF:]
    return jnp.concatenate([ar * br + ai * bi, ai * br - ar * bi], axis=0)


def params():
    return pltpu.CompilerParams(
        dimension_semantics=("arbitrary",), vmem_limit_bytes=VMEM
    )


def product_kernel(cols_ref, weight_ref, out_ref):
    weight = weight_ref[:, :K].reshape(16 * K, 512)
    rows = jnp.concatenate([cols_ref[0, i, 0, j] for i in range(8) for j in range(2)], axis=1)
    out_ref[0] = dot(rows, weight).astype(BF)


def product(cols, weights):
    return pl.pallas_call(
        product_kernel,
        grid=(4,),
        in_specs=[
            pl.BlockSpec((1, 8, 1, 2, TOK, K), lambda i: (i % 2, 0, i // 2, 0, 0, 0)),
            pl.BlockSpec((16, K + 16, 512), lambda i: (0, 0, 0)),
        ],
        out_specs=pl.BlockSpec((1, TOK, 512), lambda i: (i, 0, 0)),
        out_shape=jax.ShapeDtypeStruct((4, TOK, 512), BF),
        compiler_params=params(),
        cost_estimate=pl.CostEstimate(
            flops=2 * 1024 * 2048 * 512, bytes_accessed=8 << 20, transcendentals=0
        ),
    )(cols, weights)


def whole(shape):
    return pl.BlockSpec(shape, lambda j: (0,) * len(shape))


TILES = 512 // K
PAIR = pl.BlockSpec((1, TOK, 2 * K), lambda j: (j, 0, 0))
FREQ = pl.BlockSpec((1, N, 2 * K), lambda j: (j, 0, 0))


def front_kernel(halo_ref, tok_ref, forward_ref, freq_ref):
    first, second = tok_ref[0, 0], tok_ref[1, 0]
    window = jnp.concatenate(
        [
            jnp.concatenate([halo_ref[...], first[K:]], axis=1),
            jnp.concatenate([first[:K], second[:K]], axis=1),
            jnp.concatenate([first[K:], second[K:]], axis=1),
        ],
        axis=0,
    )
    freq_ref[0] = exact_side(forward_ref, window)


def front_part(halo, tokens, forward):
    return pl.pallas_call(
        front_kernel,
        grid=(TILES,),
        in_specs=[
            pl.BlockSpec((K, K), lambda j: (0, j)),
            pl.BlockSpec((2, 1, TOK, K), lambda j: (0, 0, 0, j)),
            whole((2, N, N)),
        ],
        out_specs=FREQ,
        out_shape=jax.ShapeDtypeStruct((TILES, N, 2 * K), F32),
        compiler_params=params(),
        cost_estimate=pl.CostEstimate(
            flops=2 * CH * N * 2 * N, bytes_accessed=3 << 20, transcendentals=0
        ),
    )(halo, tokens, forward)


def grad_kernel(
    mix_ref, tok_ref, freq_ref, own_ref, lag_ref, mixed_ref, first_ref, second_ref, spec_ref, tap_ref
):
    mixed = (mix_ref[0].astype(F32) + mix_ref[1].astype(F32)).astype(BF)
    mixed = jnp.concatenate([mixed[0], mixed[1]], axis=1)
    mixed_ref[0] = mixed
    gate = jnp.concatenate([tok_ref[0, 0], tok_ref[1, 0]], axis=1)
    conv_grad = (mixed.astype(F32) * gate.astype(F32)).astype(BF)
    first_ref[...] = conv_grad[:K, :K]
    second_ref[...] = conv_grad[:K, K:]
    spec = exact_side(own_ref, conv_grad)
    spec_ref[0] = spec
    cross = times_conj(spec, freq_ref[0])
    taps = both_sides(lag_ref, cross[:, :K] + cross[:, K:])
    tap_ref[...] = taps.T.reshape(8, 16, K).astype(BF)


def grad_part(mix, tokens, sig_freq, own, lag):
    return pl.pallas_call(
        grad_kernel,
        grid=(TILES,),
        in_specs=[
            pl.BlockSpec((2, 2, TOK, K), lambda j: (0, 0, 0, j)),
            pl.BlockSpec((2, 1, TOK, K), lambda j: (0, 1, 0, j)),
            FREQ,
            whole((2, N, TOK)),
            whole((2, K, N)),
        ],
        out_specs=[
            PAIR,
            pl.BlockSpec((K, K), lambda j: (0, j)),
            pl.BlockSpec((K, K), lambda j: (0, j)),
            FREQ,
            pl.BlockSpec((8, 16, K), lambda j: (j, 0, 0)),
        ],
        out_shape=[
            jax.ShapeDtypeStruct((TILES, TOK, 2 * K), BF),
            jax.ShapeDtypeStruct((K, 512), BF),
            jax.ShapeDtypeStruct((K, 512), BF),
            jax.ShapeDtypeStruct((TILES, N, 2 * K), F32),
            jax.ShapeDtypeStruct((32, 16, K), BF),
        ],
        compiler_params=params(),
        cost_estimate=pl.CostEstimate(
            flops=2 * CH * N * (2 * TOK + 2 * K), bytes_accessed=7 << 20, transcendentals=0
        ),
    )(mix, tokens, sig_freq, own, lag)


def out_kernel(
    mixed_ref,
    freq_ref,
    spec_ref,
    inner_ref,
    outer_ref,
    tap_ref,
    head_ref,
    tail_ref,
    inv_ref,
    out_ref,
):
    upper, lower = tap_ref[0], tap_ref[1]
    high, low = head_ref[0], head_ref[1]
    tap_freq = dot(high, upper, LANES) + dot(low, upper, LANES) + dot(high, lower, LANES)
    tap_freq = jnp.concatenate([tap_freq, tap_freq], axis=1)
    conv_out = both_sides(inv_ref, times(freq_ref[0], tap_freq))
    gate = mixed_ref[0].astype(F32) * conv_out
    halo = jnp.concatenate([inner_ref[...], outer_ref[...]], axis=1)
    full = spec_ref[0] + exact_side(tail_ref, halo)
    sig = both_sides(inv_ref, times_conj(full, tap_freq))
    for i, values in enumerate((sig, gate)):
        out_ref[0, i] = values[:, :K].astype(BF)
        out_ref[1, i] = values[:, K:].astype(BF)


def out_part(mixed, sig_freq, spec, inner, outer, taps, head, tail, inv):
    return pl.pallas_call(
        out_kernel,
        grid=(TILES,),
        in_specs=[
            PAIR,
            FREQ,
            FREQ,
            pl.BlockSpec((K, K), lambda j: (0, j)),
            pl.BlockSpec((K, K), lambda j: (0, j)),
            pl.BlockSpec((2, K, K), lambda j: (0, j, 0)),
            whole((2, N, K)),
            whole((2, N, K)),
            whole((2, TOK, N)),
        ],
        out_specs=pl.BlockSpec((2, 2, TOK, K), lambda j: (0, 0, 0, j)),
        out_shape=jax.ShapeDtypeStruct((2, 2, TOK, 512), BF),
        compiler_params=params(),
        cost_estimate=pl.CostEstimate(
            flops=2 * CH * N * (5 * K + 6 * TOK), bytes_accessed=6 << 20, transcendentals=0
        ),
    )(mixed, sig_freq, spec, inner, outer, taps, head, tail, inv)


def join_kernel(parts_ref, place_ref, sig_ref, gate_ref):
    for i, out_ref in enumerate((sig_ref, gate_ref)):
        rows = jnp.concatenate([parts_ref[0, i], parts_ref[1, i]], axis=1)
        out_ref[...] = dot(rows, place_ref[...]).astype(BF)


def join_part(parts, place):
    out = pl.BlockSpec((TOK, 2 * K), lambda j: (0, j))
    return pl.pallas_call(
        join_kernel,
        grid=(TILES,),
        in_specs=[
            pl.BlockSpec((2, 2, TOK, K), lambda j: (0, 0, 0, j)),
            whole((2 * K, 2 * K)),
        ],
        out_specs=[out, out],
        out_shape=[jax.ShapeDtypeStruct((TOK, CH), BF)] * 2,
        compiler_params=params(),
        cost_estimate=pl.CostEstimate(
            flops=4 * TOK * CH * 256, bytes_accessed=2 << 20, transcendentals=0
        ),
    )(parts, place)


def chooser():
    source = np.arange(2 * K).reshape(8, 2, 16).transpose(1, 0, 2).reshape(-1)
    matrix = np.zeros((2 * K, 2 * K), np.float32)
    matrix[source, np.arange(2 * K)] = 1.0
    return matrix.astype(jnp.bfloat16)


def by_core(values, place):
    rows = values.shape[0]
    chosen = dot(values.reshape(rows * 4, 2 * K), place).astype(BF)
    return chosen.reshape(rows, 4, 2, K).transpose(2, 0, 1, 3).reshape(2, rows, 512)


def on_device(out_grad, out_weight, signal, gate_input, filter_taps):
    chips = ("z", "h")
    period = SPAN // (2 * TOK)
    fwd, inv = transforms()
    place = chooser()

    turned = by_core(out_weight.T, place)
    tap_rows = filter_taps.T
    tap_high = lax.optimization_barrier(tap_rows.astype(BF))
    tap_low = (tap_rows - tap_high.astype(F32)).astype(BF)
    tap_pack = jnp.concatenate([tap_high, tap_low, jnp.zeros((16, 256), BF)], axis=1)
    turned = lax.all_to_all(turned, "c", split_axis=0, concat_axis=0).reshape(K, 512)
    block = jnp.concatenate([turned, tap_pack], axis=0)

    cols = out_grad.reshape(TOK, 2, 2, K).transpose(2, 1, 0, 3)
    block, cols, signal, gate_input = lax.optimization_barrier((block, cols, signal, gate_input))
    weights = lax.all_gather(block, "z", axis=0, tiled=False)
    cols = lax.all_to_all(cols, "h", split_axis=0, concat_axis=0)

    tokens = jnp.concatenate([by_core(signal, place), by_core(gate_input, place)], axis=1)
    tokens = lax.all_to_all(
        tokens.reshape(2, 2, TOK, 512), "c", split_axis=0, concat_axis=0
    )
    ahead = [(i, i + 1) for i in range(31) if (i + 1) % period]
    back = [(j, i) for i, j in ahead]
    sig_halo = lax.ppermute(tokens[1, 0, TOK - K :], chips, ahead)
    sig_freq = front_part(sig_halo, tokens, fwd[:, :, :N])

    cols, sig_freq = lax.optimization_barrier((cols, sig_freq))
    cols = lax.all_to_all(
        jnp.broadcast_to(cols[None], (8, 2, 2, TOK, K)), ("x", "l"), split_axis=0, concat_axis=0
    )
    cols = lax.all_to_all(
        jnp.broadcast_to(cols[None], (2, 8, 2, 2, TOK, K)), "c", split_axis=0, concat_axis=0
    )

    partial = product(cols, weights)
    mix = lax.all_to_all(
        partial.reshape(2, 2, TOK, 512), "h", split_axis=0, concat_axis=0
    )
    mixed, first_head, inner, spec, tap_grad = grad_part(
        mix, tokens, sig_freq, fwd[:, :, K:N], inv[:, :K]
    )
    outer = lax.ppermute(first_head, chips, back)
    tap_grad = lax.all_to_all(tap_grad, chips, split_axis=0, concat_axis=0)
    filter_grad = jnp.sum(tap_grad.astype(F32), axis=0).T

    weights, spec = lax.optimization_barrier((weights, spec))
    taps = weights[:, K:, : 2 * K].reshape(16, 16, 2, K).transpose(2, 0, 1, 3)
    other = lax.ppermute(taps, "h", [(0, 1), (1, 0)])
    upper_half = lax.axis_index("h") == 0
    taps = jnp.stack(
        [jnp.where(upper_half, taps, other), jnp.where(upper_half, other, taps)], axis=2
    ).reshape(2, 512, K)

    own = out_part(
        mixed, sig_freq, spec, inner, outer, taps, fwd[:, :, :K], fwd[:, :, N:], inv[:, K:]
    )
    other = lax.all_to_all(own, "c", split_axis=0, concat_axis=0)
    signal_grad, gate_grad = join_part(other, place.T)
    return signal_grad, gate_grad, filter_grad


def solution(mesh):
    fine = Mesh(mesh.devices.reshape(16, 2, 2, 4, 2), ("z", "h", "c", "x", "l"))
    ctx, tp = ("z", "h", "c"), ("x", "l")
    in_specs = (P(ctx, tp), P(tp, ctx), P(ctx, tp), P(ctx, tp), P(None, tp + ctx))
    out_specs = (P(ctx, tp), P(ctx, tp), P(None, tp + ctx))
    return jax.shard_map(
        on_device, mesh=fine, in_specs=in_specs, out_specs=out_specs, check_vma=False
    )
```

time: 176 us -> 189 us (1.074)
  Pallas kernels: 24.6 us -> 28.5 us
  local copies, waits for them, and re-layouts: 6.61 us -> 9.89 us
  waiting for transfers between devices: 20 us -> 23.1 us
  blocking collectives: 71.2 us -> 74 us
    all_gather x1, waiting for transfers between devices: 13.8 us -> 5.91 us  [on_device(): weights = lax.all_gather(block, 'z', axis=0, tiled=False)]
    all_to_all x2, waiting for transfers between devices: 5.37 us -> 11.3 us  [the longest x1 11.3 us: on_device(): tap_grad = lax.all_to_all(tap_grad, chips, split_axis=0, concat_axis=0)]
    ppermute x1, waiting for transfers between devices: 0.01 us -> 3.98 us  [on_device(): other = lax.ppermute(taps, 'h', [(0, 1), (1, 0)])]
    pallas_call x3 -> x4, Pallas kernels: 18.3 us -> 22.3 us  [the longest x1 8.66 us: out_part(): pl.pallas_call(out_kernel, grid=(TILES,), in_specs=[PAIR, FREQ, FREQ, pl....]
    all_to_all x2 -> x3, blocking collectives: 33.4 us -> 36.2 us  [the longest x1 17.8 us: on_device(): other = lax.all_to_all(own, 'c', split_axis=0, concat_axis=0)]
    ppermute x2, starting transfers between devices: 4.72 us -> 2.59 us  [the longest x1 1.3 us: on_device(): sig_halo = lax.ppermute(tokens[1, 0, TOK - K:], chips, ahead)]
    reshape x3 -> x9, local copies, waits for them, and re-layouts: 1.02 us -> 3.09 us  [the longest x3 1.69 us: by_core(): chosen = dot(values.reshape(rows * 4, 2 * K), place).astype(BF)]
  transfers between devices with their start and end apart: 7 -> 7, of which waited for: 3 -> 5; matrix products, arithmetic and copies ran while one was open for 4% -> 5% of each run, Pallas kernels for 7% -> 4%
where the time goes in v6:
time: 189 us; the launch traced here: 185 us
  blocking collectives  74 us (39%)
  starting transfers between devices  29.5 us (16%)
  Pallas kernels  28.5 us (15%)
  waiting for transfers between devices  23.1 us (12%)
  between operations  14.3 us (8%)
  local copies, waits for them, and re-layouts  9.89 us (5%)
  other arithmetic  4.47 us (2%)
    all_to_all x1, blocking collectives, on_device(): lax.all_to_all(jnp.broadcast_to(cols[None], (8, 2, 2, TOK, K)), ('x', 'l'...  27.5 us
    all_to_all x1, blocking collectives, on_device(): other = lax.all_to_all(own, 'c', split_axis=0, concat_axis=0)  17.8 us
    all_to_all x1, blocking collectives, on_device(): lax.all_to_all(partial.reshape(2, 2, TOK, 512), 'h', split_axis=0, concat...  14.2 us
    all_to_all x1, waiting for transfers between devices, on_device(): tap_grad = lax.all_to_all(tap_grad, chips, split_axis=0, concat_axis=0)  11.3 us
    all_to_all x1, starting transfers between devices, on_device(): tap_grad = lax.all_to_all(tap_grad, chips, split_axis=0, concat_axis=0)  11.3 us
    all_to_all x1, starting transfers between devices, on_device(): lax.all_to_all(turned, 'c', split_axis=0, concat_axis=0).reshape(K, 512)  10.2 us
    all_to_all x1, blocking collectives, on_device(): lax.all_to_all(jnp.broadcast_to(cols[None], (2, 8, 2, 2, TOK, K)), 'c', s...  10.2 us
    pallas_call x1, Pallas kernels, out_part(): pl.pallas_call(out_kernel, grid=(TILES,), in_specs=[PAIR, FREQ, FREQ, pl....  8.66 us
  transfers between devices with their start and end apart: 7, of which 5 were waited for; matrix products, arithmetic and copies ran while one was open for 5% of the time, Pallas kernels for 4%

profile of v6, /device:TPU:1, one launch (start us, length us, event | category | flops | bytes accessed | tf_op | source)
XLA Modules:
  0.0 185.5 jit_solution(10328652711072975987)
XLA Ops:
  7.2 1.1 reshape.53
  8.2 1.1 fusion
  10.3 10.2 %all-to-all-start = ((bf16[2,64,512]{2,1,0:T(8,128)(2,1)}), bf16[2,64,512]{2,1,0:T(8,128)(2,1)S(1)}, u32[]{:S(2)}, u32[]{:S(2)}) async-start(bf16[2,64,512]{2,1,0:T(8,128)(2,1)} %reshape.55), calls=%async_computation | async-start | bytes 262144 | tf_op jit(solution)/shard_map/all_to_all | solution.py:280
  21.9 1.1 copy.37
  26.3 4.3 %all_to_all.40.tok_ref = bf16[2,2,256,512]{3,2,1,0:T(8,128)(2,1)S(1)} all-to-all(bf16[2,2,256,512]{3,2,1,0:T(8,128)(2,1)S(1)} %bitcast.50), channel_id=1, replica_groups=mesh['z'=16,'h'=2,'c'=2,'x'=4,'l'=2] {'c'}, dimensions={0} | all-to-all | bytes 2097152 | tf_op jit(solution)/shard_map/all_to_all | solution.py:289
  30.6 1.3 collective-permute-start
  32.8 3.4 %all-to-all-start.1 = ((bf16[2,2,256,128]{3,1,2,0:T(2,128)(2,1)}), bf16[2,2,256,128]{3,1,2,0:T(2,128)(2,1)S(1)}, u32[]{:S(2)}, u32[]{:S(2)}) async-start(bf16[2,2,256,128]{3,1,2,0:T(2,128)(2,1)} %copy.38), calls=%async_computation.1 | async-start | bytes 524288 | tf_op jit(solution)/shard_map/all_to_all | solution.py:286
  36.9 4.4 %shard_map.148.freq_ref = f32[4,384,256]{2,1,0:T(8,128)} custom-call(bf16[128,512]{1,0:T(8,128)(2,1)} %copy-done.4, bf16[2,2,256,512]{3,2,1,0:T(8,128)(2,1)} %copy-done, bf16[2,384,384]{2,1,0:T(8,128)(2,1)} %constant.29.clone.forward_ref), custom_call_target="tpu_custom_call" | custom-call | flops 603979776 | bytes 3145728 | tf_op jit(solution)/shard_map/pallas_call | solution.py:116
  41.3 1.4 all-to-all-done.1
  43.2 27.5 %all_to_all.41 = bf16[8,2,2,256,128]{4,3,2,1,0:T(8,128)(2,1)S(1)} all-to-all(bf16[8,2,2,256,128]{4,3,2,1,0:T(8,128)(2,1)S(1)} %broadcast_in_dim.7), channel_id=1, replica_groups=mesh['z'=16,'h'=2,'c'=2,'x'=4,'l'=2] {'x','l'}, dimensions={0} | all-to-all | bytes 4194304 | tf_op jit(solution)/shard_map/all_to_all | solution.py:298
  70.7 1.4 broadcast_in_dim.8
  72.1 10.2 %all_to_all.42.cols_ref = bf16[2,8,2,2,256,128]{5,4,3,2,1,0:T(8,128)(2,1)} all-to-all(bf16[2,8,2,2,256,128]{5,4,3,2,1,0:T(8,128)(2,1)S(1)} %broadcast_in_dim.8), channel_id=1, replica_groups=mesh['z'=16,'h'=2,'c'=2,'x'=4,'l'=2] {'c'}, dimensions={0} | all-to-all | bytes 8388608 | tf_op jit(solution)/shard_map/all_to_all | solution.py:301
  82.4 5.9 %all-gather.3.cloned.1.call-done = bf16[2304,512]{1,0:T(8,128)(2,1)} async-done(((bf16[144,512]{1,0:T(8,128)(2,1)}), bf16[2304,512]{1,0:T(8,128)(2,1)}) %all-gather.3.cloned.1.call-update) | async-done | bytes 2359312 | tf_op jit(solution)/shard_map/all_gather | solution.py:285
  88.3 6.3 %shard_map.149 = bf16[4,256,512]{2,1,0:T(8,128)(2,1)} custom-call(bf16[2,8,2,2,256,128]{5,4,3,2,1,0:T(8,128)(2,1)} %all_to_all.42.cols_ref, bf16[16,144,512]{2,1,0:T(8,128)(2,1)} %bitcast.59), custom_call_target="tpu_custom_call" | custom-call | flops 2147483648 | bytes 8388608 | tf_op jit(solution)/shard_map/pallas_call | solution.py:77
  94.5 14.2 %all_to_all.43.mix_ref = bf16[2,2,256,512]{3,2,1,0:T(8,128)(2,1)} all-to-all(bf16[2,2,256,512]{3,2,1,0:T(8,128)(2,1)} %bitcast.53), channel_id=1, replica_groups=mesh['z'=16,'h'=2,'c'=2,'x'=4,'l'=2] {'h'}, dimensions={0} | all-to-all | bytes 2097152 | tf_op jit(solution)/shard_map/all_to_all | solution.py:306
  108.7 5.4 %shard_map.150 = (bf16[4,256,256]{2,1,0:T(8,128)(2,1)}, bf16[128,512]{1,0:T(8,128)(2,1)}, bf16[128,512]{1,0:T(8,128)(2,1)}, f32[4,384,256]{2,1,0:T(8,128)}, bf16[32,16,128]{2,1,0:T(8,128)(2,1)}) custom-call(bf16[2,2,256,512]{3,2,1,0:T(8,128)(2,1)} %all_to_all.43.mix_ref, bf16[2,2,256,512]{3,2,1,0:T(8,128)(2,1)} %copy-done, ...), custom_call_target="tpu_custom_call" | custom-call | flops 603979776 | bytes 7340032 | tf_op jit(solution)/shard_map/pallas_call | solution.py:151
  115.1 1.9 %collective-permute-start.2 = (bf16[2,16,16,128]{3,2,1,0:T(8,128)(2,1)S(1)}, bf16[2,16,16,128]{3,2,1,0:T(8,128)(2,1)S(1)}, u32[]{:S(2)}, u32[]{:S(2)}) collective-permute-start(bf16[2,16,16,128]{3,2,1,0:T(8,128)(2,1)S(1)} %bitcast_bitcast_fusion), channel_id=1, source_target_pairs={{0,16},{16,0},{1,17},{17,1},{2,18},{18,2},{3,19},{19,3},{4,20},{20... | collective-permute-start | bytes 393224 | tf_op jit(solution)/shard_map/ppermute | solution.py:318
  117.0 1.3 collective-permute-start.1
  118.3 4.0 %collective-permute-done.2 = bf16[2,16,16,128]{3,2,1,0:T(8,128)(2,1)S(1)} collective-permute-done((bf16[2,16,16,128]{3,2,1,0:T(8,128)(2,1)S(1)}, bf16[2,16,16,128]{3,2,1,0:T(8,128)(2,1)S(1)}, u32[]{:S(2)}, u32[]{:S(2)}) %collective-permute-start.2) | collective-permute-done | bytes 131104 | tf_op jit(solution)/shard_map/ppermute | solution.py:318
  125.1 8.7 %shard_map.151 = bf16[2,2,256,512]{3,2,1,0:T(8,128)(2,1)} custom-call(bf16[4,256,256]{2,1,0:T(8,128)(2,1)} %get-tuple-element.24.mixed_ref, f32[4,384,256]{2,1,0:T(8,128)} %shard_map.148.freq_ref, f32[4,384,256]{2,1,0:T(8,128)} %get-tuple-element.26.spec_ref, bf16[128,512]{1,0:T(8,128)(2,1)} %get-tuple-element.27.inner_ref, bf16[128,512]{1,0:T(8,128)(2,1)} %copy-done.5, ...), custom_call_target="tpu_custom_call" | custom-call | flops 1711276032 | bytes 6291456 | tf_op jit(solution)/shard_map/pallas_call | solution.py:209
  133.7 17.8 %all_to_all.44.parts_ref = bf16[2,2,256,512]{3,2,1,0:T(8,128)(2,1)} all-to-all(bf16[2,2,256,512]{3,2,1,0:T(8,128)(2,1)} %shard_map.151), channel_id=1, replica_groups=mesh['z'=16,'h'=2,'c'=2,'x'=4,'l'=2] {'c'}, dimensions={0} | all-to-all | bytes 2097152 | tf_op jit(solution)/shard_map/all_to_all | solution.py:327
  151.5 11.3 %all-to-all-start.7 = ((bf16[32,16,128]{2,1,0:T(8,128)(2,1)}), bf16[32,16,128]{2,1,0:T(8,128)(2,1)S(1)}, u32[]{:S(2)}, u32[]{:S(2)}) async-start(bf16[32,16,128]{2,1,0:T(8,128)(2,1)} %get-tuple-element.32), calls=%async_computation.7 | async-start | bytes 262144 | tf_op jit(solution)/shard_map/all_to_all | solution.py:313
  162.8 3.8 %shard_map.152 = (bf16[256,1024]{1,0:T(8,128)(2,1)}, bf16[256,1024]{1,0:T(8,128)(2,1)}) custom-call(bf16[2,2,256,512]{3,2,1,0:T(8,128)(2,1)} %all_to_all.44.parts_ref, bf16[256,256]{1,0:T(8,128)(2,1)} %constant.35.clone.place_ref), custom_call_target="tpu_custom_call" | custom-call | flops 268435456 | bytes 2097152 | tf_op jit(solution)/shard_map/pallas_call | solution.py:240
  166.7 11.3 %all-to-all-done.7 = bf16[32,16,128]{2,1,0:T(8,128)(2,1)S(1)} async-done(((bf16[32,16,128]{2,1,0:T(8,128)(2,1)}), bf16[32,16,128]{2,1,0:T(8,128)(2,1)S(1)}, u32[]{:S(2)}, u32[]{:S(2)}) %all-to-all-start.7) | async-done | bytes 131104 | tf_op jit(solution)/shard_map/all_to_all | solution.py:313
  (44 shorter events, 11.9 us)
Async XLA Ops:
  7.2 16.9 %copy-start.1 = (bf16[256,256]{1,0:T(8,128)(2,1)S(1)}, bf16[256,256]{1,0:T(8,128)(2,1)}, u32[]{:S(2)}) copy-start(bf16[256,256]{1,0:T(8,128)(2,1)} %constant.28.clone) | copy-start | bytes 393220
  7.2 16.6 %copy-start.2 = (bf16[256,1024]{1,0:T(8,128)(2,1)S(1)}, bf16[256,1024]{1,0:T(8,128)(2,1)}, u32[]{:S(2)}) copy-start(bf16[256,1024]{1,0:T(8,128)(2,1)} %param.15) | copy-start | bytes 1572868
  10.3 12.7 %all-to-all-start = ((bf16[2,64,512]{2,1,0:T(8,128)(2,1)}), bf16[2,64,512]{2,1,0:T(8,128)(2,1)S(1)}, u32[]{:S(2)}, u32[]{:S(2)}) async-start(bf16[2,64,512]{2,1,0:T(8,128)(2,1)} %reshape.55), calls=%async_computation | async-start | bytes 262144 | tf_op jit(solution)/shard_map/all_to_all | solution.py:280
  20.5 67.7 %all-gather.3.cloned.1.call-start = ((), (), s32[]{:S(2)}) async-start(), calls=%async_computation.8 | async-start | bytes 2506752 | tf_op jit(solution)/shard_map/all_gather | solution.py:285
  24.1 1.0 copy-start.3
  30.6 5.7 %copy-start = (bf16[2,2,256,512]{3,2,1,0:T(8,128)(2,1)}, bf16[2,2,256,512]{3,2,1,0:T(8,128)(2,1)S(1)}, u32[]{:S(2)}) copy-start(bf16[2,2,256,512]{3,2,1,0:T(8,128)(2,1)S(1)} %all_to_all.40.tok_ref) | copy-start | bytes 3145732
  30.6 5.6 %collective-permute-start = (bf16[128,512]{1,0:T(8,128)(2,1)S(1)}, bf16[128,512]{1,0:T(8,128)(2,1)S(1)}, u32[]{:S(2)}, u32[]{:S(2)}) collective-permute-start(bf16[128,512]{1,0:T(8,128)(2,1)S(1)} %slice_bitcast_fusion), channel_id=1, source_target_pairs={{0,16},{16,32},{32,48},{48,64},{64,80},{80,96},{96,112},{112,128},... | collective-permute-start | bytes 393224 | tf_op jit(solution)/shard_map/ppermute | solution.py:294
  32.8 9.9 %all-to-all-start.1 = ((bf16[2,2,256,128]{3,1,2,0:T(2,128)(2,1)}), bf16[2,2,256,128]{3,1,2,0:T(2,128)(2,1)S(1)}, u32[]{:S(2)}, u32[]{:S(2)}) async-start(bf16[2,2,256,128]{3,1,2,0:T(2,128)(2,1)} %copy.38), calls=%async_computation.1 | async-start | bytes 524288 | tf_op jit(solution)/shard_map/all_to_all | solution.py:286
  36.2 0.7 copy-start.4
  115.1 7.2 %collective-permute-start.2 = (bf16[2,16,16,128]{3,2,1,0:T(8,128)(2,1)S(1)}, bf16[2,16,16,128]{3,2,1,0:T(8,128)(2,1)S(1)}, u32[]{:S(2)}, u32[]{:S(2)}) collective-permute-start(bf16[2,16,16,128]{3,2,1,0:T(8,128)(2,1)S(1)} %bitcast_bitcast_fusion), channel_id=1, source_target_pairs={{0,16},{16,0},{1,17},{17,1},{2,18},{18,2},{3,19},{19,3},{4,20},{20... | collective-permute-start | bytes 393224 | tf_op jit(solution)/shard_map/ppermute | solution.py:318
  117.0 7.4 %collective-permute-start.1 = (bf16[128,512]{1,0:T(8,128)(2,1)}, bf16[128,512]{1,0:T(8,128)(2,1)S(1)}, u32[]{:S(2)}, u32[]{:S(2)}) collective-permute-start(bf16[128,512]{1,0:T(8,128)(2,1)} %get-tuple-element.28), channel_id=1, source_target_pairs={{16,0},{32,16},{48,32},{64,48},{80,64},{96,80},{112,96},{128,112},... | collective-permute-start | bytes 393224 | tf_op jit(solution)/shard_map/ppermute | solution.py:312
  124.4 0.6 copy-start.5
  151.5 26.5 %all-to-all-start.7 = ((bf16[32,16,128]{2,1,0:T(8,128)(2,1)}), bf16[32,16,128]{2,1,0:T(8,128)(2,1)S(1)}, u32[]{:S(2)}, u32[]{:S(2)}) async-start(bf16[32,16,128]{2,1,0:T(8,128)(2,1)} %get-tuple-element.32), calls=%async_computation.7 | async-start | bytes 262144 | tf_op jit(solution)/shard_map/all_to_all | solution.py:313
Sparse Core Ops, SparseCore 0:
  24.0 64.2 all-gather.2

commit v7 on v6

v7 whole, which is shorter than its diff:
```python
import jax
import jax.numpy as jnp
import numpy as np
from jax import lax
from jax.experimental import pallas as pl
from jax.experimental.pallas import tpu as pltpu
from jax.sharding import Mesh, PartitionSpec as P

K = 128
TOK = 256
CH = 1024
SPAN = 8192
N = K + TOK
HALF = N // 2
TILE = 256
VMEM = 56 * 1024 * 1024

BF = jnp.bfloat16
F32 = jnp.float32
ROWS = ((1,), (0,))
LANES = ((1,), (1,))


def transforms():
    freq = 2.0 * np.pi * (np.arange(HALF) + 0.5) / N
    angle = freq[:, None] * np.arange(N + K)[None, :]
    forward = np.concatenate([np.cos(angle), -np.sin(angle)], axis=0)
    angle = angle[:, :N].T
    inverse = np.concatenate([np.cos(angle), -np.sin(angle)], axis=1) * (2.0 / N)
    return two(forward), two(inverse)


def two(values):
    values = np.asarray(values, np.float32)
    upper = values.astype(jnp.bfloat16)
    lower = (values - upper.astype(np.float32)).astype(jnp.bfloat16)
    return np.stack([upper, lower])


def dot(a, b, dims=ROWS):
    return lax.dot_general(a, b, (dims, ((), ())), preferred_element_type=F32)


def exact_side(matrix, values):
    return dot(matrix[0], values) + dot(matrix[1], values)


def both_sides(matrix, values):
    high = values.astype(BF)
    low = (values - high.astype(F32)).astype(BF)
    return dot(matrix[0], high) + dot(matrix[1], high) + dot(matrix[0], low)


def times(a, b):
    ar, ai, br, bi = a[:HALF], a[HALF:], b[:HALF], b[HALF:]
    return jnp.concatenate([ar * br - ai * bi, ar * bi + ai * br], axis=0)


def times_conj(a, b):
    ar, ai, br, bi = a[:HALF], a[HALF:], b[:HALF], b[HALF:]
    return jnp.concatenate([ar * br + ai * bi, ai * br - ar * bi], axis=0)


def params():
    return pltpu.CompilerParams(
        dimension_semantics=("arbitrary",), vmem_limit_bytes=VMEM
    )


def product_kernel(cols_ref, weight_ref, out_ref):
    weight = weight_ref[:, :K].reshape(16 * K, 512)
    rows = jnp.concatenate([cols_ref[0, i, 0, j] for i in range(8) for j in range(2)], axis=1)
    out_ref[0] = dot(rows, weight).astype(BF)


def product(cols, weights):
    return pl.pallas_call(
        product_kernel,
        grid=(4,),
        in_specs=[
            pl.BlockSpec((1, 8, 1, 2, TOK, K), lambda i: (i % 2, 0, i // 2, 0, 0, 0)),
            pl.BlockSpec((16, K + 16, 512), lambda i: (0, 0, 0)),
        ],
        out_specs=pl.BlockSpec((1, TOK, 512), lambda i: (i, 0, 0)),
        out_shape=jax.ShapeDtypeStruct((4, TOK, 512), BF),
        compiler_params=params(),
        cost_estimate=pl.CostEstimate(
            flops=2 * 1024 * 2048 * 512, bytes_accessed=8 << 20, transcendentals=0
        ),
    )(cols, weights)


def whole(shape):
    return pl.BlockSpec(shape, lambda j: (0,) * len(shape))


def scalar():
    return pl.BlockSpec(memory_space=pltpu.SMEM)


TILES = 512 // K
PAIR = pl.BlockSpec((1, TOK, 2 * K), lambda j: (j, 0, 0))
FREQ = pl.BlockSpec((1, N, 2 * K), lambda j: (j, 0, 0))


def plain_kernel(window_ref, forward_ref, freq_ref):
    freq_ref[...] = exact_side(forward_ref, window_ref[...])


def plain_part(window, forward):
    tile = pl.BlockSpec((N, 2 * K), lambda j: (0, j))
    return pl.pallas_call(
        plain_kernel,
        grid=(TILES,),
        in_specs=[tile, whole((2, N, N))],
        out_specs=tile,
        out_shape=jax.ShapeDtypeStruct((N, CH), F32),
        compiler_params=params(),
        cost_estimate=pl.CostEstimate(
            flops=2 * CH * N * 2 * N, bytes_accessed=3 << 20, transcendentals=0
        ),
    )(window, forward)


def front_kernel(halo_ref, tok_ref, forward_ref, freq_ref):
    first, second = tok_ref[0, 0], tok_ref[1, 0]
    window = jnp.concatenate(
        [
            jnp.concatenate([halo_ref[...], first[K:]], axis=1),
            jnp.concatenate([first[:K], second[:K]], axis=1),
            jnp.concatenate([first[K:], second[K:]], axis=1),
        ],
        axis=0,
    )
    freq_ref[0] = exact_side(forward_ref, window)


def front_part(halo, tokens, forward):
    return pl.pallas_call(
        front_kernel,
        grid=(TILES,),
        in_specs=[
            pl.BlockSpec((K, K), lambda j: (0, j)),
            pl.BlockSpec((2, 1, TOK, K), lambda j: (0, 0, 0, j)),
            whole((2, N, N)),
        ],
        out_specs=FREQ,
        out_shape=jax.ShapeDtypeStruct((TILES, N, 2 * K), F32),
        compiler_params=params(),
        cost_estimate=pl.CostEstimate(
            flops=2 * CH * N * 2 * N, bytes_accessed=3 << 20, transcendentals=0
        ),
    )(halo, tokens, forward)


def grad_kernel(
    core_ref,
    mix_ref,
    tok_ref,
    freq_ref,
    own_ref,
    lag_ref,
    keep_ref,
    send_ref,
    first_ref,
    inner_ref,
    cross_ref,
    tap_ref,
):
    is_first = core_ref[0] == 0
    early = (mix_ref[0, 0].astype(F32) + mix_ref[1, 0].astype(F32)).astype(BF).astype(F32)
    late = (mix_ref[0, 1].astype(F32) + mix_ref[1, 1].astype(F32)).astype(BF).astype(F32)
    keep_ref[...] = jnp.where(is_first, early, late).astype(BF)
    send_ref[...] = jnp.where(is_first, late, early).astype(BF)
    early = early * tok_ref[0, 0].astype(F32)
    late = late * tok_ref[1, 0].astype(F32)
    first_ref[...] = early[:K].astype(BF)
    inner_ref[...] = late[:K].astype(BF)
    cross_ref[...] = jnp.where(is_first, early[:K], late[:K]).astype(BF)
    conv_grad = jnp.concatenate([early, late], axis=1).astype(BF)
    cross = times_conj(exact_side(own_ref, conv_grad), freq_ref[0])
    taps = both_sides(lag_ref, cross[:, :K] + cross[:, K:])
    tap_ref[...] = taps.T.reshape(8, 16, K).astype(tap_ref.dtype)


def grad_part(core, mix, tokens, sig_freq, own, lag):
    head = pl.BlockSpec((K, K), lambda j: (0, j))
    half = pl.BlockSpec((TOK, K), lambda j: (0, j))
    return pl.pallas_call(
        grad_kernel,
        grid=(TILES,),
        in_specs=[
            scalar(),
            pl.BlockSpec((2, 2, TOK, K), lambda j: (0, 0, 0, j)),
            pl.BlockSpec((2, 1, TOK, K), lambda j: (0, 1, 0, j)),
            FREQ,
            whole((2, N, TOK)),
            whole((2, K, N)),
        ],
        out_specs=[half, half, head, head, head, pl.BlockSpec((8, 16, K), lambda j: (j, 0, 0))],
        out_shape=[jax.ShapeDtypeStruct((TOK, 512), BF)] * 2
        + [jax.ShapeDtypeStruct((K, 512), BF)] * 3
        + [jax.ShapeDtypeStruct((32, 16, K), BF)],
        compiler_params=params(),
        cost_estimate=pl.CostEstimate(
            flops=2 * CH * N * (2 * TOK + 2 * K), bytes_accessed=5 << 20, transcendentals=0
        ),
    )(core, mix, tokens, sig_freq, own, lag)


def out_kernel(
    core_ref,
    keep_ref,
    other_ref,
    inner_ref,
    near_ref,
    far_ref,
    gate_in_ref,
    freq_ref,
    tap_ref,
    forward_ref,
    inv_ref,
    place_ref,
    gate_ref,
    sig_ref,
):
    is_first = core_ref[0] == 0

    def joined(left, right):
        return dot(jnp.concatenate([left, right], axis=1), place_ref[...])

    keep, other = keep_ref[...], other_ref[...]
    mixed = joined(jnp.where(is_first, keep, other), jnp.where(is_first, other, keep))
    near = near_ref[...]
    halo = joined(
        jnp.where(is_first, inner_ref[...], near), jnp.where(is_first, near, far_ref[...])
    ).astype(BF)
    conv_grad = (mixed * gate_in_ref[...].astype(F32)).astype(BF)
    window = jnp.concatenate([conv_grad, halo], axis=0)
    full = exact_side(forward_ref[:, :, K:], window)
    upper, lower = tap_ref[0], tap_ref[1]
    high, low = forward_ref[0, :, :K], forward_ref[1, :, :K]
    tap_freq = dot(high, upper, LANES) + dot(low, upper, LANES) + dot(high, lower, LANES)
    conv_out = both_sides(inv_ref, times(freq_ref[...], tap_freq))
    gate_ref[...] = (mixed * conv_out).astype(BF)
    sig_ref[...] = both_sides(inv_ref, times_conj(full, tap_freq)).astype(BF)


def out_part(core, keep, other, inner, near, far, gate, sig_freq, taps, forward, inv, place):
    head = pl.BlockSpec((K, K), lambda j: (0, j))
    half = pl.BlockSpec((TOK, K), lambda j: (0, j))

    def tile(rows):
        return pl.BlockSpec((rows, 2 * K), lambda j: (0, j))

    return pl.pallas_call(
        out_kernel,
        grid=(TILES,),
        in_specs=[
            scalar(),
            half,
            half,
            head,
            head,
            head,
            tile(TOK),
            tile(N),
            pl.BlockSpec((2, 2 * K, K), lambda j: (0, j, 0)),
            whole((2, N, N + K)),
            whole((2, TOK, N)),
            whole((2 * K, 2 * K)),
        ],
        out_specs=[tile(TOK), tile(TOK)],
        out_shape=[jax.ShapeDtypeStruct((TOK, CH), BF)] * 2,
        compiler_params=params(),
        cost_estimate=pl.CostEstimate(
            flops=2 * CH * N * (5 * K + 8 * TOK), bytes_accessed=6 << 20, transcendentals=0
        ),
    )(core, keep, other, inner, near, far, gate, sig_freq, taps, forward, inv, place)


def chooser():
    source = np.arange(2 * K).reshape(8, 2, 16).transpose(1, 0, 2).reshape(-1)
    matrix = np.zeros((2 * K, 2 * K), np.float32)
    matrix[source, np.arange(2 * K)] = 1.0
    return matrix.astype(jnp.bfloat16)


def by_core(values, place):
    rows = values.shape[0]
    chosen = dot(values.reshape(rows * 4, 2 * K), place).astype(BF)
    return chosen.reshape(rows, 4, 2, K).transpose(2, 0, 1, 3).reshape(2, rows, 512)


def on_device(out_grad, out_weight, signal, gate_input, filter_taps):
    chips, ctx = ("z", "h"), ("z", "h", "c")
    period = SPAN // TOK
    fwd, inv = transforms()
    place = chooser()
    core = lax.axis_index("c").reshape(1)

    turned = by_core(out_weight.T, place)
    tap_rows = filter_taps.T
    tap_high = lax.optimization_barrier(tap_rows.astype(BF))
    tap_low = (tap_rows - tap_high.astype(F32)).astype(BF)
    tap_pack = jnp.concatenate([tap_high, tap_low, jnp.zeros((16, 256), BF)], axis=1)
    message = jnp.concatenate([turned, jnp.broadcast_to(tap_pack[None], (2, 16, 512))], axis=1)
    got = lax.all_to_all(message, "c", split_axis=0, concat_axis=0)
    block = jnp.concatenate(
        [
            got[:, :64].reshape(K, 512),
            jnp.concatenate([got[0, 64:, :256], got[1, 64:, :256]], axis=1),
        ],
        axis=0,
    )

    cols = out_grad.reshape(TOK, 2, 2, K).transpose(2, 1, 0, 3)
    block, cols, signal, gate_input = lax.optimization_barrier((block, cols, signal, gate_input))
    weights = lax.all_gather(block, "z", axis=0, tiled=False)
    cols = lax.all_to_all(cols, "h", split_axis=0, concat_axis=0)

    ahead = [(i, i + 1) for i in range(63) if (i + 1) % period]
    window = jnp.concatenate([lax.ppermute(signal[TOK - K :], ctx, ahead), signal], axis=0)
    sig_freq = plain_part(window, fwd[:, :, :N])
    tokens = jnp.concatenate([by_core(signal, place), by_core(gate_input, place)], axis=1)
    tokens = lax.all_to_all(
        tokens.reshape(2, 2, TOK, 512), "c", split_axis=0, concat_axis=0
    )
    ahead = [(i, i + 1) for i in range(31) if (i + 1) % (period // 2)]
    sig_halo = lax.ppermute(tokens[1, 0, TOK - K :], chips, ahead)
    own_freq = front_part(sig_halo, tokens, fwd[:, :, :N])

    cols, sig_freq, own_freq = lax.optimization_barrier((cols, sig_freq, own_freq))
    cols = lax.all_to_all(
        jnp.broadcast_to(cols[None], (8, 2, 2, TOK, K)), ("x", "l"), split_axis=0, concat_axis=0
    )
    cols = lax.all_to_all(
        jnp.broadcast_to(cols[None], (2, 8, 2, 2, TOK, K)), "c", split_axis=0, concat_axis=0
    )

    partial = product(cols, weights)
    mix = lax.all_to_all(
        partial.reshape(2, 2, TOK, 512), "h", split_axis=0, concat_axis=0
    )
    keep, send, first, inner, cross, tap_grad = grad_part(
        core, mix, tokens, own_freq, fwd[:, :, K:N], inv[:, :K]
    )
    tap_grad = lax.all_to_all(tap_grad, chips, split_axis=0, concat_axis=0)
    filter_grad = jnp.sum(tap_grad.astype(F32), axis=0).T

    other = lax.ppermute(send, "c", [(0, 1), (1, 0)])
    follows = [(2 * i + 2, 2 * i + 1) for i in range(31) if (i + 1) % (period // 2)]
    near = lax.ppermute(cross, ctx, follows + [(2 * i + 1, 2 * i) for i in range(32)])
    far = lax.ppermute(first, ctx, [(i + 1, j) for i, j in follows])

    weights, keep = lax.optimization_barrier((weights, keep))
    taps = weights[:, K:].reshape(16, 16, 2, 2, K).transpose(3, 0, 2, 1, 4)
    more = lax.ppermute(taps, "h", [(0, 1), (1, 0)])
    upper_half = lax.axis_index("h") == 0
    taps = jnp.stack(
        [jnp.where(upper_half, taps, more), jnp.where(upper_half, more, taps)], axis=2
    ).reshape(2, CH, K)

    gate_grad, signal_grad = out_part(
        core, keep, other, inner, near, far, gate_input, sig_freq, taps, fwd, inv[:, K:], place.T
    )
    return signal_grad, gate_grad, filter_grad


def solution(mesh):
    fine = Mesh(mesh.devices.reshape(16, 2, 2, 4, 2), ("z", "h", "c", "x", "l"))
    ctx, tp = ("z", "h", "c"), ("x", "l")
    in_specs = (P(ctx, tp), P(tp, ctx), P(ctx, tp), P(ctx, tp), P(None, tp + ctx))
    out_specs = (P(ctx, tp), P(ctx, tp), P(None, tp + ctx))
    return jax.shard_map(
        on_device, mesh=fine, in_specs=in_specs, out_specs=out_specs, check_vma=False
    )
```

time: 189 us -> 176 us (0.931); the launches traced: 185 us -> 175 us
  blocking collectives: 74 us -> 38.4 us
  starting transfers between devices: 29.5 us -> 58 us
  waiting for transfers between devices: 23.1 us -> 18.2 us
  other arithmetic: 4.47 us -> 6.42 us
    all_to_all x3 -> x0, blocking collectives: 36.2 us -> none  [the longest x1 17.8 us: on_device(): other = lax.all_to_all(own, 'c', split_axis=0, concat_axis=0)]
    ppermute x2 -> x5, starting transfers between devices: 3.22 us -> 17.4 us  [the longest x1 10.4 us: on_device(): other = lax.ppermute(send, 'c', [(0, 1), (1, 0)])]
    all_to_all x1 -> x3, waiting for transfers between devices: 0.01 us -> 10.7 us  [the longest x1 9.74 us: on_device(): lax.all_to_all(partial.reshape(2, 2, TOK, 512), 'h', split_axis=0, concat...]
    all_to_all x1 -> x3, starting transfers between devices: 10.2 us -> 20 us  [the longest x1 10.3 us: on_device(): got = lax.all_to_all(message, 'c', split_axis=0, concat_axis=0)]
    all_gather x1, waiting for transfers between devices: 5.91 us -> 0.01 us  [on_device(): weights = lax.all_gather(block, 'z', axis=0, tiled=False)]
    ppermute x2 -> x5, waiting for transfers between devices: 4.43 us -> 0.01 us  [the longest x1 0.01 us: on_device(): more = lax.ppermute(taps, 'h', [(0, 1), (1, 0)])]
    all_to_all x1, starting transfers between devices: 11.3 us -> 15.6 us  [on_device(): tap_grad = lax.all_to_all(tap_grad, chips, split_axis=0, concat_axis=0)]
    all_to_all x1, waiting for transfers between devices: 11.3 us -> 7.2 us  [on_device(): tap_grad = lax.all_to_all(tap_grad, chips, split_axis=0, concat_axis=0)]
  transfers between devices with their start and end apart: 7 -> 12, of which waited for: 5 -> 4; matrix products, arithmetic and copies ran while one was open for 5% -> 5% of each run, Pallas kernels for 4% -> 9%
where the time goes in v7:
time: 176 us; the launch traced here: 175 us
  starting transfers between devices  58 us (33%)
  blocking collectives  38.4 us (22%)
  Pallas kernels  28.2 us (16%)
  waiting for transfers between devices  18.2 us (10%)
  between operations  14.4 us (8%)
  local copies, waits for them, and re-layouts  9.5 us (5%)
  other arithmetic  6.42 us (4%)
    all_to_all x1, blocking collectives, on_device(): lax.all_to_all(jnp.broadcast_to(cols[None], (8, 2, 2, TOK, K)), ('x', 'l'...  30.2 us
    all_to_all x1, starting transfers between devices, on_device(): tap_grad = lax.all_to_all(tap_grad, chips, split_axis=0, concat_axis=0)  15.6 us
    ppermute x1, starting transfers between devices, on_device(): other = lax.ppermute(send, 'c', [(0, 1), (1, 0)])  10.4 us
    all_to_all x1, starting transfers between devices, on_device(): got = lax.all_to_all(message, 'c', split_axis=0, concat_axis=0)  10.3 us
    all_to_all x1, waiting for transfers between devices, on_device(): lax.all_to_all(partial.reshape(2, 2, TOK, 512), 'h', split_axis=0, concat...  9.74 us
    all_to_all x1, blocking collectives, on_device(): lax.all_to_all(jnp.broadcast_to(cols[None], (2, 8, 2, 2, TOK, K)), 'c', s...  8.16 us
    pallas_call x1, Pallas kernels, out_part(): pl.pallas_call(out_kernel, grid=(TILES,), in_specs=[scalar(), half, half,...  7.72 us
    all_to_all x1, waiting for transfers between devices, on_device(): tap_grad = lax.all_to_all(tap_grad, chips, split_axis=0, concat_axis=0)  7.2 us
  transfers between devices with their start and end apart: 12, of which 4 were waited for; matrix products, arithmetic and copies ran while one was open for 5% of the time, Pallas kernels for 9%

profile of v7, /device:TPU:1, one launch (start us, length us, event | category | flops | bytes accessed | tf_op | source)
XLA Modules:
  0.0 174.9 jit_solution(7883820376752693997)
XLA Ops:
  8.7 1.0 reshape.58
  9.7 1.1 fusion
  11.8 10.3 %all-to-all-start = ((bf16[2,80,512]{2,1,0:T(8,128)(2,1)}), bf16[2,80,512]{2,1,0:T(8,128)(2,1)S(1)}, u32[]{:S(2)}, u32[]{:S(2)}) async-start(bf16[2,80,512]{2,1,0:T(8,128)(2,1)} %pad_maximum_fusion.3), calls=%async_computation | async-start | bytes 327680 | tf_op jit(solution)/shard_map/all_to_all | solution.py:308
  26.4 1.1 pad_maximum_fusion
  27.5 3.9 %all-to-all-start.2 = ((bf16[2,2,256,512]{3,2,1,0:T(8,128)(2,1)}), bf16[2,2,256,512]{3,2,1,0:T(8,128)(2,1)S(1)}, u32[]{:S(2)}, u32[]{:S(2)}) async-start(bf16[2,2,256,512]{3,2,1,0:T(8,128)(2,1)} %bitcast.13), calls=%async_computation.2 | async-start | bytes 2097152 | tf_op jit(solution)/shard_map/all_to_all | solution.py:326
  31.4 1.9 %collective-permute-start = (bf16[128,1024]{1,0:T(8,128)(2,1)S(1)}, bf16[128,1024]{1,0:T(8,128)(2,1)S(1)}, u32[]{:S(2)}, u32[]{:S(2)}) collective-permute-start(bf16[128,1024]{1,0:T(8,128)(2,1)S(1)} %slice.21), channel_id=1, source_target_pairs={{0,8},{8,16},{16,24},{24,32},{32,40},{40,48},{48,56},{56,64},{64,7... | collective-permute-start | bytes 786440 | tf_op jit(solution)/shard_map/ppermute | solution.py:323
  33.4 1.3 collective-permute-start.1
  35.6 3.6 %all-to-all-start.1 = ((bf16[2,2,256,128]{3,1,2,0:T(2,128)(2,1)}), bf16[2,2,256,128]{3,1,2,0:T(2,128)(2,1)S(1)}, u32[]{:S(2)}, u32[]{:S(2)}) async-start(bf16[2,2,256,128]{3,1,2,0:T(2,128)(2,1)} %copy.45), calls=%async_computation.1 | async-start | bytes 524288 | tf_op jit(solution)/shard_map/all_to_all | solution.py:320
  40.1 4.3 %shard_map.149.freq_ref = f32[4,384,256]{2,1,0:T(8,128)} custom-call(bf16[128,512]{1,0:T(8,128)(2,1)} %copy-done.6, bf16[2,2,256,512]{3,2,1,0:T(8,128)(2,1)} %copy-done, bf16[2,384,384]{2,1,0:T(8,128)(2,1)} %constant.31.clone.forward_ref), custom_call_target="tpu_custom_call" | custom-call | flops 603979776 | bytes 3145728 | tf_op jit(solution)/shard_map/pallas_call | solution.py:139
  45.4 4.4 %shard_map.148.freq_ref = f32[384,1024]{1,0:T(8,128)} custom-call(bf16[384,1024]{1,0:T(8,128)(2,1)} %pad_maximum_fusion.1.window_ref, bf16[2,384,384]{2,1,0:T(8,128)(2,1)} %constant.31.clone.forward_ref), custom_call_target="tpu_custom_call" | custom-call | flops 603979776 | bytes 3145728 | tf_op jit(solution)/shard_map/pallas_call | solution.py:112
  50.4 30.2 %all_to_all.35 = bf16[8,2,2,256,128]{4,3,2,1,0:T(8,128)(2,1)S(1)} all-to-all(bf16[8,2,2,256,128]{4,3,2,1,0:T(8,128)(2,1)S(1)} %broadcast_in_dim.10), channel_id=1, replica_groups=mesh['z'=16,'h'=2,'c'=2,'x'=4,'l'=2] {'x','l'}, dimensions={0} | all-to-all | bytes 4194304 | tf_op jit(solution)/shard_map/all_to_all | solution.py:334
  80.6 1.4 broadcast_in_dim.11
  82.0 8.2 %all_to_all.36.cols_ref = bf16[2,8,2,2,256,128]{5,4,3,2,1,0:T(8,128)(2,1)} all-to-all(bf16[2,8,2,2,256,128]{5,4,3,2,1,0:T(8,128)(2,1)S(1)} %broadcast_in_dim.11), channel_id=1, replica_groups=mesh['z'=16,'h'=2,'c'=2,'x'=4,'l'=2] {'c'}, dimensions={0} | all-to-all | bytes 8388608 | tf_op jit(solution)/shard_map/all_to_all | solution.py:337
  90.2 6.3 %shard_map.150 = bf16[4,256,512]{2,1,0:T(8,128)(2,1)} custom-call(bf16[2,8,2,2,256,128]{5,4,3,2,1,0:T(8,128)(2,1)} %all_to_all.36.cols_ref, bf16[16,144,512]{2,1,0:T(8,128)(2,1)} %bitcast.55), custom_call_target="tpu_custom_call" | custom-call | flops 2147483648 | bytes 8388608 | tf_op jit(solution)/shard_map/pallas_call | solution.py:77
  96.5 5.8 %all-to-all-start.5 = ((bf16[2,2,256,512]{3,2,1,0:T(8,128)(2,1)}), bf16[2,2,256,512]{3,2,1,0:T(8,128)(2,1)S(1)}, u32[]{:S(2)}, u32[]{:S(2)}) async-start(bf16[2,2,256,512]{3,2,1,0:T(8,128)(2,1)} %bitcast.48), calls=%async_computation.5 | async-start | bytes 2097152 | tf_op jit(solution)/shard_map/all_to_all | solution.py:342
  102.2 9.7 %all-to-all-done.5.mix_ref = bf16[2,2,256,512]{3,2,1,0:T(8,128)(2,1)S(1)} async-done(((bf16[2,2,256,512]{3,2,1,0:T(8,128)(2,1)}), bf16[2,2,256,512]{3,2,1,0:T(8,128)(2,1)S(1)}, u32[]{:S(2)}, u32[]{:S(2)}) %all-to-all-start.5) | async-done | bytes 1048608 | tf_op jit(solution)/shard_map/all_to_all | solution.py:342
  113.0 5.5 %shard_map.151 = (bf16[256,512]{1,0:T(8,128)(2,1)}, bf16[256,512]{1,0:T(8,128)(2,1)}, bf16[128,512]{1,0:T(8,128)(2,1)}, bf16[128,512]{1,0:T(8,128)(2,1)}, bf16[1...) custom-call(s32[1]{0:T(128)} %bitcast.core_ref, bf16[2,2,256,512]{3,2,1,0:T(8,128)(2,1)} %copy-done.1, ...), custom_call_target="tpu_custom_call" | custom-call | flops 603979776 | bytes 5242880 | tf_op jit(solution)/shard_map/pallas_call | solution.py:189
  119.5 1.9 %collective-permute-start.5 = (bf16[2,16,2,16,128]{4,3,2,1,0:T(8,128)(2,1)S(1)}, bf16[2,16,2,16,128]{4,3,2,1,0:T(8,128)(2,1)S(1)}, u32[]{:S(2)}, u32[]{:S(2)}) collective-permute-start(bf16[2,16,2,16,128]{4,3,2,1,0:T(8,128)(2,1)S(1)} %bitcast.53), channel_id=1, source_target_pairs={{0,16},{16,0},{1,17},{17,1},{2,18},{18,2},{3,19},{19,3},{4,20},{20... | collective-permute-start | bytes 786440 | tf_op jit(solution)/shard_map/ppermute | solution.py:358
  121.5 10.4 %collective-permute-start.2 = (bf16[256,512]{1,0:T(8,128)(2,1)}, bf16[256,512]{1,0:T(8,128)(2,1)S(1)}, u32[]{:S(2)}, u32[]{:S(2)}) collective-permute-start(bf16[256,512]{1,0:T(8,128)(2,1)} %get-tuple-element.28), channel_id=1, source_target_pairs={{0,8},{8,0},{1,9},{9,1},{2,10},{10,2},{3,11},{11,3},{4,12},{12,4},... | collective-permute-start | bytes 786440 | tf_op jit(solution)/shard_map/ppermute | solution.py:351
  131.8 1.9 %collective-permute-start.3 = (bf16[128,512]{1,0:T(8,128)(2,1)}, bf16[128,512]{1,0:T(8,128)(2,1)S(1)}, u32[]{:S(2)}, u32[]{:S(2)}) collective-permute-start(bf16[128,512]{1,0:T(8,128)(2,1)} %get-tuple-element.30), channel_id=1, source_target_pairs={{16,8},{32,24},{48,40},{64,56},{80,72},{96,88},{112,104},{128,120}... | collective-permute-start | bytes 393224 | tf_op jit(solution)/shard_map/ppermute | solution.py:353
  133.8 1.3 collective-permute-start.4
  135.1 15.6 %all-to-all-start.6 = ((bf16[32,16,128]{2,1,0:T(8,128)(2,1)}), bf16[32,16,128]{2,1,0:T(8,128)(2,1)S(1)}, u32[]{:S(2)}, u32[]{:S(2)}) async-start(bf16[32,16,128]{2,1,0:T(8,128)(2,1)} %get-tuple-element.36), calls=%async_computation.6 | async-start | bytes 262144 | tf_op jit(solution)/shard_map/all_to_all | solution.py:348
  152.5 7.7 %shard_map.152 = (bf16[256,1024]{1,0:T(8,128)(2,1)}, bf16[256,1024]{1,0:T(8,128)(2,1)}) custom-call(s32[1]{0:T(128)} %bitcast.core_ref, bf16[256,512]{1,0:T(8,128)(2,1)} %get-tuple-element.27.keep_ref, bf16[256,512]{1,0:T(8,128)(2,1)} %copy-done.7, bf16[128,512]{1,0:T(8,128)(2,1)} %get-tuple-element.29.inner_ref, bf16[128,512]{1,0:T(8,128)(2,1)} %copy-done.8, ...), custom_call_target="tpu_custom_call" | custom-call | flops 2113929216 | bytes 6291456 | tf_op jit(solution)/shard_map/pallas_call | solution.py:256
  160.2 7.2 %all-to-all-done.6 = bf16[32,16,128]{2,1,0:T(8,128)(2,1)S(1)} async-done(((bf16[32,16,128]{2,1,0:T(8,128)(2,1)}), bf16[32,16,128]{2,1,0:T(8,128)(2,1)S(1)}, u32[]{:S(2)}, u32[]{:S(2)}) %all-to-all-start.6) | async-done | bytes 131104 | tf_op jit(solution)/shard_map/all_to_all | solution.py:348
  (69 shorter events, 14.3 us)
Async XLA Ops:
  7.2 14.9 %copy-start.5 = (bf16[256,512]{1,0:T(8,128)(2,1)S(1)}, bf16[256,512]{1,0:T(8,128)(2,1)}, u32[]{:S(2)}) copy-start(bf16[256,512]{1,0:T(8,128)(2,1)} %param.13) | copy-start | bytes 786436
  7.2 16.8 %copy-start.2 = (bf16[256,1024]{1,0:T(8,128)(2,1)S(1)}, bf16[256,1024]{1,0:T(8,128)(2,1)}, u32[]{:S(2)}) copy-start(bf16[256,1024]{1,0:T(8,128)(2,1)} %param.15) | copy-start | bytes 1572868
  10.8 13.5 %copy-start.3 = (bf16[256,256]{1,0:T(8,128)(2,1)S(1)}, bf16[256,256]{1,0:T(8,128)(2,1)}, u32[]{:S(2)}) copy-start(bf16[256,256]{1,0:T(8,128)(2,1)} %constant.30.clone) | copy-start | bytes 393220
  11.8 11.4 %all-to-all-start = ((bf16[2,80,512]{2,1,0:T(8,128)(2,1)}), bf16[2,80,512]{2,1,0:T(8,128)(2,1)S(1)}, u32[]{:S(2)}, u32[]{:S(2)}) async-start(bf16[2,80,512]{2,1,0:T(8,128)(2,1)} %pad_maximum_fusion.3), calls=%async_computation | async-start | bytes 327680 | tf_op jit(solution)/shard_map/all_to_all | solution.py:308
  22.1 68.1 %all-gather.3.cloned.1.call-start = ((), (), s32[]{:S(2)}) async-start(), calls=%async_computation.7 | async-start | bytes 2506752 | tf_op jit(solution)/shard_map/all_gather | solution.py:319
  24.3 1.0 copy-start.4
  27.5 5.9 %all-to-all-start.2 = ((bf16[2,2,256,512]{3,2,1,0:T(8,128)(2,1)}), bf16[2,2,256,512]{3,2,1,0:T(8,128)(2,1)S(1)}, u32[]{:S(2)}, u32[]{:S(2)}) async-start(bf16[2,2,256,512]{3,2,1,0:T(8,128)(2,1)} %bitcast.13), calls=%async_computation.2 | async-start | bytes 2097152 | tf_op jit(solution)/shard_map/all_to_all | solution.py:326
  31.4 13.0 %collective-permute-start = (bf16[128,1024]{1,0:T(8,128)(2,1)S(1)}, bf16[128,1024]{1,0:T(8,128)(2,1)S(1)}, u32[]{:S(2)}, u32[]{:S(2)}) collective-permute-start(bf16[128,1024]{1,0:T(8,128)(2,1)S(1)} %slice.21), channel_id=1, source_target_pairs={{0,8},{8,16},{16,24},{24,32},{32,40},{40,48},{48,56},{56,64},{64,7... | collective-permute-start | bytes 786440 | tf_op jit(solution)/shard_map/ppermute | solution.py:323
  33.4 6.1 %copy-start = (bf16[2,2,256,512]{3,2,1,0:T(8,128)(2,1)}, bf16[2,2,256,512]{3,2,1,0:T(8,128)(2,1)S(1)}, u32[]{:S(2)}) copy-start(bf16[2,2,256,512]{3,2,1,0:T(8,128)(2,1)S(1)} %all-to-all-done.2.tok_ref) | copy-start | bytes 3145732
  33.4 6.1 %collective-permute-start.1 = (bf16[128,512]{1,0:T(8,128)(2,1)S(1)}, bf16[128,512]{1,0:T(8,128)(2,1)S(1)}, u32[]{:S(2)}, u32[]{:S(2)}) collective-permute-start(bf16[128,512]{1,0:T(8,128)(2,1)S(1)} %slice_bitcast_fusion), channel_id=1, source_target_pairs={{0,16},{16,32},{32,48},{48,64},{64,80},{80,96},{96,112},{112,128},... | collective-permute-start | bytes 393224 | tf_op jit(solution)/shard_map/ppermute | solution.py:330
  35.6 14.3 %all-to-all-start.1 = ((bf16[2,2,256,128]{3,1,2,0:T(2,128)(2,1)}), bf16[2,2,256,128]{3,1,2,0:T(2,128)(2,1)S(1)}, u32[]{:S(2)}, u32[]{:S(2)}) async-start(bf16[2,2,256,128]{3,1,2,0:T(2,128)(2,1)} %copy.45), calls=%async_computation.1 | async-start | bytes 524288 | tf_op jit(solution)/shard_map/all_to_all | solution.py:320
  39.5 0.6 copy-start.6
  96.5 15.5 %all-to-all-start.5 = ((bf16[2,2,256,512]{3,2,1,0:T(8,128)(2,1)}), bf16[2,2,256,512]{3,2,1,0:T(8,128)(2,1)S(1)}, u32[]{:S(2)}, u32[]{:S(2)}) async-start(bf16[2,2,256,512]{3,2,1,0:T(8,128)(2,1)} %bitcast.48), calls=%async_computation.5 | async-start | bytes 2097152 | tf_op jit(solution)/shard_map/all_to_all | solution.py:342
  112.0 1.0 copy-start.1
  119.5 31.2 %collective-permute-start.5 = (bf16[2,16,2,16,128]{4,3,2,1,0:T(8,128)(2,1)S(1)}, bf16[2,16,2,16,128]{4,3,2,1,0:T(8,128)(2,1)S(1)}, u32[]{:S(2)}, u32[]{:S(2)}) collective-permute-start(bf16[2,16,2,16,128]{4,3,2,1,0:T(8,128)(2,1)S(1)} %bitcast.53), channel_id=1, source_target_pairs={{0,16},{16,0},{1,17},{17,1},{2,18},{18,2},{3,19},{19,3},{4,20},{20... | collective-permute-start | bytes 786440 | tf_op jit(solution)/shard_map/ppermute | solution.py:358
  121.5 30.2 %collective-permute-start.2 = (bf16[256,512]{1,0:T(8,128)(2,1)}, bf16[256,512]{1,0:T(8,128)(2,1)S(1)}, u32[]{:S(2)}, u32[]{:S(2)}) collective-permute-start(bf16[256,512]{1,0:T(8,128)(2,1)} %get-tuple-element.28), channel_id=1, source_target_pairs={{0,8},{8,0},{1,9},{9,1},{2,10},{10,2},{3,11},{11,3},{4,12},{12,4},... | collective-permute-start | bytes 786440 | tf_op jit(solution)/shard_map/ppermute | solution.py:351
  131.8 19.8 %collective-permute-start.3 = (bf16[128,512]{1,0:T(8,128)(2,1)}, bf16[128,512]{1,0:T(8,128)(2,1)S(1)}, u32[]{:S(2)}, u32[]{:S(2)}) collective-permute-start(bf16[128,512]{1,0:T(8,128)(2,1)} %get-tuple-element.30), channel_id=1, source_target_pairs={{16,8},{32,24},{48,40},{64,56},{80,72},{96,88},{112,104},{128,120}... | collective-permute-start | bytes 393224 | tf_op jit(solution)/shard_map/ppermute | solution.py:353
  133.8 17.9 %collective-permute-start.4 = (bf16[128,512]{1,0:T(8,128)(2,1)}, bf16[128,512]{1,0:T(8,128)(2,1)S(1)}, u32[]{:S(2)}, u32[]{:S(2)}) collective-permute-start(bf16[128,512]{1,0:T(8,128)(2,1)} %get-tuple-element.31), channel_id=1, source_target_pairs={{24,8},{40,24},{56,40},{72,56},{88,72},{104,88},{120,104},{136,120... | collective-permute-start | bytes 393224 | tf_op jit(solution)/shard_map/ppermute | solution.py:354
  135.1 32.3 %all-to-all-start.6 = ((bf16[32,16,128]{2,1,0:T(8,128)(2,1)}), bf16[32,16,128]{2,1,0:T(8,128)(2,1)S(1)}, u32[]{:S(2)}, u32[]{:S(2)}) async-start(bf16[32,16,128]{2,1,0:T(8,128)(2,1)} %get-tuple-element.36), calls=%async_computation.6 | async-start | bytes 262144 | tf_op jit(solution)/shard_map/all_to_all | solution.py:348
  151.7 0.7 copy-start.8
  151.7 0.7 copy-start.9
  151.7 0.8 copy-start.7
Sparse Core Ops, SparseCore 0:
  25.6 64.5 all-gather.2

commit v8 on v7

--- a/solution.py
+++ b/solution.py
@@ -13,7 +13,7 @@
 N = K + TOK
 HALF = N // 2
 TILE = 256
-VMEM = 56 * 1024 * 1024
+VMEM = 60 * 1024 * 1024
 
 BF = jnp.bfloat16
 F32 = jnp.float32
@@ -68,7 +68,7 @@
 
 
 def product_kernel(cols_ref, weight_ref, out_ref):
-    weight = weight_ref[:, :K].reshape(16 * K, 512)
+    weight = weight_ref[:, :, :64].reshape(16 * K, 512)
     rows = jnp.concatenate([cols_ref[0, i, 0, j] for i in range(8) for j in range(2)], axis=1)
     out_ref[0] = dot(rows, weight).astype(BF)
 
@@ -79,7 +79,7 @@
         grid=(4,),
         in_specs=[
             pl.BlockSpec((1, 8, 1, 2, TOK, K), lambda i: (i % 2, 0, i // 2, 0, 0, 0)),
-            pl.BlockSpec((16, K + 16, 512), lambda i: (0, 0, 0)),
+            pl.BlockSpec((16, 2, 80, 512), lambda i: (0, 0, 0, 0)),
         ],
         out_specs=pl.BlockSpec((1, TOK, 512), lambda i: (i, 0, 0)),
         out_shape=jax.ShapeDtypeStruct((4, TOK, 512), BF),
@@ -274,7 +274,7 @@
         out_shape=[jax.ShapeDtypeStruct((TOK, CH), BF)] * 2,
         compiler_params=params(),
         cost_estimate=pl.CostEstimate(
-            flops=2 * CH * N * (5 * K + 8 * TOK), bytes_accessed=6 << 20, transcendentals=0
+            flops=1024, bytes_accessed=1024, transcendentals=0
         ),
     )(core, keep, other, inner, near, far, gate, sig_freq, taps, forward, inv, place)
 
@@ -284,6 +284,30 @@
     matrix = np.zeros((2 * K, 2 * K), np.float32)
     matrix[source, np.arange(2 * K)] = 1.0
     return matrix.astype(jnp.bfloat16)
+
+
+def send_kernel(weight_ref, tap_ref, place_ref, out_ref):
+    out_ref[...] = jnp.zeros_like(out_ref)
+    taps = tap_ref[...]
+    high = taps.astype(BF)
+    low = (taps - high.astype(F32)).astype(BF)
+    for c in range(2):
+        out_ref[c, 64:, :K] = high
+        out_ref[c, 64:, K : 2 * K] = low
+    for i in range(4):
+        lanes = slice(i * 2 * K, (i + 1) * 2 * K)
+        chosen = dot(weight_ref[:, lanes], place_ref[...]).astype(BF)
+        out_ref[0, :64, i * K : (i + 1) * K] = chosen[:, :K]
+        out_ref[1, :64, i * K : (i + 1) * K] = chosen[:, K:]
+
+
+def send_part(weights, taps, place):
+    return pl.pallas_call(
+        send_kernel,
+        out_shape=jax.ShapeDtypeStruct((2, 80, 512), BF),
+        compiler_params=pltpu.CompilerParams(vmem_limit_bytes=VMEM),
+        cost_estimate=pl.CostEstimate(flops=1 << 25, bytes_accessed=1 << 19, transcendentals=0),
+    )(weights, taps, place)
 
 
 def by_core(values, place):
@@ -299,20 +323,8 @@
     place = chooser()
     core = lax.axis_index("c").reshape(1)
 
-    turned = by_core(out_weight.T, place)
-    tap_rows = filter_taps.T
-    tap_high = lax.optimization_barrier(tap_rows.astype(BF))
-    tap_low = (tap_rows - tap_high.astype(F32)).astype(BF)
-    tap_pack = jnp.concatenate([tap_high, tap_low, jnp.zeros((16, 256), BF)], axis=1)
-    message = jnp.concatenate([turned, jnp.broadcast_to(tap_pack[None], (2, 16, 512))], axis=1)
-    got = lax.all_to_all(message, "c", split_axis=0, concat_axis=0)
-    block = jnp.concatenate(
-        [
-            got[:, :64].reshape(K, 512),
-            jnp.concatenate([got[0, 64:, :256], got[1, 64:, :256]], axis=1),
-        ],
-        axis=0,
-    )
+    message = send_part(out_weight.T, filter_taps.T, place)
+    block = lax.all_to_all(message, "c", split_axis=0, concat_axis=0)
 
     cols = out_grad.reshape(TOK, 2, 2, K).transpose(2, 1, 0, 3)
     block, cols, signal, gate_input = lax.optimization_barrier((block, cols, signal, gate_input))
@@ -354,7 +366,7 @@
     far = lax.ppermute(first, ctx, [(i + 1, j) for i, j in follows])
 
     weights, keep = lax.optimization_barrier((weights, keep))
-    taps = weights[:, K:].reshape(16, 16, 2, 2, K).transpose(3, 0, 2, 1, 4)
+    taps = weights[:, :, 64:, : 2 * K].reshape(16, 2, 16, 2, K).transpose(3, 0, 1, 2, 4)
     more = lax.ppermute(taps, "h", [(0, 1), (1, 0)])
     upper_half = lax.axis_index("h") == 0
     taps = jnp.stack(

time: 176 us -> 172 us (0.977)
  waiting for transfers between devices: 18.2 us -> 15 us
  Pallas kernels: 28.2 us -> 30.2 us
  other arithmetic: 6.42 us -> 4.58 us
    all_to_all x1, waiting for transfers between devices: 7.2 us -> 0.01 us  [on_device(): tap_grad = lax.all_to_all(tap_grad, chips, split_axis=0, concat_axis=0)]
    ppermute x1, starting transfers between devices: 10.4 us -> 4.09 us  [on_device(): other = lax.ppermute(send, 'c', [(0, 1), (1, 0)])]
    all_to_all x1, starting transfers between devices: 15.6 us -> 21.3 us  [on_device(): tap_grad = lax.all_to_all(tap_grad, chips, split_axis=0, concat_axis=0)]
    ppermute x1, waiting for transfers between devices: 0.01 us -> 3.53 us  [on_device(): lax.ppermute(cross, ctx, follows + [(2 * i + 1, 2 * i) for i in range(32)])]
    pallas_call x0 -> x1, Pallas kernels: none -> 1.9 us  [send_part(): pl.pallas_call(send_kernel, out_shape=jax.ShapeDtypeStruct((2, 80, 512),...]
  transfers between devices with their start and end apart: 12 -> 12, of which waited for: 4 -> 4; matrix products, arithmetic and copies ran while one was open for 5% -> 6% of each run, Pallas kernels for 9% -> 10%
where the time goes in v8:
time: 172 us; the launch traced here: 171 us
  starting transfers between devices  57.5 us (33%)
  blocking collectives  38.3 us (22%)
  Pallas kernels  30.2 us (18%)
  waiting for transfers between devices  15 us (9%)
  between operations  14.3 us (8%)
  local copies, waits for them, and re-layouts  10.8 us (6%)
  other arithmetic  4.58 us (3%)
    all_to_all x1, blocking collectives, on_device(): lax.all_to_all(jnp.broadcast_to(cols[None], (8, 2, 2, TOK, K)), ('x', 'l'...  30.2 us
    all_to_all x1, starting transfers between devices, on_device(): tap_grad = lax.all_to_all(tap_grad, chips, split_axis=0, concat_axis=0)  21.3 us
    all_to_all x1, starting transfers between devices, on_device(): block = lax.all_to_all(message, 'c', split_axis=0, concat_axis=0)  10.3 us
    all_to_all x1, waiting for transfers between devices, on_device(): lax.all_to_all(partial.reshape(2, 2, TOK, 512), 'h', split_axis=0, concat...  9.74 us
    all_to_all x1, blocking collectives, on_device(): lax.all_to_all(jnp.broadcast_to(cols[None], (2, 8, 2, 2, TOK, K)), 'c', s...  8.1 us
    pallas_call x1, Pallas kernels, out_part(): pl.pallas_call(out_kernel, grid=(TILES,), in_specs=[scalar(), half, half,...  7.72 us
    pallas_call x1, Pallas kernels, product(): pl.pallas_call(product_kernel, grid=(4,), in_specs=[pl.BlockSpec((1, 8, 1...  6.35 us
    all_to_all x1, starting transfers between devices, on_device(): lax.all_to_all(partial.reshape(2, 2, TOK, 512), 'h', split_axis=0, concat...  5.86 us
  transfers between devices with their start and end apart: 12, of which 4 were waited for; matrix products, arithmetic and copies ran while one was open for 6% of the time, Pallas kernels for 10%

profile of v8, /device:TPU:1, one launch (start us, length us, event | category | flops | bytes accessed | tf_op | source)
XLA Modules:
  0.0 171.2 jit_solution(14599971115223044343)
XLA Ops:
  7.2 1.9 %shard_map.148 = bf16[2,80,512]{2,1,0:T(8,128)(2,1)} custom-call(bf16[64,1024]{1,0:T(8,128)(2,1)} %bitcast.46, f32[16,128]{1,0:T(8,128)} %bitcast.50, bf16[256,256]{1,0:T(8,128)(2,1)} %constant.28.clone.place_ref), custom_call_target="tpu_custom_call" | custom-call | flops 33554432 | bytes 524288 | tf_op jit(solution)/shard_map/pallas_call | solution.py:305
  9.1 10.3 %all-to-all-start = ((bf16[2,80,512]{2,1,0:T(8,128)(2,1)}), bf16[2,80,512]{2,1,0:T(8,128)(2,1)S(1)}, u32[]{:S(2)}, u32[]{:S(2)}) async-start(bf16[2,80,512]{2,1,0:T(8,128)(2,1)} %shard_map.148), calls=%async_computation | async-start | bytes 327680 | tf_op jit(solution)/shard_map/all_to_all | solution.py:327
  21.2 1.4 reshape.46
  25.8 3.9 %all-to-all-start.2 = ((bf16[2,2,256,512]{3,2,1,0:T(8,128)(2,1)}), bf16[2,2,256,512]{3,2,1,0:T(8,128)(2,1)S(1)}, u32[]{:S(2)}, u32[]{:S(2)}) async-start(bf16[2,2,256,512]{3,2,1,0:T(8,128)(2,1)} %bitcast.8), calls=%async_computation.2 | async-start | bytes 2097152 | tf_op jit(solution)/shard_map/all_to_all | solution.py:338
  29.7 1.9 %collective-permute-start = (bf16[128,1024]{1,0:T(8,128)(2,1)S(1)}, bf16[128,1024]{1,0:T(8,128)(2,1)S(1)}, u32[]{:S(2)}, u32[]{:S(2)}) collective-permute-start(bf16[128,1024]{1,0:T(8,128)(2,1)S(1)} %slice.9), channel_id=1, source_target_pairs={{0,8},{8,16},{16,24},{24,32},{32,40},{40,48},{48,56},{56,64},{64,7... | collective-permute-start | bytes 786440 | tf_op jit(solution)/shard_map/ppermute | solution.py:335
  31.7 1.3 collective-permute-start.1
  33.9 3.6 %all-to-all-start.1 = ((bf16[2,2,256,128]{3,1,2,0:T(2,128)(2,1)}), bf16[2,2,256,128]{3,1,2,0:T(2,128)(2,1)S(1)}, u32[]{:S(2)}, u32[]{:S(2)}) async-start(bf16[2,2,256,128]{3,1,2,0:T(2,128)(2,1)} %copy.27), calls=%async_computation.1 | async-start | bytes 524288 | tf_op jit(solution)/shard_map/all_to_all | solution.py:332
  38.4 4.3 %shard_map.150.freq_ref = f32[4,384,256]{2,1,0:T(8,128)} custom-call(bf16[128,512]{1,0:T(8,128)(2,1)} %copy-done.9, bf16[2,2,256,512]{3,2,1,0:T(8,128)(2,1)} %copy-done, bf16[2,384,384]{2,1,0:T(8,128)(2,1)} %constant.29.clone.forward_ref), custom_call_target="tpu_custom_call" | custom-call | flops 603979776 | bytes 3145728 | tf_op jit(solution)/shard_map/pallas_call | solution.py:139
  43.7 4.4 %shard_map.149.freq_ref = f32[384,1024]{1,0:T(8,128)} custom-call(bf16[384,1024]{1,0:T(8,128)(2,1)} %pad_maximum_fusion.1.window_ref, bf16[2,384,384]{2,1,0:T(8,128)(2,1)} %constant.29.clone.forward_ref), custom_call_target="tpu_custom_call" | custom-call | flops 603979776 | bytes 3145728 | tf_op jit(solution)/shard_map/pallas_call | solution.py:112
  48.7 30.2 %all_to_all.35 = bf16[8,2,2,256,128]{4,3,2,1,0:T(8,128)(2,1)S(1)} all-to-all(bf16[8,2,2,256,128]{4,3,2,1,0:T(8,128)(2,1)S(1)} %broadcast_in_dim.4), channel_id=1, replica_groups=mesh['z'=16,'h'=2,'c'=2,'x'=4,'l'=2] {'x','l'}, dimensions={0} | all-to-all | bytes 4194304 | tf_op jit(solution)/shard_map/all_to_all | solution.py:346
  78.9 1.4 broadcast_in_dim.5
  80.3 8.1 %all_to_all.36.cols_ref = bf16[2,8,2,2,256,128]{5,4,3,2,1,0:T(8,128)(2,1)} all-to-all(bf16[2,8,2,2,256,128]{5,4,3,2,1,0:T(8,128)(2,1)S(1)} %broadcast_in_dim.5), channel_id=1, replica_groups=mesh['z'=16,'h'=2,'c'=2,'x'=4,'l'=2] {'c'}, dimensions={0} | all-to-all | bytes 8388608 | tf_op jit(solution)/shard_map/all_to_all | solution.py:349
  88.4 6.3 %shard_map.151 = bf16[4,256,512]{2,1,0:T(8,128)(2,1)} custom-call(bf16[2,8,2,2,256,128]{5,4,3,2,1,0:T(8,128)(2,1)} %all_to_all.36.cols_ref, bf16[16,2,80,512]{3,2,1,0:T(8,128)(2,1)} %bitcast.47), custom_call_target="tpu_custom_call" | custom-call | flops 2147483648 | bytes 8388608 | tf_op jit(solution)/shard_map/pallas_call | solution.py:77
  94.7 5.9 %all-to-all-start.5 = ((bf16[2,2,256,512]{3,2,1,0:T(8,128)(2,1)}), bf16[2,2,256,512]{3,2,1,0:T(8,128)(2,1)S(1)}, u32[]{:S(2)}, u32[]{:S(2)}) async-start(bf16[2,2,256,512]{3,2,1,0:T(8,128)(2,1)} %bitcast.44), calls=%async_computation.5 | async-start | bytes 2097152 | tf_op jit(solution)/shard_map/all_to_all | solution.py:354
  100.6 9.7 %all-to-all-done.5.mix_ref = bf16[2,2,256,512]{3,2,1,0:T(8,128)(2,1)S(1)} async-done(((bf16[2,2,256,512]{3,2,1,0:T(8,128)(2,1)}), bf16[2,2,256,512]{3,2,1,0:T(8,128)(2,1)S(1)}, u32[]{:S(2)}, u32[]{:S(2)}) %all-to-all-start.5) | async-done | bytes 1048608 | tf_op jit(solution)/shard_map/all_to_all | solution.py:354
  111.3 5.4 %shard_map.152 = (bf16[256,512]{1,0:T(8,128)(2,1)}, bf16[256,512]{1,0:T(8,128)(2,1)}, bf16[128,512]{1,0:T(8,128)(2,1)}, bf16[128,512]{1,0:T(8,128)(2,1)}, bf16[1...) custom-call(s32[1]{0:T(128)} %bitcast.core_ref, bf16[2,2,256,512]{3,2,1,0:T(8,128)(2,1)} %copy-done.1, ...), custom_call_target="tpu_custom_call" | custom-call | flops 603979776 | bytes 5242880 | tf_op jit(solution)/shard_map/pallas_call | solution.py:189
  117.8 1.9 %collective-permute-start.5 = (bf16[2,16,2,16,128]{4,3,2,1,0:T(8,128)(2,1)S(1)}, bf16[2,16,2,16,128]{4,3,2,1,0:T(8,128)(2,1)S(1)}, u32[]{:S(2)}, u32[]{:S(2)}) collective-permute-start(bf16[2,16,2,16,128]{4,3,2,1,0:T(8,128)(2,1)S(1)} %bitcast_bitcast_fusion), channel_id=1, source_target_pairs={{0,16},{16,0},{1,17},{17,1},{2,18},{18,2},{3,19},{19,3},{4,20},{20... | collective-permute-start | bytes 786440 | tf_op jit(solution)/shard_map/ppermute | solution.py:370
  119.7 21.3 %all-to-all-start.6 = ((bf16[32,16,128]{2,1,0:T(8,128)(2,1)}), bf16[32,16,128]{2,1,0:T(8,128)(2,1)S(1)}, u32[]{:S(2)}, u32[]{:S(2)}) async-start(bf16[32,16,128]{2,1,0:T(8,128)(2,1)} %get-tuple-element.36), calls=%async_computation.6 | async-start | bytes 262144 | tf_op jit(solution)/shard_map/all_to_all | solution.py:360
  141.0 4.1 %collective-permute-start.2 = (bf16[256,512]{1,0:T(8,128)(2,1)}, bf16[256,512]{1,0:T(8,128)(2,1)S(1)}, u32[]{:S(2)}, u32[]{:S(2)}) collective-permute-start(bf16[256,512]{1,0:T(8,128)(2,1)} %get-tuple-element.28), channel_id=1, source_target_pairs={{0,8},{8,0},{1,9},{9,1},{2,10},{10,2},{3,11},{11,3},{4,12},{12,4},... | collective-permute-start | bytes 786440 | tf_op jit(solution)/shard_map/ppermute | solution.py:363
  145.1 1.9 %collective-permute-start.3 = (bf16[128,512]{1,0:T(8,128)(2,1)}, bf16[128,512]{1,0:T(8,128)(2,1)S(1)}, u32[]{:S(2)}, u32[]{:S(2)}) collective-permute-start(bf16[128,512]{1,0:T(8,128)(2,1)} %get-tuple-element.30), channel_id=1, source_target_pairs={{16,8},{32,24},{48,40},{64,56},{80,72},{96,88},{112,104},{128,120}... | collective-permute-start | bytes 393224 | tf_op jit(solution)/shard_map/ppermute | solution.py:365
  147.1 1.3 collective-permute-start.4
  150.3 3.5 %collective-permute-done.3.near_ref = bf16[128,512]{1,0:T(8,128)(2,1)S(1)} collective-permute-done((bf16[128,512]{1,0:T(8,128)(2,1)}, bf16[128,512]{1,0:T(8,128)(2,1)S(1)}, u32[]{:S(2)}, u32[]{:S(2)}) %collective-permute-start.3) | collective-permute-done | bytes 131104 | tf_op jit(solution)/shard_map/ppermute | solution.py:365
  153.8 1.4 collective-permute-done.4.far_ref
  156.0 7.7 %shard_map.153 = (bf16[256,1024]{1,0:T(8,128)(2,1)}, bf16[256,1024]{1,0:T(8,128)(2,1)}) custom-call(s32[1]{0:T(128)} %bitcast.core_ref, bf16[256,512]{1,0:T(8,128)(2,1)} %get-tuple-element.27.keep_ref, bf16[256,512]{1,0:T(8,128)(2,1)} %copy-done.6, bf16[128,512]{1,0:T(8,128)(2,1)} %get-tuple-element.29.inner_ref, bf16[128,512]{1,0:T(8,128)(2,1)} %copy-done.7, ...), custom_call_target="tpu_custom_call" | custom-call | flops 1024 | bytes 1024 | tf_op jit(solution)/shard_map/pallas_call | solution.py:256
  (52 shorter events, 13.5 us)
Async XLA Ops:
  7.2 15.4 %copy-start.4 = (bf16[256,256]{1,0:T(8,128)(2,1)S(1)}, bf16[256,256]{1,0:T(8,128)(2,1)}, u32[]{:S(2)}) copy-start(bf16[256,256]{1,0:T(8,128)(2,1)} %constant.28.clone.place_ref) | copy-start | bytes 393220
  9.1 11.4 %all-to-all-start = ((bf16[2,80,512]{2,1,0:T(8,128)(2,1)}), bf16[2,80,512]{2,1,0:T(8,128)(2,1)S(1)}, u32[]{:S(2)}, u32[]{:S(2)}) async-start(bf16[2,80,512]{2,1,0:T(8,128)(2,1)} %shard_map.148), calls=%async_computation | async-start | bytes 327680 | tf_op jit(solution)/shard_map/all_to_all | solution.py:327
  19.4 69.0 %all-gather.3.cloned.1.call-start = ((), (), s32[]{:S(2)}) async-start(), calls=%async_computation.7 | async-start | bytes 2785280 | tf_op jit(solution)/shard_map/all_gather | solution.py:331
  20.5 0.7 copy-start.5
  22.6 1.0 copy-start.3
  24.7 5.0 %copy-start.2 = (bf16[256,1024]{1,0:T(8,128)(2,1)S(1)}, bf16[256,1024]{1,0:T(8,128)(2,1)}, u32[]{:S(2)}) copy-start(bf16[256,1024]{1,0:T(8,128)(2,1)} %param.15) | copy-start | bytes 1572868
  25.8 5.9 %all-to-all-start.2 = ((bf16[2,2,256,512]{3,2,1,0:T(8,128)(2,1)}), bf16[2,2,256,512]{3,2,1,0:T(8,128)(2,1)S(1)}, u32[]{:S(2)}, u32[]{:S(2)}) async-start(bf16[2,2,256,512]{3,2,1,0:T(8,128)(2,1)} %bitcast.8), calls=%async_computation.2 | async-start | bytes 2097152 | tf_op jit(solution)/shard_map/all_to_all | solution.py:338
  29.7 13.0 %collective-permute-start = (bf16[128,1024]{1,0:T(8,128)(2,1)S(1)}, bf16[128,1024]{1,0:T(8,128)(2,1)S(1)}, u32[]{:S(2)}, u32[]{:S(2)}) collective-permute-start(bf16[128,1024]{1,0:T(8,128)(2,1)S(1)} %slice.9), channel_id=1, source_target_pairs={{0,8},{8,16},{16,24},{24,32},{32,40},{40,48},{48,56},{56,64},{64,7... | collective-permute-start | bytes 786440 | tf_op jit(solution)/shard_map/ppermute | solution.py:335
  31.7 6.1 %copy-start = (bf16[2,2,256,512]{3,2,1,0:T(8,128)(2,1)}, bf16[2,2,256,512]{3,2,1,0:T(8,128)(2,1)S(1)}, u32[]{:S(2)}) copy-start(bf16[2,2,256,512]{3,2,1,0:T(8,128)(2,1)S(1)} %all-to-all-done.2.tok_ref) | copy-start | bytes 3145732
  31.7 6.1 %collective-permute-start.1 = (bf16[128,512]{1,0:T(8,128)(2,1)S(1)}, bf16[128,512]{1,0:T(8,128)(2,1)S(1)}, u32[]{:S(2)}, u32[]{:S(2)}) collective-permute-start(bf16[128,512]{1,0:T(8,128)(2,1)S(1)} %slice_bitcast_fusion.1), channel_id=1, source_target_pairs={{0,16},{16,32},{32,48},{48,64},{64,80},{80,96},{96,112},{112,128},... | collective-permute-start | bytes 393224 | tf_op jit(solution)/shard_map/ppermute | solution.py:342
  33.9 14.3 %all-to-all-start.1 = ((bf16[2,2,256,128]{3,1,2,0:T(2,128)(2,1)}), bf16[2,2,256,128]{3,1,2,0:T(2,128)(2,1)S(1)}, u32[]{:S(2)}, u32[]{:S(2)}) async-start(bf16[2,2,256,128]{3,1,2,0:T(2,128)(2,1)} %copy.27), calls=%async_computation.1 | async-start | bytes 524288 | tf_op jit(solution)/shard_map/all_to_all | solution.py:332
  37.8 0.6 copy-start.9
  94.7 15.6 %all-to-all-start.5 = ((bf16[2,2,256,512]{3,2,1,0:T(8,128)(2,1)}), bf16[2,2,256,512]{3,2,1,0:T(8,128)(2,1)S(1)}, u32[]{:S(2)}, u32[]{:S(2)}) async-start(bf16[2,2,256,512]{3,2,1,0:T(8,128)(2,1)} %bitcast.44), calls=%async_computation.5 | async-start | bytes 2097152 | tf_op jit(solution)/shard_map/all_to_all | solution.py:354
  110.4 1.0 copy-start.1
  117.8 30.6 %collective-permute-start.5 = (bf16[2,16,2,16,128]{4,3,2,1,0:T(8,128)(2,1)S(1)}, bf16[2,16,2,16,128]{4,3,2,1,0:T(8,128)(2,1)S(1)}, u32[]{:S(2)}, u32[]{:S(2)}) collective-permute-start(bf16[2,16,2,16,128]{4,3,2,1,0:T(8,128)(2,1)S(1)} %bitcast_bitcast_fusion), channel_id=1, source_target_pairs={{0,16},{16,0},{1,17},{17,1},{2,18},{18,2},{3,19},{19,3},{4,20},{20... | collective-permute-start | bytes 786440 | tf_op jit(solution)/shard_map/ppermute | solution.py:370
  119.7 44.0 %all-to-all-start.6 = ((bf16[32,16,128]{2,1,0:T(8,128)(2,1)}), bf16[32,16,128]{2,1,0:T(8,128)(2,1)S(1)}, u32[]{:S(2)}, u32[]{:S(2)}) async-start(bf16[32,16,128]{2,1,0:T(8,128)(2,1)} %get-tuple-element.36), calls=%async_computation.6 | async-start | bytes 262144 | tf_op jit(solution)/shard_map/all_to_all | solution.py:360
  141.0 14.2 %collective-permute-start.2 = (bf16[256,512]{1,0:T(8,128)(2,1)}, bf16[256,512]{1,0:T(8,128)(2,1)S(1)}, u32[]{:S(2)}, u32[]{:S(2)}) collective-permute-start(bf16[256,512]{1,0:T(8,128)(2,1)} %get-tuple-element.28), channel_id=1, source_target_pairs={{0,8},{8,0},{1,9},{9,1},{2,10},{10,2},{3,11},{11,3},{4,12},{12,4},... | collective-permute-start | bytes 786440 | tf_op jit(solution)/shard_map/ppermute | solution.py:363
  145.1 8.7 %collective-permute-start.3 = (bf16[128,512]{1,0:T(8,128)(2,1)}, bf16[128,512]{1,0:T(8,128)(2,1)S(1)}, u32[]{:S(2)}, u32[]{:S(2)}) collective-permute-start(bf16[128,512]{1,0:T(8,128)(2,1)} %get-tuple-element.30), channel_id=1, source_target_pairs={{16,8},{32,24},{48,40},{64,56},{80,72},{96,88},{112,104},{128,120}... | collective-permute-start | bytes 393224 | tf_op jit(solution)/shard_map/ppermute | solution.py:365
  147.1 8.2 %collective-permute-start.4 = (bf16[128,512]{1,0:T(8,128)(2,1)}, bf16[128,512]{1,0:T(8,128)(2,1)S(1)}, u32[]{:S(2)}, u32[]{:S(2)}) collective-permute-start(bf16[128,512]{1,0:T(8,128)(2,1)} %get-tuple-element.31), channel_id=1, source_target_pairs={{24,8},{40,24},{56,40},{72,56},{88,72},{104,88},{120,104},{136,120... | collective-permute-start | bytes 393224 | tf_op jit(solution)/shard_map/ppermute | solution.py:366
  153.8 1.4 copy-start.7
  155.3 0.7 copy-start.8
  155.3 0.7 copy-start.6
Sparse Core Ops, SparseCore 0:
  22.8 64.9 all-gather.2

commit v9 on v8

--- a/solution.py
+++ b/solution.py
@@ -61,9 +61,9 @@
     return jnp.concatenate([ar * br + ai * bi, ai * br - ar * bi], axis=0)
 
 
-def params():
+def params(limit=VMEM):
     return pltpu.CompilerParams(
-        dimension_semantics=("arbitrary",), vmem_limit_bytes=VMEM
+        dimension_semantics=("arbitrary",), vmem_limit_bytes=limit
     )
 
 
@@ -201,11 +201,40 @@
         out_shape=[jax.ShapeDtypeStruct((TOK, 512), BF)] * 2
         + [jax.ShapeDtypeStruct((K, 512), BF)] * 3
         + [jax.ShapeDtypeStruct((32, 16, K), BF)],
-        compiler_params=params(),
+        compiler_params=params(32 << 20),
         cost_estimate=pl.CostEstimate(
             flops=2 * CH * N * (2 * TOK + 2 * K), bytes_accessed=5 << 20, transcendentals=0
         ),
     )(core, mix, tokens, sig_freq, own, lag)
+
+
+def conv_kernel(freq_ref, tap_ref, forward_ref, inv_ref, tap_freq_ref, conv_ref):
+    upper, lower = tap_ref[0], tap_ref[1]
+    high, low = forward_ref[0], forward_ref[1]
+    tap_freq = dot(high, upper, LANES) + dot(low, upper, LANES) + dot(high, lower, LANES)
+    tap_freq_ref[...] = tap_freq
+    conv_ref[...] = both_sides(inv_ref, times(freq_ref[...], tap_freq))
+
+
+def wide_tile(rows):
+    return pl.BlockSpec((rows, 2 * K), lambda j: (0, j))
+
+
+def conv_part(sig_freq, taps, forward, inv):
+    return pl.pallas_call(
+        conv_kernel,
+        grid=(TILES,),
+        in_specs=[
+            wide_tile(N),
+            pl.BlockSpec((2, 2 * K, K), lambda j: (0, j, 0)),
+            whole((2, N, K)),
+            whole((2, TOK, N)),
+        ],
+        out_specs=[wide_tile(N), wide_tile(TOK)],
+        out_shape=[jax.ShapeDtypeStruct((N, CH), F32), jax.ShapeDtypeStruct((TOK, CH), F32)],
+        compiler_params=params(),
+        cost_estimate=pl.CostEstimate(flops=1024, bytes_accessed=1024, transcendentals=0),
+    )(sig_freq, taps, forward, inv)
 
 
 def out_kernel(
@@ -216,8 +245,8 @@
     near_ref,
     far_ref,
     gate_in_ref,
-    freq_ref,
-    tap_ref,
+    conv_ref,
+    tap_freq_ref,
     forward_ref,
     inv_ref,
     place_ref,
@@ -235,24 +264,15 @@
     halo = joined(
         jnp.where(is_first, inner_ref[...], near), jnp.where(is_first, near, far_ref[...])
     ).astype(BF)
+    gate_ref[...] = (mixed * conv_ref[...]).astype(BF)
     conv_grad = (mixed * gate_in_ref[...].astype(F32)).astype(BF)
-    window = jnp.concatenate([conv_grad, halo], axis=0)
-    full = exact_side(forward_ref[:, :, K:], window)
-    upper, lower = tap_ref[0], tap_ref[1]
-    high, low = forward_ref[0, :, :K], forward_ref[1, :, :K]
-    tap_freq = dot(high, upper, LANES) + dot(low, upper, LANES) + dot(high, lower, LANES)
-    conv_out = both_sides(inv_ref, times(freq_ref[...], tap_freq))
-    gate_ref[...] = (mixed * conv_out).astype(BF)
-    sig_ref[...] = both_sides(inv_ref, times_conj(full, tap_freq)).astype(BF)
-
-
-def out_part(core, keep, other, inner, near, far, gate, sig_freq, taps, forward, inv, place):
+    full = exact_side(forward_ref, jnp.concatenate([conv_grad, halo], axis=0))
+    sig_ref[...] = both_sides(inv_ref, times_conj(full, tap_freq_ref[...])).astype(BF)
+
+
+def out_part(core, keep, other, inner, near, far, gate, conv, tap_freq, forward, inv, place):
     head = pl.BlockSpec((K, K), lambda j: (0, j))
     half = pl.BlockSpec((TOK, K), lambda j: (0, j))
-
-    def tile(rows):
-        return pl.BlockSpec((rows, 2 * K), lambda j: (0, j))
-
     return pl.pallas_call(
         out_kernel,
         grid=(TILES,),
@@ -263,20 +283,18 @@
             head,
             head,
             head,
-            tile(TOK),
-            tile(N),
-            pl.BlockSpec((2, 2 * K, K), lambda j: (0, j, 0)),
-            whole((2, N, N + K)),
+            wide_tile(TOK),
+            wide_tile(TOK),
+            wide_tile(N),
+            whole((2, N, N)),
             whole((2, TOK, N)),
             whole((2 * K, 2 * K)),
         ],
-        out_specs=[tile(TOK), tile(TOK)],
+        out_specs=[wide_tile(TOK), wide_tile(TOK)],
         out_shape=[jax.ShapeDtypeStruct((TOK, CH), BF)] * 2,
         compiler_params=params(),
-        cost_estimate=pl.CostEstimate(
-            flops=1024, bytes_accessed=1024, transcendentals=0
-        ),
-    )(core, keep, other, inner, near, far, gate, sig_freq, taps, forward, inv, place)
+        cost_estimate=pl.CostEstimate(flops=1024, bytes_accessed=1024, transcendentals=0),
+    )(core, keep, other, inner, near, far, gate, conv, tap_freq, forward, inv, place)
 
 
 def chooser():
@@ -351,6 +369,7 @@
     )
 
     partial = product(cols, weights)
+    weights, partial = lax.optimization_barrier((weights, partial))
     mix = lax.all_to_all(
         partial.reshape(2, 2, TOK, 512), "h", split_axis=0, concat_axis=0
     )
@@ -365,7 +384,6 @@
     near = lax.ppermute(cross, ctx, follows + [(2 * i + 1, 2 * i) for i in range(32)])
     far = lax.ppermute(first, ctx, [(i + 1, j) for i, j in follows])
 
-    weights, keep = lax.optimization_barrier((weights, keep))
     taps = weights[:, :, 64:, : 2 * K].reshape(16, 2, 16, 2, K).transpose(3, 0, 1, 2, 4)
     more = lax.ppermute(taps, "h", [(0, 1), (1, 0)])
     upper_half = lax.axis_index("h") == 0
@@ -373,8 +391,20 @@
         [jnp.where(upper_half, taps, more), jnp.where(upper_half, more, taps)], axis=2
     ).reshape(2, CH, K)
 
+    tap_freq, conv = conv_part(sig_freq, taps, fwd[:, :, :K], inv[:, K:])
     gate_grad, signal_grad = out_part(
-        core, keep, other, inner, near, far, gate_input, sig_freq, taps, fwd, inv[:, K:], place.T
+        core,
+        keep,
+        other,
+        inner,
+        near,
+        far,
+        gate_input,
+        conv,
+        tap_freq,
+        fwd[:, :, K:],
+        inv[:, K:],
+        place.T,
     )
     return signal_grad, gate_grad, filter_grad
 

time: 172 us -> 173 us (level)
  the two profiles are of different devices: /device:TPU:1 before, /device:TPU:35 now
where the time goes in v9:
time: 173 us; the launch traced here: 172 us
  starting transfers between devices  61.7 us (36%)
  blocking collectives  38.3 us (22%)
  Pallas kernels  35.7 us (21%)
  between operations  14.3 us (8%)
  local copies, waits for them, and re-layouts  13.2 us (8%)
  other arithmetic  4.6 us (3%)
  waiting for transfers between devices  3.34 us (2%)
    all_to_all x1, blocking collectives, on_device(): lax.all_to_all(jnp.broadcast_to(cols[None], (8, 2, 2, TOK, K)), ('x', 'l'...  29.7 us
    all_to_all x1, starting transfers between devices, on_device(): tap_grad = lax.all_to_all(tap_grad, chips, split_axis=0, concat_axis=0)  18.2 us
    all_to_all x1, blocking collectives, on_device(): lax.all_to_all(jnp.broadcast_to(cols[None], (2, 8, 2, 2, TOK, K)), 'c', s...  8.61 us
    pallas_call x1, Pallas kernels, out_part(): pl.pallas_call(out_kernel, grid=(TILES,), in_specs=[scalar(), half, half,...  7.65 us
    pallas_call x1, Pallas kernels, product(): pl.pallas_call(product_kernel, grid=(4,), in_specs=[pl.BlockSpec((1, 8, 1...  6.42 us
    ppermute x1, starting transfers between devices, on_device(): other = lax.ppermute(send, 'c', [(0, 1), (1, 0)])  6.31 us
    unnamed x35, local copies, waits for them, and re-layouts  6.07 us
    pallas_call x1, Pallas kernels, conv_part(): pl.pallas_call(conv_kernel, grid=(TILES,), in_specs=[wide_tile(N), pl.Blo...  6 us
  transfers between devices with their start and end apart: 12, of which 1 were waited for; matrix products, arithmetic and copies ran while one was open for 7% of the time, Pallas kernels for 16%

profile of v9, /device:TPU:35, one launch (start us, length us, event | category | flops | bytes accessed | tf_op | source)
XLA Modules:
  0.0 171.7 jit_solution(53744715616168738)
XLA Ops:
  7.2 1.9 %shard_map.166 = bf16[2,80,512]{2,1,0:T(8,128)(2,1)} custom-call(bf16[64,1024]{1,0:T(8,128)(2,1)} %bitcast.46, f32[16,128]{1,0:T(8,128)} %bitcast.50, bf16[256,256]{1,0:T(8,128)(2,1)} %constant.30.clone.place_ref), custom_call_target="tpu_custom_call" | custom-call | flops 33554432 | bytes 524288 | tf_op jit(solution)/shard_map/pallas_call | solution.py:323
  9.1 4.1 %all-to-all-start = ((bf16[2,80,512]{2,1,0:T(8,128)(2,1)}), bf16[2,80,512]{2,1,0:T(8,128)(2,1)S(1)}, u32[]{:S(2)}, u32[]{:S(2)}) async-start(bf16[2,80,512]{2,1,0:T(8,128)(2,1)} %shard_map.166), calls=%async_computation | async-start | bytes 327680 | tf_op jit(solution)/shard_map/all_to_all | solution.py:345
  15.0 1.4 reshape.46
  19.6 3.9 %all-to-all-start.2 = ((bf16[2,2,256,512]{3,2,1,0:T(8,128)(2,1)}), bf16[2,2,256,512]{3,2,1,0:T(8,128)(2,1)S(1)}, u32[]{:S(2)}, u32[]{:S(2)}) async-start(bf16[2,2,256,512]{3,2,1,0:T(8,128)(2,1)} %bitcast.8), calls=%async_computation.2 | async-start | bytes 2097152 | tf_op jit(solution)/shard_map/all_to_all | solution.py:356
  23.5 4.7 %collective-permute-start = (bf16[128,1024]{1,0:T(8,128)(2,1)S(1)}, bf16[128,1024]{1,0:T(8,128)(2,1)S(1)}, u32[]{:S(2)}, u32[]{:S(2)}) collective-permute-start(bf16[128,1024]{1,0:T(8,128)(2,1)S(1)} %slice.9), channel_id=1, source_target_pairs={{0,8},{8,16},{16,24},{24,32},{32,40},{40,48},{48,56},{56,64},{64,7... | collective-permute-start | bytes 786440 | tf_op jit(solution)/shard_map/ppermute | solution.py:353
  28.3 3.3 %collective-permute-start.1 = (bf16[128,512]{1,0:T(8,128)(2,1)S(1)}, bf16[128,512]{1,0:T(8,128)(2,1)S(1)}, u32[]{:S(2)}, u32[]{:S(2)}) collective-permute-start(bf16[128,512]{1,0:T(8,128)(2,1)S(1)} %slice_bitcast_fusion.1), channel_id=1, source_target_pairs={{0,16},{16,32},{32,48},{48,64},{64,80},{80,96},{96,112},{112,128},... | collective-permute-start | bytes 393224 | tf_op jit(solution)/shard_map/ppermute | solution.py:360
  32.5 4.2 %all-to-all-start.1 = ((bf16[2,2,256,128]{3,1,2,0:T(2,128)(2,1)}), bf16[2,2,256,128]{3,1,2,0:T(2,128)(2,1)S(1)}, u32[]{:S(2)}, u32[]{:S(2)}) async-start(bf16[2,2,256,128]{3,1,2,0:T(2,128)(2,1)} %copy.29), calls=%async_computation.1 | async-start | bytes 524288 | tf_op jit(solution)/shard_map/all_to_all | solution.py:350
  37.3 4.3 %shard_map.168.freq_ref = f32[4,384,256]{2,1,0:T(8,128)} custom-call(bf16[128,512]{1,0:T(8,128)(2,1)} %copy-done.16, bf16[2,2,256,512]{3,2,1,0:T(8,128)(2,1)} %copy-done, bf16[2,384,384]{2,1,0:T(8,128)(2,1)} %constant.31.clone.forward_ref), custom_call_target="tpu_custom_call" | custom-call | flops 603979776 | bytes 3145728 | tf_op jit(solution)/shard_map/pallas_call | solution.py:139
  42.6 4.4 %shard_map.167.freq_ref = f32[384,1024]{1,0:T(8,128)} custom-call(bf16[384,1024]{1,0:T(8,128)(2,1)} %pad_maximum_fusion.1.window_ref, bf16[2,384,384]{2,1,0:T(8,128)(2,1)} %constant.31.clone.forward_ref), custom_call_target="tpu_custom_call" | custom-call | flops 603979776 | bytes 3145728 | tf_op jit(solution)/shard_map/pallas_call | solution.py:112
  47.6 29.7 %all_to_all.35 = bf16[8,2,2,256,128]{4,3,2,1,0:T(8,128)(2,1)S(1)} all-to-all(bf16[8,2,2,256,128]{4,3,2,1,0:T(8,128)(2,1)S(1)} %broadcast_in_dim.4), channel_id=1, replica_groups=mesh['z'=16,'h'=2,'c'=2,'x'=4,'l'=2] {'x','l'}, dimensions={0} | all-to-all | bytes 4194304 | tf_op jit(solution)/shard_map/all_to_all | solution.py:364
  77.2 1.4 broadcast_in_dim.5
  78.7 8.6 %all_to_all.36.cols_ref = bf16[2,8,2,2,256,128]{5,4,3,2,1,0:T(8,128)(2,1)} all-to-all(bf16[2,8,2,2,256,128]{5,4,3,2,1,0:T(8,128)(2,1)S(1)} %broadcast_in_dim.5), channel_id=1, replica_groups=mesh['z'=16,'h'=2,'c'=2,'x'=4,'l'=2] {'c'}, dimensions={0} | all-to-all | bytes 8388608 | tf_op jit(solution)/shard_map/all_to_all | solution.py:367
  87.3 6.4 %shard_map.169 = bf16[4,256,512]{2,1,0:T(8,128)(2,1)} custom-call(bf16[2,8,2,2,256,128]{5,4,3,2,1,0:T(8,128)(2,1)} %all_to_all.36.cols_ref, bf16[16,2,80,512]{3,2,1,0:T(8,128)(2,1)} %bitcast.47), custom_call_target="tpu_custom_call" | custom-call | flops 2147483648 | bytes 8388608 | tf_op jit(solution)/shard_map/pallas_call | solution.py:77
  93.7 5.4 %all-to-all-start.5 = ((bf16[2,2,256,512]{3,2,1,0:T(8,128)(2,1)}), bf16[2,2,256,512]{3,2,1,0:T(8,128)(2,1)}, u32[]{:S(2)}, u32[]{:S(2)}) async-start(bf16[2,2,256,512]{3,2,1,0:T(8,128)(2,1)} %bitcast.44), calls=%async_computation.5 | async-start | bytes 2097152 | tf_op jit(solution)/shard_map/all_to_all | solution.py:373
  99.1 1.7 bitcast_bitcast_fusion
  100.8 5.1 %collective-permute-start.5 = (bf16[2,16,2,16,128]{4,3,2,1,0:T(8,128)(2,1)}, bf16[2,16,2,16,128]{4,3,2,1,0:T(8,128)(2,1)}, u32[]{:S(2)}, u32[]{:S(2)}) collective-permute-start(bf16[2,16,2,16,128]{4,3,2,1,0:T(8,128)(2,1)} %bitcast_bitcast_fusion), channel_id=1, source_target_pairs={{0,16},{16,0},{1,17},{17,1},{2,18},{18,2},{3,19},{19,3},{4,20},{20... | collective-permute-start | bytes 786440 | tf_op jit(solution)/shard_map/ppermute | solution.py:388
  105.8 3.3 %all-to-all-done.5.mix_ref = bf16[2,2,256,512]{3,2,1,0:T(8,128)(2,1)} async-done(((bf16[2,2,256,512]{3,2,1,0:T(8,128)(2,1)}), bf16[2,2,256,512]{3,2,1,0:T(8,128)(2,1)}, u32[]{:S(2)}, u32[]{:S(2)}) %all-to-all-start.5) | async-done | bytes 1048608 | tf_op jit(solution)/shard_map/all_to_all | solution.py:373
  109.1 4.9 %shard_map.170 = (bf16[256,512]{1,0:T(8,128)(2,1)S(1)}, bf16[256,512]{1,0:T(8,128)(2,1)S(1)}, bf16[128,512]{1,0:T(8,128)(2,1)S(1)}, bf16[128,512]{1,0:T(8,128)(2...) custom-call(s32[1]{0:T(128)} %bitcast.core_ref, bf16[2,2,256,512]{3,2,1,0:T(8,128)(2,1)} %all-to-all-done.5.mix_ref, ...), custom_call_target="tpu_custom_call" | custom-call | flops 603979776 | bytes 5242880 | tf_op jit(solution)/shard_map/pallas_call | solution.py:189
  116.7 18.2 %all-to-all-start.6 = ((bf16[32,16,128]{2,1,0:T(8,128)(2,1)}), bf16[32,16,128]{2,1,0:T(8,128)(2,1)S(1)}, u32[]{:S(2)}, u32[]{:S(2)}) async-start(bf16[32,16,128]{2,1,0:T(8,128)(2,1)} %get-tuple-element.40), calls=%async_computation.6 | async-start | bytes 262144 | tf_op jit(solution)/shard_map/all_to_all | solution.py:379
  134.9 6.3 %collective-permute-start.2 = (bf16[256,512]{1,0:T(8,128)(2,1)S(1)}, bf16[256,512]{1,0:T(8,128)(2,1)S(1)}, u32[]{:S(2)}, u32[]{:S(2)}) collective-permute-start(bf16[256,512]{1,0:T(8,128)(2,1)S(1)} %get-tuple-element.30), channel_id=1, source_target_pairs={{0,8},{8,0},{1,9},{9,1},{2,10},{10,2},{3,11},{11,3},{4,12},{12,4},... | collective-permute-start | bytes 786440 | tf_op jit(solution)/shard_map/ppermute | solution.py:382
  141.2 1.9 %collective-permute-start.3 = (bf16[128,512]{1,0:T(8,128)(2,1)}, bf16[128,512]{1,0:T(8,128)(2,1)S(1)}, u32[]{:S(2)}, u32[]{:S(2)}) collective-permute-start(bf16[128,512]{1,0:T(8,128)(2,1)} %copy-done.8), channel_id=1, source_target_pairs={{16,8},{32,24},{48,40},{64,56},{80,72},{96,88},{112,104},{128,120}... | collective-permute-start | bytes 393224 | tf_op jit(solution)/shard_map/ppermute | solution.py:384
  143.2 4.6 %collective-permute-start.4 = (bf16[128,512]{1,0:T(8,128)(2,1)}, bf16[128,512]{1,0:T(8,128)(2,1)S(1)}, u32[]{:S(2)}, u32[]{:S(2)}) collective-permute-start(bf16[128,512]{1,0:T(8,128)(2,1)} %copy-done.7), channel_id=1, source_target_pairs={{24,8},{40,24},{56,40},{72,56},{88,72},{104,88},{120,104},{136,120... | collective-permute-start | bytes 393224 | tf_op jit(solution)/shard_map/ppermute | solution.py:385
  149.8 6.0 %shard_map.171 = (f32[384,1024]{1,0:T(8,128)}, f32[256,1024]{1,0:T(8,128)}) custom-call(f32[384,1024]{1,0:T(8,128)} %shard_map.167.freq_ref, bf16[2,1024,128]{2,1,0:T(8,128)(2,1)} %bitcast.43, bf16[2,384,128]{2,1,0:T(8,128)(2,1)} %constant.34.clone.forward_ref, bf16[2,256,384]{2,1,0:T(8,128)(2,1)} %constant.35.clone.inv_ref), custom_call_target="tpu_custom_call" | custom-call | flops 1024 | bytes 1024 | tf_op jit(solution)/shard_map/pallas_call | solution.py:224
  156.6 7.7 %shard_map.172 = (bf16[256,1024]{1,0:T(8,128)(2,1)}, bf16[256,1024]{1,0:T(8,128)(2,1)}) custom-call(s32[1]{0:T(128)} %bitcast.core_ref, bf16[256,512]{1,0:T(8,128)(2,1)} %copy-done.4, bf16[256,512]{1,0:T(8,128)(2,1)} %copy-done.13, bf16[128,512]{1,0:T(8,128)(2,1)} %copy-done.6, bf16[128,512]{1,0:T(8,128)(2,1)} %copy-done.14, bf16[128,512]{1,0:T(8,128)(2,1)} %copy-done.15, ...), custom_call_target="tpu_custom_call" | custom-call | flops 1024 | bytes 1024 | tf_op jit(solution)/shard_map/pallas_call | solution.py:276
  (67 shorter events, 14.0 us)
Async XLA Ops:
  7.2 9.2 %copy-start.11 = (bf16[256,256]{1,0:T(8,128)(2,1)S(1)}, bf16[256,256]{1,0:T(8,128)(2,1)}, u32[]{:S(2)}) copy-start(bf16[256,256]{1,0:T(8,128)(2,1)} %constant.30.clone.place_ref) | copy-start | bytes 393220
  9.1 5.2 %all-to-all-start = ((bf16[2,80,512]{2,1,0:T(8,128)(2,1)}), bf16[2,80,512]{2,1,0:T(8,128)(2,1)S(1)}, u32[]{:S(2)}, u32[]{:S(2)}) async-start(bf16[2,80,512]{2,1,0:T(8,128)(2,1)} %shard_map.166), calls=%async_computation | async-start | bytes 327680 | tf_op jit(solution)/shard_map/all_to_all | solution.py:345
  13.2 74.1 %all-gather.3.cloned.1.call-start = ((), (), s32[]{:S(2)}) async-start(), calls=%async_computation.7 | async-start | bytes 2785280 | tf_op jit(solution)/shard_map/all_gather | solution.py:349
  14.3 0.7 copy-start.12
  16.4 1.0 copy-start.10
  18.5 5.0 %copy-start.9 = (bf16[256,1024]{1,0:T(8,128)(2,1)S(1)}, bf16[256,1024]{1,0:T(8,128)(2,1)}, u32[]{:S(2)}) copy-start(bf16[256,1024]{1,0:T(8,128)(2,1)} %param.17) | copy-start | bytes 1572868
  19.6 8.7 %all-to-all-start.2 = ((bf16[2,2,256,512]{3,2,1,0:T(8,128)(2,1)}), bf16[2,2,256,512]{3,2,1,0:T(8,128)(2,1)S(1)}, u32[]{:S(2)}, u32[]{:S(2)}) async-start(bf16[2,2,256,512]{3,2,1,0:T(8,128)(2,1)} %bitcast.8), calls=%async_computation.2 | async-start | bytes 2097152 | tf_op jit(solution)/shard_map/all_to_all | solution.py:356
  23.5 18.2 %collective-permute-start = (bf16[128,1024]{1,0:T(8,128)(2,1)S(1)}, bf16[128,1024]{1,0:T(8,128)(2,1)S(1)}, u32[]{:S(2)}, u32[]{:S(2)}) collective-permute-start(bf16[128,1024]{1,0:T(8,128)(2,1)S(1)} %slice.9), channel_id=1, source_target_pairs={{0,8},{8,16},{16,24},{24,32},{32,40},{40,48},{48,56},{56,64},{64,7... | collective-permute-start | bytes 786440 | tf_op jit(solution)/shard_map/ppermute | solution.py:353
  28.3 8.4 %copy-start = (bf16[2,2,256,512]{3,2,1,0:T(8,128)(2,1)}, bf16[2,2,256,512]{3,2,1,0:T(8,128)(2,1)S(1)}, u32[]{:S(2)}) copy-start(bf16[2,2,256,512]{3,2,1,0:T(8,128)(2,1)S(1)} %all-to-all-done.2.tok_ref) | copy-start | bytes 3145732
  28.3 8.4 %collective-permute-start.1 = (bf16[128,512]{1,0:T(8,128)(2,1)S(1)}, bf16[128,512]{1,0:T(8,128)(2,1)S(1)}, u32[]{:S(2)}, u32[]{:S(2)}) collective-permute-start(bf16[128,512]{1,0:T(8,128)(2,1)S(1)} %slice_bitcast_fusion.1), channel_id=1, source_target_pairs={{0,16},{16,32},{32,48},{48,64},{64,80},{80,96},{96,112},{112,128},... | collective-permute-start | bytes 393224 | tf_op jit(solution)/shard_map/ppermute | solution.py:360
  32.5 14.5 %all-to-all-start.1 = ((bf16[2,2,256,128]{3,1,2,0:T(2,128)(2,1)}), bf16[2,2,256,128]{3,1,2,0:T(2,128)(2,1)S(1)}, u32[]{:S(2)}, u32[]{:S(2)}) async-start(bf16[2,2,256,128]{3,1,2,0:T(2,128)(2,1)} %copy.29), calls=%async_computation.1 | async-start | bytes 524288 | tf_op jit(solution)/shard_map/all_to_all | solution.py:350
  87.3 21.8 %copy-start.3 = (bf16[2,384,256]{2,1,0:T(8,128)(2,1)S(1)}, bf16[2,384,256]{2,1,0:T(8,128)(2,1)}, u32[]{:S(2)}) copy-start(bf16[2,384,256]{2,1,0:T(8,128)(2,1)} %constant.32.clone.own_ref) | copy-start | bytes 1179652
  87.3 21.8 %copy-start.5 = (bf16[2,128,384]{2,1,0:T(8,128)(2,1)S(1)}, bf16[2,128,384]{2,1,0:T(8,128)(2,1)}, u32[]{:S(2)}) copy-start(bf16[2,128,384]{2,1,0:T(8,128)(2,1)} %constant.33.clone.lag_ref) | copy-start | bytes 589828
  93.7 15.4 %copy-start.1 = (bf16[2,2,256,512]{3,2,1,0:T(8,128)(2,1)S(1)}, bf16[2,2,256,512]{3,2,1,0:T(8,128)(2,1)}, u32[]{:S(2)}) copy-start(bf16[2,2,256,512]{3,2,1,0:T(8,128)(2,1)} %copy-done) | copy-start | bytes 3145732
  93.7 15.4 %copy-start.2 = (f32[4,384,256]{2,1,0:T(8,128)S(1)}, f32[4,384,256]{2,1,0:T(8,128)}, u32[]{:S(2)}) copy-start(f32[4,384,256]{2,1,0:T(8,128)} %shard_map.168.freq_ref) | copy-start | bytes 4718596
  93.7 15.4 %all-to-all-start.5 = ((bf16[2,2,256,512]{3,2,1,0:T(8,128)(2,1)}), bf16[2,2,256,512]{3,2,1,0:T(8,128)(2,1)}, u32[]{:S(2)}, u32[]{:S(2)}) async-start(bf16[2,2,256,512]{3,2,1,0:T(8,128)(2,1)} %bitcast.44), calls=%async_computation.5 | async-start | bytes 2097152 | tf_op jit(solution)/shard_map/all_to_all | solution.py:373
  100.8 47.0 %collective-permute-start.5 = (bf16[2,16,2,16,128]{4,3,2,1,0:T(8,128)(2,1)}, bf16[2,16,2,16,128]{4,3,2,1,0:T(8,128)(2,1)}, u32[]{:S(2)}, u32[]{:S(2)}) collective-permute-start(bf16[2,16,2,16,128]{4,3,2,1,0:T(8,128)(2,1)} %bitcast_bitcast_fusion), channel_id=1, source_target_pairs={{0,16},{16,0},{1,17},{17,1},{2,18},{18,2},{3,19},{19,3},{4,20},{20... | collective-permute-start | bytes 786440 | tf_op jit(solution)/shard_map/ppermute | solution.py:388
  114.1 0.7 copy-start.4
  116.7 47.5 %all-to-all-start.6 = ((bf16[32,16,128]{2,1,0:T(8,128)(2,1)}), bf16[32,16,128]{2,1,0:T(8,128)(2,1)S(1)}, u32[]{:S(2)}, u32[]{:S(2)}) async-start(bf16[32,16,128]{2,1,0:T(8,128)(2,1)} %get-tuple-element.40), calls=%async_computation.6 | async-start | bytes 262144 | tf_op jit(solution)/shard_map/all_to_all | solution.py:379
  134.9 20.9 %collective-permute-start.2 = (bf16[256,512]{1,0:T(8,128)(2,1)S(1)}, bf16[256,512]{1,0:T(8,128)(2,1)S(1)}, u32[]{:S(2)}, u32[]{:S(2)}) collective-permute-start(bf16[256,512]{1,0:T(8,128)(2,1)S(1)} %get-tuple-element.30), channel_id=1, source_target_pairs={{0,8},{8,0},{1,9},{9,1},{2,10},{10,2},{3,11},{11,3},{4,12},{12,4},... | collective-permute-start | bytes 786440 | tf_op jit(solution)/shard_map/ppermute | solution.py:382
  141.2 14.5 %collective-permute-start.3 = (bf16[128,512]{1,0:T(8,128)(2,1)}, bf16[128,512]{1,0:T(8,128)(2,1)S(1)}, u32[]{:S(2)}, u32[]{:S(2)}) collective-permute-start(bf16[128,512]{1,0:T(8,128)(2,1)} %copy-done.8), channel_id=1, source_target_pairs={{16,8},{32,24},{48,40},{64,56},{80,72},{96,88},{112,104},{128,120}... | collective-permute-start | bytes 393224 | tf_op jit(solution)/shard_map/ppermute | solution.py:384
  143.2 12.6 %collective-permute-start.4 = (bf16[128,512]{1,0:T(8,128)(2,1)}, bf16[128,512]{1,0:T(8,128)(2,1)S(1)}, u32[]{:S(2)}, u32[]{:S(2)}) collective-permute-start(bf16[128,512]{1,0:T(8,128)(2,1)} %copy-done.7), channel_id=1, source_target_pairs={{24,8},{40,24},{56,40},{72,56},{88,72},{104,88},{120,104},{136,120... | collective-permute-start | bytes 393224 | tf_op jit(solution)/shard_map/ppermute | solution.py:385
  155.8 0.7 copy-start.15
  155.8 0.8 copy-start.13
  (5 other events, 3.3 us)
Sparse Core Ops, SparseCore 0:
  16.6 69.2 all-gather.2

commit v10 on v8

--- a/solution.py
+++ b/solution.py
@@ -351,6 +351,7 @@
     )
 
     partial = product(cols, weights)
+    weights, partial = lax.optimization_barrier((weights, partial))
     mix = lax.all_to_all(
         partial.reshape(2, 2, TOK, 512), "h", split_axis=0, concat_axis=0
     )
@@ -365,7 +366,6 @@
     near = lax.ppermute(cross, ctx, follows + [(2 * i + 1, 2 * i) for i in range(32)])
     far = lax.ppermute(first, ctx, [(i + 1, j) for i, j in follows])
 
-    weights, keep = lax.optimization_barrier((weights, keep))
     taps = weights[:, :, 64:, : 2 * K].reshape(16, 2, 16, 2, K).transpose(3, 0, 1, 2, 4)
     more = lax.ppermute(taps, "h", [(0, 1), (1, 0)])
     upper_half = lax.axis_index("h") == 0

time: 172 us -> 168 us (0.977)
  waiting for transfers between devices: 15 us -> 9.11 us
    all_to_all x1, waiting for transfers between devices: 9.74 us -> 3.85 us  [on_device(): lax.all_to_all(partial.reshape(2, 2, TOK, 512), 'h', split_axis=0, concat...]
    ppermute x1, starting transfers between devices: 1.92 us -> 4.88 us  [on_device(): more = lax.ppermute(taps, 'h', [(0, 1), (1, 0)])]
    all_to_all x1, starting transfers between devices: 21.3 us -> 18.6 us  [on_device(): tap_grad = lax.all_to_all(tap_grad, chips, split_axis=0, concat_axis=0)]
  transfers between devices with their start and end apart: 12 -> 12, of which waited for: 4 -> 4; matrix products, arithmetic and copies ran while one was open for 6% -> 7% of each run, Pallas kernels for 10% -> 13%
where the time goes in v10:
time: 168 us; the launch traced here: 167 us
  starting transfers between devices  58.7 us (35%)
  blocking collectives  38.3 us (23%)
  Pallas kernels  30.2 us (18%)
  between operations  14.3 us (9%)
  local copies, waits for them, and re-layouts  10.8 us (6%)
  waiting for transfers between devices  9.11 us (5%)
  other arithmetic  4.58 us (3%)
    all_to_all x1, blocking collectives, on_device(): lax.all_to_all(jnp.broadcast_to(cols[None], (8, 2, 2, TOK, K)), ('x', 'l'...  30.2 us
    all_to_all x1, starting transfers between devices, on_device(): tap_grad = lax.all_to_all(tap_grad, chips, split_axis=0, concat_axis=0)  18.6 us
    all_to_all x1, starting transfers between devices, on_device(): block = lax.all_to_all(message, 'c', split_axis=0, concat_axis=0)  10.3 us
    all_to_all x1, blocking collectives, on_device(): lax.all_to_all(jnp.broadcast_to(cols[None], (2, 8, 2, 2, TOK, K)), 'c', s...  8.1 us
    pallas_call x1, Pallas kernels, out_part(): pl.pallas_call(out_kernel, grid=(TILES,), in_specs=[scalar(), half, half,...  7.72 us
    pallas_call x1, Pallas kernels, product(): pl.pallas_call(product_kernel, grid=(4,), in_specs=[pl.BlockSpec((1, 8, 1...  6.35 us
    all_to_all x1, starting transfers between devices, on_device(): lax.all_to_all(partial.reshape(2, 2, TOK, 512), 'h', split_axis=0, concat...  5.86 us
    pallas_call x1, Pallas kernels, grad_part(): pl.pallas_call(grad_kernel, grid=(TILES,), in_specs=[scalar(), pl.BlockSp...  5.44 us
  transfers between devices with their start and end apart: 12, of which 4 were waited for; matrix products, arithmetic and copies ran while one was open for 7% of the time, Pallas kernels for 13%

profile of v10, /device:TPU:1, one launch (start us, length us, event | category | flops | bytes accessed | tf_op | source)
XLA Modules:
  0.0 166.5 jit_solution(834010362341360428)
XLA Ops:
  7.2 1.9 %shard_map.148 = bf16[2,80,512]{2,1,0:T(8,128)(2,1)} custom-call(bf16[64,1024]{1,0:T(8,128)(2,1)} %bitcast.46, f32[16,128]{1,0:T(8,128)} %bitcast.50, bf16[256,256]{1,0:T(8,128)(2,1)} %constant.28.clone.place_ref), custom_call_target="tpu_custom_call" | custom-call | flops 33554432 | bytes 524288 | tf_op jit(solution)/shard_map/pallas_call | solution.py:305
  9.1 10.3 %all-to-all-start = ((bf16[2,80,512]{2,1,0:T(8,128)(2,1)}), bf16[2,80,512]{2,1,0:T(8,128)(2,1)S(1)}, u32[]{:S(2)}, u32[]{:S(2)}) async-start(bf16[2,80,512]{2,1,0:T(8,128)(2,1)} %shard_map.148), calls=%async_computation | async-start | bytes 327680 | tf_op jit(solution)/shard_map/all_to_all | solution.py:327
  21.2 1.4 reshape.46
  25.8 3.9 %all-to-all-start.2 = ((bf16[2,2,256,512]{3,2,1,0:T(8,128)(2,1)}), bf16[2,2,256,512]{3,2,1,0:T(8,128)(2,1)S(1)}, u32[]{:S(2)}, u32[]{:S(2)}) async-start(bf16[2,2,256,512]{3,2,1,0:T(8,128)(2,1)} %bitcast.8), calls=%async_computation.2 | async-start | bytes 2097152 | tf_op jit(solution)/shard_map/all_to_all | solution.py:338
  29.7 1.9 %collective-permute-start = (bf16[128,1024]{1,0:T(8,128)(2,1)S(1)}, bf16[128,1024]{1,0:T(8,128)(2,1)S(1)}, u32[]{:S(2)}, u32[]{:S(2)}) collective-permute-start(bf16[128,1024]{1,0:T(8,128)(2,1)S(1)} %slice.9), channel_id=1, source_target_pairs={{0,8},{8,16},{16,24},{24,32},{32,40},{40,48},{48,56},{56,64},{64,7... | collective-permute-start | bytes 786440 | tf_op jit(solution)/shard_map/ppermute | solution.py:335
  31.7 1.3 collective-permute-start.1
  33.9 3.6 %all-to-all-start.1 = ((bf16[2,2,256,128]{3,1,2,0:T(2,128)(2,1)}), bf16[2,2,256,128]{3,1,2,0:T(2,128)(2,1)S(1)}, u32[]{:S(2)}, u32[]{:S(2)}) async-start(bf16[2,2,256,128]{3,1,2,0:T(2,128)(2,1)} %copy.27), calls=%async_computation.1 | async-start | bytes 524288 | tf_op jit(solution)/shard_map/all_to_all | solution.py:332
  38.4 4.3 %shard_map.150.freq_ref = f32[4,384,256]{2,1,0:T(8,128)} custom-call(bf16[128,512]{1,0:T(8,128)(2,1)} %copy-done.9, bf16[2,2,256,512]{3,2,1,0:T(8,128)(2,1)} %copy-done, bf16[2,384,384]{2,1,0:T(8,128)(2,1)} %constant.29.clone.forward_ref), custom_call_target="tpu_custom_call" | custom-call | flops 603979776 | bytes 3145728 | tf_op jit(solution)/shard_map/pallas_call | solution.py:139
  43.7 4.4 %shard_map.149.freq_ref = f32[384,1024]{1,0:T(8,128)} custom-call(bf16[384,1024]{1,0:T(8,128)(2,1)} %pad_maximum_fusion.1.window_ref, bf16[2,384,384]{2,1,0:T(8,128)(2,1)} %constant.29.clone.forward_ref), custom_call_target="tpu_custom_call" | custom-call | flops 603979776 | bytes 3145728 | tf_op jit(solution)/shard_map/pallas_call | solution.py:112
  48.7 30.2 %all_to_all.35 = bf16[8,2,2,256,128]{4,3,2,1,0:T(8,128)(2,1)S(1)} all-to-all(bf16[8,2,2,256,128]{4,3,2,1,0:T(8,128)(2,1)S(1)} %broadcast_in_dim.4), channel_id=1, replica_groups=mesh['z'=16,'h'=2,'c'=2,'x'=4,'l'=2] {'x','l'}, dimensions={0} | all-to-all | bytes 4194304 | tf_op jit(solution)/shard_map/all_to_all | solution.py:346
  78.9 1.4 broadcast_in_dim.5
  80.3 8.1 %all_to_all.36.cols_ref = bf16[2,8,2,2,256,128]{5,4,3,2,1,0:T(8,128)(2,1)} all-to-all(bf16[2,8,2,2,256,128]{5,4,3,2,1,0:T(8,128)(2,1)S(1)} %broadcast_in_dim.5), channel_id=1, replica_groups=mesh['z'=16,'h'=2,'c'=2,'x'=4,'l'=2] {'c'}, dimensions={0} | all-to-all | bytes 8388608 | tf_op jit(solution)/shard_map/all_to_all | solution.py:349
  88.4 6.3 %shard_map.151 = bf16[4,256,512]{2,1,0:T(8,128)(2,1)} custom-call(bf16[2,8,2,2,256,128]{5,4,3,2,1,0:T(8,128)(2,1)} %all_to_all.36.cols_ref, bf16[16,2,80,512]{3,2,1,0:T(8,128)(2,1)} %bitcast.47), custom_call_target="tpu_custom_call" | custom-call | flops 2147483648 | bytes 8388608 | tf_op jit(solution)/shard_map/pallas_call | solution.py:77
  94.7 5.9 %all-to-all-start.5 = ((bf16[2,2,256,512]{3,2,1,0:T(8,128)(2,1)}), bf16[2,2,256,512]{3,2,1,0:T(8,128)(2,1)S(1)}, u32[]{:S(2)}, u32[]{:S(2)}) async-start(bf16[2,2,256,512]{3,2,1,0:T(8,128)(2,1)} %bitcast.44), calls=%async_computation.5 | async-start | bytes 2097152 | tf_op jit(solution)/shard_map/all_to_all | solution.py:355
  101.6 4.9 %collective-permute-start.5 = (bf16[2,16,2,16,128]{4,3,2,1,0:T(8,128)(2,1)S(1)}, bf16[2,16,2,16,128]{4,3,2,1,0:T(8,128)(2,1)S(1)}, u32[]{:S(2)}, u32[]{:S(2)}) collective-permute-start(bf16[2,16,2,16,128]{4,3,2,1,0:T(8,128)(2,1)S(1)} %bitcast_bitcast_fusion), channel_id=1, source_target_pairs={{0,16},{16,0},{1,17},{17,1},{2,18},{18,2},{3,19},{19,3},{4,20},{20... | collective-permute-start | bytes 786440 | tf_op jit(solution)/shard_map/ppermute | solution.py:370
  106.5 3.8 %all-to-all-done.5.mix_ref = bf16[2,2,256,512]{3,2,1,0:T(8,128)(2,1)S(1)} async-done(((bf16[2,2,256,512]{3,2,1,0:T(8,128)(2,1)}), bf16[2,2,256,512]{3,2,1,0:T(8,128)(2,1)S(1)}, u32[]{:S(2)}, u32[]{:S(2)}) %all-to-all-start.5) | async-done | bytes 1048608 | tf_op jit(solution)/shard_map/all_to_all | solution.py:355
  111.3 5.4 %shard_map.152 = (bf16[256,512]{1,0:T(8,128)(2,1)}, bf16[256,512]{1,0:T(8,128)(2,1)}, bf16[128,512]{1,0:T(8,128)(2,1)}, bf16[128,512]{1,0:T(8,128)(2,1)}, bf16[1...) custom-call(s32[1]{0:T(128)} %bitcast.core_ref, bf16[2,2,256,512]{3,2,1,0:T(8,128)(2,1)} %copy-done.1, ...), custom_call_target="tpu_custom_call" | custom-call | flops 603979776 | bytes 5242880 | tf_op jit(solution)/shard_map/pallas_call | solution.py:189
  116.8 18.6 %all-to-all-start.6 = ((bf16[32,16,128]{2,1,0:T(8,128)(2,1)}), bf16[32,16,128]{2,1,0:T(8,128)(2,1)S(1)}, u32[]{:S(2)}, u32[]{:S(2)}) async-start(bf16[32,16,128]{2,1,0:T(8,128)(2,1)} %get-tuple-element.36), calls=%async_computation.6 | async-start | bytes 262144 | tf_op jit(solution)/shard_map/all_to_all | solution.py:361
  135.4 5.0 %collective-permute-start.2 = (bf16[256,512]{1,0:T(8,128)(2,1)}, bf16[256,512]{1,0:T(8,128)(2,1)S(1)}, u32[]{:S(2)}, u32[]{:S(2)}) collective-permute-start(bf16[256,512]{1,0:T(8,128)(2,1)} %get-tuple-element.28), channel_id=1, source_target_pairs={{0,8},{8,0},{1,9},{9,1},{2,10},{10,2},{3,11},{11,3},{4,12},{12,4},... | collective-permute-start | bytes 786440 | tf_op jit(solution)/shard_map/ppermute | solution.py:364
  140.4 1.9 %collective-permute-start.3 = (bf16[128,512]{1,0:T(8,128)(2,1)}, bf16[128,512]{1,0:T(8,128)(2,1)S(1)}, u32[]{:S(2)}, u32[]{:S(2)}) collective-permute-start(bf16[128,512]{1,0:T(8,128)(2,1)} %get-tuple-element.30), channel_id=1, source_target_pairs={{16,8},{32,24},{48,40},{64,56},{80,72},{96,88},{112,104},{128,120}... | collective-permute-start | bytes 393224 | tf_op jit(solution)/shard_map/ppermute | solution.py:366
  142.4 1.3 collective-permute-start.4
  145.6 3.5 %collective-permute-done.3.near_ref = bf16[128,512]{1,0:T(8,128)(2,1)S(1)} collective-permute-done((bf16[128,512]{1,0:T(8,128)(2,1)}, bf16[128,512]{1,0:T(8,128)(2,1)S(1)}, u32[]{:S(2)}, u32[]{:S(2)}) %collective-permute-start.3) | collective-permute-done | bytes 131104 | tf_op jit(solution)/shard_map/ppermute | solution.py:366
  149.2 1.4 collective-permute-done.4.far_ref
  151.3 7.7 %shard_map.153 = (bf16[256,1024]{1,0:T(8,128)(2,1)}, bf16[256,1024]{1,0:T(8,128)(2,1)}) custom-call(s32[1]{0:T(128)} %bitcast.core_ref, bf16[256,512]{1,0:T(8,128)(2,1)} %get-tuple-element.27.keep_ref, bf16[256,512]{1,0:T(8,128)(2,1)} %copy-done.6, bf16[128,512]{1,0:T(8,128)(2,1)} %get-tuple-element.29.inner_ref, bf16[128,512]{1,0:T(8,128)(2,1)} %copy-done.7, ...), custom_call_target="tpu_custom_call" | custom-call | flops 1024 | bytes 1024 | tf_op jit(solution)/shard_map/pallas_call | solution.py:256
  (52 shorter events, 13.5 us)
Async XLA Ops:
  7.2 15.4 %copy-start.4 = (bf16[256,256]{1,0:T(8,128)(2,1)S(1)}, bf16[256,256]{1,0:T(8,128)(2,1)}, u32[]{:S(2)}) copy-start(bf16[256,256]{1,0:T(8,128)(2,1)} %constant.28.clone.place_ref) | copy-start | bytes 393220
  9.1 11.4 %all-to-all-start = ((bf16[2,80,512]{2,1,0:T(8,128)(2,1)}), bf16[2,80,512]{2,1,0:T(8,128)(2,1)S(1)}, u32[]{:S(2)}, u32[]{:S(2)}) async-start(bf16[2,80,512]{2,1,0:T(8,128)(2,1)} %shard_map.148), calls=%async_computation | async-start | bytes 327680 | tf_op jit(solution)/shard_map/all_to_all | solution.py:327
  19.4 69.0 %all-gather.3.cloned.1.call-start = ((), (), s32[]{:S(2)}) async-start(), calls=%async_computation.7 | async-start | bytes 2785280 | tf_op jit(solution)/shard_map/all_gather | solution.py:331
  20.5 0.7 copy-start.5
  22.6 1.0 copy-start.3
  24.7 5.0 %copy-start.2 = (bf16[256,1024]{1,0:T(8,128)(2,1)S(1)}, bf16[256,1024]{1,0:T(8,128)(2,1)}, u32[]{:S(2)}) copy-start(bf16[256,1024]{1,0:T(8,128)(2,1)} %param.15) | copy-start | bytes 1572868
  25.8 5.9 %all-to-all-start.2 = ((bf16[2,2,256,512]{3,2,1,0:T(8,128)(2,1)}), bf16[2,2,256,512]{3,2,1,0:T(8,128)(2,1)S(1)}, u32[]{:S(2)}, u32[]{:S(2)}) async-start(bf16[2,2,256,512]{3,2,1,0:T(8,128)(2,1)} %bitcast.8), calls=%async_computation.2 | async-start | bytes 2097152 | tf_op jit(solution)/shard_map/all_to_all | solution.py:338
  29.7 13.0 %collective-permute-start = (bf16[128,1024]{1,0:T(8,128)(2,1)S(1)}, bf16[128,1024]{1,0:T(8,128)(2,1)S(1)}, u32[]{:S(2)}, u32[]{:S(2)}) collective-permute-start(bf16[128,1024]{1,0:T(8,128)(2,1)S(1)} %slice.9), channel_id=1, source_target_pairs={{0,8},{8,16},{16,24},{24,32},{32,40},{40,48},{48,56},{56,64},{64,7... | collective-permute-start | bytes 786440 | tf_op jit(solution)/shard_map/ppermute | solution.py:335
  31.7 6.1 %copy-start = (bf16[2,2,256,512]{3,2,1,0:T(8,128)(2,1)}, bf16[2,2,256,512]{3,2,1,0:T(8,128)(2,1)S(1)}, u32[]{:S(2)}) copy-start(bf16[2,2,256,512]{3,2,1,0:T(8,128)(2,1)S(1)} %all-to-all-done.2.tok_ref) | copy-start | bytes 3145732
  31.7 6.1 %collective-permute-start.1 = (bf16[128,512]{1,0:T(8,128)(2,1)S(1)}, bf16[128,512]{1,0:T(8,128)(2,1)S(1)}, u32[]{:S(2)}, u32[]{:S(2)}) collective-permute-start(bf16[128,512]{1,0:T(8,128)(2,1)S(1)} %slice_bitcast_fusion.1), channel_id=1, source_target_pairs={{0,16},{16,32},{32,48},{48,64},{64,80},{80,96},{96,112},{112,128},... | collective-permute-start | bytes 393224 | tf_op jit(solution)/shard_map/ppermute | solution.py:342
  33.9 14.3 %all-to-all-start.1 = ((bf16[2,2,256,128]{3,1,2,0:T(2,128)(2,1)}), bf16[2,2,256,128]{3,1,2,0:T(2,128)(2,1)S(1)}, u32[]{:S(2)}, u32[]{:S(2)}) async-start(bf16[2,2,256,128]{3,1,2,0:T(2,128)(2,1)} %copy.27), calls=%async_computation.1 | async-start | bytes 524288 | tf_op jit(solution)/shard_map/all_to_all | solution.py:332
  37.8 0.6 copy-start.9
  94.7 15.6 %all-to-all-start.5 = ((bf16[2,2,256,512]{3,2,1,0:T(8,128)(2,1)}), bf16[2,2,256,512]{3,2,1,0:T(8,128)(2,1)S(1)}, u32[]{:S(2)}, u32[]{:S(2)}) async-start(bf16[2,2,256,512]{3,2,1,0:T(8,128)(2,1)} %bitcast.44), calls=%async_computation.5 | async-start | bytes 2097152 | tf_op jit(solution)/shard_map/all_to_all | solution.py:355
  101.6 42.1 %collective-permute-start.5 = (bf16[2,16,2,16,128]{4,3,2,1,0:T(8,128)(2,1)S(1)}, bf16[2,16,2,16,128]{4,3,2,1,0:T(8,128)(2,1)S(1)}, u32[]{:S(2)}, u32[]{:S(2)}) collective-permute-start(bf16[2,16,2,16,128]{4,3,2,1,0:T(8,128)(2,1)S(1)} %bitcast_bitcast_fusion), channel_id=1, source_target_pairs={{0,16},{16,0},{1,17},{17,1},{2,18},{18,2},{3,19},{19,3},{4,20},{20... | collective-permute-start | bytes 786440 | tf_op jit(solution)/shard_map/ppermute | solution.py:370
  110.4 1.0 copy-start.1
  116.8 42.3 %all-to-all-start.6 = ((bf16[32,16,128]{2,1,0:T(8,128)(2,1)}), bf16[32,16,128]{2,1,0:T(8,128)(2,1)S(1)}, u32[]{:S(2)}, u32[]{:S(2)}) async-start(bf16[32,16,128]{2,1,0:T(8,128)(2,1)} %get-tuple-element.36), calls=%async_computation.6 | async-start | bytes 262144 | tf_op jit(solution)/shard_map/all_to_all | solution.py:361
  135.4 15.1 %collective-permute-start.2 = (bf16[256,512]{1,0:T(8,128)(2,1)}, bf16[256,512]{1,0:T(8,128)(2,1)S(1)}, u32[]{:S(2)}, u32[]{:S(2)}) collective-permute-start(bf16[256,512]{1,0:T(8,128)(2,1)} %get-tuple-element.28), channel_id=1, source_target_pairs={{0,8},{8,0},{1,9},{9,1},{2,10},{10,2},{3,11},{11,3},{4,12},{12,4},... | collective-permute-start | bytes 786440 | tf_op jit(solution)/shard_map/ppermute | solution.py:364
  140.4 8.7 %collective-permute-start.3 = (bf16[128,512]{1,0:T(8,128)(2,1)}, bf16[128,512]{1,0:T(8,128)(2,1)S(1)}, u32[]{:S(2)}, u32[]{:S(2)}) collective-permute-start(bf16[128,512]{1,0:T(8,128)(2,1)} %get-tuple-element.30), channel_id=1, source_target_pairs={{16,8},{32,24},{48,40},{64,56},{80,72},{96,88},{112,104},{128,120}... | collective-permute-start | bytes 393224 | tf_op jit(solution)/shard_map/ppermute | solution.py:366
  142.4 8.2 %collective-permute-start.4 = (bf16[128,512]{1,0:T(8,128)(2,1)}, bf16[128,512]{1,0:T(8,128)(2,1)S(1)}, u32[]{:S(2)}, u32[]{:S(2)}) collective-permute-start(bf16[128,512]{1,0:T(8,128)(2,1)} %get-tuple-element.31), channel_id=1, source_target_pairs={{24,8},{40,24},{56,40},{72,56},{88,72},{104,88},{120,104},{136,120... | collective-permute-start | bytes 393224 | tf_op jit(solution)/shard_map/ppermute | solution.py:367
  149.2 1.4 copy-start.7
  150.6 0.7 copy-start.8
  150.6 0.7 copy-start.6
Sparse Core Ops, SparseCore 0:
  22.8 64.9 all-gather.2

commit v11 on v9

--- a/solution.py
+++ b/solution.py
@@ -42,13 +42,19 @@
 
 
 def exact_side(matrix, values):
-    return dot(matrix[0], values) + dot(matrix[1], values)
+    return dot(
+        jnp.concatenate([matrix[0], matrix[1]], axis=1),
+        jnp.concatenate([values, values], axis=0),
+    )
 
 
 def both_sides(matrix, values):
     high = values.astype(BF)
     low = (values - high.astype(F32)).astype(BF)
-    return dot(matrix[0], high) + dot(matrix[1], high) + dot(matrix[0], low)
+    return dot(
+        jnp.concatenate([matrix[0], matrix[1], matrix[0]], axis=1),
+        jnp.concatenate([high, high, low], axis=0),
+    )
 
 
 def times(a, b):
@@ -69,19 +75,20 @@
 
 def product_kernel(cols_ref, weight_ref, out_ref):
     weight = weight_ref[:, :, :64].reshape(16 * K, 512)
-    rows = jnp.concatenate([cols_ref[0, i, 0, j] for i in range(8) for j in range(2)], axis=1)
-    out_ref[0] = dot(rows, weight).astype(BF)
+    for b in range(2):
+        rows = jnp.concatenate([cols_ref[b, i, 0, j] for i in range(8) for j in range(2)], axis=1)
+        out_ref[b] = dot(rows, weight).astype(BF)
 
 
 def product(cols, weights):
     return pl.pallas_call(
         product_kernel,
-        grid=(4,),
+        grid=(2,),
         in_specs=[
-            pl.BlockSpec((1, 8, 1, 2, TOK, K), lambda i: (i % 2, 0, i // 2, 0, 0, 0)),
+            pl.BlockSpec((2, 8, 1, 2, TOK, K), lambda i: (0, 0, i, 0, 0, 0)),
             pl.BlockSpec((16, 2, 80, 512), lambda i: (0, 0, 0, 0)),
         ],
-        out_specs=pl.BlockSpec((1, TOK, 512), lambda i: (i, 0, 0)),
+        out_specs=pl.BlockSpec((2, TOK, 512), lambda i: (i, 0, 0)),
         out_shape=jax.ShapeDtypeStruct((4, TOK, 512), BF),
         compiler_params=params(),
         cost_estimate=pl.CostEstimate(
@@ -98,9 +105,10 @@
     return pl.BlockSpec(memory_space=pltpu.SMEM)
 
 
-TILES = 512 // K
+L = 256
+TILES = 512 // L
 PAIR = pl.BlockSpec((1, TOK, 2 * K), lambda j: (j, 0, 0))
-FREQ = pl.BlockSpec((1, N, 2 * K), lambda j: (j, 0, 0))
+FREQ = pl.BlockSpec((1, N, 2 * L), lambda j: (j, 0, 0))
 
 
 def plain_kernel(window_ref, forward_ref, freq_ref):
@@ -108,7 +116,7 @@
 
 
 def plain_part(window, forward):
-    tile = pl.BlockSpec((N, 2 * K), lambda j: (0, j))
+    tile = pl.BlockSpec((N, 2 * L), lambda j: (0, j))
     return pl.pallas_call(
         plain_kernel,
         grid=(TILES,),
@@ -140,12 +148,12 @@
         front_kernel,
         grid=(TILES,),
         in_specs=[
-            pl.BlockSpec((K, K), lambda j: (0, j)),
-            pl.BlockSpec((2, 1, TOK, K), lambda j: (0, 0, 0, j)),
+            pl.BlockSpec((K, L), lambda j: (0, j)),
+            pl.BlockSpec((2, 1, TOK, L), lambda j: (0, 0, 0, j)),
             whole((2, N, N)),
         ],
         out_specs=FREQ,
-        out_shape=jax.ShapeDtypeStruct((TILES, N, 2 * K), F32),
+        out_shape=jax.ShapeDtypeStruct((TILES, N, 2 * L), F32),
         compiler_params=params(),
         cost_estimate=pl.CostEstimate(
             flops=2 * CH * N * 2 * N, bytes_accessed=3 << 20, transcendentals=0
@@ -179,29 +187,29 @@
     cross_ref[...] = jnp.where(is_first, early[:K], late[:K]).astype(BF)
     conv_grad = jnp.concatenate([early, late], axis=1).astype(BF)
     cross = times_conj(exact_side(own_ref, conv_grad), freq_ref[0])
-    taps = both_sides(lag_ref, cross[:, :K] + cross[:, K:])
-    tap_ref[...] = taps.T.reshape(8, 16, K).astype(tap_ref.dtype)
+    taps = both_sides(lag_ref, cross[:, :L] + cross[:, L:])
+    tap_ref[...] = taps.T.reshape(L // 16, 16, K).astype(tap_ref.dtype)
 
 
 def grad_part(core, mix, tokens, sig_freq, own, lag):
-    head = pl.BlockSpec((K, K), lambda j: (0, j))
-    half = pl.BlockSpec((TOK, K), lambda j: (0, j))
+    head = pl.BlockSpec((K, L), lambda j: (0, j))
+    half = pl.BlockSpec((TOK, L), lambda j: (0, j))
     return pl.pallas_call(
         grad_kernel,
         grid=(TILES,),
         in_specs=[
             scalar(),
-            pl.BlockSpec((2, 2, TOK, K), lambda j: (0, 0, 0, j)),
-            pl.BlockSpec((2, 1, TOK, K), lambda j: (0, 1, 0, j)),
+            pl.BlockSpec((2, 2, TOK, L), lambda j: (0, 0, 0, j)),
+            pl.BlockSpec((2, 1, TOK, L), lambda j: (0, 1, 0, j)),
             FREQ,
             whole((2, N, TOK)),
             whole((2, K, N)),
         ],
-        out_specs=[half, half, head, head, head, pl.BlockSpec((8, 16, K), lambda j: (j, 0, 0))],
+        out_specs=[half, half, head, head, head, pl.BlockSpec((L // 16, 16, K), lambda j: (j, 0, 0))],
         out_shape=[jax.ShapeDtypeStruct((TOK, 512), BF)] * 2
         + [jax.ShapeDtypeStruct((K, 512), BF)] * 3
         + [jax.ShapeDtypeStruct((32, 16, K), BF)],
-        compiler_params=params(32 << 20),
+        compiler_params=params(),
         cost_estimate=pl.CostEstimate(
             flops=2 * CH * N * (2 * TOK + 2 * K), bytes_accessed=5 << 20, transcendentals=0
         ),
@@ -217,7 +225,7 @@
 
 
 def wide_tile(rows):
-    return pl.BlockSpec((rows, 2 * K), lambda j: (0, j))
+    return pl.BlockSpec((rows, 2 * L), lambda j: (0, j))
 
 
 def conv_part(sig_freq, taps, forward, inv):
@@ -226,7 +234,7 @@
         grid=(TILES,),
         in_specs=[
             wide_tile(N),
-            pl.BlockSpec((2, 2 * K, K), lambda j: (0, j, 0)),
+            pl.BlockSpec((2, 2 * L, K), lambda j: (0, j, 0)),
             whole((2, N, K)),
             whole((2, TOK, N)),
         ],
@@ -256,7 +264,16 @@
     is_first = core_ref[0] == 0
 
     def joined(left, right):
-        return dot(jnp.concatenate([left, right], axis=1), place_ref[...])
+        return jnp.concatenate(
+            [
+                dot(
+                    jnp.concatenate([left[:, i : i + K], right[:, i : i + K]], axis=1),
+                    place_ref[...],
+                )
+                for i in range(0, L, K)
+            ],
+            axis=1,
+        )
 
     keep, other = keep_ref[...], other_ref[...]
     mixed = joined(jnp.where(is_first, keep, other), jnp.where(is_first, other, keep))
@@ -271,8 +288,8 @@
 
 
 def out_part(core, keep, other, inner, near, far, gate, conv, tap_freq, forward, inv, place):
-    head = pl.BlockSpec((K, K), lambda j: (0, j))
-    half = pl.BlockSpec((TOK, K), lambda j: (0, j))
+    head = pl.BlockSpec((K, L), lambda j: (0, j))
+    half = pl.BlockSpec((TOK, L), lambda j: (0, j))
     return pl.pallas_call(
         out_kernel,
         grid=(TILES,),

time: 173 us -> 164 us (0.948)
  the two profiles are of different devices: /device:TPU:35 before, /device:TPU:1 now
where the time goes in v11:
time: 164 us; the launch traced here: 161 us
  starting transfers between devices  58.1 us (35%)
  blocking collectives  38.3 us (23%)
  Pallas kernels  27.4 us (17%)
  between operations  14.3 us (9%)
  local copies, waits for them, and re-layouts  10.8 us (7%)
  waiting for transfers between devices  6.74 us (4%)
  other arithmetic  4.58 us (3%)
    all_to_all x1, blocking collectives, on_device(): lax.all_to_all(jnp.broadcast_to(cols[None], (8, 2, 2, TOK, K)), ('x', 'l'...  30.2 us
    all_to_all x1, starting transfers between devices, on_device(): tap_grad = lax.all_to_all(tap_grad, chips, split_axis=0, concat_axis=0)  16.1 us
    all_to_all x1, starting transfers between devices, on_device(): block = lax.all_to_all(message, 'c', split_axis=0, concat_axis=0)  10.3 us
    ppermute x1, starting transfers between devices, on_device(): other = lax.ppermute(send, 'c', [(0, 1), (1, 0)])  8.9 us
    all_to_all x1, blocking collectives, on_device(): lax.all_to_all(jnp.broadcast_to(cols[None], (2, 8, 2, 2, TOK, K)), 'c', s...  8.16 us
    pallas_call x1, Pallas kernels, product(): pl.pallas_call(product_kernel, grid=(2,), in_specs=[pl.BlockSpec((2, 8, 1...  5.7 us
    pallas_call x1, Pallas kernels, out_part(): pl.pallas_call(out_kernel, grid=(TILES,), in_specs=[scalar(), half, half,...  5.23 us
    ppermute x1, starting transfers between devices, on_device(): more = lax.ppermute(taps, 'h', [(0, 1), (1, 0)])  4.88 us
  transfers between devices with their start and end apart: 12, of which 4 were waited for; matrix products, arithmetic and copies ran while one was open for 7% of the time, Pallas kernels for 12%

profile of v11, /device:TPU:1, one launch (start us, length us, event | category | flops | bytes accessed | tf_op | source)
XLA Modules:
  0.0 160.8 jit_solution(17626439433302312808)
XLA Ops:
  7.2 1.9 %shard_map.166 = bf16[2,80,512]{2,1,0:T(8,128)(2,1)} custom-call(bf16[64,1024]{1,0:T(8,128)(2,1)} %bitcast.46, f32[16,128]{1,0:T(8,128)} %bitcast.50, bf16[256,256]{1,0:T(8,128)(2,1)} %constant.30.clone.place_ref), custom_call_target="tpu_custom_call" | custom-call | flops 33554432 | bytes 524288 | tf_op jit(solution)/shard_map/pallas_call | solution.py:340
  9.1 10.3 %all-to-all-start = ((bf16[2,80,512]{2,1,0:T(8,128)(2,1)}), bf16[2,80,512]{2,1,0:T(8,128)(2,1)S(1)}, u32[]{:S(2)}, u32[]{:S(2)}) async-start(bf16[2,80,512]{2,1,0:T(8,128)(2,1)} %shard_map.166), calls=%async_computation | async-start | bytes 327680 | tf_op jit(solution)/shard_map/all_to_all | solution.py:362
  21.2 1.4 reshape.46
  25.8 3.9 %all-to-all-start.2 = ((bf16[2,2,256,512]{3,2,1,0:T(8,128)(2,1)}), bf16[2,2,256,512]{3,2,1,0:T(8,128)(2,1)S(1)}, u32[]{:S(2)}, u32[]{:S(2)}) async-start(bf16[2,2,256,512]{3,2,1,0:T(8,128)(2,1)} %bitcast.8), calls=%async_computation.2 | async-start | bytes 2097152 | tf_op jit(solution)/shard_map/all_to_all | solution.py:373
  29.7 1.9 %collective-permute-start = (bf16[128,1024]{1,0:T(8,128)(2,1)S(1)}, bf16[128,1024]{1,0:T(8,128)(2,1)S(1)}, u32[]{:S(2)}, u32[]{:S(2)}) collective-permute-start(bf16[128,1024]{1,0:T(8,128)(2,1)S(1)} %slice.9), channel_id=1, source_target_pairs={{0,8},{8,16},{16,24},{24,32},{32,40},{40,48},{48,56},{56,64},{64,7... | collective-permute-start | bytes 786440 | tf_op jit(solution)/shard_map/ppermute | solution.py:370
  31.7 1.3 collective-permute-start.1
  33.9 3.6 %all-to-all-start.1 = ((bf16[2,2,256,128]{3,1,2,0:T(2,128)(2,1)}), bf16[2,2,256,128]{3,1,2,0:T(2,128)(2,1)S(1)}, u32[]{:S(2)}, u32[]{:S(2)}) async-start(bf16[2,2,256,128]{3,1,2,0:T(2,128)(2,1)} %copy.29), calls=%async_computation.1 | async-start | bytes 524288 | tf_op jit(solution)/shard_map/all_to_all | solution.py:367
  38.4 3.1 %shard_map.168.freq_ref = f32[2,384,512]{2,1,0:T(8,128)} custom-call(bf16[128,512]{1,0:T(8,128)(2,1)} %copy-done.9, bf16[2,2,256,512]{3,2,1,0:T(8,128)(2,1)} %copy-done, bf16[2,384,384]{2,1,0:T(8,128)(2,1)} %constant.31.clone.forward_ref), custom_call_target="tpu_custom_call" | custom-call | flops 603979776 | bytes 3145728 | tf_op jit(solution)/shard_map/pallas_call | solution.py:147
  42.4 3.1 %shard_map.167.freq_ref = f32[384,1024]{1,0:T(8,128)} custom-call(bf16[384,1024]{1,0:T(8,128)(2,1)} %pad_maximum_fusion.1.window_ref, bf16[2,384,384]{2,1,0:T(8,128)(2,1)} %constant.31.clone.forward_ref), custom_call_target="tpu_custom_call" | custom-call | flops 603979776 | bytes 3145728 | tf_op jit(solution)/shard_map/pallas_call | solution.py:120
  46.1 30.2 %all_to_all.35 = bf16[8,2,2,256,128]{4,3,2,1,0:T(8,128)(2,1)S(1)} all-to-all(bf16[8,2,2,256,128]{4,3,2,1,0:T(8,128)(2,1)S(1)} %broadcast_in_dim.4), channel_id=1, replica_groups=mesh['z'=16,'h'=2,'c'=2,'x'=4,'l'=2] {'x','l'}, dimensions={0} | all-to-all | bytes 4194304 | tf_op jit(solution)/shard_map/all_to_all | solution.py:381
  76.3 1.4 broadcast_in_dim.5
  77.7 8.2 %all_to_all.36.cols_ref = bf16[2,8,2,2,256,128]{5,4,3,2,1,0:T(8,128)(2,1)} all-to-all(bf16[2,8,2,2,256,128]{5,4,3,2,1,0:T(8,128)(2,1)S(1)} %broadcast_in_dim.5), channel_id=1, replica_groups=mesh['z'=16,'h'=2,'c'=2,'x'=4,'l'=2] {'c'}, dimensions={0} | all-to-all | bytes 8388608 | tf_op jit(solution)/shard_map/all_to_all | solution.py:384
  85.8 2.1 %all-gather.3.cloned.1.call-done = bf16[32,80,512]{2,1,0:T(8,128)(2,1)} async-done(((bf16[2,80,512]{2,1,0:T(8,128)(2,1)}), bf16[32,80,512]{2,1,0:T(8,128)(2,1)}) %all-gather.3.cloned.1.call-update) | async-done | bytes 2621456 | tf_op jit(solution)/shard_map/all_gather | solution.py:366
  88.0 5.7 %shard_map.169 = bf16[4,256,512]{2,1,0:T(8,128)(2,1)} custom-call(bf16[2,8,2,2,256,128]{5,4,3,2,1,0:T(8,128)(2,1)} %all_to_all.36.cols_ref, bf16[16,2,80,512]{3,2,1,0:T(8,128)(2,1)} %bitcast.47), custom_call_target="tpu_custom_call" | custom-call | flops 2147483648 | bytes 8388608 | tf_op jit(solution)/shard_map/pallas_call | solution.py:84
  93.7 4.0 %all-to-all-start.5 = ((bf16[2,2,256,512]{3,2,1,0:T(8,128)(2,1)}), bf16[2,2,256,512]{3,2,1,0:T(8,128)(2,1)S(1)}, u32[]{:S(2)}, u32[]{:S(2)}) async-start(bf16[2,2,256,512]{3,2,1,0:T(8,128)(2,1)} %bitcast.44), calls=%async_computation.5 | async-start | bytes 2097152 | tf_op jit(solution)/shard_map/all_to_all | solution.py:390
  98.7 4.9 %collective-permute-start.5 = (bf16[2,16,2,16,128]{4,3,2,1,0:T(8,128)(2,1)S(1)}, bf16[2,16,2,16,128]{4,3,2,1,0:T(8,128)(2,1)S(1)}, u32[]{:S(2)}, u32[]{:S(2)}) collective-permute-start(bf16[2,16,2,16,128]{4,3,2,1,0:T(8,128)(2,1)S(1)} %bitcast_bitcast_fusion), channel_id=1, source_target_pairs={{0,16},{16,0},{1,17},{17,1},{2,18},{18,2},{3,19},{19,3},{4,20},{20... | collective-permute-start | bytes 786440 | tf_op jit(solution)/shard_map/ppermute | solution.py:405
  103.6 3.8 %all-to-all-done.5.mix_ref = bf16[2,2,256,512]{3,2,1,0:T(8,128)(2,1)S(1)} async-done(((bf16[2,2,256,512]{3,2,1,0:T(8,128)(2,1)}), bf16[2,2,256,512]{3,2,1,0:T(8,128)(2,1)S(1)}, u32[]{:S(2)}, u32[]{:S(2)}) %all-to-all-start.5) | async-done | bytes 1048608 | tf_op jit(solution)/shard_map/all_to_all | solution.py:390
  108.4 4.0 %shard_map.170 = (bf16[256,512]{1,0:T(8,128)(2,1)}, bf16[256,512]{1,0:T(8,128)(2,1)}, bf16[128,512]{1,0:T(8,128)(2,1)}, bf16[128,512]{1,0:T(8,128)(2,1)}, bf16[1...) custom-call(s32[1]{0:T(128)} %bitcast.core_ref, bf16[2,2,256,512]{3,2,1,0:T(8,128)(2,1)} %copy-done.1, ...), custom_call_target="tpu_custom_call" | custom-call | flops 603979776 | bytes 5242880 | tf_op jit(solution)/shard_map/pallas_call | solution.py:197
  112.4 16.1 %all-to-all-start.6 = ((bf16[32,16,128]{2,1,0:T(8,128)(2,1)}), bf16[32,16,128]{2,1,0:T(8,128)(2,1)S(1)}, u32[]{:S(2)}, u32[]{:S(2)}) async-start(bf16[32,16,128]{2,1,0:T(8,128)(2,1)} %get-tuple-element.40), calls=%async_computation.6 | async-start | bytes 262144 | tf_op jit(solution)/shard_map/all_to_all | solution.py:396
  128.5 8.9 %collective-permute-start.2 = (bf16[256,512]{1,0:T(8,128)(2,1)}, bf16[256,512]{1,0:T(8,128)(2,1)S(1)}, u32[]{:S(2)}, u32[]{:S(2)}) collective-permute-start(bf16[256,512]{1,0:T(8,128)(2,1)} %get-tuple-element.30), channel_id=1, source_target_pairs={{0,8},{8,0},{1,9},{9,1},{2,10},{10,2},{3,11},{11,3},{4,12},{12,4},... | collective-permute-start | bytes 786440 | tf_op jit(solution)/shard_map/ppermute | solution.py:399
  137.4 1.9 %collective-permute-start.3 = (bf16[128,512]{1,0:T(8,128)(2,1)}, bf16[128,512]{1,0:T(8,128)(2,1)S(1)}, u32[]{:S(2)}, u32[]{:S(2)}) collective-permute-start(bf16[128,512]{1,0:T(8,128)(2,1)} %get-tuple-element.32), channel_id=1, source_target_pairs={{16,8},{32,24},{48,40},{64,56},{80,72},{96,88},{112,104},{128,120}... | collective-permute-start | bytes 393224 | tf_op jit(solution)/shard_map/ppermute | solution.py:401
  139.3 1.3 collective-permute-start.4
  142.6 4.3 %shard_map.171 = (f32[384,1024]{1,0:T(8,128)}, f32[256,1024]{1,0:T(8,128)}) custom-call(f32[384,1024]{1,0:T(8,128)} %shard_map.167.freq_ref, bf16[2,1024,128]{2,1,0:T(8,128)(2,1)} %bitcast.43, bf16[2,384,128]{2,1,0:T(8,128)(2,1)} %constant.34.clone.forward_ref, bf16[2,256,384]{2,1,0:T(8,128)(2,1)} %constant.35.clone.inv_ref), custom_call_target="tpu_custom_call" | custom-call | flops 1024 | bytes 1024 | tf_op jit(solution)/shard_map/pallas_call | solution.py:232
  148.1 5.2 %shard_map.172 = (bf16[256,1024]{1,0:T(8,128)(2,1)}, bf16[256,1024]{1,0:T(8,128)(2,1)}) custom-call(s32[1]{0:T(128)} %bitcast.core_ref, bf16[256,512]{1,0:T(8,128)(2,1)} %get-tuple-element.29.keep_ref, bf16[256,512]{1,0:T(8,128)(2,1)} %copy-done.6, bf16[128,512]{1,0:T(8,128)(2,1)} %get-tuple-element.31.inner_ref, bf16[128,512]{1,0:T(8,128)(2,1)} %copy-done.7, ...), custom_call_target="tpu_custom_call" | custom-call | flops 1024 | bytes 1024 | tf_op jit(solution)/shard_map/pallas_call | solution.py:293
  (53 shorter events, 14.0 us)
Async XLA Ops:
  7.2 15.4 %copy-start.4 = (bf16[256,256]{1,0:T(8,128)(2,1)S(1)}, bf16[256,256]{1,0:T(8,128)(2,1)}, u32[]{:S(2)}) copy-start(bf16[256,256]{1,0:T(8,128)(2,1)} %constant.30.clone.place_ref) | copy-start | bytes 393220
  9.1 11.4 %all-to-all-start = ((bf16[2,80,512]{2,1,0:T(8,128)(2,1)}), bf16[2,80,512]{2,1,0:T(8,128)(2,1)S(1)}, u32[]{:S(2)}, u32[]{:S(2)}) async-start(bf16[2,80,512]{2,1,0:T(8,128)(2,1)} %shard_map.166), calls=%async_computation | async-start | bytes 327680 | tf_op jit(solution)/shard_map/all_to_all | solution.py:362
  19.4 68.6 %all-gather.3.cloned.1.call-start = ((), (), s32[]{:S(2)}) async-start(), calls=%async_computation.7 | async-start | bytes 2785280 | tf_op jit(solution)/shard_map/all_gather | solution.py:366
  20.5 0.7 copy-start.5
  22.6 1.0 copy-start.3
  24.7 5.0 %copy-start.2 = (bf16[256,1024]{1,0:T(8,128)(2,1)S(1)}, bf16[256,1024]{1,0:T(8,128)(2,1)}, u32[]{:S(2)}) copy-start(bf16[256,1024]{1,0:T(8,128)(2,1)} %param.17) | copy-start | bytes 1572868
  25.8 5.9 %all-to-all-start.2 = ((bf16[2,2,256,512]{3,2,1,0:T(8,128)(2,1)}), bf16[2,2,256,512]{3,2,1,0:T(8,128)(2,1)S(1)}, u32[]{:S(2)}, u32[]{:S(2)}) async-start(bf16[2,2,256,512]{3,2,1,0:T(8,128)(2,1)} %bitcast.8), calls=%async_computation.2 | async-start | bytes 2097152 | tf_op jit(solution)/shard_map/all_to_all | solution.py:373
  29.7 11.7 %collective-permute-start = (bf16[128,1024]{1,0:T(8,128)(2,1)S(1)}, bf16[128,1024]{1,0:T(8,128)(2,1)S(1)}, u32[]{:S(2)}, u32[]{:S(2)}) collective-permute-start(bf16[128,1024]{1,0:T(8,128)(2,1)S(1)} %slice.9), channel_id=1, source_target_pairs={{0,8},{8,16},{16,24},{24,32},{32,40},{40,48},{48,56},{56,64},{64,7... | collective-permute-start | bytes 786440 | tf_op jit(solution)/shard_map/ppermute | solution.py:370
  31.7 6.1 %copy-start = (bf16[2,2,256,512]{3,2,1,0:T(8,128)(2,1)}, bf16[2,2,256,512]{3,2,1,0:T(8,128)(2,1)S(1)}, u32[]{:S(2)}) copy-start(bf16[2,2,256,512]{3,2,1,0:T(8,128)(2,1)S(1)} %all-to-all-done.2.tok_ref) | copy-start | bytes 3145732
  31.7 6.1 %collective-permute-start.1 = (bf16[128,512]{1,0:T(8,128)(2,1)S(1)}, bf16[128,512]{1,0:T(8,128)(2,1)S(1)}, u32[]{:S(2)}, u32[]{:S(2)}) collective-permute-start(bf16[128,512]{1,0:T(8,128)(2,1)S(1)} %slice_bitcast_fusion.1), channel_id=1, source_target_pairs={{0,16},{16,32},{32,48},{48,64},{64,80},{80,96},{96,112},{112,128},... | collective-permute-start | bytes 393224 | tf_op jit(solution)/shard_map/ppermute | solution.py:377
  33.9 11.7 %all-to-all-start.1 = ((bf16[2,2,256,128]{3,1,2,0:T(2,128)(2,1)}), bf16[2,2,256,128]{3,1,2,0:T(2,128)(2,1)S(1)}, u32[]{:S(2)}, u32[]{:S(2)}) async-start(bf16[2,2,256,128]{3,1,2,0:T(2,128)(2,1)} %copy.29), calls=%async_computation.1 | async-start | bytes 524288 | tf_op jit(solution)/shard_map/all_to_all | solution.py:367
  37.8 0.7 copy-start.9
  93.7 13.7 %all-to-all-start.5 = ((bf16[2,2,256,512]{3,2,1,0:T(8,128)(2,1)}), bf16[2,2,256,512]{3,2,1,0:T(8,128)(2,1)S(1)}, u32[]{:S(2)}, u32[]{:S(2)}) async-start(bf16[2,2,256,512]{3,2,1,0:T(8,128)(2,1)} %bitcast.44), calls=%async_computation.5 | async-start | bytes 2097152 | tf_op jit(solution)/shard_map/all_to_all | solution.py:390
  98.7 42.0 %collective-permute-start.5 = (bf16[2,16,2,16,128]{4,3,2,1,0:T(8,128)(2,1)S(1)}, bf16[2,16,2,16,128]{4,3,2,1,0:T(8,128)(2,1)S(1)}, u32[]{:S(2)}, u32[]{:S(2)}) collective-permute-start(bf16[2,16,2,16,128]{4,3,2,1,0:T(8,128)(2,1)S(1)} %bitcast_bitcast_fusion), channel_id=1, source_target_pairs={{0,16},{16,0},{1,17},{17,1},{2,18},{18,2},{3,19},{19,3},{4,20},{20... | collective-permute-start | bytes 786440 | tf_op jit(solution)/shard_map/ppermute | solution.py:405
  107.4 1.0 copy-start.1
  112.4 40.9 %all-to-all-start.6 = ((bf16[32,16,128]{2,1,0:T(8,128)(2,1)}), bf16[32,16,128]{2,1,0:T(8,128)(2,1)S(1)}, u32[]{:S(2)}, u32[]{:S(2)}) async-start(bf16[32,16,128]{2,1,0:T(8,128)(2,1)} %get-tuple-element.40), calls=%async_computation.6 | async-start | bytes 262144 | tf_op jit(solution)/shard_map/all_to_all | solution.py:396
  128.5 18.9 %collective-permute-start.2 = (bf16[256,512]{1,0:T(8,128)(2,1)}, bf16[256,512]{1,0:T(8,128)(2,1)S(1)}, u32[]{:S(2)}, u32[]{:S(2)}) collective-permute-start(bf16[256,512]{1,0:T(8,128)(2,1)} %get-tuple-element.30), channel_id=1, source_target_pairs={{0,8},{8,0},{1,9},{9,1},{2,10},{10,2},{3,11},{11,3},{4,12},{12,4},... | collective-permute-start | bytes 786440 | tf_op jit(solution)/shard_map/ppermute | solution.py:399
  137.4 9.5 %collective-permute-start.3 = (bf16[128,512]{1,0:T(8,128)(2,1)}, bf16[128,512]{1,0:T(8,128)(2,1)S(1)}, u32[]{:S(2)}, u32[]{:S(2)}) collective-permute-start(bf16[128,512]{1,0:T(8,128)(2,1)} %get-tuple-element.32), channel_id=1, source_target_pairs={{16,8},{32,24},{48,40},{64,56},{80,72},{96,88},{112,104},{128,120}... | collective-permute-start | bytes 393224 | tf_op jit(solution)/shard_map/ppermute | solution.py:401
  139.3 8.0 %collective-permute-start.4 = (bf16[128,512]{1,0:T(8,128)(2,1)}, bf16[128,512]{1,0:T(8,128)(2,1)S(1)}, u32[]{:S(2)}, u32[]{:S(2)}) collective-permute-start(bf16[128,512]{1,0:T(8,128)(2,1)} %get-tuple-element.33), channel_id=1, source_target_pairs={{24,8},{40,24},{56,40},{72,56},{88,72},{104,88},{120,104},{136,120... | collective-permute-start | bytes 393224 | tf_op jit(solution)/shard_map/ppermute | solution.py:402
  146.9 0.6 copy-start.7
  147.4 0.7 copy-start.8
  147.4 0.7 copy-start.6
Sparse Core Ops, SparseCore 0:
  22.8 65.0 all-gather.2

commit v12 on v11

--- a/solution.py
+++ b/solution.py
@@ -361,8 +361,10 @@
     message = send_part(out_weight.T, filter_taps.T, place)
     block = lax.all_to_all(message, "c", split_axis=0, concat_axis=0)
 
+    block, out_grad, signal, gate_input = lax.optimization_barrier(
+        (block, out_grad, signal, gate_input)
+    )
     cols = out_grad.reshape(TOK, 2, 2, K).transpose(2, 1, 0, 3)
-    block, cols, signal, gate_input = lax.optimization_barrier((block, cols, signal, gate_input))
     weights = lax.all_gather(block, "z", axis=0, tiled=False)
     cols = lax.all_to_all(cols, "h", split_axis=0, concat_axis=0)
 

time: 164 us -> 164 us (level)
  blocking collectives: 38.3 us -> 50.6 us
  starting transfers between devices: 58.1 us -> 48.9 us
  waiting for transfers between devices: 6.74 us -> 4.58 us
  local copies, waits for them, and re-layouts: 10.8 us -> 9.09 us
    all_to_all x0 -> x1, blocking collectives: none -> 12.2 us  [on_device(): block = lax.all_to_all(message, 'c', split_axis=0, concat_axis=0)]
    all_to_all x1 -> x0, starting transfers between devices: 10.3 us -> none  [on_device(): block = lax.all_to_all(message, 'c', split_axis=0, concat_axis=0)]
    ppermute x1, starting transfers between devices: 8.9 us -> 4.36 us  [on_device(): other = lax.ppermute(send, 'c', [(0, 1), (1, 0)])]
    all_to_all x1, starting transfers between devices: 16.1 us -> 19.7 us  [on_device(): tap_grad = lax.all_to_all(tap_grad, chips, split_axis=0, concat_axis=0)]
    all_gather x1, waiting for transfers between devices: 2.13 us -> 0.01 us  [on_device(): weights = lax.all_gather(block, 'z', axis=0, tiled=False)]
    unnamed x21 -> x20, local copies, waits for them, and re-layouts: 4.39 us -> 2.52 us
    all_to_all x1, starting transfers between devices: 4 us -> 5.85 us  [on_device(): lax.all_to_all(partial.reshape(2, 2, TOK, 512), 'h', split_axis=0, concat...]
  transfers between devices with their start and end apart: 12 -> 11, of which waited for: 4 -> 3; matrix products, arithmetic and copies ran while one was open for 7% -> 7% of each run, Pallas kernels for 12% -> 12%
where the time goes in v12:
time: 164 us; the launch traced here: 161 us
  blocking collectives  50.6 us (31%)
  starting transfers between devices  48.9 us (30%)
  Pallas kernels  27.3 us (17%)
  between operations  14.3 us (9%)
  local copies, waits for them, and re-layouts  9.09 us (6%)
  other arithmetic  4.59 us (3%)
  waiting for transfers between devices  4.58 us (3%)
    all_to_all x1, blocking collectives, on_device(): lax.all_to_all(jnp.broadcast_to(cols[None], (8, 2, 2, TOK, K)), ('x', 'l'...  30.4 us
    all_to_all x1, starting transfers between devices, on_device(): tap_grad = lax.all_to_all(tap_grad, chips, split_axis=0, concat_axis=0)  19.7 us
    all_to_all x1, blocking collectives, on_device(): block = lax.all_to_all(message, 'c', split_axis=0, concat_axis=0)  12.2 us
    all_to_all x1, blocking collectives, on_device(): lax.all_to_all(jnp.broadcast_to(cols[None], (2, 8, 2, 2, TOK, K)), 'c', s...  8.11 us
    all_to_all x1, starting transfers between devices, on_device(): lax.all_to_all(partial.reshape(2, 2, TOK, 512), 'h', split_axis=0, concat...  5.85 us
    pallas_call x1, Pallas kernels, product(): pl.pallas_call(product_kernel, grid=(2,), in_specs=[pl.BlockSpec((2, 8, 1...  5.68 us
    pallas_call x1, Pallas kernels, out_part(): pl.pallas_call(out_kernel, grid=(TILES,), in_specs=[scalar(), half, half,...  5.23 us
    ppermute x1, starting transfers between devices, on_device(): more = lax.ppermute(taps, 'h', [(0, 1), (1, 0)])  4.88 us
  transfers between devices with their start and end apart: 11, of which 3 were waited for; matrix products, arithmetic and copies ran while one was open for 7% of the time, Pallas kernels for 12%

profile of v12, /device:TPU:1, one launch (start us, length us, event | category | flops | bytes accessed | tf_op | source)
XLA Modules:
  0.0 160.9 jit_solution(7238593270093202009)
XLA Ops:
  7.2 1.9 %shard_map.166 = bf16[2,80,512]{2,1,0:T(8,128)(2,1)} custom-call(bf16[64,1024]{1,0:T(8,128)(2,1)} %bitcast.46, f32[16,128]{1,0:T(8,128)} %bitcast.50, bf16[256,256]{1,0:T(8,128)(2,1)} %constant.30.clone.place_ref), custom_call_target="tpu_custom_call" | custom-call | flops 33554432 | bytes 524288 | tf_op jit(solution)/shard_map/pallas_call | solution.py:340
  9.1 12.2 %all_to_all.35 = bf16[2,80,512]{2,1,0:T(8,128)(2,1)} all-to-all(bf16[2,80,512]{2,1,0:T(8,128)(2,1)} %shard_map.166), channel_id=1, replica_groups=mesh['z'=16,'h'=2,'c'=2,'x'=4,'l'=2] {'c'}, dimensions={0} | all-to-all | bytes 327680 | tf_op jit(solution)/shard_map/all_to_all | solution.py:362
  21.3 1.4 reshape.46
  22.6 1.2 convolution_convert_fusion.1
  26.7 3.9 %all-to-all-start.2 = ((bf16[2,2,256,512]{3,2,1,0:T(8,128)(2,1)}), bf16[2,2,256,512]{3,2,1,0:T(8,128)(2,1)S(1)}, u32[]{:S(2)}, u32[]{:S(2)}) async-start(bf16[2,2,256,512]{3,2,1,0:T(8,128)(2,1)} %bitcast.8), calls=%async_computation.2 | async-start | bytes 2097152 | tf_op jit(solution)/shard_map/all_to_all | solution.py:375
  30.7 1.9 %collective-permute-start = (bf16[128,1024]{1,0:T(8,128)(2,1)S(1)}, bf16[128,1024]{1,0:T(8,128)(2,1)S(1)}, u32[]{:S(2)}, u32[]{:S(2)}) collective-permute-start(bf16[128,1024]{1,0:T(8,128)(2,1)S(1)} %slice.9), channel_id=1, source_target_pairs={{0,8},{8,16},{16,24},{24,32},{32,40},{40,48},{48,56},{56,64},{64,7... | collective-permute-start | bytes 786440 | tf_op jit(solution)/shard_map/ppermute | solution.py:372
  32.6 1.3 collective-permute-start.1
  35.0 3.6 %all-to-all-start.1 = ((bf16[2,2,256,128]{3,1,2,0:T(2,128)(2,1)}), bf16[2,2,256,128]{3,1,2,0:T(2,128)(2,1)S(1)}, u32[]{:S(2)}, u32[]{:S(2)}) async-start(bf16[2,2,256,128]{3,1,2,0:T(2,128)(2,1)} %copy.29), calls=%async_computation.1 | async-start | bytes 524288 | tf_op jit(solution)/shard_map/all_to_all | solution.py:369
  39.3 3.0 %shard_map.168.freq_ref = f32[2,384,512]{2,1,0:T(8,128)} custom-call(bf16[128,512]{1,0:T(8,128)(2,1)} %copy-done.9, bf16[2,2,256,512]{3,2,1,0:T(8,128)(2,1)} %copy-done, bf16[2,384,384]{2,1,0:T(8,128)(2,1)} %constant.31.clone.forward_ref), custom_call_target="tpu_custom_call" | custom-call | flops 603979776 | bytes 3145728 | tf_op jit(solution)/shard_map/pallas_call | solution.py:147
  43.3 3.1 %shard_map.167.freq_ref = f32[384,1024]{1,0:T(8,128)} custom-call(bf16[384,1024]{1,0:T(8,128)(2,1)} %pad_maximum_fusion.1.window_ref, bf16[2,384,384]{2,1,0:T(8,128)(2,1)} %constant.31.clone.forward_ref), custom_call_target="tpu_custom_call" | custom-call | flops 603979776 | bytes 3145728 | tf_op jit(solution)/shard_map/pallas_call | solution.py:120
  47.0 30.4 %all_to_all.36 = bf16[8,2,2,256,128]{4,3,2,1,0:T(8,128)(2,1)S(1)} all-to-all(bf16[8,2,2,256,128]{4,3,2,1,0:T(8,128)(2,1)S(1)} %broadcast_in_dim.4), channel_id=1, replica_groups=mesh['z'=16,'h'=2,'c'=2,'x'=4,'l'=2] {'x','l'}, dimensions={0} | all-to-all | bytes 4194304 | tf_op jit(solution)/shard_map/all_to_all | solution.py:383
  77.4 1.4 broadcast_in_dim.5
  78.8 8.1 %all_to_all.37.cols_ref = bf16[2,8,2,2,256,128]{5,4,3,2,1,0:T(8,128)(2,1)} all-to-all(bf16[2,8,2,2,256,128]{5,4,3,2,1,0:T(8,128)(2,1)S(1)} %broadcast_in_dim.5), channel_id=1, replica_groups=mesh['z'=16,'h'=2,'c'=2,'x'=4,'l'=2] {'c'}, dimensions={0} | all-to-all | bytes 8388608 | tf_op jit(solution)/shard_map/all_to_all | solution.py:386
  86.9 5.7 %shard_map.169 = bf16[4,256,512]{2,1,0:T(8,128)(2,1)} custom-call(bf16[2,8,2,2,256,128]{5,4,3,2,1,0:T(8,128)(2,1)} %all_to_all.37.cols_ref, bf16[16,2,80,512]{3,2,1,0:T(8,128)(2,1)} %bitcast.47), custom_call_target="tpu_custom_call" | custom-call | flops 2147483648 | bytes 8388608 | tf_op jit(solution)/shard_map/pallas_call | solution.py:84
  92.6 5.9 %all-to-all-start.5 = ((bf16[2,2,256,512]{3,2,1,0:T(8,128)(2,1)}), bf16[2,2,256,512]{3,2,1,0:T(8,128)(2,1)S(1)}, u32[]{:S(2)}, u32[]{:S(2)}) async-start(bf16[2,2,256,512]{3,2,1,0:T(8,128)(2,1)} %bitcast.44), calls=%async_computation.5 | async-start | bytes 2097152 | tf_op jit(solution)/shard_map/all_to_all | solution.py:392
  99.4 4.9 %collective-permute-start.5 = (bf16[2,16,2,16,128]{4,3,2,1,0:T(8,128)(2,1)S(1)}, bf16[2,16,2,16,128]{4,3,2,1,0:T(8,128)(2,1)S(1)}, u32[]{:S(2)}, u32[]{:S(2)}) collective-permute-start(bf16[2,16,2,16,128]{4,3,2,1,0:T(8,128)(2,1)S(1)} %bitcast_bitcast_fusion), channel_id=1, source_target_pairs={{0,16},{16,0},{1,17},{17,1},{2,18},{18,2},{3,19},{19,3},{4,20},{20... | collective-permute-start | bytes 786440 | tf_op jit(solution)/shard_map/ppermute | solution.py:407
  104.3 3.8 %all-to-all-done.5.mix_ref = bf16[2,2,256,512]{3,2,1,0:T(8,128)(2,1)S(1)} async-done(((bf16[2,2,256,512]{3,2,1,0:T(8,128)(2,1)}), bf16[2,2,256,512]{3,2,1,0:T(8,128)(2,1)S(1)}, u32[]{:S(2)}, u32[]{:S(2)}) %all-to-all-start.5) | async-done | bytes 1048608 | tf_op jit(solution)/shard_map/all_to_all | solution.py:392
  109.2 4.0 %shard_map.170 = (bf16[256,512]{1,0:T(8,128)(2,1)}, bf16[256,512]{1,0:T(8,128)(2,1)}, bf16[128,512]{1,0:T(8,128)(2,1)}, bf16[128,512]{1,0:T(8,128)(2,1)}, bf16[1...) custom-call(s32[1]{0:T(128)} %bitcast.core_ref, bf16[2,2,256,512]{3,2,1,0:T(8,128)(2,1)} %copy-done.1, ...), custom_call_target="tpu_custom_call" | custom-call | flops 603979776 | bytes 5242880 | tf_op jit(solution)/shard_map/pallas_call | solution.py:197
  113.2 19.7 %all-to-all-start.6 = ((bf16[32,16,128]{2,1,0:T(8,128)(2,1)}), bf16[32,16,128]{2,1,0:T(8,128)(2,1)S(1)}, u32[]{:S(2)}, u32[]{:S(2)}) async-start(bf16[32,16,128]{2,1,0:T(8,128)(2,1)} %get-tuple-element.40), calls=%async_computation.6 | async-start | bytes 262144 | tf_op jit(solution)/shard_map/all_to_all | solution.py:398
  132.9 4.4 %collective-permute-start.2 = (bf16[256,512]{1,0:T(8,128)(2,1)}, bf16[256,512]{1,0:T(8,128)(2,1)S(1)}, u32[]{:S(2)}, u32[]{:S(2)}) collective-permute-start(bf16[256,512]{1,0:T(8,128)(2,1)} %get-tuple-element.30), channel_id=1, source_target_pairs={{0,8},{8,0},{1,9},{9,1},{2,10},{10,2},{3,11},{11,3},{4,12},{12,4},... | collective-permute-start | bytes 786440 | tf_op jit(solution)/shard_map/ppermute | solution.py:401
  137.3 1.9 %collective-permute-start.3 = (bf16[128,512]{1,0:T(8,128)(2,1)}, bf16[128,512]{1,0:T(8,128)(2,1)S(1)}, u32[]{:S(2)}, u32[]{:S(2)}) collective-permute-start(bf16[128,512]{1,0:T(8,128)(2,1)} %get-tuple-element.32), channel_id=1, source_target_pairs={{16,8},{32,24},{48,40},{64,56},{80,72},{96,88},{112,104},{128,120}... | collective-permute-start | bytes 393224 | tf_op jit(solution)/shard_map/ppermute | solution.py:403
  139.2 1.3 collective-permute-start.4
  142.5 4.3 %shard_map.171 = (f32[384,1024]{1,0:T(8,128)}, f32[256,1024]{1,0:T(8,128)}) custom-call(f32[384,1024]{1,0:T(8,128)} %shard_map.167.freq_ref, bf16[2,1024,128]{2,1,0:T(8,128)(2,1)} %bitcast.43, bf16[2,384,128]{2,1,0:T(8,128)(2,1)} %constant.34.clone.forward_ref, bf16[2,256,384]{2,1,0:T(8,128)(2,1)} %constant.35.clone.inv_ref), custom_call_target="tpu_custom_call" | custom-call | flops 1024 | bytes 1024 | tf_op jit(solution)/shard_map/pallas_call | solution.py:232
  148.2 5.2 %shard_map.172 = (bf16[256,1024]{1,0:T(8,128)(2,1)}, bf16[256,1024]{1,0:T(8,128)(2,1)}) custom-call(s32[1]{0:T(128)} %bitcast.core_ref, bf16[256,512]{1,0:T(8,128)(2,1)} %get-tuple-element.29.keep_ref, bf16[256,512]{1,0:T(8,128)(2,1)} %copy-done.6, bf16[128,512]{1,0:T(8,128)(2,1)} %get-tuple-element.31.inner_ref, bf16[128,512]{1,0:T(8,128)(2,1)} %copy-done.7, ...), custom_call_target="tpu_custom_call" | custom-call | flops 1024 | bytes 1024 | tf_op jit(solution)/shard_map/pallas_call | solution.py:293
  (52 shorter events, 12.0 us)
Async XLA Ops:
  7.2 79.7 %all-gather.3.cloned.1.call-start = ((), (), s32[]{:S(2)}) async-start(), calls=%async_computation.7 | async-start | bytes 2785280 | tf_op jit(solution)/shard_map/all_gather | solution.py:368
  22.6 1.8 %copy-start.3 = (bf16[256,1024]{1,0:T(8,128)(2,1)S(1)}, bf16[256,1024]{1,0:T(8,128)(2,1)}, u32[]{:S(2)}) copy-start(bf16[256,1024]{1,0:T(8,128)(2,1)} %gate_in_ref) | copy-start | bytes 1572868
  23.9 0.9 copy-start.4
  25.6 5.0 %copy-start.2 = (bf16[256,1024]{1,0:T(8,128)(2,1)S(1)}, bf16[256,1024]{1,0:T(8,128)(2,1)}, u32[]{:S(2)}) copy-start(bf16[256,1024]{1,0:T(8,128)(2,1)} %param.17) | copy-start | bytes 1572868
  25.6 8.3 %copy-start.5 = (bf16[256,512]{1,0:T(8,128)(2,1)S(1)}, bf16[256,512]{1,0:T(8,128)(2,1)}, u32[]{:S(2)}) copy-start(bf16[256,512]{1,0:T(8,128)(2,1)} %param.15) | copy-start | bytes 786436
  26.7 5.9 %all-to-all-start.2 = ((bf16[2,2,256,512]{3,2,1,0:T(8,128)(2,1)}), bf16[2,2,256,512]{3,2,1,0:T(8,128)(2,1)S(1)}, u32[]{:S(2)}, u32[]{:S(2)}) async-start(bf16[2,2,256,512]{3,2,1,0:T(8,128)(2,1)} %bitcast.8), calls=%async_computation.2 | async-start | bytes 2097152 | tf_op jit(solution)/shard_map/all_to_all | solution.py:375
  30.7 11.7 %collective-permute-start = (bf16[128,1024]{1,0:T(8,128)(2,1)S(1)}, bf16[128,1024]{1,0:T(8,128)(2,1)S(1)}, u32[]{:S(2)}, u32[]{:S(2)}) collective-permute-start(bf16[128,1024]{1,0:T(8,128)(2,1)S(1)} %slice.9), channel_id=1, source_target_pairs={{0,8},{8,16},{16,24},{24,32},{32,40},{40,48},{48,56},{56,64},{64,7... | collective-permute-start | bytes 786440 | tf_op jit(solution)/shard_map/ppermute | solution.py:372
  32.6 6.1 %copy-start = (bf16[2,2,256,512]{3,2,1,0:T(8,128)(2,1)}, bf16[2,2,256,512]{3,2,1,0:T(8,128)(2,1)S(1)}, u32[]{:S(2)}) copy-start(bf16[2,2,256,512]{3,2,1,0:T(8,128)(2,1)S(1)} %all-to-all-done.2.tok_ref) | copy-start | bytes 3145732
  32.6 6.1 %collective-permute-start.1 = (bf16[128,512]{1,0:T(8,128)(2,1)S(1)}, bf16[128,512]{1,0:T(8,128)(2,1)S(1)}, u32[]{:S(2)}, u32[]{:S(2)}) collective-permute-start(bf16[128,512]{1,0:T(8,128)(2,1)S(1)} %slice_bitcast_fusion.1), channel_id=1, source_target_pairs={{0,16},{16,32},{32,48},{48,64},{64,80},{80,96},{96,112},{112,128},... | collective-permute-start | bytes 393224 | tf_op jit(solution)/shard_map/ppermute | solution.py:379
  35.0 11.5 %all-to-all-start.1 = ((bf16[2,2,256,128]{3,1,2,0:T(2,128)(2,1)}), bf16[2,2,256,128]{3,1,2,0:T(2,128)(2,1)S(1)}, u32[]{:S(2)}, u32[]{:S(2)}) async-start(bf16[2,2,256,128]{3,1,2,0:T(2,128)(2,1)} %copy.29), calls=%async_computation.1 | async-start | bytes 524288 | tf_op jit(solution)/shard_map/all_to_all | solution.py:369
  38.7 0.7 copy-start.9
  92.6 15.6 %all-to-all-start.5 = ((bf16[2,2,256,512]{3,2,1,0:T(8,128)(2,1)}), bf16[2,2,256,512]{3,2,1,0:T(8,128)(2,1)S(1)}, u32[]{:S(2)}, u32[]{:S(2)}) async-start(bf16[2,2,256,512]{3,2,1,0:T(8,128)(2,1)} %bitcast.44), calls=%async_computation.5 | async-start | bytes 2097152 | tf_op jit(solution)/shard_map/all_to_all | solution.py:392
  99.4 41.1 %collective-permute-start.5 = (bf16[2,16,2,16,128]{4,3,2,1,0:T(8,128)(2,1)S(1)}, bf16[2,16,2,16,128]{4,3,2,1,0:T(8,128)(2,1)S(1)}, u32[]{:S(2)}, u32[]{:S(2)}) collective-permute-start(bf16[2,16,2,16,128]{4,3,2,1,0:T(8,128)(2,1)S(1)} %bitcast_bitcast_fusion), channel_id=1, source_target_pairs={{0,16},{16,0},{1,17},{17,1},{2,18},{18,2},{3,19},{19,3},{4,20},{20... | collective-permute-start | bytes 786440 | tf_op jit(solution)/shard_map/ppermute | solution.py:407
  108.2 1.0 copy-start.1
  113.2 40.2 %all-to-all-start.6 = ((bf16[32,16,128]{2,1,0:T(8,128)(2,1)}), bf16[32,16,128]{2,1,0:T(8,128)(2,1)S(1)}, u32[]{:S(2)}, u32[]{:S(2)}) async-start(bf16[32,16,128]{2,1,0:T(8,128)(2,1)} %get-tuple-element.40), calls=%async_computation.6 | async-start | bytes 262144 | tf_op jit(solution)/shard_map/all_to_all | solution.py:398
  132.9 14.5 %collective-permute-start.2 = (bf16[256,512]{1,0:T(8,128)(2,1)}, bf16[256,512]{1,0:T(8,128)(2,1)S(1)}, u32[]{:S(2)}, u32[]{:S(2)}) collective-permute-start(bf16[256,512]{1,0:T(8,128)(2,1)} %get-tuple-element.30), channel_id=1, source_target_pairs={{0,8},{8,0},{1,9},{9,1},{2,10},{10,2},{3,11},{11,3},{4,12},{12,4},... | collective-permute-start | bytes 786440 | tf_op jit(solution)/shard_map/ppermute | solution.py:401
  137.3 9.5 %collective-permute-start.3 = (bf16[128,512]{1,0:T(8,128)(2,1)}, bf16[128,512]{1,0:T(8,128)(2,1)S(1)}, u32[]{:S(2)}, u32[]{:S(2)}) collective-permute-start(bf16[128,512]{1,0:T(8,128)(2,1)} %get-tuple-element.32), channel_id=1, source_target_pairs={{16,8},{32,24},{48,40},{64,56},{80,72},{96,88},{112,104},{128,120}... | collective-permute-start | bytes 393224 | tf_op jit(solution)/shard_map/ppermute | solution.py:403
  139.2 8.2 %collective-permute-start.4 = (bf16[128,512]{1,0:T(8,128)(2,1)}, bf16[128,512]{1,0:T(8,128)(2,1)S(1)}, u32[]{:S(2)}, u32[]{:S(2)}) collective-permute-start(bf16[128,512]{1,0:T(8,128)(2,1)} %get-tuple-element.33), channel_id=1, source_target_pairs={{24,8},{40,24},{56,40},{72,56},{88,72},{104,88},{120,104},{136,120... | collective-permute-start | bytes 393224 | tf_op jit(solution)/shard_map/ppermute | solution.py:404
  146.8 0.6 copy-start.7
  147.5 0.7 copy-start.8
  147.5 0.8 copy-start.6
Sparse Core Ops, SparseCore 0:
  21.4 65.1 all-gather.2

commit v13 on v12

--- a/solution.py
+++ b/solution.py
@@ -73,28 +73,30 @@
     )
 
 
-def product_kernel(cols_ref, weight_ref, out_ref):
+def product_kernel(h_ref, cols_ref, weight_ref, out_ref):
     weight = weight_ref[:, :, :64].reshape(16 * K, 512)
-    for b in range(2):
-        rows = jnp.concatenate([cols_ref[b, i, 0, j] for i in range(8) for j in range(2)], axis=1)
-        out_ref[b] = dot(rows, weight).astype(BF)
-
-
-def product(cols, weights):
+    rows = jnp.concatenate([cols_ref[0, i, 0, j] for i in range(8) for j in range(2)], axis=1)
+    out_ref[0] = dot(rows, weight).astype(BF)
+
+
+def product(h, cols, weights):
     return pl.pallas_call(
         product_kernel,
-        grid=(2,),
-        in_specs=[
-            pl.BlockSpec((2, 8, 1, 2, TOK, K), lambda i: (0, 0, i, 0, 0, 0)),
-            pl.BlockSpec((16, 2, 80, 512), lambda i: (0, 0, 0, 0)),
-        ],
-        out_specs=pl.BlockSpec((2, TOK, 512), lambda i: (i, 0, 0)),
-        out_shape=jax.ShapeDtypeStruct((4, TOK, 512), BF),
+        grid_spec=pltpu.PrefetchScalarGridSpec(
+            num_scalar_prefetch=1,
+            grid=(2,),
+            in_specs=[
+                pl.BlockSpec((1, 8, 1, 2, TOK, K), lambda i, h: (i, 0, h[0], 0, 0, 0)),
+                pl.BlockSpec((16, 2, 80, 512), lambda i, h: (0, 0, 0, 0)),
+            ],
+            out_specs=pl.BlockSpec((1, TOK, 512), lambda i, h: (i, 0, 0)),
+        ),
+        out_shape=jax.ShapeDtypeStruct((2, TOK, 512), BF),
         compiler_params=params(),
         cost_estimate=pl.CostEstimate(
-            flops=2 * 1024 * 2048 * 512, bytes_accessed=8 << 20, transcendentals=0
+            flops=1024 * 2048 * 512, bytes_accessed=5 << 20, transcendentals=0
         ),
-    )(cols, weights)
+    )(h, cols, weights)
 
 
 def whole(shape):
@@ -164,6 +166,7 @@
 def grad_kernel(
     core_ref,
     mix_ref,
+    more_ref,
     tok_ref,
     freq_ref,
     own_ref,
@@ -176,8 +179,8 @@
     tap_ref,
 ):
     is_first = core_ref[0] == 0
-    early = (mix_ref[0, 0].astype(F32) + mix_ref[1, 0].astype(F32)).astype(BF).astype(F32)
-    late = (mix_ref[0, 1].astype(F32) + mix_ref[1, 1].astype(F32)).astype(BF).astype(F32)
+    early = (mix_ref[0].astype(F32) + more_ref[0].astype(F32)).astype(BF).astype(F32)
+    late = (mix_ref[1].astype(F32) + more_ref[1].astype(F32)).astype(BF).astype(F32)
     keep_ref[...] = jnp.where(is_first, early, late).astype(BF)
     send_ref[...] = jnp.where(is_first, late, early).astype(BF)
     early = early * tok_ref[0, 0].astype(F32)
@@ -191,7 +194,7 @@
     tap_ref[...] = taps.T.reshape(L // 16, 16, K).astype(tap_ref.dtype)
 
 
-def grad_part(core, mix, tokens, sig_freq, own, lag):
+def grad_part(core, mix, more, tokens, sig_freq, own, lag):
     head = pl.BlockSpec((K, L), lambda j: (0, j))
     half = pl.BlockSpec((TOK, L), lambda j: (0, j))
     return pl.pallas_call(
@@ -199,7 +202,8 @@
         grid=(TILES,),
         in_specs=[
             scalar(),
-            pl.BlockSpec((2, 2, TOK, L), lambda j: (0, 0, 0, j)),
+            pl.BlockSpec((2, TOK, L), lambda j: (0, 0, j)),
+            pl.BlockSpec((2, TOK, L), lambda j: (0, 0, j)),
             pl.BlockSpec((2, 1, TOK, L), lambda j: (0, 1, 0, j)),
             FREQ,
             whole((2, N, TOK)),
@@ -213,7 +217,7 @@
         cost_estimate=pl.CostEstimate(
             flops=2 * CH * N * (2 * TOK + 2 * K), bytes_accessed=5 << 20, transcendentals=0
         ),
-    )(core, mix, tokens, sig_freq, own, lag)
+    )(core, mix, more, tokens, sig_freq, own, lag)
 
 
 def conv_kernel(freq_ref, tap_ref, forward_ref, inv_ref, tap_freq_ref, conv_ref):
@@ -387,13 +391,13 @@
         jnp.broadcast_to(cols[None], (2, 8, 2, 2, TOK, K)), "c", split_axis=0, concat_axis=0
     )
 
-    partial = product(cols, weights)
+    h = lax.axis_index("h").reshape(1)
+    partial = product(1 - h, cols, weights)
     weights, partial = lax.optimization_barrier((weights, partial))
-    mix = lax.all_to_all(
-        partial.reshape(2, 2, TOK, 512), "h", split_axis=0, concat_axis=0
-    )
+    more = lax.ppermute(partial, "h", [(0, 1), (1, 0)])
+    mix = product(h, cols, weights)
     keep, send, first, inner, cross, tap_grad = grad_part(
-        core, mix, tokens, own_freq, fwd[:, :, K:N], inv[:, :K]
+        core, mix, more, tokens, own_freq, fwd[:, :, K:N], inv[:, :K]
     )
     tap_grad = lax.all_to_all(tap_grad, chips, split_axis=0, concat_axis=0)
     filter_grad = jnp.sum(tap_grad.astype(F32), axis=0).T
@@ -404,10 +408,10 @@
     far = lax.ppermute(first, ctx, [(i + 1, j) for i, j in follows])
 
     taps = weights[:, :, 64:, : 2 * K].reshape(16, 2, 16, 2, K).transpose(3, 0, 1, 2, 4)
-    more = lax.ppermute(taps, "h", [(0, 1), (1, 0)])
+    others = lax.ppermute(taps, "h", [(0, 1), (1, 0)])
     upper_half = lax.axis_index("h") == 0
     taps = jnp.stack(
-        [jnp.where(upper_half, taps, more), jnp.where(upper_half, more, taps)], axis=2
+        [jnp.where(upper_half, taps, others), jnp.where(upper_half, others, taps)], axis=2
     ).reshape(2, CH, K)
 
     tap_freq, conv = conv_part(sig_freq, taps, fwd[:, :, :K], inv[:, K:])

time: 164 us -> 167 us (1.018)
  waiting for transfers between devices: 4.58 us -> 33.1 us
  blocking collectives: 50.6 us -> 26.3 us
  starting transfers between devices: 48.9 us -> 45.1 us
  Pallas kernels: 27.3 us -> 30.2 us
    all_to_all x2 -> x1, waiting for transfers between devices: 3.85 us -> 30.4 us  [on_device(): lax.all_to_all(jnp.broadcast_to(cols[None], (8, 2, 2, TOK, K)), ('x', 'l'...]
    all_to_all x1, blocking collectives: 30.4 us -> 4.73 us  [on_device(): lax.all_to_all(tokens.reshape(2, 2, TOK, 512), 'c', split_axis=0, concat_...]
    all_to_all x2 -> x1, starting transfers between devices: 9.78 us -> 4.32 us  [on_device(): lax.all_to_all(jnp.broadcast_to(cols[None], (8, 2, 2, TOK, K)), ('x', 'l'...]
    pallas_call x1 -> x2, Pallas kernels: 5.68 us -> 8.44 us  [product(): pl.pallas_call(product_kernel, grid_spec=pltpu.PrefetchScalarGridSpec(num...]
    ppermute x1 -> x2, starting transfers between devices: 4.88 us -> 7.05 us  [the longest x1 5.13 us: on_device(): more = lax.ppermute(partial, 'h', [(0, 1), (1, 0)])]
    ppermute x1 -> x2, waiting for transfers between devices: 0.01 us -> 2.08 us  [the longest x1 2.08 us: on_device(): more = lax.ppermute(partial, 'h', [(0, 1), (1, 0)])]
  transfers between devices with their start and end apart: 11 -> 11, of which waited for: 3 -> 3; matrix products, arithmetic and copies ran while one was open for 7% -> 7% of each run, Pallas kernels for 12% -> 15%
where the time goes in v13:
time: 167 us; the launch traced here: 164 us
  starting transfers between devices  45.1 us (27%)
  waiting for transfers between devices  33.1 us (20%)
  Pallas kernels  30.2 us (18%)
  blocking collectives  26.3 us (16%)
  between operations  14.3 us (9%)
  local copies, waits for them, and re-layouts  10.7 us (6%)
  other arithmetic  3.57 us (2%)
    all_to_all x1, waiting for transfers between devices, on_device(): lax.all_to_all(jnp.broadcast_to(cols[None], (8, 2, 2, TOK, K)), ('x', 'l'...  30.4 us
    all_to_all x1, starting transfers between devices, on_device(): tap_grad = lax.all_to_all(tap_grad, chips, split_axis=0, concat_axis=0)  19.6 us
    all_to_all x1, blocking collectives, on_device(): block = lax.all_to_all(message, 'c', split_axis=0, concat_axis=0)  12.2 us
    all_to_all x1, blocking collectives, on_device(): lax.all_to_all(jnp.broadcast_to(cols[None], (2, 8, 2, 2, TOK, K)), 'c', s...  9.43 us
    pallas_call x2, Pallas kernels, product(): pl.pallas_call(product_kernel, grid_spec=pltpu.PrefetchScalarGridSpec(num...  8.44 us
    pallas_call x1, Pallas kernels, out_part(): pl.pallas_call(out_kernel, grid=(TILES,), in_specs=[scalar(), half, half,...  5.23 us
    ppermute x1, starting transfers between devices, on_device(): more = lax.ppermute(partial, 'h', [(0, 1), (1, 0)])  5.13 us
    all_to_all x1, blocking collectives, on_device(): lax.all_to_all(tokens.reshape(2, 2, TOK, 512), 'c', split_axis=0, concat_...  4.73 us
  transfers between devices with their start and end apart: 11, of which 3 were waited for; matrix products, arithmetic and copies ran while one was open for 7% of the time, Pallas kernels for 15%

profile of v13, /device:TPU:1, one launch (start us, length us, event | category | flops | bytes accessed | tf_op | source)
XLA Modules:
  0.0 163.8 jit_solution(7698403538313090675)
XLA Ops:
  7.2 1.9 %shard_map.166 = bf16[2,80,512]{2,1,0:T(8,128)(2,1)} custom-call(bf16[64,1024]{1,0:T(8,128)(2,1)} %bitcast.50, f32[16,128]{1,0:T(8,128)} %bitcast.51, bf16[256,256]{1,0:T(8,128)(2,1)} %constant.32.clone.place_ref), custom_call_target="tpu_custom_call" | custom-call | flops 33554432 | bytes 524288 | tf_op jit(solution)/shard_map/pallas_call | solution.py:344
  9.2 12.2 %all_to_all.30 = bf16[2,80,512]{2,1,0:T(8,128)(2,1)} all-to-all(bf16[2,80,512]{2,1,0:T(8,128)(2,1)} %shard_map.166), channel_id=1, replica_groups=mesh['z'=16,'h'=2,'c'=2,'x'=4,'l'=2] {'c'}, dimensions={0} | all-to-all | bytes 327680 | tf_op jit(solution)/shard_map/all_to_all | solution.py:366
  22.3 1.9 %collective-permute-start = (bf16[128,1024]{1,0:T(8,128)(2,1)S(1)}, bf16[128,1024]{1,0:T(8,128)(2,1)S(1)}, u32[]{:S(2)}, u32[]{:S(2)}) collective-permute-start(bf16[128,1024]{1,0:T(8,128)(2,1)S(1)} %slice.9), channel_id=1, source_target_pairs={{0,8},{8,16},{16,24},{24,32},{32,40},{40,48},{48,56},{56,64},{64,7... | collective-permute-start | bytes 786440 | tf_op jit(solution)/shard_map/ppermute | solution.py:376
  24.3 1.4 reshape.47
  27.6 4.7 %all_to_all.31.tok_ref = bf16[2,2,256,512]{3,2,1,0:T(8,128)(2,1)S(1)} all-to-all(bf16[2,2,256,512]{3,2,1,0:T(8,128)(2,1)S(1)} %bitcast.45), channel_id=1, replica_groups=mesh['z'=16,'h'=2,'c'=2,'x'=4,'l'=2] {'c'}, dimensions={0} | all-to-all | bytes 2097152 | tf_op jit(solution)/shard_map/all_to_all | solution.py:379
  32.4 1.3 collective-permute-start.1
  34.7 3.5 %all-to-all-start.1 = ((bf16[2,2,256,128]{3,1,2,0:T(2,128)(2,1)}), bf16[2,2,256,128]{3,1,2,0:T(2,128)(2,1)S(1)}, u32[]{:S(2)}, u32[]{:S(2)}) async-start(bf16[2,2,256,128]{3,1,2,0:T(2,128)(2,1)} %copy.29), calls=%async_computation.1 | async-start | bytes 524288 | tf_op jit(solution)/shard_map/all_to_all | solution.py:373
  38.9 3.0 %shard_map.168.freq_ref = f32[2,384,512]{2,1,0:T(8,128)} custom-call(bf16[128,512]{1,0:T(8,128)(2,1)} %copy-done.9, bf16[2,2,256,512]{3,2,1,0:T(8,128)(2,1)} %copy-done, bf16[2,384,384]{2,1,0:T(8,128)(2,1)} %constant.33.clone.forward_ref), custom_call_target="tpu_custom_call" | custom-call | flops 603979776 | bytes 3145728 | tf_op jit(solution)/shard_map/pallas_call | solution.py:149
  42.8 3.1 %shard_map.167.freq_ref = f32[384,1024]{1,0:T(8,128)} custom-call(bf16[384,1024]{1,0:T(8,128)(2,1)} %pad_maximum_fusion.1.window_ref, bf16[2,384,384]{2,1,0:T(8,128)(2,1)} %constant.33.clone.forward_ref), custom_call_target="tpu_custom_call" | custom-call | flops 603979776 | bytes 3145728 | tf_op jit(solution)/shard_map/pallas_call | solution.py:122
  46.0 1.8 %broadcast_in_dim.4 = bf16[8,2,2,256,128]{4,3,2,1,0:T(8,128)(2,1)} broadcast(bf16[2,2,256,128]{3,2,1,0:T(8,128)(2,1)S(1)} %copy.32), dimensions={1,2,3,4} | broadcast | bytes 2359296 | tf_op jit(solution)/shard_map/broadcast_in_dim | solution.py:388
  47.8 4.3 %all-to-all-start.3 = ((bf16[8,2,2,256,128]{4,3,2,1,0:T(8,128)(2,1)}), bf16[8,2,2,256,128]{4,3,2,1,0:T(8,128)(2,1)S(1)}, u32[]{:S(2)}, u32[]{:S(2)}) async-start(bf16[8,2,2,256,128]{4,3,2,1,0:T(8,128)(2,1)} %broadcast_in_dim.4), calls=%async_computation.3 | async-start | bytes 4194304 | tf_op jit(solution)/shard_map/all_to_all | solution.py:387
  52.1 30.4 %all-to-all-done.3 = bf16[8,2,2,256,128]{4,3,2,1,0:T(8,128)(2,1)S(1)} async-done(((bf16[8,2,2,256,128]{4,3,2,1,0:T(8,128)(2,1)}), bf16[8,2,2,256,128]{4,3,2,1,0:T(8,128)(2,1)S(1)}, u32[]{:S(2)}, u32[]{:S(2)}) %all-to-all-start.3) | async-done | bytes 2097184 | tf_op jit(solution)/shard_map/all_to_all | solution.py:387
  83.6 9.4 %all_to_all.32.cols_ref = bf16[2,8,2,2,256,128]{5,4,3,2,1,0:T(8,128)(2,1)} all-to-all(bf16[2,8,2,2,256,128]{5,4,3,2,1,0:T(8,128)(2,1)S(1)} %broadcast_in_dim.5), channel_id=1, replica_groups=mesh['z'=16,'h'=2,'c'=2,'x'=4,'l'=2] {'c'}, dimensions={0} | all-to-all | bytes 8388608 | tf_op jit(solution)/shard_map/all_to_all | solution.py:390
  93.0 4.2 %shard_map.169 = bf16[2,256,512]{2,1,0:T(8,128)(2,1)} custom-call(s32[1]{0:T(128)S(6)} %sub.3.h_ref, bf16[2,8,2,2,256,128]{5,4,3,2,1,0:T(8,128)(2,1)} %all_to_all.32.cols_ref, bf16[16,2,80,512]{3,2,1,0:T(8,128)(2,1)} %bitcast.41), custom_call_target="tpu_custom_call" | custom-call | flops 1073741824 | bytes 5242880 | tf_op jit(solution)/shard_map/pallas_call | solution.py:83
  97.2 5.1 %collective-permute-start.2 = (bf16[2,256,512]{2,1,0:T(8,128)(2,1)}, bf16[2,256,512]{2,1,0:T(8,128)(2,1)S(1)}, u32[]{:S(2)}, u32[]{:S(2)}) collective-permute-start(bf16[2,256,512]{2,1,0:T(8,128)(2,1)} %shard_map.169), channel_id=1, source_target_pairs={{0,16},{16,0},{1,17},{17,1},{2,18},{18,2},{3,19},{19,3},{4,20},{20... | collective-permute-start | bytes 1572872 | tf_op jit(solution)/shard_map/ppermute | solution.py:397
  103.4 1.9 %collective-permute-start.6 = (bf16[2,16,2,16,128]{4,3,2,1,0:T(8,128)(2,1)S(1)}, bf16[2,16,2,16,128]{4,3,2,1,0:T(8,128)(2,1)S(1)}, u32[]{:S(2)}, u32[]{:S(2)}) collective-permute-start(bf16[2,16,2,16,128]{4,3,2,1,0:T(8,128)(2,1)S(1)} %bitcast_bitcast_fusion), channel_id=1, source_target_pairs={{0,16},{16,0},{1,17},{17,1},{2,18},{18,2},{3,19},{19,3},{4,20},{20... | collective-permute-start | bytes 786440 | tf_op jit(solution)/shard_map/ppermute | solution.py:411
  105.3 4.2 %shard_map.170.mix_ref = bf16[2,256,512]{2,1,0:T(8,128)(2,1)} custom-call(s32[1]{0:T(128)} %bitcast.1.h_ref, bf16[2,8,2,2,256,128]{5,4,3,2,1,0:T(8,128)(2,1)} %all_to_all.32.cols_ref, bf16[16,2,80,512]{3,2,1,0:T(8,128)(2,1)} %bitcast.43), custom_call_target="tpu_custom_call" | custom-call | flops 1073741824 | bytes 5242880 | tf_op jit(solution)/shard_map/pallas_call | solution.py:83
  109.5 2.1 %collective-permute-done.2.more_ref = bf16[2,256,512]{2,1,0:T(8,128)(2,1)S(1)} collective-permute-done((bf16[2,256,512]{2,1,0:T(8,128)(2,1)}, bf16[2,256,512]{2,1,0:T(8,128)(2,1)S(1)}, u32[]{:S(2)}, u32[]{:S(2)}) %collective-permute-start.2) | collective-permute-done | bytes 524320 | tf_op jit(solution)/shard_map/ppermute | solution.py:397
  112.4 4.0 %shard_map.171 = (bf16[256,512]{1,0:T(8,128)(2,1)}, bf16[256,512]{1,0:T(8,128)(2,1)}, bf16[128,512]{1,0:T(8,128)(2,1)}, bf16[128,512]{1,0:T(8,128)(2,1)}, bf16[1...) custom-call(s32[1]{0:T(128)} %bitcast.core_ref, bf16[2,256,512]{2,1,0:T(8,128)(2,1)} %shard_map.170.mix_ref, ...), custom_call_target="tpu_custom_call" | custom-call | flops 603979776 | bytes 5242880 | tf_op jit(solution)/shard_map/pallas_call | solution.py:200
  116.4 19.6 %all-to-all-start.5 = ((bf16[32,16,128]{2,1,0:T(8,128)(2,1)}), bf16[32,16,128]{2,1,0:T(8,128)(2,1)S(1)}, u32[]{:S(2)}, u32[]{:S(2)}) async-start(bf16[32,16,128]{2,1,0:T(8,128)(2,1)} %get-tuple-element.40), calls=%async_computation.5 | async-start | bytes 262144 | tf_op jit(solution)/shard_map/all_to_all | solution.py:402
  136.0 4.2 %collective-permute-start.3 = (bf16[256,512]{1,0:T(8,128)(2,1)}, bf16[256,512]{1,0:T(8,128)(2,1)S(1)}, u32[]{:S(2)}, u32[]{:S(2)}) collective-permute-start(bf16[256,512]{1,0:T(8,128)(2,1)} %get-tuple-element.31), channel_id=1, source_target_pairs={{0,8},{8,0},{1,9},{9,1},{2,10},{10,2},{3,11},{11,3},{4,12},{12,4},... | collective-permute-start | bytes 786440 | tf_op jit(solution)/shard_map/ppermute | solution.py:405
  140.2 1.9 %collective-permute-start.4 = (bf16[128,512]{1,0:T(8,128)(2,1)}, bf16[128,512]{1,0:T(8,128)(2,1)S(1)}, u32[]{:S(2)}, u32[]{:S(2)}) collective-permute-start(bf16[128,512]{1,0:T(8,128)(2,1)} %get-tuple-element.33), channel_id=1, source_target_pairs={{16,8},{32,24},{48,40},{64,56},{80,72},{96,88},{112,104},{128,120}... | collective-permute-start | bytes 393224 | tf_op jit(solution)/shard_map/ppermute | solution.py:407
  145.4 4.4 %shard_map.172 = (f32[384,1024]{1,0:T(8,128)}, f32[256,1024]{1,0:T(8,128)}) custom-call(f32[384,1024]{1,0:T(8,128)} %shard_map.167.freq_ref, bf16[2,1024,128]{2,1,0:T(8,128)(2,1)} %bitcast.48, bf16[2,384,128]{2,1,0:T(8,128)(2,1)} %constant.36.clone.forward_ref, bf16[2,256,384]{2,1,0:T(8,128)(2,1)} %constant.37.clone.inv_ref), custom_call_target="tpu_custom_call" | custom-call | flops 1024 | bytes 1024 | tf_op jit(solution)/shard_map/pallas_call | solution.py:236
  151.1 5.2 %shard_map.173 = (bf16[256,1024]{1,0:T(8,128)(2,1)}, bf16[256,1024]{1,0:T(8,128)(2,1)}) custom-call(s32[1]{0:T(128)} %bitcast.core_ref, bf16[256,512]{1,0:T(8,128)(2,1)} %get-tuple-element.30.keep_ref, bf16[256,512]{1,0:T(8,128)(2,1)} %copy-done.6, bf16[128,512]{1,0:T(8,128)(2,1)} %get-tuple-element.32.inner_ref, bf16[128,512]{1,0:T(8,128)(2,1)} %copy-done.7, ...), custom_call_target="tpu_custom_call" | custom-call | flops 1024 | bytes 1024 | tf_op jit(solution)/shard_map/pallas_call | solution.py:297
  (53 shorter events, 13.6 us)
Async XLA Ops:
  7.2 18.8 %copy-start.3 = (bf16[256,256]{1,0:T(8,128)(2,1)S(1)}, bf16[256,256]{1,0:T(8,128)(2,1)}, u32[]{:S(2)}) copy-start(bf16[256,256]{1,0:T(8,128)(2,1)} %constant.32.clone.place_ref) | copy-start | bytes 393220
  7.2 18.5 %copy-start.2 = (bf16[256,1024]{1,0:T(8,128)(2,1)S(1)}, bf16[256,1024]{1,0:T(8,128)(2,1)}, u32[]{:S(2)}) copy-start(bf16[256,1024]{1,0:T(8,128)(2,1)} %gate_in_ref) | copy-start | bytes 1572868
  7.2 85.8 %all-gather.3.cloned.1.call-start = ((), (), s32[]{:S(2)}) async-start(), calls=%async_computation.6 | async-start | bytes 2785280 | tf_op jit(solution)/shard_map/all_gather | solution.py:372
  22.3 19.5 %collective-permute-start = (bf16[128,1024]{1,0:T(8,128)(2,1)S(1)}, bf16[128,1024]{1,0:T(8,128)(2,1)S(1)}, u32[]{:S(2)}, u32[]{:S(2)}) collective-permute-start(bf16[128,1024]{1,0:T(8,128)(2,1)S(1)} %slice.9), channel_id=1, source_target_pairs={{0,8},{8,16},{16,24},{24,32},{32,40},{40,48},{48,56},{56,64},{64,7... | collective-permute-start | bytes 786440 | tf_op jit(solution)/shard_map/ppermute | solution.py:376
  27.5 6.1 %copy-start.5 = (bf16[256,512]{1,0:T(8,128)(2,1)S(1)}, bf16[256,512]{1,0:T(8,128)(2,1)}, u32[]{:S(2)}) copy-start(bf16[256,512]{1,0:T(8,128)(2,1)} %param.15) | copy-start | bytes 786436
  32.4 5.8 %copy-start = (bf16[2,2,256,512]{3,2,1,0:T(8,128)(2,1)}, bf16[2,2,256,512]{3,2,1,0:T(8,128)(2,1)S(1)}, u32[]{:S(2)}) copy-start(bf16[2,2,256,512]{3,2,1,0:T(8,128)(2,1)S(1)} %all_to_all.31.tok_ref) | copy-start | bytes 3145732
  32.4 5.8 %collective-permute-start.1 = (bf16[128,512]{1,0:T(8,128)(2,1)S(1)}, bf16[128,512]{1,0:T(8,128)(2,1)S(1)}, u32[]{:S(2)}, u32[]{:S(2)}) collective-permute-start(bf16[128,512]{1,0:T(8,128)(2,1)S(1)} %slice_bitcast_fusion.1), channel_id=1, source_target_pairs={{0,16},{16,32},{32,48},{48,64},{64,80},{80,96},{96,112},{112,128},... | collective-permute-start | bytes 393224 | tf_op jit(solution)/shard_map/ppermute | solution.py:383
  33.8 8.1 %copy-start.1 = (bf16[256,1024]{1,0:T(8,128)(2,1)S(1)}, bf16[256,1024]{1,0:T(8,128)(2,1)}, u32[]{:S(2)}) copy-start(bf16[256,1024]{1,0:T(8,128)(2,1)} %param.17) | copy-start | bytes 1572868
  34.7 11.2 %all-to-all-start.1 = ((bf16[2,2,256,128]{3,1,2,0:T(2,128)(2,1)}), bf16[2,2,256,128]{3,1,2,0:T(2,128)(2,1)S(1)}, u32[]{:S(2)}, u32[]{:S(2)}) async-start(bf16[2,2,256,128]{3,1,2,0:T(2,128)(2,1)} %copy.29), calls=%async_computation.1 | async-start | bytes 524288 | tf_op jit(solution)/shard_map/all_to_all | solution.py:373
  38.2 0.7 copy-start.9
  47.8 34.8 %all-to-all-start.3 = ((bf16[8,2,2,256,128]{4,3,2,1,0:T(8,128)(2,1)}), bf16[8,2,2,256,128]{4,3,2,1,0:T(8,128)(2,1)S(1)}, u32[]{:S(2)}, u32[]{:S(2)}) async-start(bf16[8,2,2,256,128]{4,3,2,1,0:T(8,128)(2,1)} %broadcast_in_dim.4), calls=%async_computation.3 | async-start | bytes 4194304 | tf_op jit(solution)/shard_map/all_to_all | solution.py:387
  97.2 14.4 %collective-permute-start.2 = (bf16[2,256,512]{2,1,0:T(8,128)(2,1)}, bf16[2,256,512]{2,1,0:T(8,128)(2,1)S(1)}, u32[]{:S(2)}, u32[]{:S(2)}) collective-permute-start(bf16[2,256,512]{2,1,0:T(8,128)(2,1)} %shard_map.169), channel_id=1, source_target_pairs={{0,16},{16,0},{1,17},{17,1},{2,18},{18,2},{3,19},{19,3},{4,20},{20... | collective-permute-start | bytes 1572872 | tf_op jit(solution)/shard_map/ppermute | solution.py:397
  103.4 40.1 %collective-permute-start.6 = (bf16[2,16,2,16,128]{4,3,2,1,0:T(8,128)(2,1)S(1)}, bf16[2,16,2,16,128]{4,3,2,1,0:T(8,128)(2,1)S(1)}, u32[]{:S(2)}, u32[]{:S(2)}) collective-permute-start(bf16[2,16,2,16,128]{4,3,2,1,0:T(8,128)(2,1)S(1)} %bitcast_bitcast_fusion), channel_id=1, source_target_pairs={{0,16},{16,0},{1,17},{17,1},{2,18},{18,2},{3,19},{19,3},{4,20},{20... | collective-permute-start | bytes 786440 | tf_op jit(solution)/shard_map/ppermute | solution.py:411
  111.6 0.8 copy-start.4
  116.4 39.9 %all-to-all-start.5 = ((bf16[32,16,128]{2,1,0:T(8,128)(2,1)}), bf16[32,16,128]{2,1,0:T(8,128)(2,1)S(1)}, u32[]{:S(2)}, u32[]{:S(2)}) async-start(bf16[32,16,128]{2,1,0:T(8,128)(2,1)} %get-tuple-element.40), calls=%async_computation.5 | async-start | bytes 262144 | tf_op jit(solution)/shard_map/all_to_all | solution.py:402
  136.0 14.3 %collective-permute-start.3 = (bf16[256,512]{1,0:T(8,128)(2,1)}, bf16[256,512]{1,0:T(8,128)(2,1)S(1)}, u32[]{:S(2)}, u32[]{:S(2)}) collective-permute-start(bf16[256,512]{1,0:T(8,128)(2,1)} %get-tuple-element.31), channel_id=1, source_target_pairs={{0,8},{8,0},{1,9},{9,1},{2,10},{10,2},{3,11},{11,3},{4,12},{12,4},... | collective-permute-start | bytes 786440 | tf_op jit(solution)/shard_map/ppermute | solution.py:405
  140.2 9.5 %collective-permute-start.4 = (bf16[128,512]{1,0:T(8,128)(2,1)}, bf16[128,512]{1,0:T(8,128)(2,1)S(1)}, u32[]{:S(2)}, u32[]{:S(2)}) collective-permute-start(bf16[128,512]{1,0:T(8,128)(2,1)} %get-tuple-element.33), channel_id=1, source_target_pairs={{16,8},{32,24},{48,40},{64,56},{80,72},{96,88},{112,104},{128,120}... | collective-permute-start | bytes 393224 | tf_op jit(solution)/shard_map/ppermute | solution.py:407
  142.2 8.2 %collective-permute-start.5 = (bf16[128,512]{1,0:T(8,128)(2,1)}, bf16[128,512]{1,0:T(8,128)(2,1)S(1)}, u32[]{:S(2)}, u32[]{:S(2)}) collective-permute-start(bf16[128,512]{1,0:T(8,128)(2,1)} %get-tuple-element.34), channel_id=1, source_target_pairs={{24,8},{40,24},{56,40},{72,56},{88,72},{104,88},{120,104},{136,120... | collective-permute-start | bytes 393224 | tf_op jit(solution)/shard_map/ppermute | solution.py:408
  149.8 0.7 copy-start.7
  150.4 0.7 copy-start.8
  150.4 0.7 copy-start.6
Sparse Core Ops, SparseCore 0:
  21.5 65.2 all-gather.2

commit v14 on v13

--- a/solution.py
+++ b/solution.py
@@ -408,6 +408,7 @@
     far = lax.ppermute(first, ctx, [(i + 1, j) for i, j in follows])
 
     taps = weights[:, :, 64:, : 2 * K].reshape(16, 2, 16, 2, K).transpose(3, 0, 1, 2, 4)
+    taps, keep = lax.optimization_barrier((taps, keep))
     others = lax.ppermute(taps, "h", [(0, 1), (1, 0)])
     upper_half = lax.axis_index("h") == 0
     taps = jnp.stack(

time: 167 us -> 169 us (1.012)
  blocking collectives: 26.3 us -> 20.4 us
  waiting for transfers between devices: 33.1 us -> 38.5 us
  starting transfers between devices: 45.1 us -> 48.9 us
    all_to_all x1 -> x0, blocking collectives: 4.73 us -> none  [on_device(): lax.all_to_all(tokens.reshape(2, 2, TOK, 512), 'c', split_axis=0, concat_...]
    all_to_all x0 -> x1, starting transfers between devices: none -> 3.92 us  [on_device(): lax.all_to_all(tokens.reshape(2, 2, TOK, 512), 'c', split_axis=0, concat_...]
    all_to_all x1, starting transfers between devices: 19.6 us -> 16 us  [on_device(): tap_grad = lax.all_to_all(tap_grad, chips, split_axis=0, concat_axis=0)]
    ppermute x1, starting transfers between devices: 1.92 us -> 5.5 us  [on_device(): others = lax.ppermute(taps, 'h', [(0, 1), (1, 0)])]
    ppermute x1, waiting for transfers between devices: 2.08 us -> 5.02 us  [on_device(): more = lax.ppermute(partial, 'h', [(0, 1), (1, 0)])]
  transfers between devices with their start and end apart: 11 -> 12, of which waited for: 3 -> 5; matrix products, arithmetic and copies ran while one was open for 7% -> 7% of each run, Pallas kernels for 15% -> 12%
where the time goes in v14:
time: 169 us; the launch traced here: 167 us
  starting transfers between devices  48.9 us (29%)
  waiting for transfers between devices  38.5 us (23%)
  Pallas kernels  30.1 us (18%)
  blocking collectives  20.4 us (12%)
  between operations  14.3 us (8%)
  local copies, waits for them, and re-layouts  9.77 us (6%)
  other arithmetic  3.52 us (2%)
    all_to_all x1, waiting for transfers between devices, on_device(): lax.all_to_all(jnp.broadcast_to(cols[None], (8, 2, 2, TOK, K)), ('x', 'l'...  31.7 us
    all_to_all x1, starting transfers between devices, on_device(): tap_grad = lax.all_to_all(tap_grad, chips, split_axis=0, concat_axis=0)  16 us
    all_to_all x1, blocking collectives, on_device(): block = lax.all_to_all(message, 'c', split_axis=0, concat_axis=0)  12.2 us
    pallas_call x2, Pallas kernels, product(): pl.pallas_call(product_kernel, grid_spec=pltpu.PrefetchScalarGridSpec(num...  8.44 us
    all_to_all x1, blocking collectives, on_device(): lax.all_to_all(jnp.broadcast_to(cols[None], (2, 8, 2, 2, TOK, K)), 'c', s...  8.18 us
    ppermute x1, starting transfers between devices, on_device(): others = lax.ppermute(taps, 'h', [(0, 1), (1, 0)])  5.5 us
    ppermute x1, starting transfers between devices, on_device(): more = lax.ppermute(partial, 'h', [(0, 1), (1, 0)])  5.43 us
    pallas_call x1, Pallas kernels, out_part(): pl.pallas_call(out_kernel, grid=(TILES,), in_specs=[scalar(), half, half,...  5.23 us
  transfers between devices with their start and end apart: 12, of which 5 were waited for; matrix products, arithmetic and copies ran while one was open for 7% of the time, Pallas kernels for 12%

profile of v14, /device:TPU:1, one launch (start us, length us, event | category | flops | bytes accessed | tf_op | source)
XLA Modules:
  0.0 167.0 jit_solution(12845955875895731801)
XLA Ops:
  7.2 1.9 %shard_map.166 = bf16[2,80,512]{2,1,0:T(8,128)(2,1)} custom-call(bf16[64,1024]{1,0:T(8,128)(2,1)} %bitcast.39, f32[16,128]{1,0:T(8,128)} %bitcast.40, bf16[256,256]{1,0:T(8,128)(2,1)} %constant.32.clone.place_ref), custom_call_target="tpu_custom_call" | custom-call | flops 33554432 | bytes 524288 | tf_op jit(solution)/shard_map/pallas_call | solution.py:344
  9.1 12.2 %all_to_all.30 = bf16[2,80,512]{2,1,0:T(8,128)(2,1)} all-to-all(bf16[2,80,512]{2,1,0:T(8,128)(2,1)} %shard_map.166), channel_id=1, replica_groups=mesh['z'=16,'h'=2,'c'=2,'x'=4,'l'=2] {'c'}, dimensions={0} | all-to-all | bytes 327680 | tf_op jit(solution)/shard_map/all_to_all | solution.py:366
  21.3 1.4 reshape.47
  26.7 3.9 %all-to-all-start.2 = ((bf16[2,2,256,512]{3,2,1,0:T(8,128)(2,1)}), bf16[2,2,256,512]{3,2,1,0:T(8,128)(2,1)S(1)}, u32[]{:S(2)}, u32[]{:S(2)}) async-start(bf16[2,2,256,512]{3,2,1,0:T(8,128)(2,1)} %bitcast.9), calls=%async_computation.2 | async-start | bytes 2097152 | tf_op jit(solution)/shard_map/all_to_all | solution.py:379
  30.6 1.9 %collective-permute-start = (bf16[128,1024]{1,0:T(8,128)(2,1)S(1)}, bf16[128,1024]{1,0:T(8,128)(2,1)S(1)}, u32[]{:S(2)}, u32[]{:S(2)}) collective-permute-start(bf16[128,1024]{1,0:T(8,128)(2,1)S(1)} %slice.9), channel_id=1, source_target_pairs={{0,8},{8,16},{16,24},{24,32},{32,40},{40,48},{48,56},{56,64},{64,7... | collective-permute-start | bytes 786440 | tf_op jit(solution)/shard_map/ppermute | solution.py:376
  34.9 3.6 %all-to-all-start.1 = ((bf16[2,2,256,128]{3,1,2,0:T(2,128)(2,1)}), bf16[2,2,256,128]{3,1,2,0:T(2,128)(2,1)S(1)}, u32[]{:S(2)}, u32[]{:S(2)}) async-start(bf16[2,2,256,128]{3,1,2,0:T(2,128)(2,1)} %copy.29), calls=%async_computation.1 | async-start | bytes 524288 | tf_op jit(solution)/shard_map/all_to_all | solution.py:373
  39.3 3.0 %shard_map.168.freq_ref = f32[2,384,512]{2,1,0:T(8,128)} custom-call(bf16[128,512]{1,0:T(8,128)(2,1)} %copy-done.9, bf16[2,2,256,512]{3,2,1,0:T(8,128)(2,1)} %copy-done, bf16[2,384,384]{2,1,0:T(8,128)(2,1)} %constant.33.clone.forward_ref), custom_call_target="tpu_custom_call" | custom-call | flops 603979776 | bytes 3145728 | tf_op jit(solution)/shard_map/pallas_call | solution.py:149
  43.3 3.1 %shard_map.167.freq_ref = f32[384,1024]{1,0:T(8,128)} custom-call(bf16[384,1024]{1,0:T(8,128)(2,1)} %pad_maximum_fusion.1.window_ref, bf16[2,384,384]{2,1,0:T(8,128)(2,1)} %constant.33.clone.forward_ref), custom_call_target="tpu_custom_call" | custom-call | flops 603979776 | bytes 3145728 | tf_op jit(solution)/shard_map/pallas_call | solution.py:122
  46.5 1.8 %broadcast_in_dim.4 = bf16[8,2,2,256,128]{4,3,2,1,0:T(8,128)(2,1)} broadcast(bf16[2,2,256,128]{3,2,1,0:T(8,128)(2,1)S(1)} %copy.32), dimensions={1,2,3,4} | broadcast | bytes 2359296 | tf_op jit(solution)/shard_map/broadcast_in_dim | solution.py:388
  48.3 4.3 %all-to-all-start.3 = ((bf16[8,2,2,256,128]{4,3,2,1,0:T(8,128)(2,1)}), bf16[8,2,2,256,128]{4,3,2,1,0:T(8,128)(2,1)S(1)}, u32[]{:S(2)}, u32[]{:S(2)}) async-start(bf16[8,2,2,256,128]{4,3,2,1,0:T(8,128)(2,1)} %broadcast_in_dim.4), calls=%async_computation.3 | async-start | bytes 4194304 | tf_op jit(solution)/shard_map/all_to_all | solution.py:387
  52.5 31.7 %all-to-all-done.3 = bf16[8,2,2,256,128]{4,3,2,1,0:T(8,128)(2,1)S(1)} async-done(((bf16[8,2,2,256,128]{4,3,2,1,0:T(8,128)(2,1)}), bf16[8,2,2,256,128]{4,3,2,1,0:T(8,128)(2,1)S(1)}, u32[]{:S(2)}, u32[]{:S(2)}) %all-to-all-start.3) | async-done | bytes 2097184 | tf_op jit(solution)/shard_map/all_to_all | solution.py:387
  85.2 8.2 %all_to_all.31.cols_ref = bf16[2,8,2,2,256,128]{5,4,3,2,1,0:T(8,128)(2,1)} all-to-all(bf16[2,8,2,2,256,128]{5,4,3,2,1,0:T(8,128)(2,1)S(1)} %broadcast_in_dim.5), channel_id=1, replica_groups=mesh['z'=16,'h'=2,'c'=2,'x'=4,'l'=2] {'c'}, dimensions={0} | all-to-all | bytes 8388608 | tf_op jit(solution)/shard_map/all_to_all | solution.py:390
  93.4 4.2 %shard_map.169 = bf16[2,256,512]{2,1,0:T(8,128)(2,1)} custom-call(s32[1]{0:T(128)S(6)} %sub.3.h_ref, bf16[2,8,2,2,256,128]{5,4,3,2,1,0:T(8,128)(2,1)} %all_to_all.31.cols_ref, bf16[16,2,80,512]{3,2,1,0:T(8,128)(2,1)} %bitcast.32), custom_call_target="tpu_custom_call" | custom-call | flops 1073741824 | bytes 5242880 | tf_op jit(solution)/shard_map/pallas_call | solution.py:83
  97.6 5.4 %collective-permute-start.2 = (bf16[2,256,512]{2,1,0:T(8,128)(2,1)}, bf16[2,256,512]{2,1,0:T(8,128)(2,1)S(1)}, u32[]{:S(2)}, u32[]{:S(2)}) collective-permute-start(bf16[2,256,512]{2,1,0:T(8,128)(2,1)} %shard_map.169), channel_id=1, source_target_pairs={{0,16},{16,0},{1,17},{17,1},{2,18},{18,2},{3,19},{19,3},{4,20},{20... | collective-permute-start | bytes 1572872 | tf_op jit(solution)/shard_map/ppermute | solution.py:397
  103.1 4.2 %shard_map.170.mix_ref = bf16[2,256,512]{2,1,0:T(8,128)(2,1)} custom-call(s32[1]{0:T(128)} %bitcast.4.h_ref, bf16[2,8,2,2,256,128]{5,4,3,2,1,0:T(8,128)(2,1)} %all_to_all.31.cols_ref, bf16[16,2,80,512]{3,2,1,0:T(8,128)(2,1)} %bitcast.33), custom_call_target="tpu_custom_call" | custom-call | flops 1073741824 | bytes 5242880 | tf_op jit(solution)/shard_map/pallas_call | solution.py:83
  108.3 5.0 %collective-permute-done.2.more_ref = bf16[2,256,512]{2,1,0:T(8,128)(2,1)S(1)} collective-permute-done((bf16[2,256,512]{2,1,0:T(8,128)(2,1)}, bf16[2,256,512]{2,1,0:T(8,128)(2,1)S(1)}, u32[]{:S(2)}, u32[]{:S(2)}) %collective-permute-start.2) | collective-permute-done | bytes 524320 | tf_op jit(solution)/shard_map/ppermute | solution.py:397
  114.1 4.0 %shard_map.171 = (bf16[256,512]{1,0:T(8,128)(2,1)}, bf16[256,512]{1,0:T(8,128)(2,1)}, bf16[128,512]{1,0:T(8,128)(2,1)}, bf16[128,512]{1,0:T(8,128)(2,1)}, bf16[1...) custom-call(s32[1]{0:T(128)} %bitcast.core_ref, bf16[2,256,512]{2,1,0:T(8,128)(2,1)} %shard_map.170.mix_ref, ...), custom_call_target="tpu_custom_call" | custom-call | flops 603979776 | bytes 5242880 | tf_op jit(solution)/shard_map/pallas_call | solution.py:200
  118.2 5.5 %collective-permute-start.6 = (bf16[2,16,2,16,128]{4,3,2,1,0:T(8,128)(2,1)S(1)}, bf16[2,16,2,16,128]{4,3,2,1,0:T(8,128)(2,1)S(1)}, u32[]{:S(2)}, u32[]{:S(2)}) collective-permute-start(bf16[2,16,2,16,128]{4,3,2,1,0:T(8,128)(2,1)S(1)} %bitcast_bitcast_fusion), channel_id=1, source_target_pairs={{0,16},{16,0},{1,17},{17,1},{2,18},{18,2},{3,19},{19,3},{4,20},{20... | collective-permute-start | bytes 786440 | tf_op jit(solution)/shard_map/ppermute | solution.py:412
  123.7 16.0 %all-to-all-start.5 = ((bf16[32,16,128]{2,1,0:T(8,128)(2,1)}), bf16[32,16,128]{2,1,0:T(8,128)(2,1)S(1)}, u32[]{:S(2)}, u32[]{:S(2)}) async-start(bf16[32,16,128]{2,1,0:T(8,128)(2,1)} %get-tuple-element.44), calls=%async_computation.5 | async-start | bytes 262144 | tf_op jit(solution)/shard_map/all_to_all | solution.py:402
  139.7 3.7 %collective-permute-start.3 = (bf16[256,512]{1,0:T(8,128)(2,1)}, bf16[256,512]{1,0:T(8,128)(2,1)S(1)}, u32[]{:S(2)}, u32[]{:S(2)}) collective-permute-start(bf16[256,512]{1,0:T(8,128)(2,1)} %get-tuple-element.34), channel_id=1, source_target_pairs={{0,8},{8,0},{1,9},{9,1},{2,10},{10,2},{3,11},{11,3},{4,12},{12,4},... | collective-permute-start | bytes 786440 | tf_op jit(solution)/shard_map/ppermute | solution.py:405
  143.4 1.9 %collective-permute-start.4 = (bf16[128,512]{1,0:T(8,128)(2,1)}, bf16[128,512]{1,0:T(8,128)(2,1)S(1)}, u32[]{:S(2)}, u32[]{:S(2)}) collective-permute-start(bf16[128,512]{1,0:T(8,128)(2,1)} %get-tuple-element.36), channel_id=1, source_target_pairs={{16,8},{32,24},{48,40},{64,56},{80,72},{96,88},{112,104},{128,120}... | collective-permute-start | bytes 393224 | tf_op jit(solution)/shard_map/ppermute | solution.py:407
  147.5 4.4 %shard_map.172 = (f32[384,1024]{1,0:T(8,128)}, f32[256,1024]{1,0:T(8,128)}) custom-call(f32[384,1024]{1,0:T(8,128)} %shard_map.167.freq_ref, bf16[2,1024,128]{2,1,0:T(8,128)(2,1)} %bitcast.37, bf16[2,384,128]{2,1,0:T(8,128)(2,1)} %constant.36.clone.forward_ref, bf16[2,256,384]{2,1,0:T(8,128)(2,1)} %constant.37.clone.inv_ref), custom_call_target="tpu_custom_call" | custom-call | flops 1024 | bytes 1024 | tf_op jit(solution)/shard_map/pallas_call | solution.py:236
  152.1 1.4 collective-permute-done.5.far_ref
  154.3 5.2 %shard_map.173 = (bf16[256,1024]{1,0:T(8,128)(2,1)}, bf16[256,1024]{1,0:T(8,128)(2,1)}) custom-call(s32[1]{0:T(128)} %bitcast.core_ref, bf16[256,512]{1,0:T(8,128)(2,1)} %get-tuple-element.33.keep_ref, bf16[256,512]{1,0:T(8,128)(2,1)} %copy-done.6, bf16[128,512]{1,0:T(8,128)(2,1)} %get-tuple-element.35.inner_ref, bf16[128,512]{1,0:T(8,128)(2,1)} %copy-done.7, ...), custom_call_target="tpu_custom_call" | custom-call | flops 1024 | bytes 1024 | tf_op jit(solution)/shard_map/pallas_call | solution.py:297
  (54 shorter events, 14.7 us)
Async XLA Ops:
  7.2 86.3 %all-gather.3.cloned.1.call-start = ((), (), s32[]{:S(2)}) async-start(), calls=%async_computation.6 | async-start | bytes 2785280 | tf_op jit(solution)/shard_map/all_gather | solution.py:372
  22.6 1.8 %copy-start.2 = (bf16[256,1024]{1,0:T(8,128)(2,1)S(1)}, bf16[256,1024]{1,0:T(8,128)(2,1)}, u32[]{:S(2)}) copy-start(bf16[256,1024]{1,0:T(8,128)(2,1)} %gate_in_ref) | copy-start | bytes 1572868
  23.9 0.9 copy-start.3
  25.6 5.0 %copy-start.1 = (bf16[256,1024]{1,0:T(8,128)(2,1)S(1)}, bf16[256,1024]{1,0:T(8,128)(2,1)}, u32[]{:S(2)}) copy-start(bf16[256,1024]{1,0:T(8,128)(2,1)} %param.17) | copy-start | bytes 1572868
  25.6 8.3 %copy-start.5 = (bf16[256,512]{1,0:T(8,128)(2,1)S(1)}, bf16[256,512]{1,0:T(8,128)(2,1)}, u32[]{:S(2)}) copy-start(bf16[256,512]{1,0:T(8,128)(2,1)} %param.15) | copy-start | bytes 786436
  26.7 5.9 %all-to-all-start.2 = ((bf16[2,2,256,512]{3,2,1,0:T(8,128)(2,1)}), bf16[2,2,256,512]{3,2,1,0:T(8,128)(2,1)S(1)}, u32[]{:S(2)}, u32[]{:S(2)}) async-start(bf16[2,2,256,512]{3,2,1,0:T(8,128)(2,1)} %bitcast.9), calls=%async_computation.2 | async-start | bytes 2097152 | tf_op jit(solution)/shard_map/all_to_all | solution.py:379
  30.6 11.7 %collective-permute-start = (bf16[128,1024]{1,0:T(8,128)(2,1)S(1)}, bf16[128,1024]{1,0:T(8,128)(2,1)S(1)}, u32[]{:S(2)}, u32[]{:S(2)}) collective-permute-start(bf16[128,1024]{1,0:T(8,128)(2,1)S(1)} %slice.9), channel_id=1, source_target_pairs={{0,8},{8,16},{16,24},{24,32},{32,40},{40,48},{48,56},{56,64},{64,7... | collective-permute-start | bytes 786440 | tf_op jit(solution)/shard_map/ppermute | solution.py:376
  32.6 6.1 %copy-start = (bf16[2,2,256,512]{3,2,1,0:T(8,128)(2,1)}, bf16[2,2,256,512]{3,2,1,0:T(8,128)(2,1)S(1)}, u32[]{:S(2)}) copy-start(bf16[2,2,256,512]{3,2,1,0:T(8,128)(2,1)S(1)} %all-to-all-done.2.tok_ref) | copy-start | bytes 3145732
  32.6 6.1 %collective-permute-start.1 = (bf16[128,512]{1,0:T(8,128)(2,1)S(1)}, bf16[128,512]{1,0:T(8,128)(2,1)S(1)}, u32[]{:S(2)}, u32[]{:S(2)}) collective-permute-start(bf16[128,512]{1,0:T(8,128)(2,1)S(1)} %slice_bitcast_fusion.1), channel_id=1, source_target_pairs={{0,16},{16,32},{32,48},{48,64},{64,80},{80,96},{96,112},{112,128},... | collective-permute-start | bytes 393224 | tf_op jit(solution)/shard_map/ppermute | solution.py:383
  34.9 11.5 %all-to-all-start.1 = ((bf16[2,2,256,128]{3,1,2,0:T(2,128)(2,1)}), bf16[2,2,256,128]{3,1,2,0:T(2,128)(2,1)S(1)}, u32[]{:S(2)}, u32[]{:S(2)}) async-start(bf16[2,2,256,128]{3,1,2,0:T(2,128)(2,1)} %copy.29), calls=%async_computation.1 | async-start | bytes 524288 | tf_op jit(solution)/shard_map/all_to_all | solution.py:373
  38.7 0.7 copy-start.9
  48.3 36.0 %all-to-all-start.3 = ((bf16[8,2,2,256,128]{4,3,2,1,0:T(8,128)(2,1)}), bf16[8,2,2,256,128]{4,3,2,1,0:T(8,128)(2,1)S(1)}, u32[]{:S(2)}, u32[]{:S(2)}) async-start(bf16[8,2,2,256,128]{4,3,2,1,0:T(8,128)(2,1)} %broadcast_in_dim.4), calls=%async_computation.3 | async-start | bytes 4194304 | tf_op jit(solution)/shard_map/all_to_all | solution.py:387
  97.6 15.7 %collective-permute-start.2 = (bf16[2,256,512]{2,1,0:T(8,128)(2,1)}, bf16[2,256,512]{2,1,0:T(8,128)(2,1)S(1)}, u32[]{:S(2)}, u32[]{:S(2)}) collective-permute-start(bf16[2,256,512]{2,1,0:T(8,128)(2,1)} %shard_map.169), channel_id=1, source_target_pairs={{0,16},{16,0},{1,17},{17,1},{2,18},{18,2},{3,19},{19,3},{4,20},{20... | collective-permute-start | bytes 1572872 | tf_op jit(solution)/shard_map/ppermute | solution.py:397
  113.3 0.8 copy-start.4
  118.2 28.4 %collective-permute-start.6 = (bf16[2,16,2,16,128]{4,3,2,1,0:T(8,128)(2,1)S(1)}, bf16[2,16,2,16,128]{4,3,2,1,0:T(8,128)(2,1)S(1)}, u32[]{:S(2)}, u32[]{:S(2)}) collective-permute-start(bf16[2,16,2,16,128]{4,3,2,1,0:T(8,128)(2,1)S(1)} %bitcast_bitcast_fusion), channel_id=1, source_target_pairs={{0,16},{16,0},{1,17},{17,1},{2,18},{18,2},{3,19},{19,3},{4,20},{20... | collective-permute-start | bytes 786440 | tf_op jit(solution)/shard_map/ppermute | solution.py:412
  123.7 35.8 %all-to-all-start.5 = ((bf16[32,16,128]{2,1,0:T(8,128)(2,1)}), bf16[32,16,128]{2,1,0:T(8,128)(2,1)S(1)}, u32[]{:S(2)}, u32[]{:S(2)}) async-start(bf16[32,16,128]{2,1,0:T(8,128)(2,1)} %get-tuple-element.44), calls=%async_computation.5 | async-start | bytes 262144 | tf_op jit(solution)/shard_map/all_to_all | solution.py:402
  139.7 13.9 %collective-permute-start.3 = (bf16[256,512]{1,0:T(8,128)(2,1)}, bf16[256,512]{1,0:T(8,128)(2,1)S(1)}, u32[]{:S(2)}, u32[]{:S(2)}) collective-permute-start(bf16[256,512]{1,0:T(8,128)(2,1)} %get-tuple-element.34), channel_id=1, source_target_pairs={{0,8},{8,0},{1,9},{9,1},{2,10},{10,2},{3,11},{11,3},{4,12},{12,4},... | collective-permute-start | bytes 786440 | tf_op jit(solution)/shard_map/ppermute | solution.py:405
  143.4 8.8 %collective-permute-start.4 = (bf16[128,512]{1,0:T(8,128)(2,1)}, bf16[128,512]{1,0:T(8,128)(2,1)S(1)}, u32[]{:S(2)}, u32[]{:S(2)}) collective-permute-start(bf16[128,512]{1,0:T(8,128)(2,1)} %get-tuple-element.36), channel_id=1, source_target_pairs={{16,8},{32,24},{48,40},{64,56},{80,72},{96,88},{112,104},{128,120}... | collective-permute-start | bytes 393224 | tf_op jit(solution)/shard_map/ppermute | solution.py:407
  145.3 8.3 %collective-permute-start.5 = (bf16[128,512]{1,0:T(8,128)(2,1)}, bf16[128,512]{1,0:T(8,128)(2,1)S(1)}, u32[]{:S(2)}, u32[]{:S(2)}) collective-permute-start(bf16[128,512]{1,0:T(8,128)(2,1)} %get-tuple-element.37), channel_id=1, source_target_pairs={{24,8},{40,24},{56,40},{72,56},{88,72},{104,88},{120,104},{136,120... | collective-permute-start | bytes 393224 | tf_op jit(solution)/shard_map/ppermute | solution.py:408
  152.1 1.4 copy-start.7
  153.6 0.6 copy-start.8
  153.6 0.7 copy-start.6
Sparse Core Ops, SparseCore 0:
  21.4 65.1 all-gather.2

commit v15 on v12

--- a/solution.py
+++ b/solution.py
@@ -216,8 +216,15 @@
     )(core, mix, tokens, sig_freq, own, lag)
 
 
-def conv_kernel(freq_ref, tap_ref, forward_ref, inv_ref, tap_freq_ref, conv_ref):
-    upper, lower = tap_ref[0], tap_ref[1]
+def conv_kernel(
+    h_ref, freq_ref, tap_ref, more_ref, forward_ref, inv_ref, tap_freq_ref, conv_ref
+):
+    is_first = h_ref[0] == 0
+    taps, more = tap_ref[...].astype(F32), more_ref[...].astype(F32)
+    taps = jnp.stack(
+        [jnp.where(is_first, taps, more), jnp.where(is_first, more, taps)], axis=2
+    ).astype(BF)
+    upper, lower = taps[0].reshape(2 * L, K), taps[1].reshape(2 * L, K)
     high, low = forward_ref[0], forward_ref[1]
     tap_freq = dot(high, upper, LANES) + dot(low, upper, LANES) + dot(high, lower, LANES)
     tap_freq_ref[...] = tap_freq
@@ -228,13 +235,16 @@
     return pl.BlockSpec((rows, 2 * L), lambda j: (0, j))
 
 
-def conv_part(sig_freq, taps, forward, inv):
+def conv_part(h, sig_freq, taps, more, forward, inv):
+    tap = pl.BlockSpec((2, L // 32, 2, 16, K), lambda j: (0, j, 0, 0, 0))
     return pl.pallas_call(
         conv_kernel,
         grid=(TILES,),
         in_specs=[
+            scalar(),
             wide_tile(N),
-            pl.BlockSpec((2, 2 * L, K), lambda j: (0, j, 0)),
+            tap,
+            tap,
             whole((2, N, K)),
             whole((2, TOK, N)),
         ],
@@ -242,7 +252,7 @@
         out_shape=[jax.ShapeDtypeStruct((N, CH), F32), jax.ShapeDtypeStruct((TOK, CH), F32)],
         compiler_params=params(),
         cost_estimate=pl.CostEstimate(flops=1024, bytes_accessed=1024, transcendentals=0),
-    )(sig_freq, taps, forward, inv)
+    )(h, sig_freq, taps, more, forward, inv)
 
 
 def out_kernel(
@@ -392,6 +402,9 @@
     mix = lax.all_to_all(
         partial.reshape(2, 2, TOK, 512), "h", split_axis=0, concat_axis=0
     )
+    taps = weights[:, :, 64:, : 2 * K].reshape(16, 2, 16, 2, K).transpose(3, 0, 1, 2, 4)
+    more = lax.ppermute(taps, "h", [(0, 1), (1, 0)])
+    mix, more = lax.optimization_barrier((mix, more))
     keep, send, first, inner, cross, tap_grad = grad_part(
         core, mix, tokens, own_freq, fwd[:, :, K:N], inv[:, :K]
     )
@@ -403,14 +416,9 @@
     near = lax.ppermute(cross, ctx, follows + [(2 * i + 1, 2 * i) for i in range(32)])
     far = lax.ppermute(first, ctx, [(i + 1, j) for i, j in follows])
 
-    taps = weights[:, :, 64:, : 2 * K].reshape(16, 2, 16, 2, K).transpose(3, 0, 1, 2, 4)
-    more = lax.ppermute(taps, "h", [(0, 1), (1, 0)])
-    upper_half = lax.axis_index("h") == 0
-    taps = jnp.stack(
-        [jnp.where(upper_half, taps, more), jnp.where(upper_half, more, taps)], axis=2
-    ).reshape(2, CH, K)
-
-    tap_freq, conv = conv_part(sig_freq, taps, fwd[:, :, :K], inv[:, K:])
+    tap_freq, conv = conv_part(
+        lax.axis_index("h").reshape(1), sig_freq, taps, more, fwd[:, :, :K], inv[:, K:]
+    )
     gate_grad, signal_grad = out_part(
         core,
         keep,

time: 164 us -> 167 us (1.018)
  waiting for transfers between devices: 4.58 us -> 10.3 us
  other arithmetic: 4.59 us -> 2.64 us
    ppermute x1, waiting for transfers between devices: 0.01 us -> 7.55 us  [on_device(): more = lax.ppermute(taps, 'h', [(0, 1), (1, 0)])]
    all_to_all x1, waiting for transfers between devices: 3.85 us -> 0.01 us  [on_device(): lax.all_to_all(partial.reshape(2, 2, TOK, 512), 'h', split_axis=0, concat...]
    another operation x2 -> x0, other arithmetic: 1.93 us -> none  [on_device(): jnp.stack([jnp.where(upper_half, taps, more), jnp.where(upper_half, more,...]
    all_to_all x1, starting transfers between devices: 19.7 us -> 21.5 us  [on_device(): tap_grad = lax.all_to_all(tap_grad, chips, split_axis=0, concat_axis=0)]
  transfers between devices with their start and end apart: 11 -> 11, of which waited for: 3 -> 4; matrix products, arithmetic and copies ran while one was open for 7% -> 6% of each run, Pallas kernels for 12% -> 10%
where the time goes in v15:
time: 167 us; the launch traced here: 166 us
  blocking collectives  50.7 us (30%)
  starting transfers between devices  49.6 us (30%)
  Pallas kernels  27.4 us (16%)
  between operations  14.3 us (9%)
  waiting for transfers between devices  10.3 us (6%)
  local copies, waits for them, and re-layouts  9.1 us (5%)
  other arithmetic  2.64 us (2%)
    all_to_all x1, blocking collectives, on_device(): lax.all_to_all(jnp.broadcast_to(cols[None], (8, 2, 2, TOK, K)), ('x', 'l'...  30.4 us
    all_to_all x1, starting transfers between devices, on_device(): tap_grad = lax.all_to_all(tap_grad, chips, split_axis=0, concat_axis=0)  21.5 us
    all_to_all x1, blocking collectives, on_device(): block = lax.all_to_all(message, 'c', split_axis=0, concat_axis=0)  12.2 us
    all_to_all x1, blocking collectives, on_device(): lax.all_to_all(jnp.broadcast_to(cols[None], (2, 8, 2, 2, TOK, K)), 'c', s...  8.11 us
    ppermute x1, waiting for transfers between devices, on_device(): more = lax.ppermute(taps, 'h', [(0, 1), (1, 0)])  7.55 us
    all_to_all x1, starting transfers between devices, on_device(): lax.all_to_all(partial.reshape(2, 2, TOK, 512), 'h', split_axis=0, concat...  5.85 us
    pallas_call x1, Pallas kernels, product(): pl.pallas_call(product_kernel, grid=(2,), in_specs=[pl.BlockSpec((2, 8, 1...  5.68 us
    pallas_call x1, Pallas kernels, out_part(): pl.pallas_call(out_kernel, grid=(TILES,), in_specs=[scalar(), half, half,...  5.23 us
  transfers between devices with their start and end apart: 11, of which 4 were waited for; matrix products, arithmetic and copies ran while one was open for 6% of the time, Pallas kernels for 10%

profile of v15, /device:TPU:1, one launch (start us, length us, event | category | flops | bytes accessed | tf_op | source)
XLA Modules:
  0.0 165.5 jit_solution(78556583842618238)
XLA Ops:
  7.2 1.9 %shard_map.166 = bf16[2,80,512]{2,1,0:T(8,128)(2,1)} custom-call(bf16[64,1024]{1,0:T(8,128)(2,1)} %bitcast.30, f32[16,128]{1,0:T(8,128)} %bitcast.33, bf16[256,256]{1,0:T(8,128)(2,1)} %constant.28.clone.place_ref), custom_call_target="tpu_custom_call" | custom-call | flops 33554432 | bytes 524288 | tf_op jit(solution)/shard_map/pallas_call | solution.py:350
  9.1 12.2 %all_to_all.35 = bf16[2,80,512]{2,1,0:T(8,128)(2,1)} all-to-all(bf16[2,80,512]{2,1,0:T(8,128)(2,1)} %shard_map.166), channel_id=1, replica_groups=mesh['z'=16,'h'=2,'c'=2,'x'=4,'l'=2] {'c'}, dimensions={0} | all-to-all | bytes 327680 | tf_op jit(solution)/shard_map/all_to_all | solution.py:372
  21.3 1.4 reshape.46
  26.7 3.9 %all-to-all-start.2 = ((bf16[2,2,256,512]{3,2,1,0:T(8,128)(2,1)}), bf16[2,2,256,512]{3,2,1,0:T(8,128)(2,1)S(1)}, u32[]{:S(2)}, u32[]{:S(2)}) async-start(bf16[2,2,256,512]{3,2,1,0:T(8,128)(2,1)} %bitcast.8), calls=%async_computation.2 | async-start | bytes 2097152 | tf_op jit(solution)/shard_map/all_to_all | solution.py:385
  30.6 1.9 %collective-permute-start = (bf16[128,1024]{1,0:T(8,128)(2,1)S(1)}, bf16[128,1024]{1,0:T(8,128)(2,1)S(1)}, u32[]{:S(2)}, u32[]{:S(2)}) collective-permute-start(bf16[128,1024]{1,0:T(8,128)(2,1)S(1)} %slice.9), channel_id=1, source_target_pairs={{0,8},{8,16},{16,24},{24,32},{32,40},{40,48},{48,56},{56,64},{64,7... | collective-permute-start | bytes 786440 | tf_op jit(solution)/shard_map/ppermute | solution.py:382
  32.6 1.3 collective-permute-start.1
  34.9 3.6 %all-to-all-start.1 = ((bf16[2,2,256,128]{3,1,2,0:T(2,128)(2,1)}), bf16[2,2,256,128]{3,1,2,0:T(2,128)(2,1)S(1)}, u32[]{:S(2)}, u32[]{:S(2)}) async-start(bf16[2,2,256,128]{3,1,2,0:T(2,128)(2,1)} %copy.30), calls=%async_computation.1 | async-start | bytes 524288 | tf_op jit(solution)/shard_map/all_to_all | solution.py:379
  39.3 3.0 %shard_map.168.freq_ref = f32[2,384,512]{2,1,0:T(8,128)} custom-call(bf16[128,512]{1,0:T(8,128)(2,1)} %copy-done.11, bf16[2,2,256,512]{3,2,1,0:T(8,128)(2,1)} %copy-done, bf16[2,384,384]{2,1,0:T(8,128)(2,1)} %constant.29.clone.forward_ref), custom_call_target="tpu_custom_call" | custom-call | flops 603979776 | bytes 3145728 | tf_op jit(solution)/shard_map/pallas_call | solution.py:147
  43.3 3.1 %shard_map.167.freq_ref = f32[384,1024]{1,0:T(8,128)} custom-call(bf16[384,1024]{1,0:T(8,128)(2,1)} %pad_maximum_fusion.1.window_ref, bf16[2,384,384]{2,1,0:T(8,128)(2,1)} %constant.29.clone.forward_ref), custom_call_target="tpu_custom_call" | custom-call | flops 603979776 | bytes 3145728 | tf_op jit(solution)/shard_map/pallas_call | solution.py:120
  47.0 30.4 %all_to_all.36 = bf16[8,2,2,256,128]{4,3,2,1,0:T(8,128)(2,1)S(1)} all-to-all(bf16[8,2,2,256,128]{4,3,2,1,0:T(8,128)(2,1)S(1)} %broadcast_in_dim.4), channel_id=1, replica_groups=mesh['z'=16,'h'=2,'c'=2,'x'=4,'l'=2] {'x','l'}, dimensions={0} | all-to-all | bytes 4194304 | tf_op jit(solution)/shard_map/all_to_all | solution.py:393
  77.3 1.4 broadcast_in_dim.5
  78.7 8.1 %all_to_all.37.cols_ref = bf16[2,8,2,2,256,128]{5,4,3,2,1,0:T(8,128)(2,1)} all-to-all(bf16[2,8,2,2,256,128]{5,4,3,2,1,0:T(8,128)(2,1)S(1)} %broadcast_in_dim.5), channel_id=1, replica_groups=mesh['z'=16,'h'=2,'c'=2,'x'=4,'l'=2] {'c'}, dimensions={0} | all-to-all | bytes 8388608 | tf_op jit(solution)/shard_map/all_to_all | solution.py:396
  86.9 5.7 %shard_map.169 = bf16[4,256,512]{2,1,0:T(8,128)(2,1)} custom-call(bf16[2,8,2,2,256,128]{5,4,3,2,1,0:T(8,128)(2,1)} %all_to_all.37.cols_ref, bf16[16,2,80,512]{3,2,1,0:T(8,128)(2,1)} %bitcast.31), custom_call_target="tpu_custom_call" | custom-call | flops 2147483648 | bytes 8388608 | tf_op jit(solution)/shard_map/pallas_call | solution.py:84
  92.5 5.9 %all-to-all-start.5 = ((bf16[2,2,256,512]{3,2,1,0:T(8,128)(2,1)}), bf16[2,2,256,512]{3,2,1,0:T(8,128)(2,1)S(1)}, u32[]{:S(2)}, u32[]{:S(2)}) async-start(bf16[2,2,256,512]{3,2,1,0:T(8,128)(2,1)} %bitcast.28), calls=%async_computation.5 | async-start | bytes 2097152 | tf_op jit(solution)/shard_map/all_to_all | solution.py:402
  99.4 4.9 %collective-permute-start.2 = (bf16[2,16,2,16,128]{4,3,2,1,0:T(8,128)(2,1)S(1)}, bf16[2,16,2,16,128]{4,3,2,1,0:T(8,128)(2,1)S(1)}, u32[]{:S(2)}, u32[]{:S(2)}) collective-permute-start(bf16[2,16,2,16,128]{4,3,2,1,0:T(8,128)(2,1)S(1)} %bitcast_bitcast_fusion.tap_ref), channel_id=1, source_target_pairs={{0,16},{16,0},{1,17},{17,1},{2,18},{18,2},{3,19},{19,3},{4,20},{20... | collective-permute-start | bytes 786440 | tf_op jit(solution)/shard_map/ppermute | solution.py:406
  104.3 7.6 %collective-permute-done.2.more_ref = bf16[2,16,2,16,128]{4,3,2,1,0:T(8,128)(2,1)S(1)} collective-permute-done((bf16[2,16,2,16,128]{4,3,2,1,0:T(8,128)(2,1)S(1)}, bf16[2,16,2,16,128]{4,3,2,1,0:T(8,128)(2,1)S(1)}, u32[]{:S(2)}, u32[]{:S(2)}) %collective-permute-start.2) | collective-permute-done | bytes 262176 | tf_op jit(solution)/shard_map/ppermute | solution.py:406
  112.9 4.0 %shard_map.170 = (bf16[256,512]{1,0:T(8,128)(2,1)}, bf16[256,512]{1,0:T(8,128)(2,1)}, bf16[128,512]{1,0:T(8,128)(2,1)}, bf16[128,512]{1,0:T(8,128)(2,1)}, bf16[1...) custom-call(s32[1]{0:T(128)} %bitcast.core_ref, bf16[2,2,256,512]{3,2,1,0:T(8,128)(2,1)} %copy-done.1, ...), custom_call_target="tpu_custom_call" | custom-call | flops 603979776 | bytes 5242880 | tf_op jit(solution)/shard_map/pallas_call | solution.py:197
  116.9 21.5 %all-to-all-start.6 = ((bf16[32,16,128]{2,1,0:T(8,128)(2,1)}), bf16[32,16,128]{2,1,0:T(8,128)(2,1)S(1)}, u32[]{:S(2)}, u32[]{:S(2)}) async-start(bf16[32,16,128]{2,1,0:T(8,128)(2,1)} %get-tuple-element.44), calls=%async_computation.6 | async-start | bytes 262144 | tf_op jit(solution)/shard_map/all_to_all | solution.py:411
  138.4 3.3 %collective-permute-start.3 = (bf16[256,512]{1,0:T(8,128)(2,1)}, bf16[256,512]{1,0:T(8,128)(2,1)S(1)}, u32[]{:S(2)}, u32[]{:S(2)}) collective-permute-start(bf16[256,512]{1,0:T(8,128)(2,1)} %get-tuple-element.34), channel_id=1, source_target_pairs={{0,8},{8,0},{1,9},{9,1},{2,10},{10,2},{3,11},{11,3},{4,12},{12,4},... | collective-permute-start | bytes 786440 | tf_op jit(solution)/shard_map/ppermute | solution.py:414
  141.8 1.9 %collective-permute-start.4 = (bf16[128,512]{1,0:T(8,128)(2,1)}, bf16[128,512]{1,0:T(8,128)(2,1)S(1)}, u32[]{:S(2)}, u32[]{:S(2)}) collective-permute-start(bf16[128,512]{1,0:T(8,128)(2,1)} %get-tuple-element.36), channel_id=1, source_target_pairs={{16,8},{32,24},{48,40},{64,56},{80,72},{96,88},{112,104},{128,120}... | collective-permute-start | bytes 393224 | tf_op jit(solution)/shard_map/ppermute | solution.py:416
  143.7 1.3 collective-permute-start.5
  145.0 4.4 %shard_map.171 = (f32[384,1024]{1,0:T(8,128)}, f32[256,1024]{1,0:T(8,128)}) custom-call(s32[1]{0:T(128)} %bitcast.12.h_ref, f32[384,1024]{1,0:T(8,128)} %shard_map.167.freq_ref, bf16[2,16,2,16,128]{4,3,2,1,0:T(8,128)(2,1)} %copy-done.5, bf16[2,16,2,16,128]{4,3,2,1,0:T(8,128)(2,1)} %copy-done.6, bf16[2,384,128]{2,1,0:T(8,128)(2,1)} %constant.32.clone.forward_ref, ...), custom_call_target="tpu_custom_call" | custom-call | flops 1024 | bytes 1024 | tf_op jit(solution)/shard_map/pallas_call | solution.py:240
  150.7 1.4 collective-permute-done.5.far_ref
  152.8 5.2 %shard_map.172 = (bf16[256,1024]{1,0:T(8,128)(2,1)}, bf16[256,1024]{1,0:T(8,128)(2,1)}) custom-call(s32[1]{0:T(128)} %bitcast.core_ref, bf16[256,512]{1,0:T(8,128)(2,1)} %get-tuple-element.33.keep_ref, bf16[256,512]{1,0:T(8,128)(2,1)} %copy-done.8, bf16[128,512]{1,0:T(8,128)(2,1)} %get-tuple-element.35.inner_ref, bf16[128,512]{1,0:T(8,128)(2,1)} %copy-done.9, ...), custom_call_target="tpu_custom_call" | custom-call | flops 1024 | bytes 1024 | tf_op jit(solution)/shard_map/pallas_call | solution.py:303
  (54 shorter events, 11.9 us)
Async XLA Ops:
  7.2 79.7 %all-gather.3.cloned.1.call-start = ((), (), s32[]{:S(2)}) async-start(), calls=%async_computation.7 | async-start | bytes 2785280 | tf_op jit(solution)/shard_map/all_gather | solution.py:378
  22.6 1.8 %copy-start.3 = (bf16[256,1024]{1,0:T(8,128)(2,1)S(1)}, bf16[256,1024]{1,0:T(8,128)(2,1)}, u32[]{:S(2)}) copy-start(bf16[256,1024]{1,0:T(8,128)(2,1)} %gate_in_ref) | copy-start | bytes 1572868
  23.9 0.9 copy-start.4
  25.6 5.0 %copy-start.2 = (bf16[256,1024]{1,0:T(8,128)(2,1)S(1)}, bf16[256,1024]{1,0:T(8,128)(2,1)}, u32[]{:S(2)}) copy-start(bf16[256,1024]{1,0:T(8,128)(2,1)} %param.17) | copy-start | bytes 1572868
  25.6 8.3 %copy-start.7 = (bf16[256,512]{1,0:T(8,128)(2,1)S(1)}, bf16[256,512]{1,0:T(8,128)(2,1)}, u32[]{:S(2)}) copy-start(bf16[256,512]{1,0:T(8,128)(2,1)} %param.15) | copy-start | bytes 786436
  26.7 5.9 %all-to-all-start.2 = ((bf16[2,2,256,512]{3,2,1,0:T(8,128)(2,1)}), bf16[2,2,256,512]{3,2,1,0:T(8,128)(2,1)S(1)}, u32[]{:S(2)}, u32[]{:S(2)}) async-start(bf16[2,2,256,512]{3,2,1,0:T(8,128)(2,1)} %bitcast.8), calls=%async_computation.2 | async-start | bytes 2097152 | tf_op jit(solution)/shard_map/all_to_all | solution.py:385
  30.6 11.7 %collective-permute-start = (bf16[128,1024]{1,0:T(8,128)(2,1)S(1)}, bf16[128,1024]{1,0:T(8,128)(2,1)S(1)}, u32[]{:S(2)}, u32[]{:S(2)}) collective-permute-start(bf16[128,1024]{1,0:T(8,128)(2,1)S(1)} %slice.9), channel_id=1, source_target_pairs={{0,8},{8,16},{16,24},{24,32},{32,40},{40,48},{48,56},{56,64},{64,7... | collective-permute-start | bytes 786440 | tf_op jit(solution)/shard_map/ppermute | solution.py:382
  32.6 6.1 %copy-start = (bf16[2,2,256,512]{3,2,1,0:T(8,128)(2,1)}, bf16[2,2,256,512]{3,2,1,0:T(8,128)(2,1)S(1)}, u32[]{:S(2)}) copy-start(bf16[2,2,256,512]{3,2,1,0:T(8,128)(2,1)S(1)} %all-to-all-done.2.tok_ref) | copy-start | bytes 3145732
  32.6 6.1 %collective-permute-start.1 = (bf16[128,512]{1,0:T(8,128)(2,1)S(1)}, bf16[128,512]{1,0:T(8,128)(2,1)S(1)}, u32[]{:S(2)}, u32[]{:S(2)}) collective-permute-start(bf16[128,512]{1,0:T(8,128)(2,1)S(1)} %slice_bitcast_fusion.1), channel_id=1, source_target_pairs={{0,16},{16,32},{32,48},{48,64},{64,80},{80,96},{96,112},{112,128},... | collective-permute-start | bytes 393224 | tf_op jit(solution)/shard_map/ppermute | solution.py:389
  34.9 11.5 %all-to-all-start.1 = ((bf16[2,2,256,128]{3,1,2,0:T(2,128)(2,1)}), bf16[2,2,256,128]{3,1,2,0:T(2,128)(2,1)S(1)}, u32[]{:S(2)}, u32[]{:S(2)}) async-start(bf16[2,2,256,128]{3,1,2,0:T(2,128)(2,1)} %copy.30), calls=%async_computation.1 | async-start | bytes 524288 | tf_op jit(solution)/shard_map/all_to_all | solution.py:379
  38.7 0.7 copy-start.11
  92.5 19.3 %all-to-all-start.5 = ((bf16[2,2,256,512]{3,2,1,0:T(8,128)(2,1)}), bf16[2,2,256,512]{3,2,1,0:T(8,128)(2,1)S(1)}, u32[]{:S(2)}, u32[]{:S(2)}) async-start(bf16[2,2,256,512]{3,2,1,0:T(8,128)(2,1)} %bitcast.28), calls=%async_computation.5 | async-start | bytes 2097152 | tf_op jit(solution)/shard_map/all_to_all | solution.py:402
  99.4 45.6 %copy-start.5 = (bf16[2,16,2,16,128]{4,3,2,1,0:T(8,128)(2,1)}, bf16[2,16,2,16,128]{4,3,2,1,0:T(8,128)(2,1)S(1)}, u32[]{:S(2)}) copy-start(bf16[2,16,2,16,128]{4,3,2,1,0:T(8,128)(2,1)S(1)} %bitcast_bitcast_fusion.tap_ref) | copy-start | bytes 786436
  99.4 12.4 %collective-permute-start.2 = (bf16[2,16,2,16,128]{4,3,2,1,0:T(8,128)(2,1)S(1)}, bf16[2,16,2,16,128]{4,3,2,1,0:T(8,128)(2,1)S(1)}, u32[]{:S(2)}, u32[]{:S(2)}) collective-permute-start(bf16[2,16,2,16,128]{4,3,2,1,0:T(8,128)(2,1)S(1)} %bitcast_bitcast_fusion.tap_ref), channel_id=1, source_target_pairs={{0,16},{16,0},{1,17},{17,1},{2,18},{18,2},{3,19},{19,3},{4,20},{20... | collective-permute-start | bytes 786440 | tf_op jit(solution)/shard_map/ppermute | solution.py:406
  111.8 33.2 %copy-start.6 = (bf16[2,16,2,16,128]{4,3,2,1,0:T(8,128)(2,1)}, bf16[2,16,2,16,128]{4,3,2,1,0:T(8,128)(2,1)S(1)}, u32[]{:S(2)}) copy-start(bf16[2,16,2,16,128]{4,3,2,1,0:T(8,128)(2,1)S(1)} %collective-permute-done.2.more_ref) | copy-start | bytes 786436
  111.9 1.0 copy-start.1
  116.9 41.1 %all-to-all-start.6 = ((bf16[32,16,128]{2,1,0:T(8,128)(2,1)}), bf16[32,16,128]{2,1,0:T(8,128)(2,1)S(1)}, u32[]{:S(2)}, u32[]{:S(2)}) async-start(bf16[32,16,128]{2,1,0:T(8,128)(2,1)} %get-tuple-element.44), calls=%async_computation.6 | async-start | bytes 262144 | tf_op jit(solution)/shard_map/all_to_all | solution.py:411
  138.4 13.6 %collective-permute-start.3 = (bf16[256,512]{1,0:T(8,128)(2,1)}, bf16[256,512]{1,0:T(8,128)(2,1)S(1)}, u32[]{:S(2)}, u32[]{:S(2)}) collective-permute-start(bf16[256,512]{1,0:T(8,128)(2,1)} %get-tuple-element.34), channel_id=1, source_target_pairs={{0,8},{8,0},{1,9},{9,1},{2,10},{10,2},{3,11},{11,3},{4,12},{12,4},... | collective-permute-start | bytes 786440 | tf_op jit(solution)/shard_map/ppermute | solution.py:414
  141.8 8.9 %collective-permute-start.4 = (bf16[128,512]{1,0:T(8,128)(2,1)}, bf16[128,512]{1,0:T(8,128)(2,1)S(1)}, u32[]{:S(2)}, u32[]{:S(2)}) collective-permute-start(bf16[128,512]{1,0:T(8,128)(2,1)} %get-tuple-element.36), channel_id=1, source_target_pairs={{16,8},{32,24},{48,40},{64,56},{80,72},{96,88},{112,104},{128,120}... | collective-permute-start | bytes 393224 | tf_op jit(solution)/shard_map/ppermute | solution.py:416
  143.7 8.3 %collective-permute-start.5 = (bf16[128,512]{1,0:T(8,128)(2,1)}, bf16[128,512]{1,0:T(8,128)(2,1)S(1)}, u32[]{:S(2)}, u32[]{:S(2)}) collective-permute-start(bf16[128,512]{1,0:T(8,128)(2,1)} %get-tuple-element.37), channel_id=1, source_target_pairs={{24,8},{40,24},{56,40},{72,56},{88,72},{104,88},{120,104},{136,120... | collective-permute-start | bytes 393224 | tf_op jit(solution)/shard_map/ppermute | solution.py:417
  150.7 1.4 copy-start.9
  152.1 0.6 copy-start.10
  152.1 0.7 copy-start.8
Sparse Core Ops, SparseCore 0:
  21.4 65.1 all-gather.2
